TPU v7x, 256 devices: a whole 4x4x8 slice. The times are simulated.
256 devices in a mesh: dom: 16 (over x, z_hi), col: 16 (over y, z_lo, core).
Axes of the slice: x: 4, y: 4, z: 8 (z_hi: 4, z_lo: 2; z = z_hi * 2 + z_lo), core: 2. Of those that a mesh axis runs over, the one named last changes fastest.
Arguments:
- features: float32 [32768, 1024], P('dom', 'col'), may hold values from -6 to 6
- neighbours: int32 [128, 7], replicated, may hold values from 0 to 127, as said below
- tiles: bfloat16 [128, 8, 256, 256], P('dom'), may hold values from -0.125 to 0.125
- weight: float32 [1024, 1024], P(None, 'col'), may hold values from -0.1875 to 0.1875
- cotangent: float32 [32768, 1024], P('dom', 'col'), may hold values from -6 to 6
Outputs:
- hidden: float32 [32768, 1024], P('dom', 'col')
- grad_features: float32 [32768, 1024], P('dom', 'col')
- grad_weight: float32 [1024, 1024], P('dom', 'col')
Inputs may be any that keep to these rules, and one draw needn't show every extreme that they name: `neighbours`: row blocks i of one index of dom are i from d * 8 to (d + 1) * 8 - 1 for index d, which also holds those node blocks. No entry of a row block names a block of its own index of dom, and the row blocks of one index of dom name blocks of any one other index at most 4 times in all, counting repeats; that many is reached in every draw.
All inputs are finite; a program needn't handle non-finite values.
Results may differ from a plain program's by a relative error of at most 0.0003.
Values sent between devices are 32-bit elements; how exact they have to be, the bound alone decides.
No kernel may reach another device: no remote copies, remote signals or barrier semaphores. Data moves between devices by JAX's collectives and lax.ppermute only.
A program may use at most 128 MiB of HBM per device.

v0:
```python
import jax
import jax.numpy as jnp
from jax import lax
from jax.sharding import PartitionSpec as P


def on_device(features, neighbours, tiles, weight, cotangent):
    highest = lax.Precision.HIGHEST
    blk = tiles.shape[0]
    fan = tiles.shape[1]
    width = tiles.shape[2]
    cols = features.shape[1]
    rows = blk * width
    groups = lax.axis_size("dom")
    me = lax.axis_index("dom")
    refs = blk * (fan - 1)
    mine = lax.dynamic_slice_in_dim(neighbours, me * blk, blk, 0)
    my_blocks = features.reshape(blk, width, cols)
    tiles_wide = tiles.astype(jnp.float32)
    whole = lax.all_gather(features, "dom", axis=0, tiled=True).reshape(groups * blk, width, cols)
    remote = whole[mine]
    picked = jnp.concatenate([my_blocks[:, None], remote], axis=1)
    mixed = jnp.einsum("ikab,ikbc->iac", tiles_wide, picked, precision=highest).reshape(rows, cols)
    piece = lax.all_gather(mixed, "col", axis=1, tiled=True)
    total = jnp.dot(piece, weight, precision=highest, preferred_element_type=jnp.float32)
    pre = total
    sig = jax.nn.sigmoid(pre)
    hidden = pre * sig
    slope = cotangent * sig * (1.0 + pre * (1.0 - sig))
    strip = piece
    grad_weight = lax.psum_scatter(
        lax.dot_general(
            strip,
            slope,
            (((0,), (0,)), ((), ())),
            precision=highest,
            preferred_element_type=jnp.float32,
        ),
        "dom",
        scatter_dimension=0,
        tiled=True,
    )
    strip = weight
    blocks_in = lax.psum_scatter(
        lax.dot_general(
            strip,
            slope,
            (((1,), (1,)), ((), ())),
            precision=highest,
            preferred_element_type=jnp.float32,
        ),
        "col",
        scatter_dimension=0,
        tiled=True,
    ).T.reshape(blk, width, cols)
    contrib = jnp.einsum("ikab,iac->ikbc", tiles_wide, blocks_in, precision=highest)
    local = contrib[:, 0]
    others = contrib[:, 1:].reshape(refs, width, cols)
    total = jax.ops.segment_sum(others, mine.reshape(refs), num_segments=groups * blk)
    returned = lax.psum_scatter(
        total.reshape(groups * blk * width, cols), "dom", scatter_dimension=0, tiled=True
    ).reshape(blk, width, cols)
    grad_features = (local + returned).reshape(rows, cols)
    return (hidden, grad_features, grad_weight)


def solution(mesh):
    in_specs = (P("dom", "col"), P(), P("dom", None, None, None), P(None, "col"), P("dom", "col"))
    out_specs = (P("dom", "col"), P("dom", "col"), P("dom", "col"))
    return jax.shard_map(
        on_device, mesh=mesh, in_specs=in_specs, out_specs=out_specs, check_vma=False
    )
```

profile of v0, /device:TPU:10, one launch (start us, length us, event | category | flops | bytes accessed | tf_op | source)
XLA Modules:
  0.0 589.9 jit_solution(17888407402754259926)
XLA Ops:
  7.2 0.0 copy-start
  7.2 0.0 all-gather.3.cloned.1.call-start
  7.2 0.7 all-gather.3.cloned.1.call-update
  7.9 0.0 all-gather.5.cloned.1.call-start
  8.0 0.8 compare_select_fusion
  8.7 0.1 copy.26
  8.8 0.1 reshape.31
  8.9 1.2 copy.43
  10.1 0.2 copy.28
  10.3 106.2 %all-gather.3.cloned.1.call-done = f32[32768,64]{0,1:T(8,128)} async-done(((f32[2048,64]{0,1:T(8,128)}), f32[32768,64]{0,1:T(8,128)}) %all-gather.3.cloned.1.call-update) | async-done | bytes 8388624 | tf_op jit(solution)/shard_map/all_gather | solution.py:20
  116.5 7.9 %copy.47 = f32[8,128,8,256]{3,2,0,1:T(8,128)} copy(f32[8,128,8,256]{3,2,1,0:T(8,128)} %bitcast.51) | data formatting | bytes 16777216 | tf_op jit(solution)/shard_map/reshape | solution.py:20
  124.4 6.0 %gather_fusion = f32[56,256,64]{1,2,0:T(8,128)} fusion(f32[128,256,64]{1,2,0:T(8,128)} %bitcast.50, s32[1024]{0:T(1024)S(1)} %pad_clamp_fusion), kind=kCustom, calls=%fused_computation | custom fusion | bytes 7340256 | tf_op jit(solution)/shard_map/gather | solution.py:21
  130.3 12.2 %fusion.4 = f32[8,8,8,256]{3,2,1,0:T(8,128)S(1)} fusion(bf16[8,8,256,256]{3,2,1,0:T(8,128)(2,1)} %param.7, f32[8,7,256,64]{2,3,1,0:T(8,128)} %bitcast.49, f32[8,1,256,64]{2,3,1,0:T(8,128)S(1)} %copy.28), kind=kOutput, calls=%fused_computation.9 | convolution fusion | flops 3222274048 | bytes 13107200 | tf_op jit(solution)/shard_map/ikab,ikbc->iac/dot_general | solution.py:23
  142.5 0.0 copy-start.3
  142.5 0.8 copy.41
  143.4 0.0 all-gather.5.cloned.1.call-update
  143.4 0.2 reduce-scatter.10.cloned.1.call-start
  143.6 66.3 %all-gather.5.cloned.1.call-done = f32[2048,1024]{0,1:T(8,128)} async-done(((f32[2048,64]{0,1:T(8,128)}), f32[2048,1024]{0,1:T(8,128)}) %all-gather.5.cloned.1.call-update) | async-done | bytes 8388624 | tf_op jit(solution)/shard_map/all_gather | solution.py:24
  209.9 0.0 copy-done
  209.9 8.8 %fusion.7 = (f32[2048,64]{0,1:T(8,128)}, f32[2048,64]{0,1:T(8,128)S(1)}) fusion(f32[2048,1024]{0,1:T(8,128)} %all-gather.5.cloned.1.call-done, f32[1024,64]{0,1:T(8,128)S(1)} %copy-done), kind=kOutput, calls=%fused_computation.12 | convolution fusion | flops 1611137024 | bytes 9699328 | tf_op jit(solution)/shard_map/dot_general | solution.py:25
  218.7 0.0 copy-done.3
  218.7 9.0 %convolution_bitcast_fusion = f32[1024,2048]{0,1:T(8,128)} fusion(f32[1024,64]{0,1:T(8,128)S(1)} %copy-done, f32[2048,64]{0,1:T(8,128)S(1)} %get-tuple-element.6, f32[2048,64]{0,1:T(8,128)S(1)} %copy-done.3), kind=kOutput, calls=%fused_computation.3 | convolution fusion | flops 1611661312 | bytes 9699328 | tf_op jit(solution)/shard_map/dot_general | solution.py:45
  227.7 9.1 %copy.38 = f32[1024,2048]{1,0:T(8,128)} copy(f32[1024,2048]{0,1:T(8,128)} %convolution_bitcast_fusion) | data formatting | bytes 16777216
  236.8 0.0 reduce-scatter.10.cloned.1.call-update
  236.8 0.0 reduce-scatter.6.cloned.1.call-start
  236.9 0.1 copy.32
  237.0 0.1 reshape.39
  237.0 99.2 %reduce-scatter.10.cloned.1.call-done = f32[64,2048]{1,0:T(8,128)} async-done(((f32[1024,2048]{1,0:T(8,128)}), f32[64,2048]{1,0:T(8,128)}) %reduce-scatter.10.cloned.1.call-update) | async-done | bytes 524304
  336.2 1.4 copy.39
  337.6 6.9 %convolution_bitcast_fusion.1 = f32[8,8,256,64]{2,3,1,0:T(8,128)S(1)} fusion(f32[8,256,64,1]{2,1,3,0:T(8,128)S(1)} %bitcast.52, bf16[8,8,256,256]{3,2,1,0:T(8,128)(2,1)} %param.7), kind=kOutput, calls=%fused_computation.8 | convolution fusion | flops 3221225472 | bytes 13107200 | tf_op jit(solution)/shard_map/ikab,iac->ikbc/dot_general | solution.py:56
  344.5 0.0 copy-start.2
  344.6 2.0 copy-done.2
  346.5 2.2 slice.11
  348.8 4.3 broadcast_in_dim.7
  353.0 13.1 %scatter_fusion = f32[128,256,64]{1,2,0:T(8,128)} fusion(f32[128,256,64]{1,2,0:T(8,128)} %broadcast_in_dim.7, s32[56]{0:T(128)S(1)} %reshape.39, f32[56,256,64]{1,2,0:T(8,128)} %bitcast.48), kind=kCustom, calls=%fused_computation.1 | custom fusion | flops 917504 | bytes 11010272 | tf_op jit(solution)/shard_map/scatter-add | solution.py:59
  366.2 7.4 %copy.42 = f32[128,8,8,256]{3,2,0,1:T(8,128)} copy(f32[128,8,8,256]{3,2,1,0:T(8,128)} %bitcast.46) | data formatting | bytes 16777216 | tf_op jit(solution)/shard_map/reshape | solution.py:61
  373.6 0.0 reduce-scatter.6.cloned.1.call-update
  373.6 0.0 copy-start.1
  373.6 0.3 reduce-scatter.8.cloned.1.call-start
  373.9 9.7 %fusion.9 = f32[1024,64]{1,0:T(8,128)} fusion(f32[2048,1024]{0,1:T(8,128)} %all-gather.5.cloned.1.call-done, f32[2048,64]{0,1:T(8,128)S(1)} %get-tuple-element.6, f32[2048,64]{0,1:T(8,128)S(1)} %copy-done.3), kind=kOutput, calls=%fused_computation.17 | convolution fusion | flops 1611661312 | bytes 9699328 | tf_op jit(solution)/shard_map/dot_general | solution.py:32
  383.6 0.0 reduce-scatter.8.cloned.1.call-update
  383.7 1.1 slice_bitcast_fusion
  384.8 111.3 %reduce-scatter.6.cloned.1.call-done = f32[2048,64]{0,1:T(8,128)} async-done(((f32[32768,64]{0,1:T(8,128)}), f32[2048,64]{0,1:T(8,128)}) %reduce-scatter.6.cloned.1.call-update) | async-done | bytes 524304 | tf_op jit(solution)/shard_map/reduce_scatter | solution.py:60
  496.0 1.9 add.32
  497.9 85.5 %reduce-scatter.8.cloned.1.call-done = f32[64,64]{1,0:T(8,128)} async-done(((f32[1024,64]{1,0:T(8,128)}), f32[64,64]{1,0:T(8,128)}) %reduce-scatter.8.cloned.1.call-update) | async-done | bytes 16400 | tf_op jit(solution)/shard_map/reduce_scatter | solution.py:31
  583.4 0.0 copy-done.1
  (2 shorter events, 0.0 us)
Async XLA Ops:
  7.2 202.8 %copy-start = (f32[1024,64]{0,1:T(8,128)S(1)}, f32[1024,64]{0,1:T(8,128)}, u32[]{:S(2)}) copy-start(f32[1024,64]{0,1:T(8,128)} %param.8) | copy-start | bytes 786436
  7.2 109.3 %all-gather.3.cloned.1.call-start = ((), (), s32[]{:S(2)}) async-start(), calls=%async_computation.3 | async-start | bytes 8912896 | tf_op jit(solution)/shard_map/all_gather | solution.py:20
  7.9 202.0 %all-gather.5.cloned.1.call-start = ((), (), s32[]{:S(2)}) async-start(), calls=%async_computation.4 | async-start | bytes 8912896 | tf_op jit(solution)/shard_map/all_gather | solution.py:24
  142.5 76.2 %copy-start.3 = (f32[2048,64]{0,1:T(8,128)S(1)}, f32[2048,64]{0,1:T(8,128)}, u32[]{:S(2)}) copy-start(f32[2048,64]{0,1:T(8,128)} %param.9) | copy-start | bytes 1572868
  143.4 192.8 %reduce-scatter.10.cloned.1.call-start = ((), (), s32[]{:S(2)}) async-start(), calls=%async_computation.7 | async-start | bytes 8912896
  236.8 259.2 %reduce-scatter.6.cloned.1.call-start = ((), (), s32[]{:S(2)}) async-start(), calls=%async_computation.5 | async-start | bytes 8912896 | tf_op jit(solution)/shard_map/reduce_scatter | solution.py:60
  344.5 2.0 copy-start.2
  373.6 209.8 %copy-start.1 = (f32[1024,64]{0,1:T(8,128)S(1)}, f32[1024,64]{0,1:T(8,128)}, u32[]{:S(2)}) copy-start(f32[1024,64]{0,1:T(8,128)} %param.8) | copy-start | bytes 786436
  373.6 209.8 %reduce-scatter.8.cloned.1.call-start = ((), (), s32[]{:S(2)}) async-start(), calls=%async_computation.6 | async-start | bytes 557056 | tf_op jit(solution)/shard_map/reduce_scatter | solution.py:31
Sparse Core Ops, SparseCore 0:
  10.5 105.9 all-gather.2
  143.5 66.3 all-gather.4
  237.0 99.2 reduce-scatter.9
  373.7 122.2 reduce-scatter.5
  499.9 83.4 reduce-scatter.7
where the time goes:
time: 591 us; the launch traced here: 590 us
  waiting for transfers between devices  469 us (79%)
  matrix products  46.6 us (8%)
  local copies, waits for them, and re-layouts  44 us (7%)
  other arithmetic  15.8 us (3%)
  between operations  13.9 us (2%)
    reduce_scatter x1, waiting for transfers between devices, on_device(): lax.psum_scatter(total.reshape(groups * blk * width, cols), 'dom', scatte...  111 us
    all_gather x1, waiting for transfers between devices, on_device(): lax.all_gather(features, 'dom', axis=0, tiled=True)  106 us
    unnamed x6, waiting for transfers between devices  99.9 us
    reduce_scatter x1, waiting for transfers between devices, on_device(): lax.psum_scatter(lax.dot_general(strip, slope, (((0,), (0,)), ((), ())),...  85.5 us
    all_gather x1, waiting for transfers between devices, on_device(): piece = lax.all_gather(mixed, 'col', axis=1, tiled=True)  66.3 us
    unnamed x13, local copies, waits for them, and re-layouts  14.8 us
    scatter-add x1, other arithmetic, on_device(): jax.ops.segment_sum(others, mine.reshape(refs), num_segments=groups * blk)  13.1 us
    dot_general x1, matrix products, on_device(): jnp.einsum('ikab,ikbc->iac', tiles_wide, picked, precision=highest)  12.2 us
  transfers between devices with their start and end apart: 5, of which 5 were waited for; matrix products, arithmetic and copies ran while one was open for 3% of the time, Pallas kernels for 0%

commit v1 on v0

v1 whole, which is shorter than its diff:
```python
import functools

import jax
import jax.numpy as jnp
from jax import lax
from jax.experimental import pallas as pl
from jax.experimental.pallas import tpu as pltpu
from jax.sharding import Mesh
from jax.sharding import PartitionSpec as P

DOM = ("x", "zh")
COL = ("y", "zl", "c")
NX, NZ, NY = 4, 4, 4
BLK, FAN, W, C = 8, 8, 256, 64
REFS = BLK * (FAN - 1)
SLOTS = 4
F = 1024
CHUNK = 128
f32, bf16 = jnp.float32, jnp.bfloat16
VMEM = pl.BlockSpec(memory_space=pltpu.VMEM)
SMEM = pl.BlockSpec(memory_space=pltpu.SMEM)
ANY = pl.BlockSpec(memory_space=pl.ANY)
PARAMS = pltpu.CompilerParams(vmem_limit_bytes=40 * 2**20)


def split(value):
    hi = value.astype(bf16)
    lo = (value - hi.astype(f32)).astype(bf16)
    return hi, lo


def tables(neighbours):
    me_x, me_z = lax.axis_index("x"), lax.axis_index("zh")
    rows = neighbours.reshape(NX, NZ, REFS)
    rows = lax.dynamic_index_in_dim(rows, me_z, 1, keepdims=False)
    owner, block = rows >> 3, rows & 7
    ref = jnp.arange(REFS)
    same = (owner[:, :, None] == owner[:, None, :]) & (ref[None, :, None] > ref[None, None, :])
    rank = jnp.sum(same.astype(jnp.int32), axis=2)
    wanted = me_x * NZ + ((me_z + jnp.arange(NZ)) & (NZ - 1))
    match = (owner[None, :, None, :] == wanted[:, None, None, None]) & (
        rank[None, :, None, :] == jnp.arange(SLOTS)[None, None, :, None]
    )
    table = jnp.sum(jnp.where(match, block[None, :, None, :] + 1, 0), axis=3)
    mine = lax.dynamic_index_in_dim(owner, me_x, 0, keepdims=False)
    my_rank = lax.dynamic_index_in_dim(rank, me_x, 0, keepdims=False)
    e, xs = ((mine & 3) - me_z) & 3, mine >> 2
    start = jnp.where(e == 0, 0, jnp.where(e == 2, 48, 16 + (e >> 1) * 4))
    stride = jnp.where((e & 1) == 1, 8, 4)
    where_ = start + xs * stride + my_rank
    near = table[0].reshape(16)
    mid = jnp.stack([table[1], table[3]], axis=1).reshape(32)
    far = table[2].reshape(16)
    return near, mid, far, jnp.clip(where_, 0, 63)


def pick_kernel(count, index_ref, *refs):
    sources, out, sems = refs[:count], refs[count], refs[count + 1]
    total = out.shape[0]
    copies = []
    for slot in range(total):
        source = sources[(slot // SLOTS) % count]
        index = jnp.clip(index_ref[slot] - 1, 0, BLK - 1)
        copies.append(pltpu.make_async_copy(source.at[index], out.at[slot], sems.at[slot]))
    for copy in copies:
        copy.start()
    for copy in copies:
        copy.wait()


def pick(index, *sources):
    total = NX * SLOTS * len(sources)
    return pl.pallas_call(
        functools.partial(pick_kernel, len(sources)),
        out_shape=jax.ShapeDtypeStruct((total, C, W), f32),
        in_specs=[SMEM] + [ANY] * len(sources),
        out_specs=ANY,
        scratch_shapes=[pltpu.SemaphoreType.DMA((total,))],
        cost_estimate=pl.CostEstimate(flops=0, bytes_accessed=total * C * W * 8, transcendentals=0),
    )(index, *sources)


def mixed_kernel(where_ref, own_ref, near_ref, mid_ref, far_ref, tiles_ref, out_ref, held, sems):
    i = pl.program_id(0)

    @pl.when(i == 0)
    def _():
        copies = [
            pltpu.make_async_copy(near_ref, held.at[pl.ds(0, 16)], sems.at[0]),
            pltpu.make_async_copy(mid_ref, held.at[pl.ds(16, 32)], sems.at[1]),
            pltpu.make_async_copy(far_ref, held.at[pl.ds(48, 16)], sems.at[2]),
        ]
        for copy in copies:
            copy.start()
        for copy in copies:
            copy.wait()

    acc = None
    for k in range(FAN):
        block = own_ref[0] if k == 0 else held[where_ref[i * (FAN - 1) + k - 1]]
        part = lax.dot_general(
            jnp.concatenate(split(block), axis=0),
            tiles_ref[0, k],
            (((1,), (1,)), ((), ())),
            preferred_element_type=f32,
        )
        acc = part if acc is None else acc + part
    value = acc[:C] + acc[C:]
    out_ref[0] = value[:, :CHUNK]
    out_ref[1] = value[:, CHUNK:]


def mix(where_, own, near, mid, far, tiles):
    return pl.pallas_call(
        mixed_kernel,
        grid_spec=pltpu.PrefetchScalarGridSpec(
            num_scalar_prefetch=1,
            grid=(BLK,),
            in_specs=[
                pl.BlockSpec((1, C, W), lambda i, s: (i, 0, 0)),
                ANY,
                ANY,
                ANY,
                pl.BlockSpec((1, FAN, W, W), lambda i, s: (i, 0, 0, 0)),
            ],
            out_specs=pl.BlockSpec((2, C, CHUNK), lambda i, s: (i, 0, 0)),
            scratch_shapes=[pltpu.VMEM((64, C, W), f32), pltpu.SemaphoreType.DMA((3,))],
        ),
        out_shape=jax.ShapeDtypeStruct((16, C, CHUNK), f32),
        compiler_params=PARAMS,
        cost_estimate=pl.CostEstimate(flops=2 * 64 * W * W * 2 * C, bytes_accessed=13 << 20, transcendentals=0),
    )(where_, own, near, mid, far, tiles)


def weight_kernel(in_ref, thi_ref, tlo_ref, hi_ref, lo_ref):
    value = in_ref[...]
    thi_ref[...], tlo_ref[...] = split(value)
    hi_ref[...], lo_ref[...] = split(value.T)


def weight_parts(transposed):
    step = 256
    by_row = pl.BlockSpec((step, F), lambda i: (i, 0))
    by_col = pl.BlockSpec((F, step), lambda i: (0, i))
    return pl.pallas_call(
        weight_kernel,
        grid=(F // step,),
        in_specs=[by_row],
        out_specs=[by_row, by_row, by_col, by_col],
        out_shape=[jax.ShapeDtypeStruct((F, F), bf16)] * 4,
        compiler_params=PARAMS,
        cost_estimate=pl.CostEstimate(flops=F * F * 8, bytes_accessed=12 << 20, transcendentals=0),
    )(transposed)


def dense_kernel(thi_ref, tlo_ref, hi_ref, lo_ref, mixed_ref, cot_ref, hidden_ref, slope_ref, back_ref, parts):
    step = pl.program_id(0)

    @pl.when(step == 0)
    def _():
        hi, lo = split(mixed_ref[...])
        parts[:, :CHUNK] = hi
        parts[:, CHUNK:] = lo

    both = jnp.dot(thi_ref[...], parts[...], preferred_element_type=f32)
    low = jnp.dot(tlo_ref[...], parts[:, :CHUNK], preferred_element_type=f32)
    pre = both[:, :CHUNK] + (both[:, CHUNK:] + low)
    sig = jax.nn.sigmoid(pre)
    hidden_ref[...] = pre * sig
    slope = cot_ref[...] * sig * (1.0 + pre * (1.0 - sig))
    slope_ref[...] = slope
    shi, slo = split(slope)
    both = jnp.dot(hi_ref[...], jnp.concatenate([shi, slo], axis=1), preferred_element_type=f32)
    low = jnp.dot(lo_ref[...], shi, preferred_element_type=f32)
    part = both[:, :CHUNK] + (both[:, CHUNK:] + low)

    @pl.when(step == 0)
    def _():
        back_ref[...] = part

    @pl.when(step > 0)
    def _():
        back_ref[...] += part


def dense(weights, mixed, cot):
    step = 256
    by_row = pl.BlockSpec((step, F), lambda i: (i, 0))
    by_col = pl.BlockSpec((F, step), lambda i: (0, i))
    rows = pl.BlockSpec((step, CHUNK), lambda i: (i, 0))
    whole = pl.BlockSpec((F, CHUNK), lambda i: (0, 0))
    return pl.pallas_call(
        dense_kernel,
        grid=(F // step,),
        in_specs=[by_row, by_row, by_col, by_col, whole, rows],
        out_specs=[rows, rows, whole],
        out_shape=[jax.ShapeDtypeStruct((F, CHUNK), f32)] * 3,
        scratch_shapes=[pltpu.VMEM((F, 2 * CHUNK), bf16)],
        compiler_params=PARAMS,
        cost_estimate=pl.CostEstimate(flops=12 * F * F * CHUNK, bytes_accessed=10 << 20, transcendentals=F * CHUNK),
    )(*weights, mixed, cot)


def push_kernel(where_ref, back_ref, tiles_ref, diag_ref, near_ref, mid_ref, far_ref, held, sems):
    i = pl.program_id(0)
    block = jnp.concatenate([back_ref[0], back_ref[1]], axis=1)
    both = jnp.concatenate(split(block), axis=0)
    for k in range(FAN):
        part = jnp.dot(both, tiles_ref[0, k], preferred_element_type=f32)
        value = part[:C] + part[C:]
        if k == 0:
            diag_ref[0] = value
        else:
            held[where_ref[i * (FAN - 1) + k - 1]] = value

    @pl.when(i == BLK - 1)
    def _():
        copies = [
            pltpu.make_async_copy(held.at[pl.ds(48, 16)], far_ref, sems.at[0]),
            pltpu.make_async_copy(held.at[pl.ds(16, 32)], mid_ref, sems.at[1]),
            pltpu.make_async_copy(held.at[pl.ds(0, 16)], near_ref, sems.at[2]),
        ]
        for copy in copies:
            copy.start()
        for copy in copies:
            copy.wait()


def push(where_, back, tiles):
    return pl.pallas_call(
        push_kernel,
        grid_spec=pltpu.PrefetchScalarGridSpec(
            num_scalar_prefetch=1,
            grid=(BLK,),
            in_specs=[
                pl.BlockSpec((2, C, CHUNK), lambda i, s: (i, 0, 0)),
                pl.BlockSpec((1, FAN, W, W), lambda i, s: (i, 0, 0, 0)),
            ],
            out_specs=[pl.BlockSpec((1, C, W), lambda i, s: (i, 0, 0)), ANY, ANY, ANY],
            scratch_shapes=[pltpu.VMEM((64, C, W), f32), pltpu.SemaphoreType.DMA((3,))],
        ),
        out_shape=[jax.ShapeDtypeStruct((n, C, W), f32) for n in (BLK, 16, 32, 16)],
        compiler_params=PARAMS,
        cost_estimate=pl.CostEstimate(flops=2 * 64 * W * W * 2 * C, bytes_accessed=13 << 20, transcendentals=0),
    )(where_, back, tiles)


def gather_sum_kernel(slots, first, last, index_ref, *refs):
    got_ref, out_ref = refs[0], refs[-1]
    start = refs[1] if len(refs) == 3 else None
    for block in range(BLK):
        if first <= block < last:
            out_ref[block] = start[block - first]
        else:
            out_ref[block] = jnp.zeros((C, W), f32)
    for slot in slots:
        index = index_ref[slot]

        @pl.when(index > 0)
        def _():
            out_ref[index - 1] += got_ref[slot]


def gather_sum(index, got, slots, start=None, first=0):
    last = first if start is None else first + start.shape[0]
    args = (index, got) if start is None else (index, got, start)
    return pl.pallas_call(
        functools.partial(gather_sum_kernel, slots, first, last),
        out_shape=jax.ShapeDtypeStruct((BLK, C, W), f32),
        in_specs=[SMEM] + [VMEM] * (len(args) - 1),
        out_specs=VMEM,
        compiler_params=PARAMS,
        cost_estimate=pl.CostEstimate(flops=16 * C * W, bytes_accessed=3 << 20, transcendentals=0),
    )(*args)


def shift(value, axis, size, by):
    return lax.ppermute(value, axis, [(i, (i + by) % size) for i in range(size)])


def over_x(value):
    count = value.shape[0] // NX
    out = lax.all_to_all(value.reshape(NX, count, C, W), "x", 0, 0, tiled=True)
    return out.reshape(value.shape)


def over_col(value):
    return lax.all_to_all(value, COL, 0, 0, tiled=True)


def on_device(features, neighbours, tiles, weight, cotangent):
    near_at, mid_at, far_at, where_ = tables(neighbours)
    own = features.T.reshape(C, BLK, W).transpose(1, 0, 2)

    up = shift(own, "zh", NZ, -1)
    down = shift(own, "zh", NZ, 1)
    near = over_x(pick(near_at, own))
    weights = weight_parts(lax.all_gather(weight.T, COL, axis=0, tiled=True))
    cot = over_col(cotangent.T.reshape(C, 16, CHUNK).transpose(1, 0, 2)).reshape(F, CHUNK)
    far_lo = shift(up[: BLK // 2], "zh", NZ, -1)
    far_hi = shift(down[BLK // 2 :], "zh", NZ, 1)
    mid = over_x(pick(mid_at, up, down))
    far = over_x(pick(far_at, jnp.concatenate([far_lo, far_hi], axis=0)))
    mixed = mix(where_, own, near, mid, far, tiles)

    mixed = over_col(mixed).reshape(F, CHUNK)
    hidden, slope, back = dense(weights, mixed, cot)
    back = over_col(back.reshape(16, C, CHUNK))
    hidden = over_col(hidden.reshape(16, C, CHUNK)).transpose(1, 0, 2).reshape(C, 16 * CHUNK).T

    diag, near, mid, far = push(where_, back, tiles)
    far = gather_sum(far_at, over_x(far), range(16))
    from_below = shift(far[: BLK // 2], "zh", NZ, 1)
    from_above = shift(far[BLK // 2 :], "zh", NZ, -1)
    mid = over_x(mid)
    up = gather_sum(mid_at, mid, [s for s in range(32) if s % 8 < 4], from_below, 0)
    down = gather_sum(mid_at, mid, [s for s in range(32) if s % 8 >= 4], from_above, BLK // 2)
    up = shift(up, "zh", NZ, 1)
    down = shift(down, "zh", NZ, -1)
    near = gather_sum(near_at, over_x(near), range(16), diag, 0)
    grad_features = (near + up + down).transpose(1, 0, 2).reshape(C, BLK * W).T

    me_c, me_l = lax.axis_index("c"), lax.axis_index("zl")
    by_core = slope.reshape(8, 2, C, CHUNK)

    def partial(core):
        rows = lax.dynamic_index_in_dim(by_core, core, 1, keepdims=False).reshape(8 * C, CHUNK)
        return lax.dot_general(
            rows, mixed, (((1,), (1,)), ((), ())), precision=lax.Precision.HIGH, preferred_element_type=f32
        )

    grad = partial(me_c) + shift(partial(1 - me_c), "c", 2, 1)
    grad = lax.all_to_all(grad.reshape(NY, 2 * C, F), "y", 0, 0, tiled=True).sum(axis=0).reshape(2, C, F)
    other = shift(lax.dynamic_index_in_dim(grad, 1 - me_l, 0, keepdims=False), "zl", 2, 1)
    grad = lax.dynamic_index_in_dim(grad, me_l, 0, keepdims=False) + other
    grad = grad.reshape(2, C // 2, 16, C).transpose(2, 1, 0, 3).reshape(16, C // 2, 2 * C)
    grad = lax.all_to_all(grad, DOM, 0, 0, tiled=True).sum(axis=0)
    grad_weight = grad.reshape(C // 2, 2, C).transpose(1, 0, 2).reshape(C, C).T
    return hidden, grad_features, grad_weight


def solution(mesh):
    fine = Mesh(mesh.devices.reshape(4, 4, 4, 2, 2), DOM + COL)
    in_specs = (P(DOM, COL), P(), P(DOM, None, None, None), P(None, COL), P(DOM, COL))
    out_specs = (P(DOM, COL), P(DOM, COL), P(DOM, COL))
    return jax.shard_map(on_device, mesh=fine, in_specs=in_specs, out_specs=out_specs, check_vma=False)
```

time: 591 us -> 430 us (0.73)
  waiting for transfers between devices: 469 us -> 96.8 us
  Pallas kernels: 0 us -> 154 us
  starting transfers between devices: 0.6 us -> 77.1 us
  matrix products: 46.6 us -> 6.29 us
  blocking collectives: 0 us -> 33 us
  other arithmetic: 15.8 us -> 7.27 us
  local copies, waits for them, and re-layouts: 44 us -> 37.9 us
    reduce_scatter x2 -> x0, waiting for transfers between devices: 197 us -> none  [the longest x1 111 us: on_device(): lax.psum_scatter(total.reshape(groups * blk * width, cols), 'dom', scatte...]
    all_gather x2 -> x1, waiting for transfers between devices: 172 us -> 0.01 us  [on_device(): weights = weight_parts(lax.all_gather(weight.T, COL, axis=0, tiled=True))]
    pallas_call x0 -> x11, Pallas kernels: none -> 154 us  [the longest x3 133 us: pick(): pl.pallas_call(functools.partial(pick_kernel, len(sources)), out_shape=ja...]
    unnamed x6 -> x1, waiting for transfers between devices: 99.9 us -> 0.68 us
    all_to_all x0 -> x10, waiting for transfers between devices: none -> 64.9 us  [the longest x5 39.4 us: over_x(): out = lax.all_to_all(value.reshape(NX, count, C, W), 'x', 0, 0, tiled=True)]
    all_to_all x0 -> x10, starting transfers between devices: none -> 56.3 us  [the longest x5 25.2 us: over_x(): out = lax.all_to_all(value.reshape(NX, count, C, W), 'x', 0, 0, tiled=True)]
    dot_general x5 -> x2, matrix products: 46.6 us -> 6.29 us  [partial(): lax.dot_general(rows, mixed, (((1,), (1,)), ((), ())), precision=lax.Prec...]
    all_to_all x0 -> x2, blocking collectives: none -> 33 us  [the longest x1 19.1 us: over_x(): out = lax.all_to_all(value.reshape(NX, count, C, W), 'x', 0, 0, tiled=True)]
  transfers between devices with their start and end apart: 5 -> 21, of which waited for: 5 -> 9; matrix products, arithmetic and copies ran while one was open for 3% -> 5% of each run, Pallas kernels for 0% -> 35%
where the time goes in v1:
time: 430 us; the launch traced here: 427 us
  Pallas kernels  154 us (36%)
  waiting for transfers between devices  96.8 us (23%)
  starting transfers between devices  77.1 us (18%)
  local copies, waits for them, and re-layouts  37.9 us (9%)
  blocking collectives  33 us (8%)
  between operations  14.4 us (3%)
  other arithmetic  7.27 us (2%)
  matrix products  6.29 us (1%)
    pallas_call x3, Pallas kernels, pick(): pl.pallas_call(functools.partial(pick_kernel, len(sources)), out_shape=ja...  133 us
    all_to_all x5, waiting for transfers between devices, over_x(): out = lax.all_to_all(value.reshape(NX, count, C, W), 'x', 0, 0, tiled=True)  39.4 us
    ppermute x10, waiting for transfers between devices, shift(): lax.ppermute(value, axis, [(i, (i + by) % size) for i in range(size)])  31.3 us
    unnamed x68, local copies, waits for them, and re-layouts  28.8 us
    all_to_all x5, starting transfers between devices, over_x(): out = lax.all_to_all(value.reshape(NX, count, C, W), 'x', 0, 0, tiled=True)  25.2 us
    all_to_all x1, waiting for transfers between devices, on_device(): lax.all_to_all(grad.reshape(NY, 2 * C, F), 'y', 0, 0, tiled=True)  21.8 us
    all_to_all x3, starting transfers between devices, over_col(): return lax.all_to_all(value, COL, 0, 0, tiled=True)  21.4 us
    ppermute x10, starting transfers between devices, shift(): lax.ppermute(value, axis, [(i, (i + by) % size) for i in range(size)])  20.7 us
  transfers between devices with their start and end apart: 21, of which 9 were waited for; matrix products, arithmetic and copies ran while one was open for 5% of the time, Pallas kernels for 35%

profile of v1, /device:TPU:10, one launch (start us, length us, event | category | flops | bytes accessed | tf_op | source)
XLA Modules:
  0.0 426.5 jit_solution(7523822011177925816)
XLA Ops:
  9.0 6.4 %collective-permute-start = (f32[8,64,256]{2,1,0:T(8,128)S(1)}, f32[8,64,256]{2,1,0:T(8,128)S(1)}, u32[]{:S(2)}, u32[]{:S(2)}) collective-permute-start(f32[8,64,256]{2,1,0:T(8,128)S(1)} %bitcast.85), channel_id=1, source_target_pairs={{0,48},{16,0},{32,16},{48,32},{1,49},{17,1},{33,17},{49,33},{2,50}... | collective-permute-start | bytes 1572872 | tf_op jit(solution)/shard_map/ppermute | solution.py:278
  17.6 33.7 %shard_map.77 = f32[16,64,256]{2,1,0:T(8,128)} custom-call(s32[16]{0:T(128)} %reshape_squeeze.6.index_ref, f32[8,64,256]{2,1,0:T(8,128)} %bitcast.87), custom_call_target="tpu_custom_call" | custom-call | bytes 2097152 | tf_op jit(solution)/shard_map/pallas_call | solution.py:73
  51.3 4.8 %all-to-all-start = ((f32[4,4,64,256]{3,2,1,0:T(8,128)}), f32[4,4,64,256]{3,2,1,0:T(8,128)S(1)}, u32[]{:S(2)}, u32[]{:S(2)}) async-start(f32[4,4,64,256]{3,2,1,0:T(8,128)} %bitcast.100), calls=%async_computation | async-start | bytes 2097152 | tf_op jit(solution)/shard_map/all_to_all | solution.py:283
  56.2 4.2 collective-permute-start.2
  61.1 9.0 %collective-permute-done.2 = f32[4,64,256]{2,1,0:T(8,128)} collective-permute-done((f32[4,64,256]{2,1,0:T(8,128)S(1)}, f32[4,64,256]{2,1,0:T(8,128)}, u32[]{:S(2)}, u32[]{:S(2)}) %collective-permute-start.2) | collective-permute-done | bytes 262176 | tf_op jit(solution)/shard_map/ppermute | solution.py:278
  70.1 4.3 %collective-permute-done.3 = f32[4,64,256]{2,1,0:T(8,128)S(1)} collective-permute-done((f32[4,64,256]{2,1,0:T(8,128)S(1)}, f32[4,64,256]{2,1,0:T(8,128)S(1)}, u32[]{:S(2)}, u32[]{:S(2)}) %collective-permute-start.3) | collective-permute-done | bytes 262176 | tf_op jit(solution)/shard_map/ppermute | solution.py:278
  74.4 1.8 pad_maximum_fusion.refs_0_
  76.2 33.7 %shard_map.79 = f32[16,64,256]{2,1,0:T(8,128)} custom-call(s32[16]{0:T(128)} %reshape_squeeze.7.index_ref, f32[8,64,256]{2,1,0:T(8,128)} %pad_maximum_fusion.refs_0_), custom_call_target="tpu_custom_call" | custom-call | bytes 2097152 | tf_op jit(solution)/shard_map/pallas_call | solution.py:73
  109.9 4.8 %all-to-all-start.2 = ((f32[4,4,64,256]{3,2,1,0:T(8,128)}), f32[4,4,64,256]{3,2,1,0:T(8,128)S(1)}, u32[]{:S(2)}, u32[]{:S(2)}) async-start(f32[4,4,64,256]{3,2,1,0:T(8,128)} %bitcast.101), calls=%async_computation.2 | async-start | bytes 2097152 | tf_op jit(solution)/shard_map/all_to_all | solution.py:283
  115.4 65.6 %shard_map.78 = f32[32,64,256]{2,1,0:T(8,128)} custom-call(s32[32]{0:T(128)} %reshape.189.index_ref, f32[8,64,256]{2,1,0:T(8,128)} %copy-done.31, f32[8,64,256]{2,1,0:T(8,128)} %copy-done.32), custom_call_target="tpu_custom_call" | custom-call | bytes 4194304 | tf_op jit(solution)/shard_map/pallas_call | solution.py:73
  182.1 4.8 %all-to-all-start.1 = ((f32[4,8,64,256]{3,2,1,0:T(8,128)}), f32[4,8,64,256]{3,2,1,0:T(8,128)S(1)}, u32[]{:S(2)}, u32[]{:S(2)}) async-start(f32[4,8,64,256]{3,2,1,0:T(8,128)} %bitcast.99), calls=%async_computation.1 | async-start | bytes 4194304 | tf_op jit(solution)/shard_map/all_to_all | solution.py:283
  187.7 18.8 %all-to-all-done.1 = f32[4,8,64,256]{3,2,1,0:T(8,128)S(1)} async-done(((f32[4,8,64,256]{3,2,1,0:T(8,128)}), f32[4,8,64,256]{3,2,1,0:T(8,128)S(1)}, u32[]{:S(2)}, u32[]{:S(2)}) %all-to-all-start.1) | async-done | bytes 2097184 | tf_op jit(solution)/shard_map/all_to_all | solution.py:283
  206.5 9.6 %all-to-all-start.4 = ((f32[16,64,128]{2,1,0:T(8,128)}), f32[16,64,128]{2,1,0:T(8,128)}, u32[]{:S(2)}, u32[]{:S(2)}) async-start(f32[16,64,128]{2,1,0:T(8,128)} %bitcast_bitcast_fusion.1), calls=%async_computation.4 | async-start | bytes 1048576 | tf_op jit(solution)/shard_map/all_to_all | solution.py:288
  216.2 3.4 copy-done.1
  222.0 4.8 %shard_map.80 = f32[16,64,128]{2,1,0:T(8,128)S(1)} custom-call(s32[56]{0:T(128)S(1)} %fusion.2.where_ref, f32[8,64,256]{2,1,0:T(8,128)S(1)} %bitcast.88, f32[16,64,256]{2,1,0:T(8,128)S(1)} %bitcast.90, f32[32,64,256]{2,1,0:T(8,128)S(1)} %bitcast.84, f32[16,64,256]{2,1,0:T(8,128)S(1)} %bitcast.91, bf16[8,8,256,256]{3,2,1,0:T(8,128)(2,1)S(1)} %copy-done.1), custom_call_target="tpu_custom_call" | custom-call | flops 1073741824 | bytes 13631488 | tf_op jit(solution)/shard_map/pallas_call | solution.py:114
  227.6 5.8 %all-to-all-start.3 = ((f32[16,64,128]{2,1,0:T(8,128)}), f32[16,64,128]{2,1,0:T(8,128)S(1)}, u32[]{:S(2)}, u32[]{:S(2)}) async-start(f32[16,64,128]{2,1,0:T(8,128)} %copy-done.18), calls=%async_computation.3 | async-start | bytes 1048576 | tf_op jit(solution)/shard_map/all_to_all | solution.py:288
  233.4 2.2 copy-done.5
  235.6 2.0 shard_map.76
  238.9 1.4 copy-done.14
  240.3 1.4 copy-done.16
  241.7 1.6 copy-done.13
  243.3 1.6 copy-done.15
  244.8 1.6 copy-done.17
  246.4 5.1 %shard_map.81 = (f32[1024,128]{1,0:T(8,128)S(1)}, f32[1024,128]{1,0:T(8,128)S(1)}, f32[1024,128]{1,0:T(8,128)S(1)}) custom-call(bf16[1024,1024]{1,0:T(8,128)(2,1)S(1)} %get-tuple-element.14.thi_ref, bf16[1024,1024]{1,0:T(8,128)(2,1)S(1)} %copy-done.13, bf16[1024,1024]{1,0:T(8,128)(2,1)S(1)} %copy-done.15, bf16[1024,1024]{1,0:T(8,128)(2,1)S(1)} %copy-done.17, ...), custom_call_target="tpu_custom_call" | custom-call | flops 1610612736 | bytes 10485760 | tf_op jit(solution)/shard_map/pallas_call | solution.py:192
  252.4 13.9 %all_to_all.60.back_ref = f32[16,64,128]{2,1,0:T(8,128)S(1)} all-to-all(f32[16,64,128]{2,1,0:T(8,128)S(1)} %bitcast.97), channel_id=1, replica_groups=mesh['x'=4,'zh'=4,'y'=4,'zl'=2,'c'=2] {'y','zl','c'}, dimensions={0} | all-to-all | bytes 1048576 | tf_op jit(solution)/shard_map/all_to_all | solution.py:288
  266.3 6.1 %all-to-all-start.5 = ((f32[16,64,128]{2,1,0:T(8,128)}), f32[16,64,128]{2,1,0:T(8,128)S(1)}, u32[]{:S(2)}, u32[]{:S(2)}) async-start(f32[16,64,128]{2,1,0:T(8,128)} %bitcast.96), calls=%async_computation.5 | async-start | bytes 1048576 | tf_op jit(solution)/shard_map/all_to_all | solution.py:288
  272.4 2.4 fusion.7
  274.9 3.4 copy-done.2
  278.3 3.4 shard_map.82
  284.9 19.1 %all_to_all.61 = f32[4,4,64,256]{3,2,1,0:T(8,128)} all-to-all(f32[4,4,64,256]{3,2,1,0:T(8,128)S(1)} %bitcast.94), channel_id=1, replica_groups=mesh['x'=4,'zh'=4,'y'=4,'zl'=2,'c'=2] {'x'}, dimensions={0} | all-to-all | bytes 2097152 | tf_op jit(solution)/shard_map/all_to_all | solution.py:283
  303.9 5.0 %all-to-all-start.8 = ((f32[4,8,64,256]{3,2,1,0:T(8,128)}), f32[4,8,64,256]{3,2,1,0:T(8,128)S(1)}, u32[]{:S(2)}, u32[]{:S(2)}) async-start(f32[4,8,64,256]{3,2,1,0:T(8,128)} %bitcast.92), calls=%async_computation.8 | async-start | bytes 4194304 | tf_op jit(solution)/shard_map/all_to_all | solution.py:283
  309.0 3.9 convolution_add_fusion
  312.9 20.6 %all-to-all-done.8 = f32[4,8,64,256]{3,2,1,0:T(8,128)S(1)} async-done(((f32[4,8,64,256]{3,2,1,0:T(8,128)}), f32[4,8,64,256]{3,2,1,0:T(8,128)S(1)}, u32[]{:S(2)}, u32[]{:S(2)}) %all-to-all-start.8) | async-done | bytes 2097184 | tf_op jit(solution)/shard_map/all_to_all | solution.py:283
  333.6 5.0 %all-to-all-start.10 = ((f32[4,128,1024]{2,1,0:T(8,128)}), f32[4,128,1024]{2,1,0:T(8,128)}, u32[]{:S(2)}, u32[]{:S(2)}) async-start(f32[4,128,1024]{2,1,0:T(8,128)} %bitcast.98), calls=%async_computation.10 | async-start | bytes 4194304 | tf_op jit(solution)/shard_map/all_to_all | solution.py:333
  340.5 21.8 %all-to-all-done.10 = f32[4,128,1024]{2,1,0:T(8,128)} async-done(((f32[4,128,1024]{2,1,0:T(8,128)}), f32[4,128,1024]{2,1,0:T(8,128)}, u32[]{:S(2)}, u32[]{:S(2)}) %all-to-all-start.10) | async-done | bytes 2097184 | tf_op jit(solution)/shard_map/all_to_all | solution.py:333
  362.4 5.7 %all-to-all-start.7 = ((f32[4,4,64,256]{3,2,1,0:T(8,128)}), f32[4,4,64,256]{3,2,1,0:T(8,128)}, u32[]{:S(2)}, u32[]{:S(2)}) async-start(f32[4,4,64,256]{3,2,1,0:T(8,128)} %bitcast.93), calls=%async_computation.7 | async-start | bytes 2097152 | tf_op jit(solution)/shard_map/all_to_all | solution.py:283
  369.5 3.5 collective-permute-start.6
  373.0 2.6 reduce_sum.38
  376.6 1.6 collective-permute-start.9
  378.2 6.0 %collective-permute-done.4.refs_1_ = f32[4,64,256]{2,1,0:T(8,128)S(1)} collective-permute-done((f32[4,64,256]{2,1,0:T(8,128)}, f32[4,64,256]{2,1,0:T(8,128)S(1)}, u32[]{:S(2)}, u32[]{:S(2)}) %collective-permute-start.4) | collective-permute-done | bytes 262176 | tf_op jit(solution)/shard_map/ppermute | solution.py:278
  384.2 1.7 shard_map.85
  385.9 1.6 shard_map.86
  387.4 4.1 collective-permute-start.7
  391.6 10.2 %collective-permute-done.9 = f32[64,1024]{1,0:T(8,128)} collective-permute-done((f32[64,1024]{1,0:T(8,128)S(1)}, f32[64,1024]{1,0:T(8,128)}, u32[]{:S(2)}, u32[]{:S(2)}) %collective-permute-start.9) | collective-permute-done | bytes 262176 | tf_op jit(solution)/shard_map/ppermute | solution.py:278
  404.4 4.8 %all-to-all-start.11 = ((f32[16,32,128]{2,1,0:T(8,128)}), f32[16,32,128]{2,1,0:T(8,128)S(1)}, u32[]{:S(2)}, u32[]{:S(2)}) async-start(f32[16,32,128]{2,1,0:T(8,128)} %reshape.213), calls=%async_computation.11 | async-start | bytes 524288 | tf_op jit(solution)/shard_map/all_to_all | solution.py:337
  410.0 1.4 shard_map.83
  411.5 1.8 collective-permute-done.5
  415.3 3.6 all-to-all-done.11
  (111 shorter events, 26.6 us)
Async XLA Ops:
  7.2 179.7 %copy-start = (f32[2048,64]{0,1:T(8,128)S(1)}, f32[2048,64]{0,1:T(8,128)}, u32[]{:S(2)}) copy-start(f32[2048,64]{0,1:T(8,128)} %param.9) | copy-start | bytes 1572868
  7.2 226.2 %all-gather.2.cloned.1.call-start = ((), (), s32[]{:S(2)}) async-start(), calls=%async_computation.12 | async-start | bytes 4456448 | tf_op jit(solution)/shard_map/all_gather | solution.py:298
  9.0 8.6 %copy-start.3 = (f32[8,8,8,256]{3,2,0,1:T(8,128)}, f32[8,8,8,256]{3,2,0,1:T(8,128)S(1)}, u32[]{:S(2)}) copy-start(f32[8,8,8,256]{3,2,0,1:T(8,128)S(1)} %copy.44) | copy-start | bytes 1572868
  9.0 47.1 %collective-permute-start = (f32[8,64,256]{2,1,0:T(8,128)S(1)}, f32[8,64,256]{2,1,0:T(8,128)S(1)}, u32[]{:S(2)}, u32[]{:S(2)}) collective-permute-start(f32[8,64,256]{2,1,0:T(8,128)S(1)} %bitcast.85), channel_id=1, source_target_pairs={{0,48},{16,0},{32,16},{48,32},{1,49},{17,1},{33,17},{49,33},{2,50}... | collective-permute-start | bytes 1572872 | tf_op jit(solution)/shard_map/ppermute | solution.py:278
  15.4 45.0 %collective-permute-start.1 = (f32[8,64,256]{2,1,0:T(8,128)S(1)}, f32[8,64,256]{2,1,0:T(8,128)S(1)}, u32[]{:S(2)}, u32[]{:S(2)}) collective-permute-start(f32[8,64,256]{2,1,0:T(8,128)S(1)} %bitcast.86), channel_id=1, source_target_pairs={{0,16},{16,32},{32,48},{48,0},{1,17},{17,33},{33,49},{49,1},{2,18}... | collective-permute-start | bytes 1572872 | tf_op jit(solution)/shard_map/ppermute | solution.py:278
  51.3 58.6 %all-to-all-start = ((f32[4,4,64,256]{3,2,1,0:T(8,128)}), f32[4,4,64,256]{3,2,1,0:T(8,128)S(1)}, u32[]{:S(2)}, u32[]{:S(2)}) async-start(f32[4,4,64,256]{3,2,1,0:T(8,128)} %bitcast.100), calls=%async_computation | async-start | bytes 2097152 | tf_op jit(solution)/shard_map/all_to_all | solution.py:283
  56.1 53.8 %copy-start.31 = (f32[8,64,256]{2,1,0:T(8,128)}, f32[8,64,256]{2,1,0:T(8,128)S(1)}, u32[]{:S(2)}) copy-start(f32[8,64,256]{2,1,0:T(8,128)S(1)} %collective-permute-done.refs_0_) | copy-start | bytes 1572868
  56.2 13.9 %collective-permute-start.2 = (f32[4,64,256]{2,1,0:T(8,128)S(1)}, f32[4,64,256]{2,1,0:T(8,128)}, u32[]{:S(2)}, u32[]{:S(2)}) collective-permute-start(f32[4,64,256]{2,1,0:T(8,128)S(1)} %slice.36), channel_id=1, source_target_pairs={{0,48},{16,0},{32,16},{48,32},{1,49},{17,1},{33,17},{49,33},{2,50}... | collective-permute-start | bytes 786440 | tf_op jit(solution)/shard_map/ppermute | solution.py:278
  60.4 49.6 %copy-start.32 = (f32[8,64,256]{2,1,0:T(8,128)}, f32[8,64,256]{2,1,0:T(8,128)S(1)}, u32[]{:S(2)}) copy-start(f32[8,64,256]{2,1,0:T(8,128)S(1)} %collective-permute-done.1.refs_1_) | copy-start | bytes 1572868
  60.4 14.0 %collective-permute-start.3 = (f32[4,64,256]{2,1,0:T(8,128)S(1)}, f32[4,64,256]{2,1,0:T(8,128)S(1)}, u32[]{:S(2)}, u32[]{:S(2)}) collective-permute-start(f32[4,64,256]{2,1,0:T(8,128)S(1)} %slice.37), channel_id=1, source_target_pairs={{0,16},{16,32},{32,48},{48,0},{1,17},{17,33},{33,49},{49,1},{2,18}... | collective-permute-start | bytes 786440 | tf_op jit(solution)/shard_map/ppermute | solution.py:278
  109.9 71.1 %copy-start.7 = (f32[4,4,64,256]{3,2,1,0:T(8,128)}, f32[4,4,64,256]{3,2,1,0:T(8,128)S(1)}, u32[]{:S(2)}) copy-start(f32[4,4,64,256]{3,2,1,0:T(8,128)S(1)} %all-to-all-done) | copy-start | bytes 3145732
  109.9 71.1 %all-to-all-start.2 = ((f32[4,4,64,256]{3,2,1,0:T(8,128)}), f32[4,4,64,256]{3,2,1,0:T(8,128)S(1)}, u32[]{:S(2)}, u32[]{:S(2)}) async-start(f32[4,4,64,256]{3,2,1,0:T(8,128)} %bitcast.101), calls=%async_computation.2 | async-start | bytes 2097152 | tf_op jit(solution)/shard_map/all_to_all | solution.py:283
  182.1 24.4 %all-to-all-start.1 = ((f32[4,8,64,256]{3,2,1,0:T(8,128)}), f32[4,8,64,256]{3,2,1,0:T(8,128)S(1)}, u32[]{:S(2)}, u32[]{:S(2)}) async-start(f32[4,8,64,256]{3,2,1,0:T(8,128)} %bitcast.99), calls=%async_computation.1 | async-start | bytes 4194304 | tf_op jit(solution)/shard_map/all_to_all | solution.py:283
  186.9 29.2 %copy-start.4 = (f32[8,8,8,256]{3,2,0,1:T(8,128)S(1)}, f32[8,8,8,256]{3,2,0,1:T(8,128)}, u32[]{:S(2)}) copy-start(f32[8,8,8,256]{3,2,0,1:T(8,128)} %copy-done.3) | copy-start | bytes 1572868
  206.5 21.1 %all-to-all-start.4 = ((f32[16,64,128]{2,1,0:T(8,128)}), f32[16,64,128]{2,1,0:T(8,128)}, u32[]{:S(2)}, u32[]{:S(2)}) async-start(f32[16,64,128]{2,1,0:T(8,128)} %bitcast_bitcast_fusion.1), calls=%async_computation.4 | async-start | bytes 1048576 | tf_op jit(solution)/shard_map/all_to_all | solution.py:288
  216.1 3.4 copy-start.1
  219.5 1.2 copy-start.8
  227.6 14.1 %all-to-all-start.3 = ((f32[16,64,128]{2,1,0:T(8,128)}), f32[16,64,128]{2,1,0:T(8,128)S(1)}, u32[]{:S(2)}, u32[]{:S(2)}) async-start(f32[16,64,128]{2,1,0:T(8,128)} %copy-done.18), calls=%async_computation.3 | async-start | bytes 1048576 | tf_op jit(solution)/shard_map/all_to_all | solution.py:288
  233.4 2.2 copy-start.5
  237.6 1.4 copy-start.12
  238.9 1.4 copy-start.14
  240.3 1.4 copy-start.16
  241.7 1.6 copy-start.13
  243.3 1.6 copy-start.15
  244.8 1.6 copy-start.17
  252.4 13.9 %copy-start.24 = (f32[1024,128]{1,0:T(8,128)}, f32[1024,128]{1,0:T(8,128)S(1)}, u32[]{:S(2)}) copy-start(f32[1024,128]{1,0:T(8,128)S(1)} %get-tuple-element.18) | copy-start | bytes 1572868
  252.4 20.0 %copy-start.23 = (f32[1024,128]{1,0:T(8,128)S(1)}, f32[1024,128]{1,0:T(8,128)}, u32[]{:S(2)}) copy-start(f32[1024,128]{1,0:T(8,128)} %copy-done.22) | copy-start | bytes 1572868
  266.3 18.6 %all-to-all-start.5 = ((f32[16,64,128]{2,1,0:T(8,128)}), f32[16,64,128]{2,1,0:T(8,128)S(1)}, u32[]{:S(2)}, u32[]{:S(2)}) async-start(f32[16,64,128]{2,1,0:T(8,128)} %bitcast.96), calls=%async_computation.5 | async-start | bytes 1048576 | tf_op jit(solution)/shard_map/all_to_all | solution.py:288
  274.8 34.2 %collective-permute-start.8 = (f32[512,1024]{1,0:T(8,128)}, f32[512,1024]{1,0:T(8,128)}, u32[]{:S(2)}, u32[]{:S(2)}) collective-permute-start(f32[512,1024]{1,0:T(8,128)} %fusion.7), channel_id=1, source_target_pairs={{0,1},{1,0},{2,3},{3,2},{4,5},{5,4},{6,7},{7,6},{8,9},{9,8},{10,11... | collective-permute-start | bytes 6291464 | tf_op jit(solution)/shard_map/ppermute | solution.py:278
  274.9 3.4 copy-start.2
  281.8 1.4 copy-start.11
  284.9 19.1 %copy-start.28 = (f32[16,64,128]{2,1,0:T(8,128)}, f32[16,64,128]{2,1,0:T(8,128)S(1)}, u32[]{:S(2)}) copy-start(f32[16,64,128]{2,1,0:T(8,128)S(1)} %all-to-all-done.5) | copy-start | bytes 1572868
  303.9 29.6 %all-to-all-start.8 = ((f32[4,8,64,256]{3,2,1,0:T(8,128)}), f32[4,8,64,256]{3,2,1,0:T(8,128)S(1)}, u32[]{:S(2)}, u32[]{:S(2)}) async-start(f32[4,8,64,256]{3,2,1,0:T(8,128)} %bitcast.92), calls=%async_computation.8 | async-start | bytes 4194304 | tf_op jit(solution)/shard_map/all_to_all | solution.py:283
  333.6 5.0 %copy-start.27 = (s32[16]{0:T(128)S(1)}, s32[16]{0:T(128)}, u32[]{:S(2)}) copy-start(s32[16]{0:T(128)} %reshape_squeeze.7.index_ref) | copy-start | bytes 196
  333.6 28.8 %all-to-all-start.10 = ((f32[4,128,1024]{2,1,0:T(8,128)}), f32[4,128,1024]{2,1,0:T(8,128)}, u32[]{:S(2)}, u32[]{:S(2)}) async-start(f32[4,128,1024]{2,1,0:T(8,128)} %bitcast.98), calls=%async_computation.10 | async-start | bytes 4194304 | tf_op jit(solution)/shard_map/all_to_all | solution.py:333
  338.5 1.2 copy-start.6
  362.4 42.0 %all-to-all-start.7 = ((f32[4,4,64,256]{3,2,1,0:T(8,128)}), f32[4,4,64,256]{3,2,1,0:T(8,128)}, u32[]{:S(2)}, u32[]{:S(2)}) async-start(f32[4,4,64,256]{3,2,1,0:T(8,128)} %bitcast.93), calls=%async_computation.7 | async-start | bytes 2097152 | tf_op jit(solution)/shard_map/all_to_all | solution.py:283
  368.0 16.2 %copy-start.25 = (s32[32]{0:T(128)S(1)}, s32[32]{0:T(128)}, u32[]{:S(2)}) copy-start(s32[32]{0:T(128)} %reshape.189.index_ref) | copy-start | bytes 388
  368.9 15.3 %collective-permute-start.4 = (f32[4,64,256]{2,1,0:T(8,128)}, f32[4,64,256]{2,1,0:T(8,128)S(1)}, u32[]{:S(2)}, u32[]{:S(2)}) collective-permute-start(f32[4,64,256]{2,1,0:T(8,128)} %get-tuple-element.36), channel_id=1, source_target_pairs={{0,16},{16,32},{32,48},{48,0},{1,17},{17,33},{33,49},{49,1},{2,18}... | collective-permute-start | bytes 786440 | tf_op jit(solution)/shard_map/ppermute | solution.py:278
  369.5 16.4 %collective-permute-start.6 = (f32[4,64,256]{2,1,0:T(8,128)}, f32[4,64,256]{2,1,0:T(8,128)S(1)}, u32[]{:S(2)}, u32[]{:S(2)}) collective-permute-start(f32[4,64,256]{2,1,0:T(8,128)} %get-tuple-element.37), channel_id=1, source_target_pairs={{0,48},{16,0},{32,16},{48,32},{1,49},{17,1},{33,17},{49,33},{2,50}... | collective-permute-start | bytes 786440 | tf_op jit(solution)/shard_map/ppermute | solution.py:278
  376.6 25.2 %collective-permute-start.9 = (f32[64,1024]{1,0:T(8,128)S(1)}, f32[64,1024]{1,0:T(8,128)}, u32[]{:S(2)}, u32[]{:S(2)}) collective-permute-start(f32[64,1024]{1,0:T(8,128)S(1)} %dynamic-slice_bitcast_fusion), channel_id=1, source_target_pairs={{0,2},{2,0},{1,3},{3,1},{4,6},{6,4},{5,7},{7,5},{8,10},{10,8},{9,1... | collective-permute-start | bytes 786440 | tf_op jit(solution)/shard_map/ppermute | solution.py:278
  385.9 15.9 %copy-start.30 = (f32[128,1024]{1,0:T(8,128)S(1)}, f32[128,1024]{1,0:T(8,128)}, u32[]{:S(2)}) copy-start(f32[128,1024]{1,0:T(8,128)} %reduce_sum.38) | copy-start | bytes 1572868
  385.9 27.4 %collective-permute-start.5 = (f32[8,64,256]{2,1,0:T(8,128)}, f32[8,64,256]{2,1,0:T(8,128)}, u32[]{:S(2)}, u32[]{:S(2)}) collective-permute-start(f32[8,64,256]{2,1,0:T(8,128)} %shard_map.85), channel_id=1, source_target_pairs={{0,16},{16,32},{32,48},{48,0},{1,17},{17,33},{33,49},{49,1},{2,18}... | collective-permute-start | bytes 1572872 | tf_op jit(solution)/shard_map/ppermute | solution.py:278
  387.4 21.8 %copy-start.29 = (f32[16,64,128]{2,1,0:T(8,128)S(1)}, f32[16,64,128]{2,1,0:T(8,128)}, u32[]{:S(2)}) copy-start(f32[16,64,128]{2,1,0:T(8,128)} %copy-done.28) | copy-start | bytes 1572868
  387.4 25.8 %collective-permute-start.7 = (f32[8,64,256]{2,1,0:T(8,128)}, f32[8,64,256]{2,1,0:T(8,128)S(1)}, u32[]{:S(2)}, u32[]{:S(2)}) collective-permute-start(f32[8,64,256]{2,1,0:T(8,128)} %shard_map.86), channel_id=1, source_target_pairs={{0,48},{16,0},{32,16},{48,32},{1,49},{17,1},{33,17},{49,33},{2,50}... | collective-permute-start | bytes 1572872 | tf_op jit(solution)/shard_map/ppermute | solution.py:278
  402.8 7.3 %copy-start.21 = (f32[8,64,256]{2,1,0:T(8,128)S(1)}, f32[8,64,256]{2,1,0:T(8,128)}, u32[]{:S(2)}) copy-start(f32[8,64,256]{2,1,0:T(8,128)} %copy-done.20) | copy-start | bytes 1572868
  402.8 7.3 %copy-start.26 = (s32[16]{0:T(128)S(1)}, s32[16]{0:T(128)}, u32[]{:S(2)}) copy-start(s32[16]{0:T(128)} %reshape_squeeze.6.index_ref) | copy-start | bytes 196
  404.4 14.5 %all-to-all-start.11 = ((f32[16,32,128]{2,1,0:T(8,128)}), f32[16,32,128]{2,1,0:T(8,128)S(1)}, u32[]{:S(2)}, u32[]{:S(2)}) async-start(f32[16,32,128]{2,1,0:T(8,128)} %reshape.213), calls=%async_computation.11 | async-start | bytes 524288 | tf_op jit(solution)/shard_map/all_to_all | solution.py:337
  (6 other events, 5.7 us)
Sparse Core Ops, SparseCore 0:
  9.9 60.6 all-gather.1

commit v2 on v1

v2 whole, which is shorter than its diff:
```python
import functools

import jax
import jax.numpy as jnp
from jax import lax
from jax.experimental import pallas as pl
from jax.experimental.pallas import tpu as pltpu
from jax.sharding import Mesh
from jax.sharding import PartitionSpec as P

DOM = ("x", "zh")
COL = ("y", "zl", "c")
NX, NZ, NY = 4, 4, 4
BLK, FAN, W, C = 8, 8, 256, 64
REFS = BLK * (FAN - 1)
SLOTS = 4
HELD = 72
F = 1024
CHUNK = 128
f32, bf16 = jnp.float32, jnp.bfloat16
VMEM = pl.BlockSpec(memory_space=pltpu.VMEM)
SMEM = pl.BlockSpec(memory_space=pltpu.SMEM)
ANY = pl.BlockSpec(memory_space=pl.ANY)
PARAMS = pltpu.CompilerParams(vmem_limit_bytes=58 * 2**20)


def split(value):
    hi = value.astype(bf16)
    lo = (value - hi.astype(f32)).astype(bf16)
    return hi, lo


def tables(neighbours):
    me_x, me_z = lax.axis_index("x"), lax.axis_index("zh")
    rows = neighbours.reshape(NX, NZ, REFS)
    rows = lax.dynamic_index_in_dim(rows, me_z, 1, keepdims=False)
    rows = lax.dynamic_slice_in_dim(jnp.concatenate([rows, rows], axis=0), me_x, NX, 0)
    owner, block = rows >> 3, rows & 7
    ref = jnp.arange(REFS)
    same = (owner[:, :, None] == owner[:, None, :]) & (ref[None, :, None] > ref[None, None, :])
    rank = jnp.sum(same.astype(jnp.int32), axis=2)
    wanted = me_x * NZ + ((me_z + jnp.arange(NZ)) & (NZ - 1))
    match = (owner[None, 1:, None, :] == wanted[:, None, None, None]) & (
        rank[None, 1:, None, :] == jnp.arange(SLOTS)[None, None, :, None]
    )
    table = jnp.sum(jnp.where(match, block[None, 1:, None, :] + 1, 0), axis=3)
    e, s = ((owner[0] & 3) - me_z) & 3, (me_x - (owner[0] >> 2)) & 3
    local = jnp.where(e == 2, 0, jnp.where(e == 1, 8, 16)) + block[0]
    start = jnp.where(e == 0, 24, jnp.where(e == 2, 60, 36 + (e >> 1) * 4))
    stride = jnp.where((e & 1) == 1, 8, 4)
    place = jnp.where(s == 0, local, start + (s - 1) * stride + rank[0])
    near = table[0].reshape(12)
    mid = jnp.stack([table[1], table[3]], axis=1).reshape(24)
    far = table[2].reshape(12)
    return near, mid, far, jnp.clip(place, 0, HELD - 1)


def pick_kernel(index_ref, *refs):
    sources, outs = refs[:-3], refs[-3:]
    per = outs[0].shape[0]
    for s in range(3):
        for slot in range(per):
            index = jnp.maximum(index_ref[s * per + slot] - 1, 0)
            outs[s][slot] = sources[slot // SLOTS][index]


def pick_halves_kernel(index_ref, lo_ref, hi_ref, *refs):
    outs, held = refs[:3], refs[3]
    held[: BLK // 2] = lo_ref[...]
    held[BLK // 2 :] = hi_ref[...]
    pick_kernel(index_ref, held, *outs)


def pick(index, *sources, halves=False):
    per = SLOTS * (1 if halves else len(sources))
    return pl.pallas_call(
        pick_halves_kernel if halves else pick_kernel,
        out_shape=[jax.ShapeDtypeStruct((per, C, W), f32)] * 3,
        in_specs=[SMEM] + [VMEM] * len(sources),
        out_specs=[VMEM] * 3,
        scratch_shapes=[pltpu.VMEM((BLK, C, W), f32)] if halves else [],
        compiler_params=PARAMS,
        cost_estimate=pl.CostEstimate(flops=0, bytes_accessed=per * C * W * 24, transcendentals=0),
    )(index, *sources)


def places(refs):
    start, pairs = 0, []
    for ref in refs:
        pairs.append((pl.ds(start, ref.shape[0]), ref))
        start += ref.shape[0]
    return pairs


def mixed_kernel(place_ref, own_ref, *refs):
    sources, tiles_ref, out_ref, held, sems = refs[:13], *refs[13:]
    i = pl.program_id(0)

    @pl.when(i == 0)
    def _():
        copies = [
            pltpu.make_async_copy(ref, held.at[rows], sems.at[n]) for n, (rows, ref) in enumerate(places(sources))
        ]
        for copy in copies:
            copy.start()
        for copy in copies:
            copy.wait()

    acc = None
    for k in range(FAN):
        block = own_ref[0] if k == 0 else held[place_ref[i * (FAN - 1) + k - 1]]
        part = lax.dot_general(
            jnp.concatenate(split(block), axis=0),
            tiles_ref[0, k],
            (((1,), (1,)), ((), ())),
            preferred_element_type=f32,
        )
        acc = part if acc is None else acc + part
    value = acc[:C] + acc[C:]
    out_ref[0] = value[:, :CHUNK]
    out_ref[1] = value[:, CHUNK:]


def mix(place, own, sources, tiles):
    return pl.pallas_call(
        mixed_kernel,
        grid_spec=pltpu.PrefetchScalarGridSpec(
            num_scalar_prefetch=1,
            grid=(BLK,),
            in_specs=[pl.BlockSpec((1, C, W), lambda i, s: (i, 0, 0))]
            + [ANY] * len(sources)
            + [pl.BlockSpec((1, FAN, W, W), lambda i, s: (i, 0, 0, 0))],
            out_specs=pl.BlockSpec((2, C, CHUNK), lambda i, s: (i, 0, 0)),
            scratch_shapes=[pltpu.VMEM((HELD, C, W), f32), pltpu.SemaphoreType.DMA((len(sources),))],
        ),
        out_shape=jax.ShapeDtypeStruct((16, C, CHUNK), f32),
        compiler_params=PARAMS,
        cost_estimate=pl.CostEstimate(flops=2 * 64 * W * W * 2 * C, bytes_accessed=13 << 20, transcendentals=0),
    )(place, own, *sources, tiles)


def weight_kernel(in_ref, thi_ref, tlo_ref, hi_ref, lo_ref):
    value = in_ref[...]
    thi_ref[...], tlo_ref[...] = split(value)
    hi_ref[...], lo_ref[...] = split(value.T)


def weight_parts(transposed):
    step = 256
    by_row = pl.BlockSpec((step, F), lambda i: (i, 0))
    by_col = pl.BlockSpec((F, step), lambda i: (0, i))
    return pl.pallas_call(
        weight_kernel,
        grid=(F // step,),
        in_specs=[by_row],
        out_specs=[by_row, by_row, by_col, by_col],
        out_shape=[jax.ShapeDtypeStruct((F, F), bf16)] * 4,
        compiler_params=PARAMS,
        cost_estimate=pl.CostEstimate(flops=F * F * 8, bytes_accessed=12 << 20, transcendentals=0),
    )(transposed)


def dense_kernel(thi_ref, tlo_ref, hi_ref, lo_ref, mixed_ref, cot_ref, hidden_ref, slope_ref, back_ref, parts):
    step = pl.program_id(0)

    @pl.when(step == 0)
    def _():
        hi, lo = split(mixed_ref[...])
        parts[:, :CHUNK] = hi
        parts[:, CHUNK:] = lo

    both = jnp.dot(thi_ref[...], parts[...], preferred_element_type=f32)
    low = jnp.dot(tlo_ref[...], parts[:, :CHUNK], preferred_element_type=f32)
    pre = both[:, :CHUNK] + (both[:, CHUNK:] + low)
    sig = jax.nn.sigmoid(pre)
    hidden_ref[...] = pre * sig
    slope = cot_ref[...] * sig * (1.0 + pre * (1.0 - sig))
    slope_ref[...] = slope
    shi, slo = split(slope)
    both = jnp.dot(hi_ref[...], jnp.concatenate([shi, slo], axis=1), preferred_element_type=f32)
    low = jnp.dot(lo_ref[...], shi, preferred_element_type=f32)
    part = both[:, :CHUNK] + (both[:, CHUNK:] + low)

    @pl.when(step == 0)
    def _():
        back_ref[...] = part

    @pl.when(step > 0)
    def _():
        back_ref[...] += part


def dense(weights, mixed, cot):
    step = 256
    by_row = pl.BlockSpec((step, F), lambda i: (i, 0))
    by_col = pl.BlockSpec((F, step), lambda i: (0, i))
    rows = pl.BlockSpec((step, CHUNK), lambda i: (i, 0))
    whole = pl.BlockSpec((F, CHUNK), lambda i: (0, 0))
    return pl.pallas_call(
        dense_kernel,
        grid=(F // step,),
        in_specs=[by_row, by_row, by_col, by_col, whole, rows],
        out_specs=[rows, rows, whole],
        out_shape=[jax.ShapeDtypeStruct((F, CHUNK), f32)] * 3,
        scratch_shapes=[pltpu.VMEM((F, 2 * CHUNK), bf16)],
        compiler_params=PARAMS,
        cost_estimate=pl.CostEstimate(flops=12 * F * F * CHUNK, bytes_accessed=10 << 20, transcendentals=F * CHUNK),
    )(*weights, mixed, cot)


def push_kernel(place_ref, back_ref, tiles_ref, diag_ref, *refs):
    outs, held, sems = refs[:13], *refs[13:]
    i = pl.program_id(0)

    @pl.when(i == 0)
    def _():
        held[...] = jnp.zeros_like(held)

    block = jnp.concatenate([back_ref[0], back_ref[1]], axis=1)
    both = jnp.concatenate(split(block), axis=0)
    for k in range(FAN):
        part = jnp.dot(both, tiles_ref[0, k], preferred_element_type=f32)
        value = part[:C] + part[C:]
        if k == 0:
            diag_ref[0] = value
        else:
            held[place_ref[i * (FAN - 1) + k - 1]] += value

    @pl.when(i == BLK - 1)
    def _():
        copies = [pltpu.make_async_copy(held.at[rows], ref, sems.at[n]) for n, (rows, ref) in enumerate(places(outs))]
        for copy in copies:
            copy.start()
        for copy in copies:
            copy.wait()


def push(place, back, tiles):
    sizes = (4, 4, 8, 8, 4, 4, 4, 8, 8, 8, 4, 4, 4)
    return pl.pallas_call(
        push_kernel,
        grid_spec=pltpu.PrefetchScalarGridSpec(
            num_scalar_prefetch=1,
            grid=(BLK,),
            in_specs=[
                pl.BlockSpec((2, C, CHUNK), lambda i, s: (i, 0, 0)),
                pl.BlockSpec((1, FAN, W, W), lambda i, s: (i, 0, 0, 0)),
            ],
            out_specs=[pl.BlockSpec((1, C, W), lambda i, s: (i, 0, 0))] + [ANY] * len(sizes),
            scratch_shapes=[pltpu.VMEM((HELD, C, W), f32), pltpu.SemaphoreType.DMA((len(sizes),))],
        ),
        out_shape=[jax.ShapeDtypeStruct((n, C, W), f32) for n in (BLK,) + sizes],
        compiler_params=PARAMS,
        cost_estimate=pl.CostEstimate(flops=2 * 64 * W * W * 2 * C, bytes_accessed=13 << 20, transcendentals=0),
    )(place, back, tiles)


def add_slots(index_ref, got, group, out_ref):
    per = got[0].shape[0]
    for s in range(3):
        for t in range(SLOTS):
            slot = group * SLOTS + t
            index = index_ref[s * per + slot]

            @pl.when(index > 0)
            def _():
                out_ref[index - 1] += got[s][slot]


def far_kernel(index_ref, a_ref, b_ref, c_ref, lo_ref, hi_ref, out_lo, out_hi, total):
    total[: BLK // 2] = lo_ref[...]
    total[BLK // 2 :] = hi_ref[...]
    add_slots(index_ref, (a_ref, b_ref, c_ref), 0, total)
    out_lo[...] = total[: BLK // 2]
    out_hi[...] = total[BLK // 2 :]


def mid_kernel(index_ref, a_ref, b_ref, c_ref, up_ref, down_ref, below_ref, above_ref, out_up, out_down):
    half = BLK // 2
    out_up[:half] = up_ref[:half] + below_ref[...]
    out_up[half:] = up_ref[half:]
    out_down[:half] = down_ref[:half]
    out_down[half:] = down_ref[half:] + above_ref[...]
    add_slots(index_ref, (a_ref, b_ref, c_ref), 0, out_up)
    add_slots(index_ref, (a_ref, b_ref, c_ref), 1, out_down)


def near_kernel(index_ref, a_ref, b_ref, c_ref, diag_ref, out):
    out[...] = diag_ref[...]
    add_slots(index_ref, (a_ref, b_ref, c_ref), 0, out)


def gather_sum(kernel, shapes, scratch, index, *args):
    return pl.pallas_call(
        kernel,
        out_shape=[jax.ShapeDtypeStruct((n, C, W), f32) for n in shapes],
        in_specs=[SMEM] + [VMEM] * len(args),
        out_specs=[VMEM] * len(shapes),
        scratch_shapes=scratch,
        compiler_params=PARAMS,
        cost_estimate=pl.CostEstimate(flops=12 * C * W, bytes_accessed=3 << 20, transcendentals=0),
    )(index, *args)


def shift(value, axis, size, by):
    return lax.ppermute(value, axis, [(i, (i + by) % size) for i in range(size)])


def over_x(pieces, sign):
    return [shift(piece, "x", NX, sign * (s + 1)) for s, piece in enumerate(pieces)]


def over_col(value):
    return lax.all_to_all(value, COL, 0, 0, tiled=True)


def on_device(features, neighbours, tiles, weight, cotangent):
    near_at, mid_at, far_at, place = tables(neighbours)
    own = features.T.reshape(C, BLK, W).transpose(1, 0, 2)

    up = shift(own, "zh", NZ, -1)
    down = shift(own, "zh", NZ, 1)
    near = over_x(pick(near_at, own), 1)
    weights = weight_parts(lax.all_gather(weight.T, COL, axis=0, tiled=True))
    cot = over_col(cotangent.T.reshape(C, 16, CHUNK).transpose(1, 0, 2)).reshape(F, CHUNK)
    far_lo = shift(up[: BLK // 2], "zh", NZ, -1)
    far_hi = shift(down[BLK // 2 :], "zh", NZ, 1)
    mid = over_x(pick(mid_at, up, down), 1)
    far = over_x(pick(far_at, far_lo, far_hi, halves=True), 1)
    own, weights, cot = lax.optimization_barrier((own, weights, cot))
    mixed = mix(place, own, [far_lo, far_hi, up, down, *near, *mid, *far], tiles)

    mixed = over_col(mixed).reshape(F, CHUNK)
    hidden, slope, back = dense(weights, mixed, cot)
    back = over_col(back.reshape(16, C, CHUNK))

    diag, lo, hi, up, down, *pieces = push(place, back, tiles)
    diag, hidden, slope, mixed = lax.optimization_barrier((diag, hidden, slope, mixed))
    near, mid, far = pieces[:3], pieces[3:6], pieces[6:]
    far = over_x(far, -1)
    far, mid = lax.optimization_barrier((far, mid))
    mid = over_x(mid, -1)
    lo, hi = gather_sum(far_kernel, (4, 4), [pltpu.VMEM((BLK, C, W), f32)], far_at, *far, lo, hi)
    below = shift(lo, "zh", NZ, 1)
    above = shift(hi, "zh", NZ, -1)
    mid, near = lax.optimization_barrier((mid, near))
    near = over_x(near, -1)
    up, down = gather_sum(mid_kernel, (8, 8), [], mid_at, *mid, up, down, below, above)
    up = shift(up, "zh", NZ, 1)
    down = shift(down, "zh", NZ, -1)
    (near,) = gather_sum(near_kernel, (8,), [], near_at, *near, diag)
    grad_features = (near + up + down).transpose(1, 0, 2).reshape(C, BLK * W).T
    hidden = over_col(hidden.reshape(16, C, CHUNK)).transpose(1, 0, 2).reshape(C, 16 * CHUNK).T

    me_c, me_l = lax.axis_index("c"), lax.axis_index("zl")
    by_core = slope.reshape(8, 2, C, CHUNK)

    def partial(core):
        rows = lax.dynamic_index_in_dim(by_core, core, 1, keepdims=False).reshape(8 * C, CHUNK)
        return lax.dot_general(
            rows, mixed, (((1,), (1,)), ((), ())), precision=lax.Precision.HIGH, preferred_element_type=f32
        )

    grad = partial(me_c) + shift(partial(1 - me_c), "c", 2, 1)
    grad = lax.all_to_all(grad.reshape(NY, 2 * C, F), "y", 0, 0, tiled=True).sum(axis=0).reshape(2, C, F)
    other = shift(lax.dynamic_index_in_dim(grad, 1 - me_l, 0, keepdims=False), "zl", 2, 1)
    grad = lax.dynamic_index_in_dim(grad, me_l, 0, keepdims=False) + other
    grad = grad.reshape(2, C // 2, 16, C).transpose(2, 1, 0, 3).reshape(16, C // 2, 2 * C)
    grad = lax.all_to_all(grad, DOM, 0, 0, tiled=True).sum(axis=0)
    grad_weight = grad.reshape(C // 2, 2, C).transpose(1, 0, 2).reshape(C, C).T
    return hidden, grad_features, grad_weight


def solution(mesh):
    fine = Mesh(mesh.devices.reshape(4, 4, 4, 2, 2), DOM + COL)
    in_specs = (P(DOM, COL), P(), P(DOM, None, None, None), P(None, COL), P(DOM, COL))
    out_specs = (P(DOM, COL), P(DOM, COL), P(DOM, COL))
    return jax.shard_map(on_device, mesh=fine, in_specs=in_specs, out_specs=out_specs, check_vma=False)
```

time: 430 us -> 291 us (0.68)
  Pallas kernels: 154 us -> 51 us
  local copies, waits for them, and re-layouts: 37.9 us -> 12.1 us
  blocking collectives: 33 us -> 24.5 us
  starting transfers between devices: 77.1 us -> 83.2 us
    pallas_call x7 -> x6, Pallas kernels: 138 us -> 14.2 us  [the longest x3 7.72 us: gather_sum(): pl.pallas_call(kernel, out_shape=[jax.ShapeDtypeStruct((n, C, W), f32) fo...]
    all_to_all x5 -> x0, waiting for transfers between devices: 39.4 us -> none  [over_x(): out = lax.all_to_all(value.reshape(NX, count, C, W), 'x', 0, 0, tiled=True)]
    ppermute x10 -> x28, waiting for transfers between devices: 31.3 us -> 69.1 us  [shift(): lax.ppermute(value, axis, [(i, (i + by) % size) for i in range(size)])]
    ppermute x10 -> x28, starting transfers between devices: 20.7 us -> 51.5 us  [shift(): lax.ppermute(value, axis, [(i, (i + by) % size) for i in range(size)])]
    all_to_all x5 -> x0, starting transfers between devices: 25.2 us -> none  [over_x(): out = lax.all_to_all(value.reshape(NX, count, C, W), 'x', 0, 0, tiled=True)]
    unnamed x68 -> x52, local copies, waits for them, and re-layouts: 28.8 us -> 3.78 us
    all_to_all x1 -> x0, blocking collectives: 19.1 us -> none  [over_x(): out = lax.all_to_all(value.reshape(NX, count, C, W), 'x', 0, 0, tiled=True)]
    all_to_all x1, waiting for transfers between devices: 21.8 us -> 6.48 us  [on_device(): lax.all_to_all(grad.reshape(NY, 2 * C, F), 'y', 0, 0, tiled=True)]
  transfers between devices with their start and end apart: 21 -> 34, of which waited for: 9 -> 18; matrix products, arithmetic and copies ran while one was open for 5% -> 4% of each run, Pallas kernels for 35% -> 7%
where the time goes in v2:
time: 291 us; the launch traced here: 288 us
  waiting for transfers between devices  96.4 us (33%)
  starting transfers between devices  83.2 us (29%)
  Pallas kernels  51 us (18%)
  blocking collectives  24.5 us (8%)
  between operations  14.4 us (5%)
  local copies, waits for them, and re-layouts  12.1 us (4%)
  other arithmetic  3.41 us (1%)
  matrix products  3.32 us (1%)
    ppermute x28, waiting for transfers between devices, shift(): lax.ppermute(value, axis, [(i, (i + by) % size) for i in range(size)])  69.1 us
    ppermute x28, starting transfers between devices, shift(): lax.ppermute(value, axis, [(i, (i + by) % size) for i in range(size)])  51.5 us
    all_to_all x1, blocking collectives, over_col(): return lax.all_to_all(value, COL, 0, 0, tiled=True)  24.5 us
    all_to_all x3, starting transfers between devices, over_col(): return lax.all_to_all(value, COL, 0, 0, tiled=True)  16.3 us
    pallas_call x1, Pallas kernels, mix(): pl.pallas_call(mixed_kernel, grid_spec=pltpu.PrefetchScalarGridSpec(num_s...  11.7 us
    pallas_call x1, Pallas kernels, push(): pl.pallas_call(push_kernel, grid_spec=pltpu.PrefetchScalarGridSpec(num_sc...  11.2 us
    all_to_all x1, starting transfers between devices, on_device(): grad = lax.all_to_all(grad, DOM, 0, 0, tiled=True).sum(axis=0)  8.94 us
    all_to_all x3, waiting for transfers between devices, over_col(): return lax.all_to_all(value, COL, 0, 0, tiled=True)  8.25 us
  transfers between devices with their start and end apart: 34, of which 18 were waited for; matrix products, arithmetic and copies ran while one was open for 4% of the time, Pallas kernels for 7%

profile of v2, /device:TPU:10, one launch (start us, length us, event | category | flops | bytes accessed | tf_op | source)
XLA Modules:
  0.0 288.5 jit_solution(3191598809909885432)
XLA Ops:
  9.0 6.4 %collective-permute-start = (f32[8,64,256]{2,1,0:T(8,128)S(1)}, f32[8,64,256]{2,1,0:T(8,128)S(1)}, u32[]{:S(2)}, u32[]{:S(2)}) collective-permute-start(f32[8,64,256]{2,1,0:T(8,128)S(1)} %bitcast.60), channel_id=1, source_target_pairs={{0,48},{16,0},{32,16},{48,32},{1,49},{17,1},{33,17},{49,33},{2,50}... | collective-permute-start | bytes 1572872 | tf_op jit(solution)/shard_map/ppermute | solution.py:306
  16.2 5.4 %all-to-all-start = ((f32[16,64,128]{2,1,0:T(8,128)}), f32[16,64,128]{2,1,0:T(8,128)S(1)}, u32[]{:S(2)}, u32[]{:S(2)}) async-start(f32[16,64,128]{2,1,0:T(8,128)} %bitcast_bitcast_fusion.1), calls=%async_computation | async-start | bytes 1048576 | tf_op jit(solution)/shard_map/all_to_all | solution.py:314
  23.2 2.0 shard_map.77
  25.2 1.5 collective-permute-start.4
  27.4 10.4 %collective-permute-done.refs_0_.refs_2_ = f32[8,64,256]{2,1,0:T(8,128)S(1)} collective-permute-done((f32[8,64,256]{2,1,0:T(8,128)S(1)}, f32[8,64,256]{2,1,0:T(8,128)S(1)}, u32[]{:S(2)}, u32[]{:S(2)}) %collective-permute-start) | collective-permute-done | bytes 524320 | tf_op jit(solution)/shard_map/ppermute | solution.py:306
  37.9 4.7 %collective-permute-start.1 = (f32[4,64,256]{2,1,0:T(8,128)S(1)}, f32[4,64,256]{2,1,0:T(8,128)S(1)}, u32[]{:S(2)}, u32[]{:S(2)}) collective-permute-start(f32[4,64,256]{2,1,0:T(8,128)S(1)} %slice.49), channel_id=1, source_target_pairs={{0,48},{16,0},{32,16},{48,32},{1,49},{17,1},{33,17},{49,33},{2,50}... | collective-permute-start | bytes 786440 | tf_op jit(solution)/shard_map/ppermute | solution.py:306
  43.4 2.5 shard_map.78
  45.9 1.5 collective-permute-start.7
  48.5 2.2 collective-permute-start.6
  51.1 7.4 %collective-permute-done.3.hi_ref.refs_1_ = f32[4,64,256]{2,1,0:T(8,128)S(1)} collective-permute-done((f32[4,64,256]{2,1,0:T(8,128)S(1)}, f32[4,64,256]{2,1,0:T(8,128)S(1)}, u32[]{:S(2)}, u32[]{:S(2)}) %collective-permute-start.3) | collective-permute-done | bytes 262176 | tf_op jit(solution)/shard_map/ppermute | solution.py:306
  59.5 2.0 shard_map.79
  61.5 6.7 %collective-permute-start.10 = (f32[4,64,256]{2,1,0:T(8,128)}, f32[4,64,256]{2,1,0:T(8,128)S(1)}, u32[]{:S(2)}, u32[]{:S(2)}) collective-permute-start(f32[4,64,256]{2,1,0:T(8,128)} %get-tuple-element.74), channel_id=1, source_target_pairs={{0,64},{64,128},{128,192},{192,0},{1,65},{65,129},{129,193},{193,1... | collective-permute-start | bytes 786440 | tf_op jit(solution)/shard_map/ppermute | solution.py:306
  68.3 2.2 collective-permute-done.6.refs_6_
  70.5 2.1 collective-permute-start.11
  73.1 4.3 %all-gather.2.cloned.1.call-done.in_ref = f32[1024,1024]{1,0:T(8,128)} async-done(((f32[64,1024]{1,0:T(8,128)}), f32[1024,1024]{1,0:T(8,128)}) %all-gather.2.cloned.1.call-update) | async-done | bytes 4194320 | tf_op jit(solution)/shard_map/all_gather | solution.py:324
  77.5 6.3 %shard_map.76 = (bf16[1024,1024]{1,0:T(8,128)(2,1)}, bf16[1024,1024]{1,0:T(8,128)(2,1)}, bf16[1024,1024]{1,0:T(8,128)(2,1)}, bf16[1024,1024]{1,0:T(8,128)(2,1)}) custom-call(f32[1024,1024]{1,0:T(8,128)} %all-gather.2.cloned.1.call-done.in_ref), custom_call_target="tpu_custom_call" | custom-call | flops 8388608 | bytes 12582912 | tf_op jit(solution)/shard_map/pallas_call | solution.py:152
  83.8 2.8 collective-permute-done.9.refs_9_
  86.6 5.5 %collective-permute-done.11.refs_11_ = f32[4,64,256]{2,1,0:T(8,128)S(1)} collective-permute-done((f32[4,64,256]{2,1,0:T(8,128)}, f32[4,64,256]{2,1,0:T(8,128)S(1)}, u32[]{:S(2)}, u32[]{:S(2)}) %collective-permute-start.11) | collective-permute-done | bytes 262176 | tf_op jit(solution)/shard_map/ppermute | solution.py:306
  92.1 2.4 collective-permute-done.12.refs_12_
  94.6 11.7 %shard_map.80 = f32[16,64,128]{2,1,0:T(8,128)} custom-call(s32[56]{0:T(128)} %clamp_bitcast_fusion.place_ref, f32[8,64,256]{2,1,0:T(8,128)} %bitcast.63, f32[4,64,256]{2,1,0:T(8,128)} %copy-done.8, f32[4,64,256]{2,1,0:T(8,128)} %copy-done.9, f32[8,64,256]{2,1,0:T(8,128)} %copy-done.3, f32[8,64,256]{2,1,0:T(8,128)} %copy-done.4, f32[4,64,256]{2,1,0:T(8,128)} %copy-done.14, ...), custom_call_target="tpu_custom_call" | custom-call | flops 1073741824 | bytes 13631488 | tf_op jit(solution)/shard_map/pallas_call | solution.py:125
  106.3 24.5 %all_to_all.30 = f32[16,64,128]{2,1,0:T(8,128)} all-to-all(f32[16,64,128]{2,1,0:T(8,128)} %shard_map.80), channel_id=1, replica_groups=mesh['x'=4,'zh'=4,'y'=4,'zl'=2,'c'=2] {'y','zl','c'}, dimensions={0} | all-to-all | bytes 1048576 | tf_op jit(solution)/shard_map/all_to_all | solution.py:314
  130.8 7.7 %shard_map.81 = (f32[1024,128]{1,0:T(8,128)}, f32[1024,128]{1,0:T(8,128)}, f32[1024,128]{1,0:T(8,128)}) custom-call(bf16[1024,1024]{1,0:T(8,128)(2,1)} %get-tuple-element.63.thi_ref, bf16[1024,1024]{1,0:T(8,128)(2,1)} %get-tuple-element.64.tlo_ref, bf16[1024,1024]{1,0:T(8,128)(2,1)} %get-tuple-element.65.hi_ref, ...), custom_call_target="tpu_custom_call" | custom-call | flops 1610612736 | bytes 10485760 | tf_op jit(solution)/shard_map/pallas_call | solution.py:199
  138.5 6.1 %all-to-all-start.2 = ((f32[16,64,128]{2,1,0:T(8,128)}), f32[16,64,128]{2,1,0:T(8,128)S(1)}, u32[]{:S(2)}, u32[]{:S(2)}) async-start(f32[16,64,128]{2,1,0:T(8,128)} %bitcast.73), calls=%async_computation.2 | async-start | bytes 1048576 | tf_op jit(solution)/shard_map/all_to_all | solution.py:314
  144.6 8.2 %all-to-all-done.2.back_ref = f32[16,64,128]{2,1,0:T(8,128)S(1)} async-done(((f32[16,64,128]{2,1,0:T(8,128)}), f32[16,64,128]{2,1,0:T(8,128)S(1)}, u32[]{:S(2)}, u32[]{:S(2)}) %all-to-all-start.2) | async-done | bytes 524320 | tf_op jit(solution)/shard_map/all_to_all | solution.py:314
  153.6 11.2 %shard_map.82 = (f32[8,64,256]{2,1,0:T(8,128)}, f32[4,64,256]{2,1,0:T(8,128)}, f32[4,64,256]{2,1,0:T(8,128)}, f32[8,64,256]{2,1,0:T(8,128)}, f32[8,64,256]{2,1,0...) custom-call(s32[56]{0:T(128)} %clamp_bitcast_fusion.place_ref, ...), custom_call_target="tpu_custom_call" | custom-call | flops 1073741824 | bytes 13631488 | tf_op jit(solution)/shard_map/pallas_call | solution.py:240
  166.1 4.0 %collective-permute-done.26 = f32[512,1024]{1,0:T(8,128)S(1)} collective-permute-done((f32[512,1024]{1,0:T(8,128)S(1)}, f32[512,1024]{1,0:T(8,128)S(1)}, u32[]{:S(2)}, u32[]{:S(2)}) %collective-permute-start.26) | collective-permute-done | bytes 2097184 | tf_op jit(solution)/shard_map/ppermute | solution.py:306
  170.2 2.3 convolution_add_fusion
  172.5 6.5 %all-to-all-start.4 = ((f32[4,128,1024]{2,1,0:T(8,128)}), f32[4,128,1024]{2,1,0:T(8,128)S(1)}, u32[]{:S(2)}, u32[]{:S(2)}) async-start(f32[4,128,1024]{2,1,0:T(8,128)} %bitcast.59), calls=%async_computation.4 | async-start | bytes 4194304 | tf_op jit(solution)/shard_map/all_to_all | solution.py:365
  179.7 1.4 collective-permute-start.14
  181.1 2.6 collective-permute-start.15
  183.8 3.8 %collective-permute-done.13.a_ref = f32[4,64,256]{2,1,0:T(8,128)S(1)} collective-permute-done((f32[4,64,256]{2,1,0:T(8,128)}, f32[4,64,256]{2,1,0:T(8,128)S(1)}, u32[]{:S(2)}, u32[]{:S(2)}) %collective-permute-start.13) | collective-permute-done | bytes 262176 | tf_op jit(solution)/shard_map/ppermute | solution.py:306
  187.6 5.7 %collective-permute-done.14.b_ref = f32[4,64,256]{2,1,0:T(8,128)S(1)} collective-permute-done((f32[4,64,256]{2,1,0:T(8,128)S(1)}, f32[4,64,256]{2,1,0:T(8,128)S(1)}, u32[]{:S(2)}, u32[]{:S(2)}) %collective-permute-start.14) | collective-permute-done | bytes 262176 | tf_op jit(solution)/shard_map/ppermute | solution.py:306
  195.2 2.7 collective-permute-start.16
  197.9 6.5 %all-to-all-done.4 = f32[4,128,1024]{2,1,0:T(8,128)S(1)} async-done(((f32[4,128,1024]{2,1,0:T(8,128)}), f32[4,128,1024]{2,1,0:T(8,128)S(1)}, u32[]{:S(2)}, u32[]{:S(2)}) %all-to-all-start.4) | async-done | bytes 2097184 | tf_op jit(solution)/shard_map/all_to_all | solution.py:365
  204.4 4.8 %all-to-all-start.3 = ((f32[16,64,128]{2,1,0:T(8,128)}), f32[16,64,128]{2,1,0:T(8,128)S(1)}, u32[]{:S(2)}, u32[]{:S(2)}) async-start(f32[16,64,128]{2,1,0:T(8,128)} %bitcast.72), calls=%async_computation.3 | async-start | bytes 1048576 | tf_op jit(solution)/shard_map/all_to_all | solution.py:314
  209.3 2.2 collective-permute-start.17
  211.5 2.3 shard_map.84
  214.1 4.3 %collective-permute-start.23 = (f32[4,64,256]{2,1,0:T(8,128)}, f32[4,64,256]{2,1,0:T(8,128)}, u32[]{:S(2)}, u32[]{:S(2)}) collective-permute-start(f32[4,64,256]{2,1,0:T(8,128)} %get-tuple-element.110), channel_id=1, source_target_pairs={{0,48},{16,0},{32,16},{48,32},{1,49},{17,1},{33,17},{49,33},{2,50}... | collective-permute-start | bytes 786440 | tf_op jit(solution)/shard_map/ppermute | solution.py:306
  220.4 1.6 collective-permute-start.27
  222.0 3.1 %collective-permute-done.17.b_ref = f32[8,64,256]{2,1,0:T(8,128)} collective-permute-done((f32[8,64,256]{2,1,0:T(8,128)}, f32[8,64,256]{2,1,0:T(8,128)}, u32[]{:S(2)}, u32[]{:S(2)}) %collective-permute-start.17) | collective-permute-done | bytes 524320 | tf_op jit(solution)/shard_map/ppermute | solution.py:306
  225.1 10.5 %collective-permute-done.18.c_ref = f32[8,64,256]{2,1,0:T(8,128)} collective-permute-done((f32[8,64,256]{2,1,0:T(8,128)}, f32[8,64,256]{2,1,0:T(8,128)}, u32[]{:S(2)}, u32[]{:S(2)}) %collective-permute-start.18) | collective-permute-done | bytes 524320 | tf_op jit(solution)/shard_map/ppermute | solution.py:306
  236.2 3.2 %shard_map.85 = (f32[8,64,256]{2,1,0:T(8,128)}, f32[8,64,256]{2,1,0:T(8,128)}) custom-call(s32[24]{0:T(128)} %reshape.135.index_ref, f32[8,64,256]{2,1,0:T(8,128)} %collective-permute-done.16.a_ref, f32[8,64,256]{2,1,0:T(8,128)} %collective-permute-done.17.b_ref, f32[8,64,256]{2,1,0:T(8,128)} %collective-permute-done.18.c_ref, ...), custom_call_target="tpu_custom_call" | custom-call | flops 196608 | bytes 3145728 | tf_op jit(solution)/shard_map/pallas_call | solution.py:294
  239.4 4.6 %collective-permute-start.25 = (f32[8,64,256]{2,1,0:T(8,128)}, f32[8,64,256]{2,1,0:T(8,128)S(1)}, u32[]{:S(2)}, u32[]{:S(2)}) collective-permute-start(f32[8,64,256]{2,1,0:T(8,128)} %get-tuple-element.112), channel_id=1, source_target_pairs={{0,48},{16,0},{32,16},{48,32},{1,49},{17,1},{33,17},{49,33},{2,50}... | collective-permute-start | bytes 1572872 | tf_op jit(solution)/shard_map/ppermute | solution.py:306
  244.0 1.5 collective-permute-start.19
  249.2 8.9 %all-to-all-start.5 = ((f32[16,32,128]{2,1,0:T(8,128)}), f32[16,32,128]{2,1,0:T(8,128)S(1)}, u32[]{:S(2)}, u32[]{:S(2)}) async-start(f32[16,32,128]{2,1,0:T(8,128)} %reshape.147), calls=%async_computation.5 | async-start | bytes 524288 | tf_op jit(solution)/shard_map/all_to_all | solution.py:369
  259.8 2.3 shard_map.83
  262.0 9.2 %collective-permute-done.25 = f32[8,64,256]{2,1,0:T(8,128)S(1)} collective-permute-done((f32[8,64,256]{2,1,0:T(8,128)}, f32[8,64,256]{2,1,0:T(8,128)S(1)}, u32[]{:S(2)}, u32[]{:S(2)}) %collective-permute-start.25) | collective-permute-done | bytes 524320 | tf_op jit(solution)/shard_map/ppermute | solution.py:306
  273.2 7.6 %all-to-all-done.5 = f32[16,32,128]{2,1,0:T(8,128)S(1)} async-done(((f32[16,32,128]{2,1,0:T(8,128)}), f32[16,32,128]{2,1,0:T(8,128)S(1)}, u32[]{:S(2)}, u32[]{:S(2)}) %all-to-all-start.5) | async-done | bytes 262176 | tf_op jit(solution)/shard_map/all_to_all | solution.py:369
  (124 shorter events, 24.8 us)
Async XLA Ops:
  7.2 8.2 %copy-start = (f32[2048,64]{0,1:T(8,128)S(1)}, f32[2048,64]{0,1:T(8,128)}, u32[]{:S(2)}) copy-start(f32[2048,64]{0,1:T(8,128)} %param.9) | copy-start | bytes 1572868
  7.2 14.5 %copy-start.22 = (s32[128,7]{0,1:T(8,128)S(1)}, s32[128,7]{0,1:T(8,128)}, u32[]{:S(2)}) copy-start(s32[128,7]{0,1:T(8,128)} %param.6) | copy-start | bytes 10756
  7.2 70.3 %all-gather.2.cloned.1.call-start = ((), (), s32[]{:S(2)}) async-start(), calls=%async_computation.6 | async-start | bytes 4456448 | tf_op jit(solution)/shard_map/all_gather | solution.py:324
  9.0 14.2 %copy-start.2 = (f32[8,8,8,256]{3,2,0,1:T(8,128)}, f32[8,8,8,256]{3,2,0,1:T(8,128)S(1)}, u32[]{:S(2)}) copy-start(f32[8,8,8,256]{3,2,0,1:T(8,128)S(1)} %copy.40) | copy-start | bytes 1572868
  9.0 28.8 %collective-permute-start = (f32[8,64,256]{2,1,0:T(8,128)S(1)}, f32[8,64,256]{2,1,0:T(8,128)S(1)}, u32[]{:S(2)}, u32[]{:S(2)}) collective-permute-start(f32[8,64,256]{2,1,0:T(8,128)S(1)} %bitcast.60), channel_id=1, source_target_pairs={{0,48},{16,0},{32,16},{48,32},{1,49},{17,1},{33,17},{49,33},{2,50}... | collective-permute-start | bytes 1572872 | tf_op jit(solution)/shard_map/ppermute | solution.py:306
  15.4 27.2 %collective-permute-start.2 = (f32[8,64,256]{2,1,0:T(8,128)S(1)}, f32[8,64,256]{2,1,0:T(8,128)S(1)}, u32[]{:S(2)}, u32[]{:S(2)}) collective-permute-start(f32[8,64,256]{2,1,0:T(8,128)S(1)} %bitcast.61), channel_id=1, source_target_pairs={{0,16},{16,32},{32,48},{48,0},{1,17},{17,33},{33,49},{49,1},{2,18}... | collective-permute-start | bytes 1572872 | tf_op jit(solution)/shard_map/ppermute | solution.py:306
  16.2 67.5 %all-to-all-start = ((f32[16,64,128]{2,1,0:T(8,128)}), f32[16,64,128]{2,1,0:T(8,128)S(1)}, u32[]{:S(2)}, u32[]{:S(2)}) async-start(f32[16,64,128]{2,1,0:T(8,128)} %bitcast_bitcast_fusion.1), calls=%async_computation | async-start | bytes 1048576 | tf_op jit(solution)/shard_map/all_to_all | solution.py:314
  25.2 23.3 %collective-permute-start.4 = (f32[4,64,256]{2,1,0:T(8,128)}, f32[4,64,256]{2,1,0:T(8,128)S(1)}, u32[]{:S(2)}, u32[]{:S(2)}) collective-permute-start(f32[4,64,256]{2,1,0:T(8,128)} %get-tuple-element.68), channel_id=1, source_target_pairs={{0,64},{64,128},{128,192},{192,0},{1,65},{65,129},{129,193},{193,1... | collective-permute-start | bytes 786440 | tf_op jit(solution)/shard_map/ppermute | solution.py:306
  37.9 12.8 %collective-permute-start.1 = (f32[4,64,256]{2,1,0:T(8,128)S(1)}, f32[4,64,256]{2,1,0:T(8,128)S(1)}, u32[]{:S(2)}, u32[]{:S(2)}) collective-permute-start(f32[4,64,256]{2,1,0:T(8,128)S(1)} %slice.49), channel_id=1, source_target_pairs={{0,48},{16,0},{32,16},{48,32},{1,49},{17,1},{33,17},{49,33},{2,50}... | collective-permute-start | bytes 786440 | tf_op jit(solution)/shard_map/ppermute | solution.py:306
  42.7 15.8 %collective-permute-start.3 = (f32[4,64,256]{2,1,0:T(8,128)S(1)}, f32[4,64,256]{2,1,0:T(8,128)S(1)}, u32[]{:S(2)}, u32[]{:S(2)}) collective-permute-start(f32[4,64,256]{2,1,0:T(8,128)S(1)} %slice.50), channel_id=1, source_target_pairs={{0,16},{16,32},{32,48},{48,0},{1,17},{17,33},{33,49},{49,1},{2,18}... | collective-permute-start | bytes 786440 | tf_op jit(solution)/shard_map/ppermute | solution.py:306
  45.9 26.6 %collective-permute-start.7 = (f32[8,64,256]{2,1,0:T(8,128)}, f32[8,64,256]{2,1,0:T(8,128)S(1)}, u32[]{:S(2)}, u32[]{:S(2)}) collective-permute-start(f32[8,64,256]{2,1,0:T(8,128)} %get-tuple-element.71), channel_id=1, source_target_pairs={{0,64},{64,128},{128,192},{192,0},{1,65},{65,129},{129,193},{193,1... | collective-permute-start | bytes 1572872 | tf_op jit(solution)/shard_map/ppermute | solution.py:306
  47.4 14.1 %collective-permute-start.5 = (f32[4,64,256]{2,1,0:T(8,128)}, f32[4,64,256]{2,1,0:T(8,128)}, u32[]{:S(2)}, u32[]{:S(2)}) collective-permute-start(f32[4,64,256]{2,1,0:T(8,128)} %get-tuple-element.69), channel_id=1, source_target_pairs={{0,128},{64,192},{128,0},{192,64},{1,129},{65,193},{129,1},{193,65... | collective-permute-start | bytes 786440 | tf_op jit(solution)/shard_map/ppermute | solution.py:306
  48.5 46.0 %copy-start.14 = (f32[4,64,256]{2,1,0:T(8,128)}, f32[4,64,256]{2,1,0:T(8,128)S(1)}, u32[]{:S(2)}) copy-start(f32[4,64,256]{2,1,0:T(8,128)S(1)} %collective-permute-done.4.refs_4_) | copy-start | bytes 786436
  48.5 22.0 %collective-permute-start.6 = (f32[4,64,256]{2,1,0:T(8,128)}, f32[4,64,256]{2,1,0:T(8,128)}, u32[]{:S(2)}, u32[]{:S(2)}) collective-permute-start(f32[4,64,256]{2,1,0:T(8,128)} %get-tuple-element.70), channel_id=1, source_target_pairs={{0,192},{64,0},{128,64},{192,128},{1,193},{65,1},{129,65},{193,129... | collective-permute-start | bytes 786440 | tf_op jit(solution)/shard_map/ppermute | solution.py:306
  50.7 8.9 %copy-start.8 = (f32[4,64,256]{2,1,0:T(8,128)}, f32[4,64,256]{2,1,0:T(8,128)S(1)}, u32[]{:S(2)}) copy-start(f32[4,64,256]{2,1,0:T(8,128)S(1)} %collective-permute-done.1.lo_ref.refs_0_) | copy-start | bytes 786436
  50.7 33.1 %collective-permute-start.8 = (f32[8,64,256]{2,1,0:T(8,128)}, f32[8,64,256]{2,1,0:T(8,128)S(1)}, u32[]{:S(2)}, u32[]{:S(2)}) collective-permute-start(f32[8,64,256]{2,1,0:T(8,128)} %get-tuple-element.72), channel_id=1, source_target_pairs={{0,128},{64,192},{128,0},{192,64},{1,129},{65,193},{129,1},{193,65... | collective-permute-start | bytes 1572872 | tf_op jit(solution)/shard_map/ppermute | solution.py:306
  58.4 28.1 %collective-permute-start.9 = (f32[8,64,256]{2,1,0:T(8,128)}, f32[8,64,256]{2,1,0:T(8,128)S(1)}, u32[]{:S(2)}, u32[]{:S(2)}) collective-permute-start(f32[8,64,256]{2,1,0:T(8,128)} %get-tuple-element.73), channel_id=1, source_target_pairs={{0,192},{64,0},{128,64},{192,128},{1,193},{65,1},{129,65},{193,129... | collective-permute-start | bytes 1572872 | tf_op jit(solution)/shard_map/ppermute | solution.py:306
  61.5 25.1 %collective-permute-start.10 = (f32[4,64,256]{2,1,0:T(8,128)}, f32[4,64,256]{2,1,0:T(8,128)S(1)}, u32[]{:S(2)}, u32[]{:S(2)}) collective-permute-start(f32[4,64,256]{2,1,0:T(8,128)} %get-tuple-element.74), channel_id=1, source_target_pairs={{0,64},{64,128},{128,192},{192,0},{1,65},{65,129},{129,193},{193,1... | collective-permute-start | bytes 786440 | tf_op jit(solution)/shard_map/ppermute | solution.py:306
  70.5 21.6 %collective-permute-start.11 = (f32[4,64,256]{2,1,0:T(8,128)}, f32[4,64,256]{2,1,0:T(8,128)S(1)}, u32[]{:S(2)}, u32[]{:S(2)}) collective-permute-start(f32[4,64,256]{2,1,0:T(8,128)} %get-tuple-element.75), channel_id=1, source_target_pairs={{0,128},{64,192},{128,0},{192,64},{1,129},{65,193},{129,1},{193,65... | collective-permute-start | bytes 786440 | tf_op jit(solution)/shard_map/ppermute | solution.py:306
  72.6 11.2 %copy-start.10 = (f32[8,64,256]{2,1,0:T(8,128)}, f32[8,64,256]{2,1,0:T(8,128)S(1)}, u32[]{:S(2)}) copy-start(f32[8,64,256]{2,1,0:T(8,128)S(1)} %collective-permute-done.7.refs_7_) | copy-start | bytes 1572868
  72.6 22.0 %collective-permute-start.12 = (f32[4,64,256]{2,1,0:T(8,128)}, f32[4,64,256]{2,1,0:T(8,128)}, u32[]{:S(2)}, u32[]{:S(2)}) collective-permute-start(f32[4,64,256]{2,1,0:T(8,128)} %get-tuple-element.76), channel_id=1, source_target_pairs={{0,192},{64,0},{128,64},{192,128},{1,193},{65,1},{129,65},{193,129... | collective-permute-start | bytes 786440 | tf_op jit(solution)/shard_map/ppermute | solution.py:306
  83.8 22.5 %copy-start.5 = (f32[16,64,128]{2,1,0:T(8,128)}, f32[16,64,128]{2,1,0:T(8,128)S(1)}, u32[]{:S(2)}) copy-start(f32[16,64,128]{2,1,0:T(8,128)S(1)} %all-to-all-done) | copy-start | bytes 1572868
  83.8 10.8 %copy-start.11 = (f32[8,64,256]{2,1,0:T(8,128)}, f32[8,64,256]{2,1,0:T(8,128)S(1)}, u32[]{:S(2)}) copy-start(f32[8,64,256]{2,1,0:T(8,128)S(1)} %collective-permute-done.8.refs_8_) | copy-start | bytes 1572868
  86.6 8.0 %copy-start.12 = (f32[8,64,256]{2,1,0:T(8,128)}, f32[8,64,256]{2,1,0:T(8,128)S(1)}, u32[]{:S(2)}) copy-start(f32[8,64,256]{2,1,0:T(8,128)S(1)} %collective-permute-done.9.refs_9_) | copy-start | bytes 1572868
  138.5 14.3 %all-to-all-start.2 = ((f32[16,64,128]{2,1,0:T(8,128)}), f32[16,64,128]{2,1,0:T(8,128)S(1)}, u32[]{:S(2)}, u32[]{:S(2)}) async-start(f32[16,64,128]{2,1,0:T(8,128)} %bitcast.73), calls=%async_computation.2 | async-start | bytes 1048576 | tf_op jit(solution)/shard_map/all_to_all | solution.py:314
  144.6 20.3 %copy-start.13 = (f32[1024,128]{1,0:T(8,128)S(1)}, f32[1024,128]{1,0:T(8,128)}, u32[]{:S(2)}) copy-start(f32[1024,128]{1,0:T(8,128)} %get-tuple-element.113) | copy-start | bytes 1572868
  144.6 20.3 %copy-start.1 = (f32[16,64,128]{2,1,0:T(8,128)S(1)}, f32[16,64,128]{2,1,0:T(8,128)}, u32[]{:S(2)}) copy-start(f32[16,64,128]{2,1,0:T(8,128)} %all_to_all.30) | copy-start | bytes 1572868
  165.9 4.2 %collective-permute-start.26 = (f32[512,1024]{1,0:T(8,128)S(1)}, f32[512,1024]{1,0:T(8,128)S(1)}, u32[]{:S(2)}, u32[]{:S(2)}) collective-permute-start(f32[512,1024]{1,0:T(8,128)S(1)} %fusion.4), channel_id=1, source_target_pairs={{0,1},{1,0},{2,3},{3,2},{4,5},{5,4},{6,7},{7,6},{8,9},{9,8},{10,11... | collective-permute-start | bytes 6291464 | tf_op jit(solution)/shard_map/ppermute | solution.py:306
  172.5 8.7 %copy-start.23 = (f32[4,64,256]{2,1,0:T(8,128)S(1)}, f32[4,64,256]{2,1,0:T(8,128)}, u32[]{:S(2)}) copy-start(f32[4,64,256]{2,1,0:T(8,128)} %get-tuple-element.85) | copy-start | bytes 786436
  172.5 31.9 %all-to-all-start.4 = ((f32[4,128,1024]{2,1,0:T(8,128)}), f32[4,128,1024]{2,1,0:T(8,128)S(1)}, u32[]{:S(2)}, u32[]{:S(2)}) async-start(f32[4,128,1024]{2,1,0:T(8,128)} %bitcast.59), calls=%async_computation.4 | async-start | bytes 4194304 | tf_op jit(solution)/shard_map/all_to_all | solution.py:365
  179.0 8.7 %collective-permute-start.13 = (f32[4,64,256]{2,1,0:T(8,128)}, f32[4,64,256]{2,1,0:T(8,128)S(1)}, u32[]{:S(2)}, u32[]{:S(2)}) collective-permute-start(f32[4,64,256]{2,1,0:T(8,128)} %get-tuple-element.83), channel_id=1, source_target_pairs={{0,192},{64,0},{128,64},{192,128},{1,193},{65,1},{129,65},{193,129... | collective-permute-start | bytes 786440 | tf_op jit(solution)/shard_map/ppermute | solution.py:306
  179.7 13.6 %collective-permute-start.14 = (f32[4,64,256]{2,1,0:T(8,128)S(1)}, f32[4,64,256]{2,1,0:T(8,128)S(1)}, u32[]{:S(2)}, u32[]{:S(2)}) collective-permute-start(f32[4,64,256]{2,1,0:T(8,128)S(1)} %copy-done.24), channel_id=1, source_target_pairs={{0,128},{64,192},{128,0},{192,64},{1,129},{65,193},{129,1},{193,65... | collective-permute-start | bytes 786440 | tf_op jit(solution)/shard_map/ppermute | solution.py:306
  181.1 13.3 %collective-permute-start.15 = (f32[4,64,256]{2,1,0:T(8,128)S(1)}, f32[4,64,256]{2,1,0:T(8,128)S(1)}, u32[]{:S(2)}, u32[]{:S(2)}) collective-permute-start(f32[4,64,256]{2,1,0:T(8,128)S(1)} %copy-done.23), channel_id=1, source_target_pairs={{0,64},{64,128},{128,192},{192,0},{1,65},{65,129},{129,193},{193,1... | collective-permute-start | bytes 786440 | tf_op jit(solution)/shard_map/ppermute | solution.py:306
  187.6 23.9 %copy-start.16 = (f32[4,64,256]{2,1,0:T(8,128)}, f32[4,64,256]{2,1,0:T(8,128)S(1)}, u32[]{:S(2)}) copy-start(f32[4,64,256]{2,1,0:T(8,128)S(1)} %collective-permute-done.13.a_ref) | copy-start | bytes 786436
  195.2 25.2 %collective-permute-start.16 = (f32[8,64,256]{2,1,0:T(8,128)}, f32[8,64,256]{2,1,0:T(8,128)}, u32[]{:S(2)}, u32[]{:S(2)}) collective-permute-start(f32[8,64,256]{2,1,0:T(8,128)} %get-tuple-element.89), channel_id=1, source_target_pairs={{0,192},{64,0},{128,64},{192,128},{1,193},{65,1},{129,65},{193,129... | collective-permute-start | bytes 1572872 | tf_op jit(solution)/shard_map/ppermute | solution.py:306
  204.4 44.8 %all-to-all-start.3 = ((f32[16,64,128]{2,1,0:T(8,128)}), f32[16,64,128]{2,1,0:T(8,128)S(1)}, u32[]{:S(2)}, u32[]{:S(2)}) async-start(f32[16,64,128]{2,1,0:T(8,128)} %bitcast.72), calls=%async_computation.3 | async-start | bytes 1048576 | tf_op jit(solution)/shard_map/all_to_all | solution.py:314
  209.3 15.8 %collective-permute-start.17 = (f32[8,64,256]{2,1,0:T(8,128)}, f32[8,64,256]{2,1,0:T(8,128)}, u32[]{:S(2)}, u32[]{:S(2)}) collective-permute-start(f32[8,64,256]{2,1,0:T(8,128)} %get-tuple-element.90), channel_id=1, source_target_pairs={{0,128},{64,192},{128,0},{192,64},{1,129},{65,193},{129,1},{193,65... | collective-permute-start | bytes 1572872 | tf_op jit(solution)/shard_map/ppermute | solution.py:306
  211.4 24.1 %collective-permute-start.18 = (f32[8,64,256]{2,1,0:T(8,128)}, f32[8,64,256]{2,1,0:T(8,128)}, u32[]{:S(2)}, u32[]{:S(2)}) collective-permute-start(f32[8,64,256]{2,1,0:T(8,128)} %get-tuple-element.91), channel_id=1, source_target_pairs={{0,64},{64,128},{128,192},{192,0},{1,65},{65,129},{129,193},{193,1... | collective-permute-start | bytes 1572872 | tf_op jit(solution)/shard_map/ppermute | solution.py:306
  213.8 21.8 %collective-permute-start.22 = (f32[4,64,256]{2,1,0:T(8,128)}, f32[4,64,256]{2,1,0:T(8,128)S(1)}, u32[]{:S(2)}, u32[]{:S(2)}) collective-permute-start(f32[4,64,256]{2,1,0:T(8,128)} %get-tuple-element.109), channel_id=1, source_target_pairs={{0,16},{16,32},{32,48},{48,0},{1,17},{17,33},{33,49},{49,1},{2,18}... | collective-permute-start | bytes 786440 | tf_op jit(solution)/shard_map/ppermute | solution.py:306
  214.1 21.5 %collective-permute-start.23 = (f32[4,64,256]{2,1,0:T(8,128)}, f32[4,64,256]{2,1,0:T(8,128)}, u32[]{:S(2)}, u32[]{:S(2)}) collective-permute-start(f32[4,64,256]{2,1,0:T(8,128)} %get-tuple-element.110), channel_id=1, source_target_pairs={{0,48},{16,0},{32,16},{48,32},{1,49},{17,1},{33,17},{49,33},{2,50}... | collective-permute-start | bytes 786440 | tf_op jit(solution)/shard_map/ppermute | solution.py:306
  219.3 28.3 %copy-start.7 = (f32[128,1024]{1,0:T(8,128)S(1)}, f32[128,1024]{1,0:T(8,128)}, u32[]{:S(2)}) copy-start(f32[128,1024]{1,0:T(8,128)} %reduce_sum.38) | copy-start | bytes 1572868
  220.4 27.2 %collective-permute-start.27 = (f32[64,1024]{1,0:T(8,128)S(1)}, f32[64,1024]{1,0:T(8,128)S(1)}, u32[]{:S(2)}, u32[]{:S(2)}) collective-permute-start(f32[64,1024]{1,0:T(8,128)S(1)} %dynamic-slice_bitcast_fusion), channel_id=1, source_target_pairs={{0,2},{2,0},{1,3},{3,1},{4,6},{6,4},{5,7},{7,5},{8,10},{10,8},{9,1... | collective-permute-start | bytes 786440 | tf_op jit(solution)/shard_map/ppermute | solution.py:306
  239.4 31.8 %collective-permute-start.25 = (f32[8,64,256]{2,1,0:T(8,128)}, f32[8,64,256]{2,1,0:T(8,128)S(1)}, u32[]{:S(2)}, u32[]{:S(2)}) collective-permute-start(f32[8,64,256]{2,1,0:T(8,128)} %get-tuple-element.112), channel_id=1, source_target_pairs={{0,48},{16,0},{32,16},{48,32},{1,49},{17,1},{33,17},{49,33},{2,50}... | collective-permute-start | bytes 1572872 | tf_op jit(solution)/shard_map/ppermute | solution.py:306
  244.0 15.0 %collective-permute-start.19 = (f32[4,64,256]{2,1,0:T(8,128)}, f32[4,64,256]{2,1,0:T(8,128)S(1)}, u32[]{:S(2)}, u32[]{:S(2)}) collective-permute-start(f32[4,64,256]{2,1,0:T(8,128)} %get-tuple-element.95), channel_id=1, source_target_pairs={{0,192},{64,0},{128,64},{192,128},{1,193},{65,1},{129,65},{193,129... | collective-permute-start | bytes 786440 | tf_op jit(solution)/shard_map/ppermute | solution.py:306
  245.5 13.5 %collective-permute-start.20 = (f32[4,64,256]{2,1,0:T(8,128)}, f32[4,64,256]{2,1,0:T(8,128)}, u32[]{:S(2)}, u32[]{:S(2)}) collective-permute-start(f32[4,64,256]{2,1,0:T(8,128)} %get-tuple-element.96), channel_id=1, source_target_pairs={{0,128},{64,192},{128,0},{192,64},{1,129},{65,193},{129,1},{193,65... | collective-permute-start | bytes 786440 | tf_op jit(solution)/shard_map/ppermute | solution.py:306
  246.9 12.9 %collective-permute-start.21 = (f32[4,64,256]{2,1,0:T(8,128)}, f32[4,64,256]{2,1,0:T(8,128)}, u32[]{:S(2)}, u32[]{:S(2)}) collective-permute-start(f32[4,64,256]{2,1,0:T(8,128)} %get-tuple-element.97), channel_id=1, source_target_pairs={{0,64},{64,128},{128,192},{192,0},{1,65},{65,129},{129,193},{193,1... | collective-permute-start | bytes 786440 | tf_op jit(solution)/shard_map/ppermute | solution.py:306
  247.6 23.6 %collective-permute-start.24 = (f32[8,64,256]{2,1,0:T(8,128)}, f32[8,64,256]{2,1,0:T(8,128)S(1)}, u32[]{:S(2)}, u32[]{:S(2)}) collective-permute-start(f32[8,64,256]{2,1,0:T(8,128)} %get-tuple-element.111), channel_id=1, source_target_pairs={{0,16},{16,32},{32,48},{48,0},{1,17},{17,33},{33,49},{49,1},{2,18}... | collective-permute-start | bytes 1572872 | tf_op jit(solution)/shard_map/ppermute | solution.py:306
  249.2 31.5 %all-to-all-start.5 = ((f32[16,32,128]{2,1,0:T(8,128)}), f32[16,32,128]{2,1,0:T(8,128)S(1)}, u32[]{:S(2)}, u32[]{:S(2)}) async-start(f32[16,32,128]{2,1,0:T(8,128)} %reshape.147), calls=%async_computation.5 | async-start | bytes 524288 | tf_op jit(solution)/shard_map/all_to_all | solution.py:369
  (11 other events, 28.7 us)
Sparse Core Ops, SparseCore 0:
  9.9 67.5 all-gather.1

commit v3 on v2

--- a/solution.py
+++ b/solution.py
@@ -14,7 +14,8 @@
 BLK, FAN, W, C = 8, 8, 256, 64
 REFS = BLK * (FAN - 1)
 SLOTS = 4
-HELD = 72
+FAR = 60
+HELD = FAR + 1
 F = 1024
 CHUNK = 128
 f32, bf16 = jnp.float32, jnp.bfloat16
@@ -52,11 +53,15 @@
     near = table[0].reshape(12)
     mid = jnp.stack([table[1], table[3]], axis=1).reshape(24)
     far = table[2].reshape(12)
-    return near, mid, far, jnp.clip(place, 0, HELD - 1)
-
-
-def pick_kernel(index_ref, *refs):
-    sources, outs = refs[:-3], refs[-3:]
+    source = ((me_x - jnp.arange(1, NX)) & 3) * NZ + ((me_z + 2) & 3)
+    match = (owner[0][None, None, :] == source[:, None, None]) & (
+        rank[0][None, None, :] == jnp.arange(SLOTS)[None, :, None]
+    )
+    far_refs = jnp.sum(jnp.where(match, ref[None, None, :] + 1, 0), axis=2).reshape(12)
+    return near, mid, far, far_refs, jnp.clip(place, 0, FAR)
+
+
+def pick_slots(index_ref, sources, outs):
     per = outs[0].shape[0]
     for s in range(3):
         for slot in range(per):
@@ -64,23 +69,32 @@
             outs[s][slot] = sources[slot // SLOTS][index]
 
 
-def pick_halves_kernel(index_ref, lo_ref, hi_ref, *refs):
+def pick_near_kernel(index_ref, own_ref, *outs):
+    pick_slots(index_ref, (own_ref,), outs)
+
+
+def pick_mid_kernel(index_ref, up_ref, down_ref, lo_ref, hi_ref, *outs):
+    lo_ref[...] = up_ref[: BLK // 2]
+    hi_ref[...] = down_ref[BLK // 2 :]
+    pick_slots(index_ref, (up_ref, down_ref), outs)
+
+
+def pick_far_kernel(index_ref, lo_ref, hi_ref, *refs):
     outs, held = refs[:3], refs[3]
     held[: BLK // 2] = lo_ref[...]
     held[BLK // 2 :] = hi_ref[...]
-    pick_kernel(index_ref, held, *outs)
-
-
-def pick(index, *sources, halves=False):
-    per = SLOTS * (1 if halves else len(sources))
-    return pl.pallas_call(
-        pick_halves_kernel if halves else pick_kernel,
-        out_shape=[jax.ShapeDtypeStruct((per, C, W), f32)] * 3,
+    pick_slots(index_ref, (held,), outs)
+
+
+def pick(kernel, shapes, scratch, index, *sources):
+    return pl.pallas_call(
+        kernel,
+        out_shape=[jax.ShapeDtypeStruct((n, C, W), f32) for n in shapes],
         in_specs=[SMEM] + [VMEM] * len(sources),
-        out_specs=[VMEM] * 3,
-        scratch_shapes=[pltpu.VMEM((BLK, C, W), f32)] if halves else [],
-        compiler_params=PARAMS,
-        cost_estimate=pl.CostEstimate(flops=0, bytes_accessed=per * C * W * 24, transcendentals=0),
+        out_specs=[VMEM] * len(shapes),
+        scratch_shapes=scratch,
+        compiler_params=PARAMS,
+        cost_estimate=pl.CostEstimate(flops=0, bytes_accessed=2 << 20, transcendentals=0),
     )(index, *sources)
 
 
@@ -93,7 +107,7 @@
 
 
 def mixed_kernel(place_ref, own_ref, *refs):
-    sources, tiles_ref, out_ref, held, sems = refs[:13], *refs[13:]
+    sources, tiles_ref, out_ref, held, sems = refs[:10], *refs[10:]
     i = pl.program_id(0)
 
     @pl.when(i == 0)
@@ -103,6 +117,7 @@
         ]
         for copy in copies:
             copy.start()
+        held[FAR] = jnp.zeros((C, W), f32)
         for copy in copies:
             copy.wait()
 
@@ -116,9 +131,7 @@
             preferred_element_type=f32,
         )
         acc = part if acc is None else acc + part
-    value = acc[:C] + acc[C:]
-    out_ref[0] = value[:, :CHUNK]
-    out_ref[1] = value[:, CHUNK:]
+    out_ref[0] = acc[:C] + acc[C:]
 
 
 def mix(place, own, sources, tiles):
@@ -130,13 +143,58 @@
             in_specs=[pl.BlockSpec((1, C, W), lambda i, s: (i, 0, 0))]
             + [ANY] * len(sources)
             + [pl.BlockSpec((1, FAN, W, W), lambda i, s: (i, 0, 0, 0))],
-            out_specs=pl.BlockSpec((2, C, CHUNK), lambda i, s: (i, 0, 0)),
+            out_specs=pl.BlockSpec((1, C, W), lambda i, s: (i, 0, 0)),
             scratch_shapes=[pltpu.VMEM((HELD, C, W), f32), pltpu.SemaphoreType.DMA((len(sources),))],
         ),
-        out_shape=jax.ShapeDtypeStruct((16, C, CHUNK), f32),
+        out_shape=jax.ShapeDtypeStruct((BLK, C, W), f32),
         compiler_params=PARAMS,
         cost_estimate=pl.CostEstimate(flops=2 * 64 * W * W * 2 * C, bytes_accessed=13 << 20, transcendentals=0),
     )(place, own, *sources, tiles)
+
+
+def tile_copies(refs_ref, tiles_ref, held, sems):
+    copies = []
+    for slot in range(12):
+        ref = jnp.maximum(refs_ref[slot] - 1, 0)
+        i = ref // (FAN - 1)
+        copies.append(
+            pltpu.make_async_copy(tiles_ref.at[i, ref - i * (FAN - 1) + 1], held.at[slot], sems.at[slot])
+        )
+    for copy in copies:
+        copy.start()
+    return copies
+
+
+def mix_far_kernel(refs_ref, part_ref, a_ref, b_ref, c_ref, tiles_ref, out_ref, held, total, sems):
+    copies = tile_copies(refs_ref, tiles_ref, held, sems)
+    total[...] = part_ref[...]
+    for copy in copies:
+        copy.wait()
+    for slot in range(12):
+        both = jnp.concatenate(split((a_ref, b_ref, c_ref)[slot // SLOTS][slot % SLOTS]), axis=0)
+        part = lax.dot_general(both, held[slot], (((1,), (1,)), ((), ())), preferred_element_type=f32)
+        ref = refs_ref[slot]
+        total[jnp.maximum(ref - 1, 0) // (FAN - 1)] += jnp.where(ref > 0, part[:C] + part[C:], 0.0)
+
+    for i in range(BLK):
+        out_ref[2 * i] = total[i, :, :CHUNK]
+        out_ref[2 * i + 1] = total[i, :, CHUNK:]
+
+
+def mix_far(far_refs, part, far, tiles):
+    return pl.pallas_call(
+        mix_far_kernel,
+        out_shape=jax.ShapeDtypeStruct((16, C, CHUNK), f32),
+        in_specs=[SMEM] + [VMEM] * 4 + [ANY],
+        out_specs=VMEM,
+        scratch_shapes=[
+            pltpu.VMEM((12, W, W), bf16),
+            pltpu.VMEM((BLK, C, W), f32),
+            pltpu.SemaphoreType.DMA((12,)),
+        ],
+        compiler_params=PARAMS,
+        cost_estimate=pl.CostEstimate(flops=2 * 12 * W * W * 2 * C, bytes_accessed=4 << 20, transcendentals=0),
+    )(far_refs, part, *far, tiles)
 
 
 def weight_kernel(in_ref, thi_ref, tlo_ref, hi_ref, lo_ref):
@@ -160,7 +218,7 @@
     )(transposed)
 
 
-def dense_kernel(thi_ref, tlo_ref, hi_ref, lo_ref, mixed_ref, cot_ref, hidden_ref, slope_ref, back_ref, parts):
+def dense_kernel(thi_ref, tlo_ref, hi_ref, lo_ref, mixed_ref, cot_ref, slope_ref, out_ref, parts):
     step = pl.program_id(0)
 
     @pl.when(step == 0)
@@ -173,21 +231,22 @@
     low = jnp.dot(tlo_ref[...], parts[:, :CHUNK], preferred_element_type=f32)
     pre = both[:, :CHUNK] + (both[:, CHUNK:] + low)
     sig = jax.nn.sigmoid(pre)
-    hidden_ref[...] = pre * sig
+    hidden = (pre * sig).reshape(-1, C, CHUNK)
+    out_ref[pl.ds(step * hidden.shape[0], hidden.shape[0]), C:] = hidden
     slope = cot_ref[...] * sig * (1.0 + pre * (1.0 - sig))
     slope_ref[...] = slope
     shi, slo = split(slope)
     both = jnp.dot(hi_ref[...], jnp.concatenate([shi, slo], axis=1), preferred_element_type=f32)
     low = jnp.dot(lo_ref[...], shi, preferred_element_type=f32)
-    part = both[:, :CHUNK] + (both[:, CHUNK:] + low)
+    part = (both[:, :CHUNK] + (both[:, CHUNK:] + low)).reshape(16, C, CHUNK)
 
     @pl.when(step == 0)
     def _():
-        back_ref[...] = part
+        out_ref[:, :C] = part
 
     @pl.when(step > 0)
     def _():
-        back_ref[...] += part
+        out_ref[:, :C] += part
 
 
 def dense(weights, mixed, cot):
@@ -200,16 +259,41 @@
         dense_kernel,
         grid=(F // step,),
         in_specs=[by_row, by_row, by_col, by_col, whole, rows],
-        out_specs=[rows, rows, whole],
-        out_shape=[jax.ShapeDtypeStruct((F, CHUNK), f32)] * 3,
+        out_specs=[rows, pl.BlockSpec((16, 2 * C, CHUNK), lambda i: (0, 0, 0))],
+        out_shape=[jax.ShapeDtypeStruct((F, CHUNK), f32), jax.ShapeDtypeStruct((16, 2 * C, CHUNK), f32)],
         scratch_shapes=[pltpu.VMEM((F, 2 * CHUNK), bf16)],
         compiler_params=PARAMS,
         cost_estimate=pl.CostEstimate(flops=12 * F * F * CHUNK, bytes_accessed=10 << 20, transcendentals=F * CHUNK),
     )(*weights, mixed, cot)
 
 
+def push_far_kernel(refs_ref, back_ref, tiles_ref, a_ref, b_ref, c_ref, held, sems):
+    copies = tile_copies(refs_ref, tiles_ref, held, sems)
+    for copy in copies:
+        copy.wait()
+    for slot in range(12):
+        ref = refs_ref[slot]
+        i = jnp.maximum(ref - 1, 0) // (FAN - 1)
+        block = jnp.concatenate([back_ref[2 * i, :C], back_ref[2 * i + 1, :C]], axis=1)
+        both = jnp.concatenate(split(block), axis=0)
+        part = jnp.dot(both, held[slot], preferred_element_type=f32)
+        (a_ref, b_ref, c_ref)[slot // SLOTS][slot % SLOTS] = part[:C] + part[C:]
+
+
+def push_far(far_refs, back, tiles):
+    return pl.pallas_call(
+        push_far_kernel,
+        out_shape=[jax.ShapeDtypeStruct((SLOTS, C, W), f32)] * 3,
+        in_specs=[SMEM, VMEM, ANY],
+        out_specs=[VMEM] * 3,
+        scratch_shapes=[pltpu.VMEM((12, W, W), bf16), pltpu.SemaphoreType.DMA((12,))],
+        compiler_params=PARAMS,
+        cost_estimate=pl.CostEstimate(flops=2 * 12 * W * W * 2 * C, bytes_accessed=4 << 20, transcendentals=0),
+    )(far_refs, back, tiles)
+
+
 def push_kernel(place_ref, back_ref, tiles_ref, diag_ref, *refs):
-    outs, held, sems = refs[:13], *refs[13:]
+    outs, held, sems = refs[:10], *refs[10:]
     i = pl.program_id(0)
 
     @pl.when(i == 0)
@@ -236,7 +320,7 @@
 
 
 def push(place, back, tiles):
-    sizes = (4, 4, 8, 8, 4, 4, 4, 8, 8, 8, 4, 4, 4)
+    sizes = (4, 4, 8, 8, 4, 4, 4, 8, 8, 8)
     return pl.pallas_call(
         push_kernel,
         grid_spec=pltpu.PrefetchScalarGridSpec(
@@ -261,10 +345,7 @@
         for t in range(SLOTS):
             slot = group * SLOTS + t
             index = index_ref[s * per + slot]
-
-            @pl.when(index > 0)
-            def _():
-                out_ref[index - 1] += got[s][slot]
+            out_ref[jnp.maximum(index - 1, 0)] += jnp.where(index > 0, got[s][slot], 0.0)
 
 
 def far_kernel(index_ref, a_ref, b_ref, c_ref, lo_ref, hi_ref, out_lo, out_hi, total):
@@ -314,60 +395,107 @@
     return lax.all_to_all(value, COL, 0, 0, tiled=True)
 
 
+def grad_kernel(core_ref, slope_ref, other_ref, mixed_ref, far_ref, out_ref, wide):
+    @pl.when(pl.program_id(0) == 0)
+    def _():
+        for n, ref in enumerate((mixed_ref, far_ref)):
+            hi, lo = split(ref[...])
+            for m, value in enumerate((hi, lo, hi)):
+                start = (2 * m + n) * CHUNK
+                wide[:, start : start + CHUNK] = value
+
+    rows = out_ref.shape[0]
+    mine, other = split(slope_ref[...].reshape(rows, CHUNK)), split(other_ref[...])
+    left = jnp.concatenate([mine[0], other[0], mine[0], other[0], mine[1], other[1]], axis=1)
+    out_ref[...] = lax.dot_general(left, wide[...], (((1,), (1,)), ((), ())), preferred_element_type=f32)
+
+
+def grad_part(core, slope, other, mixed, mixed_other):
+    steps = 4
+    rows = 8 * C // steps
+    whole = pl.BlockSpec((F, CHUNK), lambda i, s: (0, 0))
+    return pl.pallas_call(
+        grad_kernel,
+        grid_spec=pltpu.PrefetchScalarGridSpec(
+            num_scalar_prefetch=1,
+            grid=(steps,),
+            in_specs=[
+                pl.BlockSpec((8 // steps, 1, C, CHUNK), lambda i, s: (i, s[0], 0, 0)),
+                pl.BlockSpec((rows, CHUNK), lambda i, s: (i, 0)),
+                whole,
+                whole,
+            ],
+            out_specs=pl.BlockSpec((rows, F), lambda i, s: (i, 0)),
+            scratch_shapes=[pltpu.VMEM((F, 6 * CHUNK), bf16)],
+        ),
+        out_shape=jax.ShapeDtypeStruct((8 * C, F), f32),
+        compiler_params=PARAMS,
+        cost_estimate=pl.CostEstimate(flops=6 * F * F * CHUNK, bytes_accessed=4 << 20, transcendentals=0),
+    )(core.reshape(1).astype(jnp.int32), slope.reshape(8, 2, C, CHUNK), other, mixed, mixed_other)
+
+
+def after(values, others):
+    flat, tree = jax.tree.flatten((values, others))
+    return jax.tree.unflatten(tree, lax.optimization_barrier(flat))
+
+
 def on_device(features, neighbours, tiles, weight, cotangent):
-    near_at, mid_at, far_at, place = tables(neighbours)
+    near_at, mid_at, far_at, far_refs, place = tables(neighbours)
     own = features.T.reshape(C, BLK, W).transpose(1, 0, 2)
+    me_c = lax.axis_index("c")
 
     up = shift(own, "zh", NZ, -1)
     down = shift(own, "zh", NZ, 1)
-    near = over_x(pick(near_at, own), 1)
-    weights = weight_parts(lax.all_gather(weight.T, COL, axis=0, tiled=True))
-    cot = over_col(cotangent.T.reshape(C, 16, CHUNK).transpose(1, 0, 2)).reshape(F, CHUNK)
-    far_lo = shift(up[: BLK // 2], "zh", NZ, -1)
-    far_hi = shift(down[BLK // 2 :], "zh", NZ, 1)
-    mid = over_x(pick(mid_at, up, down), 1)
-    far = over_x(pick(far_at, far_lo, far_hi, halves=True), 1)
-    own, weights, cot = lax.optimization_barrier((own, weights, cot))
-    mixed = mix(place, own, [far_lo, far_hi, up, down, *near, *mid, *far], tiles)
-
+    near = over_x(pick(pick_near_kernel, (4,) * 3, [], near_at, own), 1)
+    (up, down), (near, weight_t) = after((up, down), (near, weight.T))
+    weight_t = lax.all_gather(weight_t, COL, axis=0, tiled=True)
+    lo, hi, *mid = pick(pick_mid_kernel, (4, 4) + (8,) * 3, [], mid_at, up, down)
+    mid, cot = after(mid, cotangent.T)
+    lo = shift(lo, "zh", NZ, -1)
+    hi = shift(hi, "zh", NZ, 1)
+    mid = over_x(mid, 1)
+    cot = over_col(cot.reshape(C, 16, CHUNK).transpose(1, 0, 2)).reshape(F, CHUNK)
+    (lo, hi, mid), cot = after((lo, hi, mid), cot)
+    far = pick(pick_far_kernel, (4,) * 3, [pltpu.VMEM((BLK, C, W), f32)], far_at, lo, hi)
+    far = over_x(far, 1)
+    part = mix(place, own, [lo, hi, up, down, *near, *mid], tiles)
+    mixed = mix_far(far_refs, part, far, tiles)
+
+    mixed, weight_t = after(mixed, weight_t)
     mixed = over_col(mixed).reshape(F, CHUNK)
-    hidden, slope, back = dense(weights, mixed, cot)
-    back = over_col(back.reshape(16, C, CHUNK))
-
+    weights = weight_parts(weight_t)
+    slope, back = dense(weights, mixed, cot)
+    back = over_col(back)
+    hidden = back[:, C:].transpose(1, 0, 2).reshape(C, 16 * CHUNK).T
+
+    other = lax.dynamic_index_in_dim(slope.reshape(8, 2, C, CHUNK), 1 - me_c, 1, keepdims=False)
+    other = shift(other.reshape(8 * C, CHUNK), "c", 2, 1)
+    grad = grad_part(me_c, slope, other, mixed, shift(mixed, "c", 2, 1))
+    back, grad = after(back, grad)
+
+    far = push_far(far_refs, back, tiles)
+    far, grad = after(far, grad)
+    far = over_x(far, -1)
+    grad = lax.all_to_all(grad.reshape(8, C, F), ("y", "zl"), 0, 0, tiled=True)
     diag, lo, hi, up, down, *pieces = push(place, back, tiles)
-    diag, hidden, slope, mixed = lax.optimization_barrier((diag, hidden, slope, mixed))
-    near, mid, far = pieces[:3], pieces[3:6], pieces[6:]
-    far = over_x(far, -1)
-    far, mid = lax.optimization_barrier((far, mid))
+    near, mid = pieces[:3], pieces[3:]
+    far, (mid, hidden) = after(far, (mid, hidden))
     mid = over_x(mid, -1)
     lo, hi = gather_sum(far_kernel, (4, 4), [pltpu.VMEM((BLK, C, W), f32)], far_at, *far, lo, hi)
-    below = shift(lo, "zh", NZ, 1)
-    above = shift(hi, "zh", NZ, -1)
-    mid, near = lax.optimization_barrier((mid, near))
-    near = over_x(near, -1)
-    up, down = gather_sum(mid_kernel, (8, 8), [], mid_at, *mid, up, down, below, above)
+    lo = shift(lo, "zh", NZ, 1)
+    hi = shift(hi, "zh", NZ, -1)
+    grad = grad.sum(axis=0)
+    grad = grad.reshape(2, C // 2, 16, C).transpose(2, 1, 0, 3).reshape(16, C // 2, 2 * C)
+    (mid, lo, hi), (near, grad) = after((mid, lo, hi), (near, grad))
+    up, down = gather_sum(mid_kernel, (8, 8), [], mid_at, *mid, up, down, lo, hi)
+    (up, down), (near, grad) = after((up, down), (near, grad))
     up = shift(up, "zh", NZ, 1)
     down = shift(down, "zh", NZ, -1)
+    near = over_x(near, -1)
+    grad = lax.all_to_all(grad, DOM, 0, 0, tiled=True).sum(axis=0)
     (near,) = gather_sum(near_kernel, (8,), [], near_at, *near, diag)
+    grad_weight = grad.reshape(C // 2, 2, C).transpose(1, 0, 2).reshape(C, C).T
     grad_features = (near + up + down).transpose(1, 0, 2).reshape(C, BLK * W).T
-    hidden = over_col(hidden.reshape(16, C, CHUNK)).transpose(1, 0, 2).reshape(C, 16 * CHUNK).T
-
-    me_c, me_l = lax.axis_index("c"), lax.axis_index("zl")
-    by_core = slope.reshape(8, 2, C, CHUNK)
-
-    def partial(core):
-        rows = lax.dynamic_index_in_dim(by_core, core, 1, keepdims=False).reshape(8 * C, CHUNK)
-        return lax.dot_general(
-            rows, mixed, (((1,), (1,)), ((), ())), precision=lax.Precision.HIGH, preferred_element_type=f32
-        )
-
-    grad = partial(me_c) + shift(partial(1 - me_c), "c", 2, 1)
-    grad = lax.all_to_all(grad.reshape(NY, 2 * C, F), "y", 0, 0, tiled=True).sum(axis=0).reshape(2, C, F)
-    other = shift(lax.dynamic_index_in_dim(grad, 1 - me_l, 0, keepdims=False), "zl", 2, 1)
-    grad = lax.dynamic_index_in_dim(grad, me_l, 0, keepdims=False) + other
-    grad = grad.reshape(2, C // 2, 16, C).transpose(2, 1, 0, 3).reshape(16, C // 2, 2 * C)
-    grad = lax.all_to_all(grad, DOM, 0, 0, tiled=True).sum(axis=0)
-    grad_weight = grad.reshape(C // 2, 2, C).transpose(1, 0, 2).reshape(C, C).T
     return hidden, grad_features, grad_weight
 
 

time: 291 us -> 255 us (0.88)
  blocking collectives: 24.5 us -> 0 us
  waiting for transfers between devices: 96.4 us -> 74.2 us
  Pallas kernels: 51 us -> 64.6 us
  matrix products: 3.32 us -> 0 us
  local copies, waits for them, and re-layouts: 12.1 us -> 15.3 us
    all_to_all x1 -> x0, blocking collectives: 24.5 us -> none  [over_col(): return lax.all_to_all(value, COL, 0, 0, tiled=True)]
    pallas_call x3 -> x6, Pallas kernels: 6.51 us -> 20.7 us  [the longest x3 7.02 us: pick(): pl.pallas_call(kernel, out_shape=[jax.ShapeDtypeStruct((n, C, W), f32) fo...]
    ppermute x28, waiting for transfers between devices: 69.1 us -> 59.8 us  [shift(): lax.ppermute(value, axis, [(i, (i + by) % size) for i in range(size)])]
    all_to_all x1, waiting for transfers between devices: 6.48 us -> 0.01 us  [on_device(): grad = lax.all_to_all(grad.reshape(8, C, F), ('y', 'zl'), 0, 0, tiled=True)]
    ppermute x28, starting transfers between devices: 51.5 us -> 46.3 us  [shift(): lax.ppermute(value, axis, [(i, (i + by) % size) for i in range(size)])]
    all_gather x1, waiting for transfers between devices: 4.33 us -> 0.02 us  [on_device(): weight_t = lax.all_gather(weight_t, COL, axis=0, tiled=True)]
    all_to_all x3, starting transfers between devices: 16.3 us -> 20 us  [over_col(): return lax.all_to_all(value, COL, 0, 0, tiled=True)]
    unnamed x52 -> x80, local copies, waits for them, and re-layouts: 3.78 us -> 7.36 us
  transfers between devices with their start and end apart: 34 -> 34, of which waited for: 18 -> 20; matrix products, arithmetic and copies ran while one was open for 4% -> 4% of each run, Pallas kernels for 7% -> 20%
where the time goes in v3:
time: 255 us; the launch traced here: 254 us
  starting transfers between devices  80.7 us (32%)
  waiting for transfers between devices  74.2 us (29%)
  Pallas kernels  64.6 us (25%)
  local copies, waits for them, and re-layouts  15.3 us (6%)
  between operations  14.5 us (6%)
  other arithmetic  4.39 us (2%)
    ppermute x28, waiting for transfers between devices, shift(): lax.ppermute(value, axis, [(i, (i + by) % size) for i in range(size)])  59.8 us
    ppermute x28, starting transfers between devices, shift(): lax.ppermute(value, axis, [(i, (i + by) % size) for i in range(size)])  46.3 us
    all_to_all x3, starting transfers between devices, over_col(): return lax.all_to_all(value, COL, 0, 0, tiled=True)  20 us
    pallas_call x1, Pallas kernels, mix(): pl.pallas_call(mixed_kernel, grid_spec=pltpu.PrefetchScalarGridSpec(num_s...  11.4 us
    pallas_call x1, Pallas kernels, push(): pl.pallas_call(push_kernel, grid_spec=pltpu.PrefetchScalarGridSpec(num_sc...  10.8 us
    pallas_call x1, Pallas kernels, dense(): pl.pallas_call(dense_kernel, grid=(F // step,), in_specs=[by_row, by_row,...  7.85 us
    pallas_call x3, Pallas kernels, gather_sum(): pl.pallas_call(kernel, out_shape=[jax.ShapeDtypeStruct((n, C, W), f32) fo...  7.54 us
    unnamed x80, local copies, waits for them, and re-layouts  7.36 us
  transfers between devices with their start and end apart: 34, of which 20 were waited for; matrix products, arithmetic and copies ran while one was open for 4% of the time, Pallas kernels for 20%

profile of v3, /device:TPU:10, one launch (start us, length us, event | category | flops | bytes accessed | tf_op | source)
XLA Modules:
  0.0 253.7 jit_solution(11557186514548529158)
XLA Ops:
  8.4 6.4 %collective-permute-start = (f32[8,64,256]{2,1,0:T(8,128)S(1)}, f32[8,64,256]{2,1,0:T(8,128)S(1)}, u32[]{:S(2)}, u32[]{:S(2)}) collective-permute-start(f32[8,64,256]{2,1,0:T(8,128)S(1)} %bitcast.60), channel_id=1, source_target_pairs={{0,48},{16,0},{32,16},{48,32},{1,49},{17,1},{33,17},{49,33},{2,50}... | collective-permute-start | bytes 1572872 | tf_op jit(solution)/shard_map/ppermute | solution.py:387
  17.0 2.0 shard_map.76
  21.6 2.2 collective-permute-start.4
  23.8 4.7 %collective-permute-done.2.refs_4_ = f32[4,64,256]{2,1,0:T(8,128)S(1)} collective-permute-done((f32[4,64,256]{2,1,0:T(8,128)}, f32[4,64,256]{2,1,0:T(8,128)S(1)}, u32[]{:S(2)}, u32[]{:S(2)}) %collective-permute-start.2) | collective-permute-done | bytes 262176 | tf_op jit(solution)/shard_map/ppermute | solution.py:387
  28.4 3.0 %collective-permute-done.3.refs_5_ = f32[4,64,256]{2,1,0:T(8,128)S(1)} collective-permute-done((f32[4,64,256]{2,1,0:T(8,128)}, f32[4,64,256]{2,1,0:T(8,128)S(1)}, u32[]{:S(2)}, u32[]{:S(2)}) %collective-permute-start.3) | collective-permute-done | bytes 262176 | tf_op jit(solution)/shard_map/ppermute | solution.py:387
  31.4 3.2 %collective-permute-done.4.refs_6_ = f32[4,64,256]{2,1,0:T(8,128)S(1)} collective-permute-done((f32[4,64,256]{2,1,0:T(8,128)}, f32[4,64,256]{2,1,0:T(8,128)S(1)}, u32[]{:S(2)}, u32[]{:S(2)}) %collective-permute-start.4) | collective-permute-done | bytes 262176 | tf_op jit(solution)/shard_map/ppermute | solution.py:387
  34.6 2.6 %collective-permute-done.up_ref.refs_2_ = f32[8,64,256]{2,1,0:T(8,128)S(1)} collective-permute-done((f32[8,64,256]{2,1,0:T(8,128)S(1)}, f32[8,64,256]{2,1,0:T(8,128)S(1)}, u32[]{:S(2)}, u32[]{:S(2)}) %collective-permute-start) | collective-permute-done | bytes 524320 | tf_op jit(solution)/shard_map/ppermute | solution.py:387
  37.2 3.8 %collective-permute-done.1.down_ref.refs_3_ = f32[8,64,256]{2,1,0:T(8,128)S(1)} collective-permute-done((f32[8,64,256]{2,1,0:T(8,128)S(1)}, f32[8,64,256]{2,1,0:T(8,128)S(1)}, u32[]{:S(2)}, u32[]{:S(2)}) %collective-permute-start.1) | collective-permute-done | bytes 524320 | tf_op jit(solution)/shard_map/ppermute | solution.py:387
  41.9 2.7 %shard_map.77 = (f32[4,64,256]{2,1,0:T(8,128)}, f32[4,64,256]{2,1,0:T(8,128)}, f32[8,64,256]{2,1,0:T(8,128)}, f32[8,64,256]{2,1,0:T(8,128)}, f32[8,64,256]{2,1,0:T(8,128)}) custom-call(s32[24]{0:T(128)} %reshape.173.index_ref, f32[8,64,256]{2,1,0:T(8,128)} %copy-done.7, f32[8,64,256]{2,1,0:T(8,128)} %copy-done.8), custom_call_target="tpu_custom_call" | custom-call | bytes 2097152 | tf_op jit(solution)/shard_map/pallas_call | solution.py:90
  45.4 5.7 %all-to-all-start = ((f32[16,64,128]{2,1,0:T(8,128)}), f32[16,64,128]{2,1,0:T(8,128)S(1)}, u32[]{:S(2)}, u32[]{:S(2)}) async-start(f32[16,64,128]{2,1,0:T(8,128)} %bitcast_bitcast_fusion.1), calls=%async_computation | async-start | bytes 1048576 | tf_op jit(solution)/shard_map/all_to_all | solution.py:395
  51.2 1.6 collective-permute-start.7
  53.9 2.2 collective-permute-start.9
  56.5 2.5 collective-permute-start.6
  60.4 10.1 %collective-permute-done.5.refs_0_.lo_ref = f32[4,64,256]{2,1,0:T(8,128)S(1)} collective-permute-done((f32[4,64,256]{2,1,0:T(8,128)}, f32[4,64,256]{2,1,0:T(8,128)S(1)}, u32[]{:S(2)}, u32[]{:S(2)}) %collective-permute-start.5) | collective-permute-done | bytes 262176 | tf_op jit(solution)/shard_map/ppermute | solution.py:387
  71.7 7.0 %collective-permute-done.9.refs_9_ = f32[8,64,256]{2,1,0:T(8,128)S(1)} collective-permute-done((f32[8,64,256]{2,1,0:T(8,128)}, f32[8,64,256]{2,1,0:T(8,128)S(1)}, u32[]{:S(2)}, u32[]{:S(2)}) %collective-permute-start.9) | collective-permute-done | bytes 524320 | tf_op jit(solution)/shard_map/ppermute | solution.py:387
  78.7 2.3 shard_map.79
  83.9 1.6 collective-permute-start.12
  86.1 11.4 %shard_map.78.part_ref = f32[8,64,256]{2,1,0:T(8,128)} custom-call(s32[56]{0:T(128)} %fusion.3.place_ref, f32[8,64,256]{2,1,0:T(8,128)} %bitcast.63, f32[4,64,256]{2,1,0:T(8,128)} %copy-done.10, f32[4,64,256]{2,1,0:T(8,128)} %copy-done.11, f32[8,64,256]{2,1,0:T(8,128)} %copy-done.7, f32[8,64,256]{2,1,0:T(8,128)} %copy-done.8, f32[4,64,256]{2,1,0:T(8,128)} %copy-done.30, ...), custom_call_target="tpu_custom_call" | custom-call | flops 1073741824 | bytes 13631488 | tf_op jit(solution)/shard_map/pallas_call | solution.py:138
  99.1 4.3 %shard_map.80 = f32[16,64,128]{2,1,0:T(8,128)} custom-call(s32[12]{0:T(128)} %reshape.171.refs_ref, f32[8,64,256]{2,1,0:T(8,128)} %shard_map.78.part_ref, f32[4,64,256]{2,1,0:T(8,128)} %copy-done.22, f32[4,64,256]{2,1,0:T(8,128)} %copy-done.23, f32[4,64,256]{2,1,0:T(8,128)} %copy-done.24, bf16[8,8,256,256]{3,2,1,0:T(8,128)(2,1)} %tiles_ref.5), custom_call_target="tpu_custom_call" | custom-call | flops 201326592 | bytes 4194304 | tf_op jit(solution)/shard_map/pallas_call | solution.py:185
  103.5 8.0 %all-to-all-start.1 = ((f32[16,64,128]{2,1,0:T(8,128)}), f32[16,64,128]{2,1,0:T(8,128)S(1)}, u32[]{:S(2)}, u32[]{:S(2)}) async-start(f32[16,64,128]{2,1,0:T(8,128)} %shard_map.80), calls=%async_computation.1 | async-start | bytes 1048576 | tf_op jit(solution)/shard_map/all_to_all | solution.py:395
  111.4 6.3 %shard_map.81 = (bf16[1024,1024]{1,0:T(8,128)(2,1)}, bf16[1024,1024]{1,0:T(8,128)(2,1)}, bf16[1024,1024]{1,0:T(8,128)(2,1)}, bf16[1024,1024]{1,0:T(8,128)(2,1)}) custom-call(f32[1024,1024]{1,0:T(8,128)} %all-gather.2.cloned.1.call-done.in_ref), custom_call_target="tpu_custom_call" | custom-call | flops 8388608 | bytes 12582912 | tf_op jit(solution)/shard_map/pallas_call | solution.py:210
  117.7 2.0 all-to-all-done.1
  120.5 7.9 %shard_map.82 = (f32[1024,128]{1,0:T(8,128)}, f32[16,128,128]{2,1,0:T(8,128)}) custom-call(bf16[1024,1024]{1,0:T(8,128)(2,1)} %get-tuple-element.111.thi_ref, bf16[1024,1024]{1,0:T(8,128)(2,1)} %get-tuple-element.112.tlo_ref, bf16[1024,1024]{1,0:T(8,128)(2,1)} %get-tuple-element.113.hi_ref, bf16[1024,1024]{1,0:T(8,128)(2,1)} %get-tuple-element.114.lo_ref, ...), custom_call_target="tpu_custom_call" | custom-call | flops 1610612736 | bytes 10485760 | tf_op jit(solution)/shard_map/pallas_call | solution.py:258
  128.4 6.3 %all-to-all-start.2 = ((f32[16,128,128]{2,1,0:T(8,128)}), f32[16,128,128]{2,1,0:T(8,128)S(1)}, u32[]{:S(2)}, u32[]{:S(2)}) async-start(f32[16,128,128]{2,1,0:T(8,128)} %get-tuple-element.117), calls=%async_computation.2 | async-start | bytes 2097152 | tf_op jit(solution)/shard_map/all_to_all | solution.py:395
  135.4 1.7 collective-permute-done.13.other_ref
  137.9 5.4 %shard_map.83 = f32[512,1024]{1,0:T(8,128)} custom-call(s32[1]{0:T(128)} %bitcast.11.core_ref, f32[8,2,64,128]{3,2,1,0:T(8,128)} %bitcast.66, f32[512,128]{1,0:T(8,128)} %copy-done.25, f32[1024,128]{1,0:T(8,128)} %bitcast.58, f32[1024,128]{1,0:T(8,128)} %copy-done.12), custom_call_target="tpu_custom_call" | custom-call | flops 805306368 | bytes 4194304 | tf_op jit(solution)/shard_map/pallas_call | solution.py:417
  143.3 5.3 %all-to-all-done.2.back_ref = f32[16,128,128]{2,1,0:T(8,128)S(1)} async-done(((f32[16,128,128]{2,1,0:T(8,128)}), f32[16,128,128]{2,1,0:T(8,128)S(1)}, u32[]{:S(2)}, u32[]{:S(2)}) %all-to-all-start.2) | async-done | bytes 1048608 | tf_op jit(solution)/shard_map/all_to_all | solution.py:395
  149.6 3.9 %shard_map.84 = (f32[4,64,256]{2,1,0:T(8,128)}, f32[4,64,256]{2,1,0:T(8,128)}, f32[4,64,256]{2,1,0:T(8,128)}) custom-call(s32[12]{0:T(128)} %reshape.171.refs_ref, f32[16,128,128]{2,1,0:T(8,128)} %copy-done.1, bf16[8,8,256,256]{3,2,1,0:T(8,128)(2,1)} %tiles_ref.5), custom_call_target="tpu_custom_call" | custom-call | flops 201326592 | bytes 4194304 | tf_op jit(solution)/shard_map/pallas_call | solution.py:284
  153.6 7.2 %all-to-all-start.3 = ((f32[8,64,1024]{2,1,0:T(8,128)}), f32[8,64,1024]{2,1,0:T(8,128)}, u32[]{:S(2)}, u32[]{:S(2)}) async-start(f32[8,64,1024]{2,1,0:T(8,128)} %bitcast.56), calls=%async_computation.3 | async-start | bytes 4194304 | tf_op jit(solution)/shard_map/all_to_all | solution.py:479
  164.6 10.8 %shard_map.85 = (f32[8,64,256]{2,1,0:T(8,128)}, f32[4,64,256]{2,1,0:T(8,128)}, f32[4,64,256]{2,1,0:T(8,128)}, f32[8,64,256]{2,1,0:T(8,128)}, f32[8,64,256]{2,1,0...) custom-call(s32[56]{0:T(128)} %fusion.3.place_ref, ...), custom_call_target="tpu_custom_call" | custom-call | flops 1073741824 | bytes 13631488 | tf_op jit(solution)/shard_map/pallas_call | solution.py:324
  177.0 2.6 %collective-permute-start.19 = (f32[8,64,256]{2,1,0:T(8,128)}, f32[8,64,256]{2,1,0:T(8,128)S(1)}, u32[]{:S(2)}, u32[]{:S(2)}) collective-permute-start(f32[8,64,256]{2,1,0:T(8,128)} %get-tuple-element.132), channel_id=1, source_target_pairs={{0,128},{64,192},{128,0},{192,64},{1,129},{65,193},{129,1},{193,65... | collective-permute-start | bytes 1572872 | tf_op jit(solution)/shard_map/ppermute | solution.py:387
  179.6 1.8 collective-permute-start.20
  181.4 2.2 shard_map.86
  183.6 2.3 collective-permute-start.21
  186.0 2.2 collective-permute-start.22
  188.1 1.7 reduce_sum.48
  191.5 4.8 %collective-permute-done.21.below_ref = f32[4,64,256]{2,1,0:T(8,128)S(1)} collective-permute-done((f32[4,64,256]{2,1,0:T(8,128)}, f32[4,64,256]{2,1,0:T(8,128)S(1)}, u32[]{:S(2)}, u32[]{:S(2)}) %collective-permute-start.21) | collective-permute-done | bytes 262176 | tf_op jit(solution)/shard_map/ppermute | solution.py:387
  197.3 4.0 %collective-permute-done.19.b_ref = f32[8,64,256]{2,1,0:T(8,128)S(1)} collective-permute-done((f32[8,64,256]{2,1,0:T(8,128)}, f32[8,64,256]{2,1,0:T(8,128)S(1)}, u32[]{:S(2)}, u32[]{:S(2)}) %collective-permute-start.19) | collective-permute-done | bytes 524320 | tf_op jit(solution)/shard_map/ppermute | solution.py:387
  202.9 3.1 %shard_map.87 = (f32[8,64,256]{2,1,0:T(8,128)}, f32[8,64,256]{2,1,0:T(8,128)}) custom-call(s32[24]{0:T(128)} %reshape.173.index_ref, f32[8,64,256]{2,1,0:T(8,128)} %copy-done.13, f32[8,64,256]{2,1,0:T(8,128)} %copy-done.14, f32[8,64,256]{2,1,0:T(8,128)} %copy-done.15, f32[8,64,256]{2,1,0:T(8,128)} %get-tuple-element.148.up_ref, ...), custom_call_target="tpu_custom_call" | custom-call | flops 196608 | bytes 3145728 | tf_op jit(solution)/shard_map/pallas_call | solution.py:375
  206.0 2.3 collective-permute-start.26
  208.3 2.2 collective-permute-start.27
  210.5 7.1 %all-to-all-start.4 = ((f32[16,32,128]{2,1,0:T(8,128)}), f32[16,32,128]{2,1,0:T(8,128)S(1)}, u32[]{:S(2)}, u32[]{:S(2)}) async-start(f32[16,32,128]{2,1,0:T(8,128)} %reshape.183), calls=%async_computation.4 | async-start | bytes 524288 | tf_op jit(solution)/shard_map/all_to_all | solution.py:495
  217.8 2.8 %collective-permute-start.24 = (f32[4,64,256]{2,1,0:T(8,128)S(1)}, f32[4,64,256]{2,1,0:T(8,128)S(1)}, u32[]{:S(2)}, u32[]{:S(2)}) collective-permute-start(f32[4,64,256]{2,1,0:T(8,128)S(1)} %copy-done.34), channel_id=1, source_target_pairs={{0,128},{64,192},{128,0},{192,64},{1,129},{65,193},{129,1},{193,65... | collective-permute-start | bytes 786440 | tf_op jit(solution)/shard_map/ppermute | solution.py:387
  220.6 1.8 collective-permute-start.25
  222.4 5.0 %collective-permute-done.23.a_ref = f32[4,64,256]{2,1,0:T(8,128)S(1)} collective-permute-done((f32[4,64,256]{2,1,0:T(8,128)S(1)}, f32[4,64,256]{2,1,0:T(8,128)S(1)}, u32[]{:S(2)}, u32[]{:S(2)}) %collective-permute-start.23) | collective-permute-done | bytes 262176 | tf_op jit(solution)/shard_map/ppermute | solution.py:387
  227.4 6.5 %collective-permute-done.24.b_ref = f32[4,64,256]{2,1,0:T(8,128)S(1)} collective-permute-done((f32[4,64,256]{2,1,0:T(8,128)S(1)}, f32[4,64,256]{2,1,0:T(8,128)S(1)}, u32[]{:S(2)}, u32[]{:S(2)}) %collective-permute-start.24) | collective-permute-done | bytes 262176 | tf_op jit(solution)/shard_map/ppermute | solution.py:387
  234.7 2.2 shard_map.88
  237.0 7.1 %all-to-all-done.4 = f32[16,32,128]{2,1,0:T(8,128)S(1)} async-done(((f32[16,32,128]{2,1,0:T(8,128)}), f32[16,32,128]{2,1,0:T(8,128)S(1)}, u32[]{:S(2)}, u32[]{:S(2)}) %all-to-all-start.4) | async-done | bytes 262176 | tf_op jit(solution)/shard_map/all_to_all | solution.py:495
  (156 shorter events, 33.5 us)
Async XLA Ops:
  7.2 37.4 %copy-start = (f32[2048,64]{0,1:T(8,128)S(1)}, f32[2048,64]{0,1:T(8,128)}, u32[]{:S(2)}) copy-start(f32[2048,64]{0,1:T(8,128)} %param.9) | copy-start | bytes 1572868
  7.2 96.3 %all-gather.2.cloned.1.call-start = ((), (), s32[]{:S(2)}) async-start(), calls=%async_computation.5 | async-start | bytes 4456448 | tf_op jit(solution)/shard_map/all_gather | solution.py:451
  8.4 8.6 %copy-start.5 = (f32[8,8,8,256]{3,2,0,1:T(8,128)}, f32[8,8,8,256]{3,2,0,1:T(8,128)S(1)}, u32[]{:S(2)}) copy-start(f32[8,8,8,256]{3,2,0,1:T(8,128)S(1)} %copy.39) | copy-start | bytes 1572868
  8.4 28.8 %collective-permute-start = (f32[8,64,256]{2,1,0:T(8,128)S(1)}, f32[8,64,256]{2,1,0:T(8,128)S(1)}, u32[]{:S(2)}, u32[]{:S(2)}) collective-permute-start(f32[8,64,256]{2,1,0:T(8,128)S(1)} %bitcast.60), channel_id=1, source_target_pairs={{0,48},{16,0},{32,16},{48,32},{1,49},{17,1},{33,17},{49,33},{2,50}... | collective-permute-start | bytes 1572872 | tf_op jit(solution)/shard_map/ppermute | solution.py:387
  14.8 26.3 %collective-permute-start.1 = (f32[8,64,256]{2,1,0:T(8,128)S(1)}, f32[8,64,256]{2,1,0:T(8,128)S(1)}, u32[]{:S(2)}, u32[]{:S(2)}) collective-permute-start(f32[8,64,256]{2,1,0:T(8,128)S(1)} %bitcast.61), channel_id=1, source_target_pairs={{0,16},{16,32},{32,48},{48,0},{1,17},{17,33},{33,49},{49,1},{2,18}... | collective-permute-start | bytes 1572872 | tf_op jit(solution)/shard_map/ppermute | solution.py:387
  19.0 9.4 %collective-permute-start.2 = (f32[4,64,256]{2,1,0:T(8,128)}, f32[4,64,256]{2,1,0:T(8,128)S(1)}, u32[]{:S(2)}, u32[]{:S(2)}) collective-permute-start(f32[4,64,256]{2,1,0:T(8,128)} %get-tuple-element.84), channel_id=1, source_target_pairs={{0,64},{64,128},{128,192},{192,0},{1,65},{65,129},{129,193},{193,1... | collective-permute-start | bytes 786440 | tf_op jit(solution)/shard_map/ppermute | solution.py:387
  20.5 11.0 %collective-permute-start.3 = (f32[4,64,256]{2,1,0:T(8,128)}, f32[4,64,256]{2,1,0:T(8,128)S(1)}, u32[]{:S(2)}, u32[]{:S(2)}) collective-permute-start(f32[4,64,256]{2,1,0:T(8,128)} %get-tuple-element.85), channel_id=1, source_target_pairs={{0,128},{64,192},{128,0},{192,64},{1,129},{65,193},{129,1},{193,65... | collective-permute-start | bytes 786440 | tf_op jit(solution)/shard_map/ppermute | solution.py:387
  21.6 13.0 %collective-permute-start.4 = (f32[4,64,256]{2,1,0:T(8,128)}, f32[4,64,256]{2,1,0:T(8,128)S(1)}, u32[]{:S(2)}, u32[]{:S(2)}) collective-permute-start(f32[4,64,256]{2,1,0:T(8,128)} %get-tuple-element.86), channel_id=1, source_target_pairs={{0,192},{64,0},{128,64},{192,128},{1,193},{65,1},{129,65},{193,129... | collective-permute-start | bytes 786440 | tf_op jit(solution)/shard_map/ppermute | solution.py:387
  28.4 57.7 %copy-start.30 = (f32[4,64,256]{2,1,0:T(8,128)}, f32[4,64,256]{2,1,0:T(8,128)S(1)}, u32[]{:S(2)}) copy-start(f32[4,64,256]{2,1,0:T(8,128)S(1)} %collective-permute-done.2.refs_4_) | copy-start | bytes 786436
  31.4 19.7 %copy-start.31 = (f32[4,64,256]{2,1,0:T(8,128)}, f32[4,64,256]{2,1,0:T(8,128)S(1)}, u32[]{:S(2)}) copy-start(f32[4,64,256]{2,1,0:T(8,128)S(1)} %collective-permute-done.3.refs_5_) | copy-start | bytes 786436
  34.6 16.5 %copy-start.32 = (f32[4,64,256]{2,1,0:T(8,128)}, f32[4,64,256]{2,1,0:T(8,128)S(1)}, u32[]{:S(2)}) copy-start(f32[4,64,256]{2,1,0:T(8,128)S(1)} %collective-permute-done.4.refs_6_) | copy-start | bytes 786436
  45.4 33.3 %all-to-all-start = ((f32[16,64,128]{2,1,0:T(8,128)}), f32[16,64,128]{2,1,0:T(8,128)S(1)}, u32[]{:S(2)}, u32[]{:S(2)}) async-start(f32[16,64,128]{2,1,0:T(8,128)} %bitcast_bitcast_fusion.1), calls=%async_computation | async-start | bytes 1048576 | tf_op jit(solution)/shard_map/all_to_all | solution.py:395
  51.2 20.5 %collective-permute-start.7 = (f32[8,64,256]{2,1,0:T(8,128)}, f32[8,64,256]{2,1,0:T(8,128)S(1)}, u32[]{:S(2)}, u32[]{:S(2)}) collective-permute-start(f32[8,64,256]{2,1,0:T(8,128)} %get-tuple-element.94), channel_id=1, source_target_pairs={{0,64},{64,128},{128,192},{192,0},{1,65},{65,129},{129,193},{193,1... | collective-permute-start | bytes 1572872 | tf_op jit(solution)/shard_map/ppermute | solution.py:387
  52.7 19.0 %collective-permute-start.8 = (f32[8,64,256]{2,1,0:T(8,128)}, f32[8,64,256]{2,1,0:T(8,128)S(1)}, u32[]{:S(2)}, u32[]{:S(2)}) collective-permute-start(f32[8,64,256]{2,1,0:T(8,128)} %get-tuple-element.95), channel_id=1, source_target_pairs={{0,128},{64,192},{128,0},{192,64},{1,129},{65,193},{129,1},{193,65... | collective-permute-start | bytes 1572872 | tf_op jit(solution)/shard_map/ppermute | solution.py:387
  53.9 24.9 %collective-permute-start.9 = (f32[8,64,256]{2,1,0:T(8,128)}, f32[8,64,256]{2,1,0:T(8,128)S(1)}, u32[]{:S(2)}, u32[]{:S(2)}) collective-permute-start(f32[8,64,256]{2,1,0:T(8,128)} %get-tuple-element.96), channel_id=1, source_target_pairs={{0,192},{64,0},{128,64},{192,128},{1,193},{65,1},{129,65},{193,129... | collective-permute-start | bytes 1572872 | tf_op jit(solution)/shard_map/ppermute | solution.py:387
  56.1 14.3 %collective-permute-start.5 = (f32[4,64,256]{2,1,0:T(8,128)}, f32[4,64,256]{2,1,0:T(8,128)S(1)}, u32[]{:S(2)}, u32[]{:S(2)}) collective-permute-start(f32[4,64,256]{2,1,0:T(8,128)} %get-tuple-element.89), channel_id=1, source_target_pairs={{0,48},{16,0},{32,16},{48,32},{1,49},{17,1},{33,17},{49,33},{2,50}... | collective-permute-start | bytes 786440 | tf_op jit(solution)/shard_map/ppermute | solution.py:387
  56.5 15.2 %collective-permute-start.6 = (f32[4,64,256]{2,1,0:T(8,128)}, f32[4,64,256]{2,1,0:T(8,128)S(1)}, u32[]{:S(2)}, u32[]{:S(2)}) collective-permute-start(f32[4,64,256]{2,1,0:T(8,128)} %get-tuple-element.90), channel_id=1, source_target_pairs={{0,16},{16,32},{32,48},{48,0},{1,17},{17,33},{33,49},{49,1},{2,18}... | collective-permute-start | bytes 786440 | tf_op jit(solution)/shard_map/ppermute | solution.py:387
  71.7 14.4 %copy-start.16 = (f32[8,64,256]{2,1,0:T(8,128)}, f32[8,64,256]{2,1,0:T(8,128)S(1)}, u32[]{:S(2)}) copy-start(f32[8,64,256]{2,1,0:T(8,128)S(1)} %collective-permute-done.7.refs_7_) | copy-start | bytes 1572868
  71.7 14.4 %copy-start.17 = (f32[8,64,256]{2,1,0:T(8,128)}, f32[8,64,256]{2,1,0:T(8,128)S(1)}, u32[]{:S(2)}) copy-start(f32[8,64,256]{2,1,0:T(8,128)S(1)} %collective-permute-done.8.refs_8_) | copy-start | bytes 1572868
  78.7 18.8 %copy-start.6 = (f32[16,64,128]{2,1,0:T(8,128)}, f32[16,64,128]{2,1,0:T(8,128)S(1)}, u32[]{:S(2)}) copy-start(f32[16,64,128]{2,1,0:T(8,128)S(1)} %all-to-all-done) | copy-start | bytes 1572868
  81.1 16.5 %collective-permute-start.10 = (f32[4,64,256]{2,1,0:T(8,128)}, f32[4,64,256]{2,1,0:T(8,128)S(1)}, u32[]{:S(2)}, u32[]{:S(2)}) collective-permute-start(f32[4,64,256]{2,1,0:T(8,128)} %get-tuple-element.106), channel_id=1, source_target_pairs={{0,64},{64,128},{128,192},{192,0},{1,65},{65,129},{129,193},{193,1... | collective-permute-start | bytes 786440 | tf_op jit(solution)/shard_map/ppermute | solution.py:387
  82.4 15.2 %collective-permute-start.11 = (f32[4,64,256]{2,1,0:T(8,128)}, f32[4,64,256]{2,1,0:T(8,128)S(1)}, u32[]{:S(2)}, u32[]{:S(2)}) collective-permute-start(f32[4,64,256]{2,1,0:T(8,128)} %get-tuple-element.107), channel_id=1, source_target_pairs={{0,128},{64,192},{128,0},{192,64},{1,129},{65,193},{129,1},{193,65... | collective-permute-start | bytes 786440 | tf_op jit(solution)/shard_map/ppermute | solution.py:387
  83.9 13.7 %collective-permute-start.12 = (f32[4,64,256]{2,1,0:T(8,128)}, f32[4,64,256]{2,1,0:T(8,128)S(1)}, u32[]{:S(2)}, u32[]{:S(2)}) collective-permute-start(f32[4,64,256]{2,1,0:T(8,128)} %get-tuple-element.108), channel_id=1, source_target_pairs={{0,192},{64,0},{128,64},{192,128},{1,193},{65,1},{129,65},{193,129... | collective-permute-start | bytes 786440 | tf_op jit(solution)/shard_map/ppermute | solution.py:387
  103.5 16.2 %all-to-all-start.1 = ((f32[16,64,128]{2,1,0:T(8,128)}), f32[16,64,128]{2,1,0:T(8,128)S(1)}, u32[]{:S(2)}, u32[]{:S(2)}) async-start(f32[16,64,128]{2,1,0:T(8,128)} %shard_map.80), calls=%async_computation.1 | async-start | bytes 1048576 | tf_op jit(solution)/shard_map/all_to_all | solution.py:395
  128.4 20.2 %all-to-all-start.2 = ((f32[16,128,128]{2,1,0:T(8,128)}), f32[16,128,128]{2,1,0:T(8,128)S(1)}, u32[]{:S(2)}, u32[]{:S(2)}) async-start(f32[16,128,128]{2,1,0:T(8,128)} %get-tuple-element.117), calls=%async_computation.2 | async-start | bytes 2097152 | tf_op jit(solution)/shard_map/all_to_all | solution.py:395
  134.7 2.4 collective-permute-start.14
  134.9 2.1 collective-permute-start.13
  153.5 8.7 %copy-start.37 = (f32[4,64,256]{2,1,0:T(8,128)S(1)}, f32[4,64,256]{2,1,0:T(8,128)}, u32[]{:S(2)}) copy-start(f32[4,64,256]{2,1,0:T(8,128)} %get-tuple-element.125) | copy-start | bytes 786436
  153.5 8.7 %copy-start.36 = (f32[4,64,256]{2,1,0:T(8,128)S(1)}, f32[4,64,256]{2,1,0:T(8,128)}, u32[]{:S(2)}) copy-start(f32[4,64,256]{2,1,0:T(8,128)} %get-tuple-element.126) | copy-start | bytes 786436
  153.5 10.2 %copy-start.2 = (f32[16,128,128]{2,1,0:T(8,128)S(1)}, f32[16,128,128]{2,1,0:T(8,128)}, u32[]{:S(2)}) copy-start(f32[16,128,128]{2,1,0:T(8,128)} %copy-done.1) | copy-start | bytes 3145732
  153.6 34.6 %all-to-all-start.3 = ((f32[8,64,1024]{2,1,0:T(8,128)}), f32[8,64,1024]{2,1,0:T(8,128)}, u32[]{:S(2)}, u32[]{:S(2)}) async-start(f32[8,64,1024]{2,1,0:T(8,128)} %bitcast.56), calls=%async_computation.3 | async-start | bytes 4194304 | tf_op jit(solution)/shard_map/all_to_all | solution.py:479
  160.8 14.7 %collective-permute-start.15 = (f32[4,64,256]{2,1,0:T(8,128)S(1)}, f32[4,64,256]{2,1,0:T(8,128)S(1)}, u32[]{:S(2)}, u32[]{:S(2)}) collective-permute-start(f32[4,64,256]{2,1,0:T(8,128)S(1)} %copy-done.38), channel_id=1, source_target_pairs={{0,192},{64,0},{128,64},{192,128},{1,193},{65,1},{129,65},{193,129... | collective-permute-start | bytes 786440 | tf_op jit(solution)/shard_map/ppermute | solution.py:387
  162.2 13.3 %collective-permute-start.16 = (f32[4,64,256]{2,1,0:T(8,128)S(1)}, f32[4,64,256]{2,1,0:T(8,128)S(1)}, u32[]{:S(2)}, u32[]{:S(2)}) collective-permute-start(f32[4,64,256]{2,1,0:T(8,128)S(1)} %copy-done.37), channel_id=1, source_target_pairs={{0,128},{64,192},{128,0},{192,64},{1,129},{65,193},{129,1},{193,65... | collective-permute-start | bytes 786440 | tf_op jit(solution)/shard_map/ppermute | solution.py:387
  162.2 13.6 %collective-permute-start.17 = (f32[4,64,256]{2,1,0:T(8,128)S(1)}, f32[4,64,256]{2,1,0:T(8,128)S(1)}, u32[]{:S(2)}, u32[]{:S(2)}) collective-permute-start(f32[4,64,256]{2,1,0:T(8,128)S(1)} %copy-done.36), channel_id=1, source_target_pairs={{0,64},{64,128},{128,192},{192,0},{1,65},{65,129},{129,193},{193,1... | collective-permute-start | bytes 786440 | tf_op jit(solution)/shard_map/ppermute | solution.py:387
  175.8 21.5 %collective-permute-start.18 = (f32[8,64,256]{2,1,0:T(8,128)}, f32[8,64,256]{2,1,0:T(8,128)S(1)}, u32[]{:S(2)}, u32[]{:S(2)}) collective-permute-start(f32[8,64,256]{2,1,0:T(8,128)} %get-tuple-element.131), channel_id=1, source_target_pairs={{0,192},{64,0},{128,64},{192,128},{1,193},{65,1},{129,65},{193,129... | collective-permute-start | bytes 1572872 | tf_op jit(solution)/shard_map/ppermute | solution.py:387
  177.0 24.4 %collective-permute-start.19 = (f32[8,64,256]{2,1,0:T(8,128)}, f32[8,64,256]{2,1,0:T(8,128)S(1)}, u32[]{:S(2)}, u32[]{:S(2)}) collective-permute-start(f32[8,64,256]{2,1,0:T(8,128)} %get-tuple-element.132), channel_id=1, source_target_pairs={{0,128},{64,192},{128,0},{192,64},{1,129},{65,193},{129,1},{193,65... | collective-permute-start | bytes 1572872 | tf_op jit(solution)/shard_map/ppermute | solution.py:387
  179.6 22.5 %collective-permute-start.20 = (f32[8,64,256]{2,1,0:T(8,128)}, f32[8,64,256]{2,1,0:T(8,128)S(1)}, u32[]{:S(2)}, u32[]{:S(2)}) collective-permute-start(f32[8,64,256]{2,1,0:T(8,128)} %get-tuple-element.133), channel_id=1, source_target_pairs={{0,64},{64,128},{128,192},{192,0},{1,65},{65,129},{129,193},{193,1... | collective-permute-start | bytes 1572872 | tf_op jit(solution)/shard_map/ppermute | solution.py:387
  183.6 12.7 %collective-permute-start.21 = (f32[4,64,256]{2,1,0:T(8,128)}, f32[4,64,256]{2,1,0:T(8,128)S(1)}, u32[]{:S(2)}, u32[]{:S(2)}) collective-permute-start(f32[4,64,256]{2,1,0:T(8,128)} %get-tuple-element.139), channel_id=1, source_target_pairs={{0,16},{16,32},{32,48},{48,0},{1,17},{17,33},{33,49},{49,1},{2,18}... | collective-permute-start | bytes 786440 | tf_op jit(solution)/shard_map/ppermute | solution.py:387
  186.0 11.4 %collective-permute-start.22 = (f32[4,64,256]{2,1,0:T(8,128)}, f32[4,64,256]{2,1,0:T(8,128)}, u32[]{:S(2)}, u32[]{:S(2)}) collective-permute-start(f32[4,64,256]{2,1,0:T(8,128)} %get-tuple-element.140), channel_id=1, source_target_pairs={{0,48},{16,0},{32,16},{48,32},{1,49},{17,1},{33,17},{49,33},{2,50}... | collective-permute-start | bytes 786440 | tf_op jit(solution)/shard_map/ppermute | solution.py:387
  190.4 27.4 %copy-start.34 = (f32[4,64,256]{2,1,0:T(8,128)S(1)}, f32[4,64,256]{2,1,0:T(8,128)}, u32[]{:S(2)}) copy-start(f32[4,64,256]{2,1,0:T(8,128)} %get-tuple-element.159) | copy-start | bytes 786436
  190.5 30.2 %copy-start.33 = (f32[4,64,256]{2,1,0:T(8,128)S(1)}, f32[4,64,256]{2,1,0:T(8,128)}, u32[]{:S(2)}) copy-start(f32[4,64,256]{2,1,0:T(8,128)} %get-tuple-element.160) | copy-start | bytes 786436
  191.5 26.1 %copy-start.35 = (f32[4,64,256]{2,1,0:T(8,128)S(1)}, f32[4,64,256]{2,1,0:T(8,128)}, u32[]{:S(2)}) copy-start(f32[4,64,256]{2,1,0:T(8,128)} %get-tuple-element.158) | copy-start | bytes 786436
  206.0 38.8 %collective-permute-start.26 = (f32[8,64,256]{2,1,0:T(8,128)}, f32[8,64,256]{2,1,0:T(8,128)S(1)}, u32[]{:S(2)}, u32[]{:S(2)}) collective-permute-start(f32[8,64,256]{2,1,0:T(8,128)} %get-tuple-element.162), channel_id=1, source_target_pairs={{0,16},{16,32},{32,48},{48,0},{1,17},{17,33},{33,49},{49,1},{2,18}... | collective-permute-start | bytes 1572872 | tf_op jit(solution)/shard_map/ppermute | solution.py:387
  208.3 36.5 %collective-permute-start.27 = (f32[8,64,256]{2,1,0:T(8,128)}, f32[8,64,256]{2,1,0:T(8,128)S(1)}, u32[]{:S(2)}, u32[]{:S(2)}) collective-permute-start(f32[8,64,256]{2,1,0:T(8,128)} %get-tuple-element.163), channel_id=1, source_target_pairs={{0,48},{16,0},{32,16},{48,32},{1,49},{17,1},{33,17},{49,33},{2,50}... | collective-permute-start | bytes 1572872 | tf_op jit(solution)/shard_map/ppermute | solution.py:387
  210.5 33.5 %all-to-all-start.4 = ((f32[16,32,128]{2,1,0:T(8,128)}), f32[16,32,128]{2,1,0:T(8,128)S(1)}, u32[]{:S(2)}, u32[]{:S(2)}) async-start(f32[16,32,128]{2,1,0:T(8,128)} %reshape.183), calls=%async_computation.4 | async-start | bytes 524288 | tf_op jit(solution)/shard_map/all_to_all | solution.py:495
  217.6 9.8 %collective-permute-start.23 = (f32[4,64,256]{2,1,0:T(8,128)S(1)}, f32[4,64,256]{2,1,0:T(8,128)S(1)}, u32[]{:S(2)}, u32[]{:S(2)}) collective-permute-start(f32[4,64,256]{2,1,0:T(8,128)S(1)} %copy-done.35), channel_id=1, source_target_pairs={{0,192},{64,0},{128,64},{192,128},{1,193},{65,1},{129,65},{193,129... | collective-permute-start | bytes 786440 | tf_op jit(solution)/shard_map/ppermute | solution.py:387
  217.8 16.1 %collective-permute-start.24 = (f32[4,64,256]{2,1,0:T(8,128)S(1)}, f32[4,64,256]{2,1,0:T(8,128)S(1)}, u32[]{:S(2)}, u32[]{:S(2)}) collective-permute-start(f32[4,64,256]{2,1,0:T(8,128)S(1)} %copy-done.34), channel_id=1, source_target_pairs={{0,128},{64,192},{128,0},{192,64},{1,129},{65,193},{129,1},{193,65... | collective-permute-start | bytes 786440 | tf_op jit(solution)/shard_map/ppermute | solution.py:387
  220.6 13.4 %collective-permute-start.25 = (f32[4,64,256]{2,1,0:T(8,128)S(1)}, f32[4,64,256]{2,1,0:T(8,128)S(1)}, u32[]{:S(2)}, u32[]{:S(2)}) collective-permute-start(f32[4,64,256]{2,1,0:T(8,128)S(1)} %copy-done.33), channel_id=1, source_target_pairs={{0,64},{64,128},{128,192},{192,0},{1,65},{65,129},{129,193},{193,1... | collective-permute-start | bytes 786440 | tf_op jit(solution)/shard_map/ppermute | solution.py:387
  (25 other events, 91.5 us)
Sparse Core Ops, SparseCore 0:
  41.2 50.7 all-gather.1

commit v4 on v3

--- a/solution.py
+++ b/solution.py
@@ -23,6 +23,7 @@
 SMEM = pl.BlockSpec(memory_space=pltpu.SMEM)
 ANY = pl.BlockSpec(memory_space=pl.ANY)
 PARAMS = pltpu.CompilerParams(vmem_limit_bytes=58 * 2**20)
+SMALL = pltpu.CompilerParams(vmem_limit_bytes=10 * 2**20)
 
 
 def split(value):
@@ -93,7 +94,7 @@
         in_specs=[SMEM] + [VMEM] * len(sources),
         out_specs=[VMEM] * len(shapes),
         scratch_shapes=scratch,
-        compiler_params=PARAMS,
+        compiler_params=SMALL,
         cost_estimate=pl.CostEstimate(flops=0, bytes_accessed=2 << 20, transcendentals=0),
     )(index, *sources)
 
@@ -121,17 +122,18 @@
         for copy in copies:
             copy.wait()
 
-    acc = None
-    for k in range(FAN):
-        block = own_ref[0] if k == 0 else held[place_ref[i * (FAN - 1) + k - 1]]
-        part = lax.dot_general(
-            jnp.concatenate(split(block), axis=0),
-            tiles_ref[0, k],
-            (((1,), (1,)), ((), ())),
-            preferred_element_type=f32,
-        )
-        acc = part if acc is None else acc + part
-    out_ref[0] = acc[:C] + acc[C:]
+    for j in range(2):
+        acc = None
+        for k in range(FAN):
+            block = own_ref[j] if k == 0 else held[place_ref[(2 * i + j) * (FAN - 1) + k - 1]]
+            part = lax.dot_general(
+                jnp.concatenate(split(block), axis=0),
+                tiles_ref[j, k],
+                (((1,), (1,)), ((), ())),
+                preferred_element_type=f32,
+            )
+            acc = part if acc is None else acc + part
+        out_ref[j] = acc[:C] + acc[C:]
 
 
 def mix(place, own, sources, tiles):
@@ -139,11 +141,11 @@
         mixed_kernel,
         grid_spec=pltpu.PrefetchScalarGridSpec(
             num_scalar_prefetch=1,
-            grid=(BLK,),
-            in_specs=[pl.BlockSpec((1, C, W), lambda i, s: (i, 0, 0))]
+            grid=(BLK // 2,),
+            in_specs=[pl.BlockSpec((2, C, W), lambda i, s: (i, 0, 0))]
             + [ANY] * len(sources)
-            + [pl.BlockSpec((1, FAN, W, W), lambda i, s: (i, 0, 0, 0))],
-            out_specs=pl.BlockSpec((1, C, W), lambda i, s: (i, 0, 0)),
+            + [pl.BlockSpec((2, FAN, W, W), lambda i, s: (i, 0, 0, 0))],
+            out_specs=pl.BlockSpec((2, C, W), lambda i, s: (i, 0, 0)),
             scratch_shapes=[pltpu.VMEM((HELD, C, W), f32), pltpu.SemaphoreType.DMA((len(sources),))],
         ),
         out_shape=jax.ShapeDtypeStruct((BLK, C, W), f32),
@@ -197,74 +199,47 @@
     )(far_refs, part, *far, tiles)
 
 
-def weight_kernel(in_ref, thi_ref, tlo_ref, hi_ref, lo_ref):
-    value = in_ref[...]
-    thi_ref[...], tlo_ref[...] = split(value)
-    hi_ref[...], lo_ref[...] = split(value.T)
-
-
-def weight_parts(transposed):
+def dense_kernel(weight_ref, mixed_ref, cot_ref, slope_ref, out_ref, held, sems):
     step = 256
-    by_row = pl.BlockSpec((step, F), lambda i: (i, 0))
-    by_col = pl.BlockSpec((F, step), lambda i: (0, i))
-    return pl.pallas_call(
-        weight_kernel,
-        grid=(F // step,),
-        in_specs=[by_row],
-        out_specs=[by_row, by_row, by_col, by_col],
-        out_shape=[jax.ShapeDtypeStruct((F, F), bf16)] * 4,
-        compiler_params=PARAMS,
-        cost_estimate=pl.CostEstimate(flops=F * F * 8, bytes_accessed=12 << 20, transcendentals=0),
-    )(transposed)
-
-
-def dense_kernel(thi_ref, tlo_ref, hi_ref, lo_ref, mixed_ref, cot_ref, slope_ref, out_ref, parts):
-    step = pl.program_id(0)
-
-    @pl.when(step == 0)
-    def _():
-        hi, lo = split(mixed_ref[...])
-        parts[:, :CHUNK] = hi
-        parts[:, CHUNK:] = lo
-
-    both = jnp.dot(thi_ref[...], parts[...], preferred_element_type=f32)
-    low = jnp.dot(tlo_ref[...], parts[:, :CHUNK], preferred_element_type=f32)
-    pre = both[:, :CHUNK] + (both[:, CHUNK:] + low)
-    sig = jax.nn.sigmoid(pre)
-    hidden = (pre * sig).reshape(-1, C, CHUNK)
-    out_ref[pl.ds(step * hidden.shape[0], hidden.shape[0]), C:] = hidden
-    slope = cot_ref[...] * sig * (1.0 + pre * (1.0 - sig))
-    slope_ref[...] = slope
-    shi, slo = split(slope)
-    both = jnp.dot(hi_ref[...], jnp.concatenate([shi, slo], axis=1), preferred_element_type=f32)
-    low = jnp.dot(lo_ref[...], shi, preferred_element_type=f32)
-    part = (both[:, :CHUNK] + (both[:, CHUNK:] + low)).reshape(16, C, CHUNK)
-
-    @pl.when(step == 0)
-    def _():
-        out_ref[:, :C] = part
-
-    @pl.when(step > 0)
-    def _():
-        out_ref[:, :C] += part
-
-
-def dense(weights, mixed, cot):
-    step = 256
-    by_row = pl.BlockSpec((step, F), lambda i: (i, 0))
-    by_col = pl.BlockSpec((F, step), lambda i: (0, i))
-    rows = pl.BlockSpec((step, CHUNK), lambda i: (i, 0))
-    whole = pl.BlockSpec((F, CHUNK), lambda i: (0, 0))
+    copies = []
+    for j in range(F // step):
+        rows = pl.ds(j * step, step)
+        copies.append(pltpu.make_async_copy(weight_ref.at[rows], held.at[rows], sems.at[j]))
+    for copy in copies:
+        copy.start()
+    mhi, mlo = split(mixed_ref[...])
+    parts = jnp.concatenate([mhi, mlo], axis=1)
+    back = None
+    for j, copy in enumerate(copies):
+        rows = pl.ds(j * step, step)
+        copy.wait()
+        whi, wlo = split(held[rows])
+        both = jnp.dot(whi, parts, preferred_element_type=f32)
+        low = jnp.dot(wlo, mhi, preferred_element_type=f32)
+        pre = both[:, :CHUNK] + (both[:, CHUNK:] + low)
+        sig = jax.nn.sigmoid(pre)
+        out_ref[pl.ds(j * step // C, step // C), C:] = (pre * sig).reshape(step // C, C, CHUNK)
+        slope = cot_ref[rows] * sig * (1.0 + pre * (1.0 - sig))
+        slope_ref[rows] = slope
+        shi, slo = split(slope)
+        over_out = (((0,), (0,)), ((), ()))
+        both = lax.dot_general(whi, jnp.concatenate([shi, slo], axis=1), over_out, preferred_element_type=f32)
+        low = lax.dot_general(wlo, shi, over_out, preferred_element_type=f32)
+        part = both[:, :CHUNK] + (both[:, CHUNK:] + low)
+        back = part if back is None else back + part
+    out_ref[:, :C] = back.reshape(16, C, CHUNK)
+
+
+def dense(weight_t, mixed, cot):
     return pl.pallas_call(
         dense_kernel,
-        grid=(F // step,),
-        in_specs=[by_row, by_row, by_col, by_col, whole, rows],
-        out_specs=[rows, pl.BlockSpec((16, 2 * C, CHUNK), lambda i: (0, 0, 0))],
+        in_specs=[ANY, VMEM, VMEM],
+        out_specs=[VMEM, VMEM],
         out_shape=[jax.ShapeDtypeStruct((F, CHUNK), f32), jax.ShapeDtypeStruct((16, 2 * C, CHUNK), f32)],
-        scratch_shapes=[pltpu.VMEM((F, 2 * CHUNK), bf16)],
-        compiler_params=PARAMS,
-        cost_estimate=pl.CostEstimate(flops=12 * F * F * CHUNK, bytes_accessed=10 << 20, transcendentals=F * CHUNK),
-    )(*weights, mixed, cot)
+        scratch_shapes=[pltpu.VMEM((F, F), f32), pltpu.SemaphoreType.DMA((4,))],
+        compiler_params=PARAMS,
+        cost_estimate=pl.CostEstimate(flops=12 * F * F * CHUNK, bytes_accessed=8 << 20, transcendentals=F * CHUNK),
+    )(weight_t, mixed, cot)
 
 
 def push_far_kernel(refs_ref, back_ref, tiles_ref, a_ref, b_ref, c_ref, held, sems):
@@ -293,47 +268,42 @@
 
 
 def push_kernel(place_ref, back_ref, tiles_ref, diag_ref, *refs):
-    outs, held, sems = refs[:10], *refs[10:]
-    i = pl.program_id(0)
-
-    @pl.when(i == 0)
-    def _():
-        held[...] = jnp.zeros_like(held)
-
-    block = jnp.concatenate([back_ref[0], back_ref[1]], axis=1)
-    both = jnp.concatenate(split(block), axis=0)
-    for k in range(FAN):
-        part = jnp.dot(both, tiles_ref[0, k], preferred_element_type=f32)
-        value = part[:C] + part[C:]
-        if k == 0:
-            diag_ref[0] = value
-        else:
-            held[place_ref[i * (FAN - 1) + k - 1]] += value
-
-    @pl.when(i == BLK - 1)
-    def _():
-        copies = [pltpu.make_async_copy(held.at[rows], ref, sems.at[n]) for n, (rows, ref) in enumerate(places(outs))]
-        for copy in copies:
-            copy.start()
-        for copy in copies:
-            copy.wait()
+    outs, held, tiles, out_sems, tile_sems = refs[:10], *refs[10:]
+    tile_copies = [pltpu.make_async_copy(tiles_ref.at[i], tiles.at[i], tile_sems.at[i]) for i in range(BLK)]
+    for copy in tile_copies:
+        copy.start()
+    held[...] = jnp.zeros_like(held)
+    for i in range(BLK):
+        block = jnp.concatenate([back_ref[2 * i, :C], back_ref[2 * i + 1, :C]], axis=1)
+        both = jnp.concatenate(split(block), axis=0)
+        tile_copies[i].wait()
+        for k in range(FAN):
+            part = jnp.dot(both, tiles[i, k], preferred_element_type=f32)
+            value = part[:C] + part[C:]
+            if k == 0:
+                diag_ref[i] = value
+            else:
+                held[place_ref[i * (FAN - 1) + k - 1]] += value
+    copies = [pltpu.make_async_copy(held.at[rows], ref, out_sems.at[n]) for n, (rows, ref) in enumerate(places(outs))]
+    for copy in copies:
+        copy.start()
+    for copy in copies:
+        copy.wait()
 
 
 def push(place, back, tiles):
     sizes = (4, 4, 8, 8, 4, 4, 4, 8, 8, 8)
     return pl.pallas_call(
         push_kernel,
-        grid_spec=pltpu.PrefetchScalarGridSpec(
-            num_scalar_prefetch=1,
-            grid=(BLK,),
-            in_specs=[
-                pl.BlockSpec((2, C, CHUNK), lambda i, s: (i, 0, 0)),
-                pl.BlockSpec((1, FAN, W, W), lambda i, s: (i, 0, 0, 0)),
-            ],
-            out_specs=[pl.BlockSpec((1, C, W), lambda i, s: (i, 0, 0))] + [ANY] * len(sizes),
-            scratch_shapes=[pltpu.VMEM((HELD, C, W), f32), pltpu.SemaphoreType.DMA((len(sizes),))],
-        ),
+        in_specs=[SMEM, VMEM, ANY],
+        out_specs=[VMEM] + [ANY] * len(sizes),
         out_shape=[jax.ShapeDtypeStruct((n, C, W), f32) for n in (BLK,) + sizes],
+        scratch_shapes=[
+            pltpu.VMEM((HELD, C, W), f32),
+            pltpu.VMEM((BLK, FAN, W, W), bf16),
+            pltpu.SemaphoreType.DMA((len(sizes),)),
+            pltpu.SemaphoreType.DMA((BLK,)),
+        ],
         compiler_params=PARAMS,
         cost_estimate=pl.CostEstimate(flops=2 * 64 * W * W * 2 * C, bytes_accessed=13 << 20, transcendentals=0),
     )(place, back, tiles)
@@ -378,7 +348,7 @@
         in_specs=[SMEM] + [VMEM] * len(args),
         out_specs=[VMEM] * len(shapes),
         scratch_shapes=scratch,
-        compiler_params=PARAMS,
+        compiler_params=SMALL,
         cost_estimate=pl.CostEstimate(flops=12 * C * W, bytes_accessed=3 << 20, transcendentals=0),
     )(index, *args)
 
@@ -447,24 +417,21 @@
     up = shift(own, "zh", NZ, -1)
     down = shift(own, "zh", NZ, 1)
     near = over_x(pick(pick_near_kernel, (4,) * 3, [], near_at, own), 1)
-    (up, down), (near, weight_t) = after((up, down), (near, weight.T))
+    cot = over_col(cotangent.T.reshape(C, 16, CHUNK).transpose(1, 0, 2)).reshape(F, CHUNK)
+    (up, down), (near, cot, weight_t) = after((up, down), (near, cot, weight.T))
     weight_t = lax.all_gather(weight_t, COL, axis=0, tiled=True)
     lo, hi, *mid = pick(pick_mid_kernel, (4, 4) + (8,) * 3, [], mid_at, up, down)
-    mid, cot = after(mid, cotangent.T)
     lo = shift(lo, "zh", NZ, -1)
     hi = shift(hi, "zh", NZ, 1)
     mid = over_x(mid, 1)
-    cot = over_col(cot.reshape(C, 16, CHUNK).transpose(1, 0, 2)).reshape(F, CHUNK)
-    (lo, hi, mid), cot = after((lo, hi, mid), cot)
+    lo, hi, mid = lax.optimization_barrier((lo, hi, mid))
     far = pick(pick_far_kernel, (4,) * 3, [pltpu.VMEM((BLK, C, W), f32)], far_at, lo, hi)
     far = over_x(far, 1)
     part = mix(place, own, [lo, hi, up, down, *near, *mid], tiles)
     mixed = mix_far(far_refs, part, far, tiles)
 
-    mixed, weight_t = after(mixed, weight_t)
     mixed = over_col(mixed).reshape(F, CHUNK)
-    weights = weight_parts(weight_t)
-    slope, back = dense(weights, mixed, cot)
+    slope, back = dense(weight_t, mixed, cot)
     back = over_col(back)
     hidden = back[:, C:].transpose(1, 0, 2).reshape(C, 16 * CHUNK).T
 
@@ -474,7 +441,6 @@
     back, grad = after(back, grad)
 
     far = push_far(far_refs, back, tiles)
-    far, grad = after(far, grad)
     far = over_x(far, -1)
     grad = lax.all_to_all(grad.reshape(8, C, F), ("y", "zl"), 0, 0, tiled=True)
     diag, lo, hi, up, down, *pieces = push(place, back, tiles)
@@ -484,15 +450,16 @@
     lo, hi = gather_sum(far_kernel, (4, 4), [pltpu.VMEM((BLK, C, W), f32)], far_at, *far, lo, hi)
     lo = shift(lo, "zh", NZ, 1)
     hi = shift(hi, "zh", NZ, -1)
-    grad = grad.sum(axis=0)
-    grad = grad.reshape(2, C // 2, 16, C).transpose(2, 1, 0, 3).reshape(16, C // 2, 2 * C)
+    grad = grad.sum(axis=0).reshape(C, NX, W).transpose(1, 0, 2)
     (mid, lo, hi), (near, grad) = after((mid, lo, hi), (near, grad))
     up, down = gather_sum(mid_kernel, (8, 8), [], mid_at, *mid, up, down, lo, hi)
     (up, down), (near, grad) = after((up, down), (near, grad))
     up = shift(up, "zh", NZ, 1)
     down = shift(down, "zh", NZ, -1)
     near = over_x(near, -1)
-    grad = lax.all_to_all(grad, DOM, 0, 0, tiled=True).sum(axis=0)
+    grad = lax.all_to_all(grad, "x", 0, 0, tiled=True).sum(axis=0)
+    grad = grad.reshape(2, C // 2, NZ, C).transpose(2, 1, 0, 3).reshape(NZ, C // 2, 2 * C)
+    grad = lax.all_to_all(grad, "zh", 0, 0, tiled=True).sum(axis=0)
     (near,) = gather_sum(near_kernel, (8,), [], near_at, *near, diag)
     grad_weight = grad.reshape(C // 2, 2, C).transpose(1, 0, 2).reshape(C, C).T
     grad_features = (near + up + down).transpose(1, 0, 2).reshape(C, BLK * W).T

time: 255 us -> 237 us (0.929)
  Pallas kernels: 64.6 us -> 46.1 us
  blocking collectives: 0 us -> 15.5 us
  waiting for transfers between devices: 74.2 us -> 62 us
  starting transfers between devices: 80.7 us -> 74.2 us
    all_to_all x0 -> x1, blocking collectives: none -> 15.5 us  [over_col(): return lax.all_to_all(value, COL, 0, 0, tiled=True)]
    pallas_call x3 -> x2, Pallas kernels: 25 us -> 14.9 us  [the longest x1 7.89 us: push(): pl.pallas_call(push_kernel, in_specs=[SMEM, VMEM, ANY], out_specs=[VMEM]...]
    ppermute x28, waiting for transfers between devices: 59.8 us -> 50.4 us  [shift(): lax.ppermute(value, axis, [(i, (i + by) % size) for i in range(size)])]
    all_to_all x3 -> x2, starting transfers between devices: 20 us -> 11.6 us  [over_col(): return lax.all_to_all(value, COL, 0, 0, tiled=True)]
    pallas_call x3, Pallas kernels: 7.02 us -> 3.06 us  [pick(): pl.pallas_call(kernel, out_shape=[jax.ShapeDtypeStruct((n, C, W), f32) fo...]
    pallas_call x3, Pallas kernels: 7.54 us -> 4.58 us  [gather_sum(): pl.pallas_call(kernel, out_shape=[jax.ShapeDtypeStruct((n, C, W), f32) fo...]
    all_to_all x1 -> x2, starting transfers between devices: 7.13 us -> 9.67 us  [the longest x1 5.06 us: on_device(): grad = lax.all_to_all(grad, 'x', 0, 0, tiled=True).sum(axis=0)]
    all_to_all x1 -> x2, waiting for transfers between devices: 7.06 us -> 5.61 us  [the longest x1 3.63 us: on_device(): grad = lax.all_to_all(grad, 'zh', 0, 0, tiled=True).sum(axis=0)]
  transfers between devices with their start and end apart: 34 -> 34, of which waited for: 20 -> 21; matrix products, arithmetic and copies ran while one was open for 4% -> 6% of each run, Pallas kernels for 20% -> 16%
where the time goes in v4:
time: 237 us; the launch traced here: 233 us
  starting transfers between devices  74.2 us (31%)
  waiting for transfers between devices  62 us (26%)
  Pallas kernels  46.1 us (19%)
  local copies, waits for them, and re-layouts  17.1 us (7%)
  blocking collectives  15.5 us (7%)
  between operations  14.4 us (6%)
  other arithmetic  3.99 us (2%)
    ppermute x28, waiting for transfers between devices, shift(): lax.ppermute(value, axis, [(i, (i + by) % size) for i in range(size)])  50.4 us
    ppermute x28, starting transfers between devices, shift(): lax.ppermute(value, axis, [(i, (i + by) % size) for i in range(size)])  45.8 us
    all_to_all x1, blocking collectives, over_col(): return lax.all_to_all(value, COL, 0, 0, tiled=True)  15.5 us
    all_to_all x2, starting transfers between devices, over_col(): return lax.all_to_all(value, COL, 0, 0, tiled=True)  11.6 us
    pallas_call x1, Pallas kernels, mix(): pl.pallas_call(mixed_kernel, grid_spec=pltpu.PrefetchScalarGridSpec(num_s...  9.85 us
    pallas_call x1, Pallas kernels, push(): pl.pallas_call(push_kernel, in_specs=[SMEM, VMEM, ANY], out_specs=[VMEM]...  7.89 us
    all_to_all x1, starting transfers between devices, on_device(): grad = lax.all_to_all(grad.reshape(8, C, F), ('y', 'zl'), 0, 0, tiled=True)  7.07 us
    pallas_call x1, Pallas kernels, dense(): pl.pallas_call(dense_kernel, in_specs=[ANY, VMEM, VMEM], out_specs=[VMEM,...  6.99 us
  transfers between devices with their start and end apart: 34, of which 21 were waited for; matrix products, arithmetic and copies ran while one was open for 6% of the time, Pallas kernels for 16%

profile of v4, /device:TPU:10, one launch (start us, length us, event | category | flops | bytes accessed | tf_op | source)
XLA Modules:
  0.0 233.3 jit_solution(8397867485524793581)
XLA Ops:
  8.3 6.4 %collective-permute-start = (f32[8,64,256]{2,1,0:T(8,128)S(1)}, f32[8,64,256]{2,1,0:T(8,128)S(1)}, u32[]{:S(2)}, u32[]{:S(2)}) collective-permute-start(f32[8,64,256]{2,1,0:T(8,128)S(1)} %bitcast.56), channel_id=1, source_target_pairs={{0,48},{16,0},{32,16},{48,32},{1,49},{17,1},{33,17},{49,33},{2,50}... | collective-permute-start | bytes 1572872 | tf_op jit(solution)/shard_map/ppermute | solution.py:357
  15.6 5.4 %all-to-all-start = ((f32[16,64,128]{2,1,0:T(8,128)}), f32[16,64,128]{2,1,0:T(8,128)S(1)}, u32[]{:S(2)}, u32[]{:S(2)}) async-start(f32[16,64,128]{2,1,0:T(8,128)} %bitcast_bitcast_fusion.1), calls=%async_computation | async-start | bytes 1048576 | tf_op jit(solution)/shard_map/all_to_all | solution.py:365
  23.3 1.6 collective-permute-start.2
  26.0 2.2 collective-permute-start.4
  28.2 4.4 %collective-permute-done.2.refs_4_ = f32[4,64,256]{2,1,0:T(8,128)S(1)} collective-permute-done((f32[4,64,256]{2,1,0:T(8,128)S(1)}, f32[4,64,256]{2,1,0:T(8,128)S(1)}, u32[]{:S(2)}, u32[]{:S(2)}) %collective-permute-start.2) | collective-permute-done | bytes 262176 | tf_op jit(solution)/shard_map/ppermute | solution.py:357
  32.6 3.0 %collective-permute-done.3.refs_5_ = f32[4,64,256]{2,1,0:T(8,128)S(1)} collective-permute-done((f32[4,64,256]{2,1,0:T(8,128)S(1)}, f32[4,64,256]{2,1,0:T(8,128)S(1)}, u32[]{:S(2)}, u32[]{:S(2)}) %collective-permute-start.3) | collective-permute-done | bytes 262176 | tf_op jit(solution)/shard_map/ppermute | solution.py:357
  35.6 3.8 %collective-permute-done.4.refs_6_ = f32[4,64,256]{2,1,0:T(8,128)S(1)} collective-permute-done((f32[4,64,256]{2,1,0:T(8,128)S(1)}, f32[4,64,256]{2,1,0:T(8,128)S(1)}, u32[]{:S(2)}, u32[]{:S(2)}) %collective-permute-start.4) | collective-permute-done | bytes 262176 | tf_op jit(solution)/shard_map/ppermute | solution.py:357
  39.4 2.5 %collective-permute-done.1.down_ref.refs_3_ = f32[8,64,256]{2,1,0:T(8,128)S(1)} collective-permute-done((f32[8,64,256]{2,1,0:T(8,128)S(1)}, f32[8,64,256]{2,1,0:T(8,128)S(1)}, u32[]{:S(2)}, u32[]{:S(2)}) %collective-permute-start.1) | collective-permute-done | bytes 524320 | tf_op jit(solution)/shard_map/ppermute | solution.py:357
  43.7 1.8 shard_map.77
  45.6 1.5 collective-permute-start.7
  48.2 2.2 collective-permute-start.9
  50.4 3.3 %collective-permute-start.5 = (f32[4,64,256]{2,1,0:T(8,128)}, f32[4,64,256]{2,1,0:T(8,128)S(1)}, u32[]{:S(2)}, u32[]{:S(2)}) collective-permute-start(f32[4,64,256]{2,1,0:T(8,128)} %get-tuple-element.76), channel_id=1, source_target_pairs={{0,48},{16,0},{32,16},{48,32},{1,49},{17,1},{33,17},{49,33},{2,50}... | collective-permute-start | bytes 786440 | tf_op jit(solution)/shard_map/ppermute | solution.py:357
  54.5 10.2 %collective-permute-done.5.refs_0_.lo_ref = f32[4,64,256]{2,1,0:T(8,128)S(1)} collective-permute-done((f32[4,64,256]{2,1,0:T(8,128)}, f32[4,64,256]{2,1,0:T(8,128)S(1)}, u32[]{:S(2)}, u32[]{:S(2)}) %collective-permute-start.5) | collective-permute-done | bytes 262176 | tf_op jit(solution)/shard_map/ppermute | solution.py:357
  64.7 4.2 %collective-permute-done.6.refs_1_.hi_ref = f32[4,64,256]{2,1,0:T(8,128)S(1)} collective-permute-done((f32[4,64,256]{2,1,0:T(8,128)}, f32[4,64,256]{2,1,0:T(8,128)S(1)}, u32[]{:S(2)}, u32[]{:S(2)}) %collective-permute-start.6) | collective-permute-done | bytes 262176 | tf_op jit(solution)/shard_map/ppermute | solution.py:357
  68.9 3.8 %collective-permute-done.9.refs_9_ = f32[8,64,256]{2,1,0:T(8,128)} collective-permute-done((f32[8,64,256]{2,1,0:T(8,128)S(1)}, f32[8,64,256]{2,1,0:T(8,128)}, u32[]{:S(2)}, u32[]{:S(2)}) %collective-permute-start.9) | collective-permute-done | bytes 524320 | tf_op jit(solution)/shard_map/ppermute | solution.py:357
  73.3 1.6 collective-permute-start.10
  74.9 1.5 collective-permute-start.11
  76.4 1.7 collective-permute-start.12
  78.6 9.8 %shard_map.78.part_ref = f32[8,64,256]{2,1,0:T(8,128)} custom-call(s32[56]{0:T(128)} %fusion.3.place_ref, f32[8,64,256]{2,1,0:T(8,128)} %bitcast.59, f32[4,64,256]{2,1,0:T(8,128)} %copy-done.4, f32[4,64,256]{2,1,0:T(8,128)} %copy-done.5, f32[8,64,256]{2,1,0:T(8,128)} %copy-done.2, f32[8,64,256]{2,1,0:T(8,128)} %copy-done.3, f32[4,64,256]{2,1,0:T(8,128)} %copy-done.19, ...), custom_call_target="tpu_custom_call" | custom-call | flops 1073741824 | bytes 13631488 | tf_op jit(solution)/shard_map/pallas_call | solution.py:140
  89.9 4.3 %shard_map.80 = f32[16,64,128]{2,1,0:T(8,128)} custom-call(s32[12]{0:T(128)} %reshape.174.refs_ref, f32[8,64,256]{2,1,0:T(8,128)} %shard_map.78.part_ref, f32[4,64,256]{2,1,0:T(8,128)} %copy-done.15, f32[4,64,256]{2,1,0:T(8,128)} %copy-done.16, f32[4,64,256]{2,1,0:T(8,128)} %copy-done.17, bf16[8,8,256,256]{3,2,1,0:T(8,128)(2,1)} %tiles_ref.5), custom_call_target="tpu_custom_call" | custom-call | flops 201326592 | bytes 4194304 | tf_op jit(solution)/shard_map/pallas_call | solution.py:187
  94.3 15.5 %all_to_all.30 = f32[16,64,128]{2,1,0:T(8,128)} all-to-all(f32[16,64,128]{2,1,0:T(8,128)} %shard_map.80), channel_id=1, replica_groups=mesh['x'=4,'zh'=4,'y'=4,'zl'=2,'c'=2] {'y','zl','c'}, dimensions={0} | all-to-all | bytes 1048576 | tf_op jit(solution)/shard_map/all_to_all | solution.py:365
  109.8 7.0 %shard_map.81 = (f32[1024,128]{1,0:T(8,128)}, f32[16,128,128]{2,1,0:T(8,128)}) custom-call(f32[1024,1024]{1,0:T(8,128)} %all-gather.2.cloned.1.call-done.weight_ref, f32[1024,128]{1,0:T(8,128)} %bitcast.61, f32[1024,128]{1,0:T(8,128)} %bitcast.68), custom_call_target="tpu_custom_call" | custom-call | flops 1610612736 | bytes 8388608 | tf_op jit(solution)/shard_map/pallas_call | solution.py:234
  116.8 6.2 %all-to-all-start.2 = ((f32[16,128,128]{2,1,0:T(8,128)}), f32[16,128,128]{2,1,0:T(8,128)S(1)}, u32[]{:S(2)}, u32[]{:S(2)}) async-start(f32[16,128,128]{2,1,0:T(8,128)} %get-tuple-element.93), calls=%async_computation.2 | async-start | bytes 2097152 | tf_op jit(solution)/shard_map/all_to_all | solution.py:365
  126.6 5.4 %shard_map.82 = f32[512,1024]{1,0:T(8,128)} custom-call(s32[1]{0:T(128)} %bitcast.11.core_ref, f32[8,2,64,128]{3,2,1,0:T(8,128)} %bitcast.65, f32[512,128]{1,0:T(8,128)} %copy-done.18, f32[1024,128]{1,0:T(8,128)} %bitcast.62, f32[1024,128]{1,0:T(8,128)} %copy-done.13), custom_call_target="tpu_custom_call" | custom-call | flops 805306368 | bytes 4194304 | tf_op jit(solution)/shard_map/pallas_call | solution.py:387
  131.9 5.0 %all-to-all-done.2.back_ref = f32[16,128,128]{2,1,0:T(8,128)S(1)} async-done(((f32[16,128,128]{2,1,0:T(8,128)}), f32[16,128,128]{2,1,0:T(8,128)S(1)}, u32[]{:S(2)}, u32[]{:S(2)}) %all-to-all-start.2) | async-done | bytes 1048608 | tf_op jit(solution)/shard_map/all_to_all | solution.py:365
  137.0 7.1 %all-to-all-start.3 = ((f32[8,64,1024]{2,1,0:T(8,128)}), f32[8,64,1024]{2,1,0:T(8,128)}, u32[]{:S(2)}, u32[]{:S(2)}) async-start(f32[8,64,1024]{2,1,0:T(8,128)} %bitcast.60), calls=%async_computation.3 | async-start | bytes 4194304 | tf_op jit(solution)/shard_map/all_to_all | solution.py:445
  144.0 4.0 %shard_map.83 = (f32[4,64,256]{2,1,0:T(8,128)}, f32[4,64,256]{2,1,0:T(8,128)}, f32[4,64,256]{2,1,0:T(8,128)}) custom-call(s32[12]{0:T(128)} %reshape.174.refs_ref, f32[16,128,128]{2,1,0:T(8,128)} %copy-done.11, bf16[8,8,256,256]{3,2,1,0:T(8,128)(2,1)} %tiles_ref.5), custom_call_target="tpu_custom_call" | custom-call | flops 201326592 | bytes 4194304 | tf_op jit(solution)/shard_map/pallas_call | solution.py:259
  148.0 1.4 collective-permute-start.15
  149.5 2.1 collective-permute-start.16
  152.4 1.9 bitcast_bitcast_fusion
  154.2 7.9 %shard_map.84 = (f32[8,64,256]{2,1,0:T(8,128)}, f32[4,64,256]{2,1,0:T(8,128)}, f32[4,64,256]{2,1,0:T(8,128)}, f32[8,64,256]{2,1,0:T(8,128)}, f32[8,64,256]{2,1,0...) custom-call(s32[56]{0:T(128)} %fusion.3.place_ref, ...), custom_call_target="tpu_custom_call" | custom-call | flops 1073741824 | bytes 13631488 | tf_op jit(solution)/shard_map/pallas_call | solution.py:296
  163.7 1.8 collective-permute-start.18
  169.5 1.5 shard_map.85
  172.3 2.8 %collective-permute-start.22 = (f32[4,64,256]{2,1,0:T(8,128)}, f32[4,64,256]{2,1,0:T(8,128)}, u32[]{:S(2)}, u32[]{:S(2)}) collective-permute-start(f32[4,64,256]{2,1,0:T(8,128)} %get-tuple-element.112), channel_id=1, source_target_pairs={{0,48},{16,0},{32,16},{48,32},{1,49},{17,1},{33,17},{49,33},{2,50}... | collective-permute-start | bytes 786440 | tf_op jit(solution)/shard_map/ppermute | solution.py:357
  175.1 2.4 %reduce_sum.57 = f32[64,1024]{1,0:T(8,128)} reduce(f32[8,64,1024]{2,1,0:T(8,128)} %all-to-all-done.3, f32[]{:T(128)} %constant.33.clone.1), dimensions={0}, to_apply=%region_3.4 | reduce | flops 458752 | bytes 2359300 | tf_op jit(solution)/shard_map/reduce_sum | solution.py:453
  177.6 1.8 reshape.185
  180.5 5.6 %collective-permute-done.22.above_ref = f32[4,64,256]{2,1,0:T(8,128)} collective-permute-done((f32[4,64,256]{2,1,0:T(8,128)}, f32[4,64,256]{2,1,0:T(8,128)}, u32[]{:S(2)}, u32[]{:S(2)}) %collective-permute-start.22) | collective-permute-done | bytes 262176 | tf_op jit(solution)/shard_map/ppermute | solution.py:357
  186.1 3.9 %collective-permute-done.19.b_ref = f32[8,64,256]{2,1,0:T(8,128)S(1)} collective-permute-done((f32[8,64,256]{2,1,0:T(8,128)}, f32[8,64,256]{2,1,0:T(8,128)S(1)}, u32[]{:S(2)}, u32[]{:S(2)}) %collective-permute-start.19) | collective-permute-done | bytes 524320 | tf_op jit(solution)/shard_map/ppermute | solution.py:357
  190.7 2.4 %shard_map.86 = (f32[8,64,256]{2,1,0:T(8,128)}, f32[8,64,256]{2,1,0:T(8,128)}) custom-call(s32[24]{0:T(128)S(1)} %reshape.178.index_ref, f32[8,64,256]{2,1,0:T(8,128)S(1)} %collective-permute-done.18.a_ref, f32[8,64,256]{2,1,0:T(8,128)S(1)} %collective-permute-done.19.b_ref, f32[8,64,256]{2,1,0:T(8,128)} %collective-permute-done.20.c_ref, ...), custom_call_target="tpu_custom_call" | custom-call | flops 196608 | bytes 3145728 | tf_op jit(solution)/shard_map/pallas_call | solution.py:345
  194.0 3.3 %collective-permute-start.27 = (f32[8,64,256]{2,1,0:T(8,128)}, f32[8,64,256]{2,1,0:T(8,128)S(1)}, u32[]{:S(2)}, u32[]{:S(2)}) collective-permute-start(f32[8,64,256]{2,1,0:T(8,128)} %get-tuple-element.135), channel_id=1, source_target_pairs={{0,48},{16,0},{32,16},{48,32},{1,49},{17,1},{33,17},{49,33},{2,50}... | collective-permute-start | bytes 1572872 | tf_op jit(solution)/shard_map/ppermute | solution.py:357
  197.3 1.7 copy.46
  199.0 5.1 %all-to-all-start.4 = ((f32[4,64,256]{2,1,0:T(8,128)}), f32[4,64,256]{2,1,0:T(8,128)S(1)}, u32[]{:S(2)}, u32[]{:S(2)}) async-start(f32[4,64,256]{2,1,0:T(8,128)} %copy.46), calls=%async_computation.4 | async-start | bytes 524288 | tf_op jit(solution)/shard_map/all_to_all | solution.py:460
  204.2 2.8 %collective-permute-start.24 = (f32[4,64,256]{2,1,0:T(8,128)}, f32[4,64,256]{2,1,0:T(8,128)S(1)}, u32[]{:S(2)}, u32[]{:S(2)}) collective-permute-start(f32[4,64,256]{2,1,0:T(8,128)} %get-tuple-element.131), channel_id=1, source_target_pairs={{0,128},{64,192},{128,0},{192,64},{1,129},{65,193},{129,1},{193,65... | collective-permute-start | bytes 786440 | tf_op jit(solution)/shard_map/ppermute | solution.py:357
  207.0 1.8 collective-permute-start.25
  208.7 2.0 all-to-all-done.4
  211.7 4.6 %all-to-all-start.5 = ((f32[4,32,128]{2,1,0:T(8,128)}), f32[4,32,128]{2,1,0:T(8,128)S(1)}, u32[]{:S(2)}, u32[]{:S(2)}) async-start(f32[4,32,128]{2,1,0:T(8,128)} %reshape.188), calls=%async_computation.5 | async-start | bytes 131072 | tf_op jit(solution)/shard_map/all_to_all | solution.py:462
  216.3 4.1 %collective-permute-done.24.b_ref = f32[4,64,256]{2,1,0:T(8,128)S(1)} collective-permute-done((f32[4,64,256]{2,1,0:T(8,128)}, f32[4,64,256]{2,1,0:T(8,128)S(1)}, u32[]{:S(2)}, u32[]{:S(2)}) %collective-permute-start.24) | collective-permute-done | bytes 262176 | tf_op jit(solution)/shard_map/ppermute | solution.py:357
  221.1 3.6 %all-to-all-done.5 = f32[4,32,128]{2,1,0:T(8,128)S(1)} async-done(((f32[4,32,128]{2,1,0:T(8,128)}), f32[4,32,128]{2,1,0:T(8,128)S(1)}, u32[]{:S(2)}, u32[]{:S(2)}) %all-to-all-start.5) | async-done | bytes 65568 | tf_op jit(solution)/shard_map/all_to_all | solution.py:462
  (125 shorter events, 29.2 us)
Async XLA Ops:
  7.2 7.6 %copy-start = (f32[2048,64]{0,1:T(8,128)S(1)}, f32[2048,64]{0,1:T(8,128)}, u32[]{:S(2)}) copy-start(f32[2048,64]{0,1:T(8,128)} %param.9) | copy-start | bytes 1572868
  8.3 70.2 %copy-start.1 = (f32[8,8,8,256]{3,2,0,1:T(8,128)}, f32[8,8,8,256]{3,2,0,1:T(8,128)S(1)}, u32[]{:S(2)}) copy-start(f32[8,8,8,256]{3,2,0,1:T(8,128)S(1)} %copy.57) | copy-start | bytes 1572868
  8.3 31.1 %collective-permute-start = (f32[8,64,256]{2,1,0:T(8,128)S(1)}, f32[8,64,256]{2,1,0:T(8,128)S(1)}, u32[]{:S(2)}, u32[]{:S(2)}) collective-permute-start(f32[8,64,256]{2,1,0:T(8,128)S(1)} %bitcast.56), channel_id=1, source_target_pairs={{0,48},{16,0},{32,16},{48,32},{1,49},{17,1},{33,17},{49,33},{2,50}... | collective-permute-start | bytes 1572872 | tf_op jit(solution)/shard_map/ppermute | solution.py:357
  14.7 27.2 %collective-permute-start.1 = (f32[8,64,256]{2,1,0:T(8,128)S(1)}, f32[8,64,256]{2,1,0:T(8,128)S(1)}, u32[]{:S(2)}, u32[]{:S(2)}) collective-permute-start(f32[8,64,256]{2,1,0:T(8,128)S(1)} %bitcast.57), channel_id=1, source_target_pairs={{0,16},{16,32},{32,48},{48,0},{1,17},{17,33},{33,49},{49,1},{2,18}... | collective-permute-start | bytes 1572872 | tf_op jit(solution)/shard_map/ppermute | solution.py:357
  15.6 27.3 %all-to-all-start = ((f32[16,64,128]{2,1,0:T(8,128)}), f32[16,64,128]{2,1,0:T(8,128)S(1)}, u32[]{:S(2)}, u32[]{:S(2)}) async-start(f32[16,64,128]{2,1,0:T(8,128)} %bitcast_bitcast_fusion.1), calls=%async_computation | async-start | bytes 1048576 | tf_op jit(solution)/shard_map/all_to_all | solution.py:365
  21.0 88.8 %all-gather.2.cloned.1.call-start = ((), (), s32[]{:S(2)}) async-start(), calls=%async_computation.6 | async-start | bytes 4456448 | tf_op jit(solution)/shard_map/all_gather | solution.py:422
  23.3 9.2 %collective-permute-start.2 = (f32[4,64,256]{2,1,0:T(8,128)S(1)}, f32[4,64,256]{2,1,0:T(8,128)S(1)}, u32[]{:S(2)}, u32[]{:S(2)}) collective-permute-start(f32[4,64,256]{2,1,0:T(8,128)S(1)} %get-tuple-element.70), channel_id=1, source_target_pairs={{0,64},{64,128},{128,192},{192,0},{1,65},{65,129},{129,193},{193,1... | collective-permute-start | bytes 786440 | tf_op jit(solution)/shard_map/ppermute | solution.py:357
  24.9 10.7 %collective-permute-start.3 = (f32[4,64,256]{2,1,0:T(8,128)S(1)}, f32[4,64,256]{2,1,0:T(8,128)S(1)}, u32[]{:S(2)}, u32[]{:S(2)}) collective-permute-start(f32[4,64,256]{2,1,0:T(8,128)S(1)} %get-tuple-element.71), channel_id=1, source_target_pairs={{0,128},{64,192},{128,0},{192,64},{1,129},{65,193},{129,1},{193,65... | collective-permute-start | bytes 786440 | tf_op jit(solution)/shard_map/ppermute | solution.py:357
  26.0 13.4 %collective-permute-start.4 = (f32[4,64,256]{2,1,0:T(8,128)S(1)}, f32[4,64,256]{2,1,0:T(8,128)S(1)}, u32[]{:S(2)}, u32[]{:S(2)}) collective-permute-start(f32[4,64,256]{2,1,0:T(8,128)S(1)} %get-tuple-element.72), channel_id=1, source_target_pairs={{0,192},{64,0},{128,64},{192,128},{1,193},{65,1},{129,65},{193,129... | collective-permute-start | bytes 786440 | tf_op jit(solution)/shard_map/ppermute | solution.py:357
  32.6 46.0 %copy-start.19 = (f32[4,64,256]{2,1,0:T(8,128)}, f32[4,64,256]{2,1,0:T(8,128)S(1)}, u32[]{:S(2)}) copy-start(f32[4,64,256]{2,1,0:T(8,128)S(1)} %collective-permute-done.2.refs_4_) | copy-start | bytes 786436
  35.6 7.5 %copy-start.20 = (f32[4,64,256]{2,1,0:T(8,128)}, f32[4,64,256]{2,1,0:T(8,128)S(1)}, u32[]{:S(2)}) copy-start(f32[4,64,256]{2,1,0:T(8,128)S(1)} %collective-permute-done.3.refs_5_) | copy-start | bytes 786436
  39.4 11.0 %copy-start.21 = (f32[4,64,256]{2,1,0:T(8,128)}, f32[4,64,256]{2,1,0:T(8,128)S(1)}, u32[]{:S(2)}) copy-start(f32[4,64,256]{2,1,0:T(8,128)S(1)} %collective-permute-done.4.refs_6_) | copy-start | bytes 786436
  39.4 39.1 %copy-start.2 = (f32[8,64,256]{2,1,0:T(8,128)}, f32[8,64,256]{2,1,0:T(8,128)S(1)}, u32[]{:S(2)}) copy-start(f32[8,64,256]{2,1,0:T(8,128)S(1)} %collective-permute-done.up_ref.refs_2_) | copy-start | bytes 1572868
  42.0 36.6 %copy-start.3 = (f32[8,64,256]{2,1,0:T(8,128)}, f32[8,64,256]{2,1,0:T(8,128)S(1)}, u32[]{:S(2)}) copy-start(f32[8,64,256]{2,1,0:T(8,128)S(1)} %collective-permute-done.1.down_ref.refs_3_) | copy-start | bytes 1572868
  45.6 23.3 %collective-permute-start.7 = (f32[8,64,256]{2,1,0:T(8,128)}, f32[8,64,256]{2,1,0:T(8,128)}, u32[]{:S(2)}, u32[]{:S(2)}) collective-permute-start(f32[8,64,256]{2,1,0:T(8,128)} %get-tuple-element.78), channel_id=1, source_target_pairs={{0,64},{64,128},{128,192},{192,0},{1,65},{65,129},{129,193},{193,1... | collective-permute-start | bytes 1572872 | tf_op jit(solution)/shard_map/ppermute | solution.py:357
  47.0 21.8 %collective-permute-start.8 = (f32[8,64,256]{2,1,0:T(8,128)}, f32[8,64,256]{2,1,0:T(8,128)}, u32[]{:S(2)}, u32[]{:S(2)}) collective-permute-start(f32[8,64,256]{2,1,0:T(8,128)} %get-tuple-element.79), channel_id=1, source_target_pairs={{0,128},{64,192},{128,0},{192,64},{1,129},{65,193},{129,1},{193,65... | collective-permute-start | bytes 1572872 | tf_op jit(solution)/shard_map/ppermute | solution.py:357
  48.2 24.5 %collective-permute-start.9 = (f32[8,64,256]{2,1,0:T(8,128)S(1)}, f32[8,64,256]{2,1,0:T(8,128)}, u32[]{:S(2)}, u32[]{:S(2)}) collective-permute-start(f32[8,64,256]{2,1,0:T(8,128)S(1)} %get-tuple-element.80), channel_id=1, source_target_pairs={{0,192},{64,0},{128,64},{192,128},{1,193},{65,1},{129,65},{193,129... | collective-permute-start | bytes 1572872 | tf_op jit(solution)/shard_map/ppermute | solution.py:357
  50.4 14.3 %collective-permute-start.5 = (f32[4,64,256]{2,1,0:T(8,128)}, f32[4,64,256]{2,1,0:T(8,128)S(1)}, u32[]{:S(2)}, u32[]{:S(2)}) collective-permute-start(f32[4,64,256]{2,1,0:T(8,128)} %get-tuple-element.76), channel_id=1, source_target_pairs={{0,48},{16,0},{32,16},{48,32},{1,49},{17,1},{33,17},{49,33},{2,50}... | collective-permute-start | bytes 786440 | tf_op jit(solution)/shard_map/ppermute | solution.py:357
  53.7 15.2 %collective-permute-start.6 = (f32[4,64,256]{2,1,0:T(8,128)}, f32[4,64,256]{2,1,0:T(8,128)S(1)}, u32[]{:S(2)}, u32[]{:S(2)}) collective-permute-start(f32[4,64,256]{2,1,0:T(8,128)} %get-tuple-element.77), channel_id=1, source_target_pairs={{0,16},{16,32},{32,48},{48,0},{1,17},{17,33},{33,49},{49,1},{2,18}... | collective-permute-start | bytes 786440 | tf_op jit(solution)/shard_map/ppermute | solution.py:357
  64.7 13.9 %copy-start.4 = (f32[4,64,256]{2,1,0:T(8,128)}, f32[4,64,256]{2,1,0:T(8,128)S(1)}, u32[]{:S(2)}) copy-start(f32[4,64,256]{2,1,0:T(8,128)S(1)} %collective-permute-done.5.refs_0_.lo_ref) | copy-start | bytes 786436
  68.9 9.7 %copy-start.5 = (f32[4,64,256]{2,1,0:T(8,128)}, f32[4,64,256]{2,1,0:T(8,128)S(1)}, u32[]{:S(2)}) copy-start(f32[4,64,256]{2,1,0:T(8,128)S(1)} %collective-permute-done.6.refs_1_.hi_ref) | copy-start | bytes 786436
  73.3 15.1 %collective-permute-start.10 = (f32[4,64,256]{2,1,0:T(8,128)S(1)}, f32[4,64,256]{2,1,0:T(8,128)S(1)}, u32[]{:S(2)}, u32[]{:S(2)}) collective-permute-start(f32[4,64,256]{2,1,0:T(8,128)S(1)} %get-tuple-element.89), channel_id=1, source_target_pairs={{0,64},{64,128},{128,192},{192,0},{1,65},{65,129},{129,193},{193,1... | collective-permute-start | bytes 786440 | tf_op jit(solution)/shard_map/ppermute | solution.py:357
  74.9 13.6 %collective-permute-start.11 = (f32[4,64,256]{2,1,0:T(8,128)S(1)}, f32[4,64,256]{2,1,0:T(8,128)S(1)}, u32[]{:S(2)}, u32[]{:S(2)}) collective-permute-start(f32[4,64,256]{2,1,0:T(8,128)S(1)} %get-tuple-element.90), channel_id=1, source_target_pairs={{0,128},{64,192},{128,0},{192,64},{1,129},{65,193},{129,1},{193,65... | collective-permute-start | bytes 786440 | tf_op jit(solution)/shard_map/ppermute | solution.py:357
  76.4 12.4 %collective-permute-start.12 = (f32[4,64,256]{2,1,0:T(8,128)S(1)}, f32[4,64,256]{2,1,0:T(8,128)S(1)}, u32[]{:S(2)}, u32[]{:S(2)}) collective-permute-start(f32[4,64,256]{2,1,0:T(8,128)S(1)} %get-tuple-element.91), channel_id=1, source_target_pairs={{0,192},{64,0},{128,64},{192,128},{1,193},{65,1},{129,65},{193,129... | collective-permute-start | bytes 786440 | tf_op jit(solution)/shard_map/ppermute | solution.py:357
  109.8 13.3 %copy-start.12 = (f32[16,64,128]{2,1,0:T(8,128)S(1)}, f32[16,64,128]{2,1,0:T(8,128)}, u32[]{:S(2)}) copy-start(f32[16,64,128]{2,1,0:T(8,128)} %all_to_all.30) | copy-start | bytes 1572868
  116.8 20.2 %all-to-all-start.2 = ((f32[16,128,128]{2,1,0:T(8,128)}), f32[16,128,128]{2,1,0:T(8,128)S(1)}, u32[]{:S(2)}, u32[]{:S(2)}) async-start(f32[16,128,128]{2,1,0:T(8,128)} %get-tuple-element.93), calls=%async_computation.2 | async-start | bytes 2097152 | tf_op jit(solution)/shard_map/all_to_all | solution.py:365
  123.0 2.0 collective-permute-start.14
  124.2 1.6 collective-permute-start.13
  137.0 7.1 %copy-start.11 = (f32[16,128,128]{2,1,0:T(8,128)}, f32[16,128,128]{2,1,0:T(8,128)S(1)}, u32[]{:S(2)}) copy-start(f32[16,128,128]{2,1,0:T(8,128)S(1)} %all-to-all-done.2.back_ref) | copy-start | bytes 3145732
  137.0 38.2 %all-to-all-start.3 = ((f32[8,64,1024]{2,1,0:T(8,128)}), f32[8,64,1024]{2,1,0:T(8,128)}, u32[]{:S(2)}, u32[]{:S(2)}) async-start(f32[8,64,1024]{2,1,0:T(8,128)} %bitcast.60), calls=%async_computation.3 | async-start | bytes 4194304 | tf_op jit(solution)/shard_map/all_to_all | solution.py:445
  148.0 14.1 %collective-permute-start.15 = (f32[4,64,256]{2,1,0:T(8,128)}, f32[4,64,256]{2,1,0:T(8,128)S(1)}, u32[]{:S(2)}, u32[]{:S(2)}) collective-permute-start(f32[4,64,256]{2,1,0:T(8,128)} %get-tuple-element.96), channel_id=1, source_target_pairs={{0,192},{64,0},{128,64},{192,128},{1,193},{65,1},{129,65},{193,129... | collective-permute-start | bytes 786440 | tf_op jit(solution)/shard_map/ppermute | solution.py:357
  149.5 13.5 %collective-permute-start.16 = (f32[4,64,256]{2,1,0:T(8,128)}, f32[4,64,256]{2,1,0:T(8,128)S(1)}, u32[]{:S(2)}, u32[]{:S(2)}) collective-permute-start(f32[4,64,256]{2,1,0:T(8,128)} %get-tuple-element.97), channel_id=1, source_target_pairs={{0,128},{64,192},{128,0},{192,64},{1,129},{65,193},{129,1},{193,65... | collective-permute-start | bytes 786440 | tf_op jit(solution)/shard_map/ppermute | solution.py:357
  151.6 12.1 %collective-permute-start.17 = (f32[4,64,256]{2,1,0:T(8,128)}, f32[4,64,256]{2,1,0:T(8,128)S(1)}, u32[]{:S(2)}, u32[]{:S(2)}) collective-permute-start(f32[4,64,256]{2,1,0:T(8,128)} %get-tuple-element.98), channel_id=1, source_target_pairs={{0,64},{64,128},{128,192},{192,0},{1,65},{65,129},{129,193},{193,1... | collective-permute-start | bytes 786440 | tf_op jit(solution)/shard_map/ppermute | solution.py:357
  162.1 28.6 %copy-start.7 = (f32[8,64,256]{2,1,0:T(8,128)S(1)}, f32[8,64,256]{2,1,0:T(8,128)}, u32[]{:S(2)}) copy-start(f32[8,64,256]{2,1,0:T(8,128)} %get-tuple-element.120.up_ref) | copy-start | bytes 1572868
  162.2 28.6 %copy-start.8 = (f32[8,64,256]{2,1,0:T(8,128)S(1)}, f32[8,64,256]{2,1,0:T(8,128)}, u32[]{:S(2)}) copy-start(f32[8,64,256]{2,1,0:T(8,128)} %get-tuple-element.121.down_ref) | copy-start | bytes 1572868
  163.7 22.4 %collective-permute-start.18 = (f32[8,64,256]{2,1,0:T(8,128)}, f32[8,64,256]{2,1,0:T(8,128)S(1)}, u32[]{:S(2)}, u32[]{:S(2)}) collective-permute-start(f32[8,64,256]{2,1,0:T(8,128)} %get-tuple-element.103), channel_id=1, source_target_pairs={{0,192},{64,0},{128,64},{192,128},{1,193},{65,1},{129,65},{193,129... | collective-permute-start | bytes 1572872 | tf_op jit(solution)/shard_map/ppermute | solution.py:357
  165.5 24.5 %collective-permute-start.19 = (f32[8,64,256]{2,1,0:T(8,128)}, f32[8,64,256]{2,1,0:T(8,128)S(1)}, u32[]{:S(2)}, u32[]{:S(2)}) collective-permute-start(f32[8,64,256]{2,1,0:T(8,128)} %get-tuple-element.104), channel_id=1, source_target_pairs={{0,128},{64,192},{128,0},{192,64},{1,129},{65,193},{129,1},{193,65... | collective-permute-start | bytes 1572872 | tf_op jit(solution)/shard_map/ppermute | solution.py:357
  166.6 24.1 %collective-permute-start.20 = (f32[8,64,256]{2,1,0:T(8,128)}, f32[8,64,256]{2,1,0:T(8,128)}, u32[]{:S(2)}, u32[]{:S(2)}) collective-permute-start(f32[8,64,256]{2,1,0:T(8,128)} %get-tuple-element.105), channel_id=1, source_target_pairs={{0,64},{64,128},{128,192},{192,0},{1,65},{65,129},{129,193},{193,1... | collective-permute-start | bytes 1572872 | tf_op jit(solution)/shard_map/ppermute | solution.py:357
  171.0 49.4 %copy-start.6 = (f32[8,64,256]{2,1,0:T(8,128)S(1)}, f32[8,64,256]{2,1,0:T(8,128)}, u32[]{:S(2)}) copy-start(f32[8,64,256]{2,1,0:T(8,128)} %get-tuple-element.133.diag_ref) | copy-start | bytes 1572868
  171.0 9.5 %collective-permute-start.21 = (f32[4,64,256]{2,1,0:T(8,128)}, f32[4,64,256]{2,1,0:T(8,128)S(1)}, u32[]{:S(2)}, u32[]{:S(2)}) collective-permute-start(f32[4,64,256]{2,1,0:T(8,128)} %get-tuple-element.111), channel_id=1, source_target_pairs={{0,16},{16,32},{32,48},{48,0},{1,17},{17,33},{33,49},{49,1},{2,18}... | collective-permute-start | bytes 786440 | tf_op jit(solution)/shard_map/ppermute | solution.py:357
  172.3 13.8 %collective-permute-start.22 = (f32[4,64,256]{2,1,0:T(8,128)}, f32[4,64,256]{2,1,0:T(8,128)}, u32[]{:S(2)}, u32[]{:S(2)}) collective-permute-start(f32[4,64,256]{2,1,0:T(8,128)} %get-tuple-element.112), channel_id=1, source_target_pairs={{0,48},{16,0},{32,16},{48,32},{1,49},{17,1},{33,17},{49,33},{2,50}... | collective-permute-start | bytes 786440 | tf_op jit(solution)/shard_map/ppermute | solution.py:357
  193.2 32.4 %collective-permute-start.26 = (f32[8,64,256]{2,1,0:T(8,128)}, f32[8,64,256]{2,1,0:T(8,128)S(1)}, u32[]{:S(2)}, u32[]{:S(2)}) collective-permute-start(f32[8,64,256]{2,1,0:T(8,128)} %get-tuple-element.134), channel_id=1, source_target_pairs={{0,16},{16,32},{32,48},{48,0},{1,17},{17,33},{33,49},{49,1},{2,18}... | collective-permute-start | bytes 1572872 | tf_op jit(solution)/shard_map/ppermute | solution.py:357
  194.0 31.5 %collective-permute-start.27 = (f32[8,64,256]{2,1,0:T(8,128)}, f32[8,64,256]{2,1,0:T(8,128)S(1)}, u32[]{:S(2)}, u32[]{:S(2)}) collective-permute-start(f32[8,64,256]{2,1,0:T(8,128)} %get-tuple-element.135), channel_id=1, source_target_pairs={{0,48},{16,0},{32,16},{48,32},{1,49},{17,1},{33,17},{49,33},{2,50}... | collective-permute-start | bytes 1572872 | tf_op jit(solution)/shard_map/ppermute | solution.py:357
  199.0 11.8 %all-to-all-start.4 = ((f32[4,64,256]{2,1,0:T(8,128)}), f32[4,64,256]{2,1,0:T(8,128)S(1)}, u32[]{:S(2)}, u32[]{:S(2)}) async-start(f32[4,64,256]{2,1,0:T(8,128)} %copy.46), calls=%async_computation.4 | async-start | bytes 524288 | tf_op jit(solution)/shard_map/all_to_all | solution.py:460
  204.0 12.3 %collective-permute-start.23 = (f32[4,64,256]{2,1,0:T(8,128)}, f32[4,64,256]{2,1,0:T(8,128)S(1)}, u32[]{:S(2)}, u32[]{:S(2)}) collective-permute-start(f32[4,64,256]{2,1,0:T(8,128)} %get-tuple-element.130), channel_id=1, source_target_pairs={{0,192},{64,0},{128,64},{192,128},{1,193},{65,1},{129,65},{193,129... | collective-permute-start | bytes 786440 | tf_op jit(solution)/shard_map/ppermute | solution.py:357
  204.2 16.2 %collective-permute-start.24 = (f32[4,64,256]{2,1,0:T(8,128)}, f32[4,64,256]{2,1,0:T(8,128)S(1)}, u32[]{:S(2)}, u32[]{:S(2)}) collective-permute-start(f32[4,64,256]{2,1,0:T(8,128)} %get-tuple-element.131), channel_id=1, source_target_pairs={{0,128},{64,192},{128,0},{192,64},{1,129},{65,193},{129,1},{193,65... | collective-permute-start | bytes 786440 | tf_op jit(solution)/shard_map/ppermute | solution.py:357
  207.0 13.4 %collective-permute-start.25 = (f32[4,64,256]{2,1,0:T(8,128)}, f32[4,64,256]{2,1,0:T(8,128)S(1)}, u32[]{:S(2)}, u32[]{:S(2)}) collective-permute-start(f32[4,64,256]{2,1,0:T(8,128)} %get-tuple-element.132), channel_id=1, source_target_pairs={{0,64},{64,128},{128,192},{192,0},{1,65},{65,129},{129,193},{193,1... | collective-permute-start | bytes 786440 | tf_op jit(solution)/shard_map/ppermute | solution.py:357
  211.7 13.0 %all-to-all-start.5 = ((f32[4,32,128]{2,1,0:T(8,128)}), f32[4,32,128]{2,1,0:T(8,128)S(1)}, u32[]{:S(2)}, u32[]{:S(2)}) async-start(f32[4,32,128]{2,1,0:T(8,128)} %reshape.188), calls=%async_computation.5 | async-start | bytes 131072 | tf_op jit(solution)/shard_map/all_to_all | solution.py:462
  (8 other events, 6.4 us)
Sparse Core Ops, SparseCore 0:
  43.1 47.5 all-gather.1

commit v5 on v4

--- a/solution.py
+++ b/solution.py
@@ -154,30 +154,39 @@
     )(place, own, *sources, tiles)
 
 
-def tile_copies(refs_ref, tiles_ref, held, sems):
+def far_tiles_kernel(refs_ref, tiles_ref, out_ref, sems):
     copies = []
     for slot in range(12):
         ref = jnp.maximum(refs_ref[slot] - 1, 0)
         i = ref // (FAN - 1)
         copies.append(
-            pltpu.make_async_copy(tiles_ref.at[i, ref - i * (FAN - 1) + 1], held.at[slot], sems.at[slot])
+            pltpu.make_async_copy(tiles_ref.at[i, ref - i * (FAN - 1) + 1], out_ref.at[slot], sems.at[slot])
         )
     for copy in copies:
         copy.start()
-    return copies
-
-
-def mix_far_kernel(refs_ref, part_ref, a_ref, b_ref, c_ref, tiles_ref, out_ref, held, total, sems):
-    copies = tile_copies(refs_ref, tiles_ref, held, sems)
-    total[...] = part_ref[...]
     for copy in copies:
         copy.wait()
+
+
+def far_tiles(far_refs, tiles):
+    return pl.pallas_call(
+        far_tiles_kernel,
+        out_shape=jax.ShapeDtypeStruct((12, W, W), bf16),
+        in_specs=[SMEM, ANY],
+        out_specs=VMEM,
+        scratch_shapes=[pltpu.SemaphoreType.DMA((12,))],
+        compiler_params=PARAMS,
+        cost_estimate=pl.CostEstimate(flops=0, bytes_accessed=3 << 20, transcendentals=0),
+    )(far_refs, tiles)
+
+
+def mix_far_kernel(refs_ref, part_ref, a_ref, b_ref, c_ref, tiles_ref, out_ref, total):
+    total[...] = part_ref[...]
     for slot in range(12):
         both = jnp.concatenate(split((a_ref, b_ref, c_ref)[slot // SLOTS][slot % SLOTS]), axis=0)
-        part = lax.dot_general(both, held[slot], (((1,), (1,)), ((), ())), preferred_element_type=f32)
+        part = lax.dot_general(both, tiles_ref[slot], (((1,), (1,)), ((), ())), preferred_element_type=f32)
         ref = refs_ref[slot]
         total[jnp.maximum(ref - 1, 0) // (FAN - 1)] += jnp.where(ref > 0, part[:C] + part[C:], 0.0)
-
     for i in range(BLK):
         out_ref[2 * i] = total[i, :, :CHUNK]
         out_ref[2 * i + 1] = total[i, :, CHUNK:]
@@ -187,20 +196,16 @@
     return pl.pallas_call(
         mix_far_kernel,
         out_shape=jax.ShapeDtypeStruct((16, C, CHUNK), f32),
-        in_specs=[SMEM] + [VMEM] * 4 + [ANY],
+        in_specs=[SMEM] + [VMEM] * 5,
         out_specs=VMEM,
-        scratch_shapes=[
-            pltpu.VMEM((12, W, W), bf16),
-            pltpu.VMEM((BLK, C, W), f32),
-            pltpu.SemaphoreType.DMA((12,)),
-        ],
-        compiler_params=PARAMS,
+        scratch_shapes=[pltpu.VMEM((BLK, C, W), f32)],
+        compiler_params=SMALL,
         cost_estimate=pl.CostEstimate(flops=2 * 12 * W * W * 2 * C, bytes_accessed=4 << 20, transcendentals=0),
     )(far_refs, part, *far, tiles)
 
 
 def dense_kernel(weight_ref, mixed_ref, cot_ref, slope_ref, out_ref, held, sems):
-    step = 256
+    step = F // 2
     copies = []
     for j in range(F // step):
         rows = pl.ds(j * step, step)
@@ -221,13 +226,12 @@
         out_ref[pl.ds(j * step // C, step // C), C:] = (pre * sig).reshape(step // C, C, CHUNK)
         slope = cot_ref[rows] * sig * (1.0 + pre * (1.0 - sig))
         slope_ref[rows] = slope
-        shi, slo = split(slope)
-        over_out = (((0,), (0,)), ((), ()))
-        both = lax.dot_general(whi, jnp.concatenate([shi, slo], axis=1), over_out, preferred_element_type=f32)
-        low = lax.dot_general(wlo, shi, over_out, preferred_element_type=f32)
-        part = both[:, :CHUNK] + (both[:, CHUNK:] + low)
+        shi, slo = split(slope.T)
+        both = jnp.dot(jnp.concatenate([shi, slo], axis=0), whi, preferred_element_type=f32)
+        low = jnp.dot(shi, wlo, preferred_element_type=f32)
+        part = both[:CHUNK] + (both[CHUNK:] + low)
         back = part if back is None else back + part
-    out_ref[:, :C] = back.reshape(16, C, CHUNK)
+    out_ref[:, :C] = back.T.reshape(16, C, CHUNK)
 
 
 def dense(weight_t, mixed, cot):
@@ -236,22 +240,18 @@
         in_specs=[ANY, VMEM, VMEM],
         out_specs=[VMEM, VMEM],
         out_shape=[jax.ShapeDtypeStruct((F, CHUNK), f32), jax.ShapeDtypeStruct((16, 2 * C, CHUNK), f32)],
-        scratch_shapes=[pltpu.VMEM((F, F), f32), pltpu.SemaphoreType.DMA((4,))],
+        scratch_shapes=[pltpu.VMEM((F, F), f32), pltpu.SemaphoreType.DMA((2,))],
         compiler_params=PARAMS,
         cost_estimate=pl.CostEstimate(flops=12 * F * F * CHUNK, bytes_accessed=8 << 20, transcendentals=F * CHUNK),
     )(weight_t, mixed, cot)
 
 
-def push_far_kernel(refs_ref, back_ref, tiles_ref, a_ref, b_ref, c_ref, held, sems):
-    copies = tile_copies(refs_ref, tiles_ref, held, sems)
-    for copy in copies:
-        copy.wait()
+def push_far_kernel(refs_ref, back_ref, tiles_ref, a_ref, b_ref, c_ref):
     for slot in range(12):
-        ref = refs_ref[slot]
-        i = jnp.maximum(ref - 1, 0) // (FAN - 1)
+        i = jnp.maximum(refs_ref[slot] - 1, 0) // (FAN - 1)
         block = jnp.concatenate([back_ref[2 * i, :C], back_ref[2 * i + 1, :C]], axis=1)
         both = jnp.concatenate(split(block), axis=0)
-        part = jnp.dot(both, held[slot], preferred_element_type=f32)
+        part = jnp.dot(both, tiles_ref[slot], preferred_element_type=f32)
         (a_ref, b_ref, c_ref)[slot // SLOTS][slot % SLOTS] = part[:C] + part[C:]
 
 
@@ -259,10 +259,9 @@
     return pl.pallas_call(
         push_far_kernel,
         out_shape=[jax.ShapeDtypeStruct((SLOTS, C, W), f32)] * 3,
-        in_specs=[SMEM, VMEM, ANY],
+        in_specs=[SMEM, VMEM, VMEM],
         out_specs=[VMEM] * 3,
-        scratch_shapes=[pltpu.VMEM((12, W, W), bf16), pltpu.SemaphoreType.DMA((12,))],
-        compiler_params=PARAMS,
+        compiler_params=SMALL,
         cost_estimate=pl.CostEstimate(flops=2 * 12 * W * W * 2 * C, bytes_accessed=4 << 20, transcendentals=0),
     )(far_refs, back, tiles)
 
@@ -418,7 +417,8 @@
     down = shift(own, "zh", NZ, 1)
     near = over_x(pick(pick_near_kernel, (4,) * 3, [], near_at, own), 1)
     cot = over_col(cotangent.T.reshape(C, 16, CHUNK).transpose(1, 0, 2)).reshape(F, CHUNK)
-    (up, down), (near, cot, weight_t) = after((up, down), (near, cot, weight.T))
+    some = far_tiles(far_refs, tiles)
+    (up, down), (near, cot, weight_t, some) = after((up, down), (near, cot, weight.T, some))
     weight_t = lax.all_gather(weight_t, COL, axis=0, tiled=True)
     lo, hi, *mid = pick(pick_mid_kernel, (4, 4) + (8,) * 3, [], mid_at, up, down)
     lo = shift(lo, "zh", NZ, -1)
@@ -428,7 +428,7 @@
     far = pick(pick_far_kernel, (4,) * 3, [pltpu.VMEM((BLK, C, W), f32)], far_at, lo, hi)
     far = over_x(far, 1)
     part = mix(place, own, [lo, hi, up, down, *near, *mid], tiles)
-    mixed = mix_far(far_refs, part, far, tiles)
+    mixed = mix_far(far_refs, part, far, some)
 
     mixed = over_col(mixed).reshape(F, CHUNK)
     slope, back = dense(weight_t, mixed, cot)
@@ -440,7 +440,7 @@
     grad = grad_part(me_c, slope, other, mixed, shift(mixed, "c", 2, 1))
     back, grad = after(back, grad)
 
-    far = push_far(far_refs, back, tiles)
+    far = push_far(far_refs, back, some)
     far = over_x(far, -1)
     grad = lax.all_to_all(grad.reshape(8, C, F), ("y", "zl"), 0, 0, tiled=True)
     diag, lo, hi, up, down, *pieces = push(place, back, tiles)

time: 237 us -> 231 us (0.975)
  waiting for transfers between devices: 62 us -> 57.8 us
  Pallas kernels: 46.1 us -> 42.4 us
    ppermute x28, waiting for transfers between devices: 50.4 us -> 45 us  [shift(): lax.ppermute(value, axis, [(i, (i + by) % size) for i in range(size)])]
    pallas_call x0 -> x1, Pallas kernels: none -> 3.43 us  [far_tiles(): pl.pallas_call(far_tiles_kernel, out_shape=jax.ShapeDtypeStruct((12, W, W...]
    pallas_call x1, Pallas kernels: 4.34 us -> 1.22 us  [mix_far(): pl.pallas_call(mix_far_kernel, out_shape=jax.ShapeDtypeStruct((16, C, CHU...]
    pallas_call x1, Pallas kernels: 3.97 us -> 0.91 us  [push_far(): pl.pallas_call(push_far_kernel, out_shape=[jax.ShapeDtypeStruct((SLOTS, C...]
    unnamed x46 -> x42, local copies, waits for them, and re-layouts: 6 us -> 7.75 us
  transfers between devices with their start and end apart: 34 -> 34, of which waited for: 21 -> 19; matrix products, arithmetic and copies ran while one was open for 6% -> 6% of each run, Pallas kernels for 16% -> 15%
where the time goes in v5:
time: 231 us; the launch traced here: 227 us
  starting transfers between devices  75.8 us (33%)
  waiting for transfers between devices  57.8 us (25%)
  Pallas kernels  42.4 us (18%)
  local copies, waits for them, and re-layouts  16.9 us (7%)
  blocking collectives  15.5 us (7%)
  between operations  14.4 us (6%)
  other arithmetic  4.01 us (2%)
    ppermute x28, starting transfers between devices, shift(): lax.ppermute(value, axis, [(i, (i + by) % size) for i in range(size)])  46.5 us
    ppermute x28, waiting for transfers between devices, shift(): lax.ppermute(value, axis, [(i, (i + by) % size) for i in range(size)])  45 us
    all_to_all x1, blocking collectives, over_col(): return lax.all_to_all(value, COL, 0, 0, tiled=True)  15.5 us
    all_to_all x2, starting transfers between devices, over_col(): return lax.all_to_all(value, COL, 0, 0, tiled=True)  11.5 us
    pallas_call x1, Pallas kernels, mix(): pl.pallas_call(mixed_kernel, grid_spec=pltpu.PrefetchScalarGridSpec(num_s...  9.94 us
    pallas_call x1, Pallas kernels, push(): pl.pallas_call(push_kernel, in_specs=[SMEM, VMEM, ANY], out_specs=[VMEM]...  7.88 us
    unnamed x42, local copies, waits for them, and re-layouts  7.75 us
    all_to_all x1, starting transfers between devices, on_device(): grad = lax.all_to_all(grad.reshape(8, C, F), ('y', 'zl'), 0, 0, tiled=True)  7.07 us
  transfers between devices with their start and end apart: 34, of which 19 were waited for; matrix products, arithmetic and copies ran while one was open for 6% of the time, Pallas kernels for 15%

profile of v5, /device:TPU:10, one launch (start us, length us, event | category | flops | bytes accessed | tf_op | source)
XLA Modules:
  0.0 226.8 jit_solution(5938143068008604293)
XLA Ops:
  8.3 6.4 %collective-permute-start = (f32[8,64,256]{2,1,0:T(8,128)S(1)}, f32[8,64,256]{2,1,0:T(8,128)S(1)}, u32[]{:S(2)}, u32[]{:S(2)}) collective-permute-start(f32[8,64,256]{2,1,0:T(8,128)S(1)} %bitcast.56), channel_id=1, source_target_pairs={{0,48},{16,0},{32,16},{48,32},{1,49},{17,1},{33,17},{49,33},{2,50}... | collective-permute-start | bytes 1572872 | tf_op jit(solution)/shard_map/ppermute | solution.py:356
  17.0 1.6 collective-permute-start.2
  19.7 2.2 collective-permute-start.4
  22.7 5.4 %all-to-all-start = ((f32[16,64,128]{2,1,0:T(8,128)}), f32[16,64,128]{2,1,0:T(8,128)S(1)}, u32[]{:S(2)}, u32[]{:S(2)}) async-start(f32[16,64,128]{2,1,0:T(8,128)} %bitcast_bitcast_fusion.1), calls=%async_computation | async-start | bytes 1048576 | tf_op jit(solution)/shard_map/all_to_all | solution.py:364
  29.0 3.4 %shard_map.77.tiles_ref = bf16[12,256,256]{2,1,0:T(8,128)(2,1)} custom-call(s32[12]{0:T(128)} %reshape.174.refs_ref, bf16[8,8,256,256]{3,2,1,0:T(8,128)(2,1)} %tiles_ref.3), custom_call_target="tpu_custom_call" | custom-call | bytes 3145728 | tf_op jit(solution)/shard_map/pallas_call | solution.py:172
  32.6 4.5 %collective-permute-done.up_ref.refs_2_ = f32[8,64,256]{2,1,0:T(8,128)S(1)} collective-permute-done((f32[8,64,256]{2,1,0:T(8,128)S(1)}, f32[8,64,256]{2,1,0:T(8,128)S(1)}, u32[]{:S(2)}, u32[]{:S(2)}) %collective-permute-start) | collective-permute-done | bytes 524320 | tf_op jit(solution)/shard_map/ppermute | solution.py:356
  37.2 3.8 %collective-permute-done.1.down_ref.refs_3_ = f32[8,64,256]{2,1,0:T(8,128)S(1)} collective-permute-done((f32[8,64,256]{2,1,0:T(8,128)S(1)}, f32[8,64,256]{2,1,0:T(8,128)S(1)}, u32[]{:S(2)}, u32[]{:S(2)}) %collective-permute-start.1) | collective-permute-done | bytes 524320 | tf_op jit(solution)/shard_map/ppermute | solution.py:356
  41.0 2.0 all-to-all-done
  43.8 1.6 shard_map.78
  45.4 1.4 collective-permute-start.7
  46.8 1.5 collective-permute-start.8
  48.4 1.7 collective-permute-start.9
  50.1 3.3 %collective-permute-start.5 = (f32[4,64,256]{2,1,0:T(8,128)}, f32[4,64,256]{2,1,0:T(8,128)S(1)}, u32[]{:S(2)}, u32[]{:S(2)}) collective-permute-start(f32[4,64,256]{2,1,0:T(8,128)} %get-tuple-element.77), channel_id=1, source_target_pairs={{0,48},{16,0},{32,16},{48,32},{1,49},{17,1},{33,17},{49,33},{2,50}... | collective-permute-start | bytes 786440 | tf_op jit(solution)/shard_map/ppermute | solution.py:356
  53.5 10.9 %collective-permute-done.5.refs_0_.lo_ref = f32[4,64,256]{2,1,0:T(8,128)S(1)} collective-permute-done((f32[4,64,256]{2,1,0:T(8,128)}, f32[4,64,256]{2,1,0:T(8,128)S(1)}, u32[]{:S(2)}, u32[]{:S(2)}) %collective-permute-start.5) | collective-permute-done | bytes 262176 | tf_op jit(solution)/shard_map/ppermute | solution.py:356
  64.4 4.2 %collective-permute-done.6.refs_1_.hi_ref = f32[4,64,256]{2,1,0:T(8,128)S(1)} collective-permute-done((f32[4,64,256]{2,1,0:T(8,128)}, f32[4,64,256]{2,1,0:T(8,128)S(1)}, u32[]{:S(2)}, u32[]{:S(2)}) %collective-permute-start.6) | collective-permute-done | bytes 262176 | tf_op jit(solution)/shard_map/ppermute | solution.py:356
  68.6 4.0 %collective-permute-done.9.refs_9_ = f32[8,64,256]{2,1,0:T(8,128)} collective-permute-done((f32[8,64,256]{2,1,0:T(8,128)S(1)}, f32[8,64,256]{2,1,0:T(8,128)}, u32[]{:S(2)}, u32[]{:S(2)}) %collective-permute-start.9) | collective-permute-done | bytes 524320 | tf_op jit(solution)/shard_map/ppermute | solution.py:356
  74.5 1.7 collective-permute-start.11
  76.2 1.6 collective-permute-start.12
  78.3 9.9 %shard_map.79.part_ref = f32[8,64,256]{2,1,0:T(8,128)} custom-call(s32[56]{0:T(128)} %fusion.3.place_ref, f32[8,64,256]{2,1,0:T(8,128)} %bitcast.59, f32[4,64,256]{2,1,0:T(8,128)} %copy-done.7, f32[4,64,256]{2,1,0:T(8,128)} %copy-done.8, f32[8,64,256]{2,1,0:T(8,128)} %copy-done.4, f32[8,64,256]{2,1,0:T(8,128)} %copy-done.5, ...), custom_call_target="tpu_custom_call" | custom-call | flops 1073741824 | bytes 13631488 | tf_op jit(solution)/shard_map/pallas_call | solution.py:140
  90.6 15.5 %all_to_all.30 = f32[16,64,128]{2,1,0:T(8,128)} all-to-all(f32[16,64,128]{2,1,0:T(8,128)S(1)} %shard_map.81), channel_id=1, replica_groups=mesh['x'=4,'zh'=4,'y'=4,'zl'=2,'c'=2] {'y','zl','c'}, dimensions={0} | all-to-all | bytes 1048576 | tf_op jit(solution)/shard_map/all_to_all | solution.py:364
  106.1 6.3 %shard_map.82 = (f32[1024,128]{1,0:T(8,128)}, f32[16,128,128]{2,1,0:T(8,128)}) custom-call(f32[1024,1024]{1,0:T(8,128)} %all-gather.2.cloned.1.call-done.weight_ref, f32[1024,128]{1,0:T(8,128)} %bitcast.61, f32[1024,128]{1,0:T(8,128)} %bitcast.68), custom_call_target="tpu_custom_call" | custom-call | flops 1610612736 | bytes 8388608 | tf_op jit(solution)/shard_map/pallas_call | solution.py:238
  112.4 6.2 %all-to-all-start.2 = ((f32[16,128,128]{2,1,0:T(8,128)}), f32[16,128,128]{2,1,0:T(8,128)S(1)}, u32[]{:S(2)}, u32[]{:S(2)}) async-start(f32[16,128,128]{2,1,0:T(8,128)} %get-tuple-element.95), calls=%async_computation.2 | async-start | bytes 2097152 | tf_op jit(solution)/shard_map/all_to_all | solution.py:364
  122.0 5.4 %shard_map.83 = f32[512,1024]{1,0:T(8,128)} custom-call(s32[1]{0:T(128)} %bitcast.11.core_ref, f32[8,2,64,128]{3,2,1,0:T(8,128)} %bitcast.65, f32[512,128]{1,0:T(8,128)} %copy-done.19, f32[1024,128]{1,0:T(8,128)} %bitcast.63, f32[1024,128]{1,0:T(8,128)} %collective-permute-done.14.far_ref), custom_call_target="tpu_custom_call" | custom-call | flops 805306368 | bytes 4194304 | tf_op jit(solution)/shard_map/pallas_call | solution.py:386
  127.4 5.1 %all-to-all-done.2.back_ref = f32[16,128,128]{2,1,0:T(8,128)S(1)} async-done(((f32[16,128,128]{2,1,0:T(8,128)}), f32[16,128,128]{2,1,0:T(8,128)S(1)}, u32[]{:S(2)}, u32[]{:S(2)}) %all-to-all-start.2) | async-done | bytes 1048608 | tf_op jit(solution)/shard_map/all_to_all | solution.py:364
  132.5 7.1 %all-to-all-start.3 = ((f32[8,64,1024]{2,1,0:T(8,128)}), f32[8,64,1024]{2,1,0:T(8,128)}, u32[]{:S(2)}, u32[]{:S(2)}) async-start(f32[8,64,1024]{2,1,0:T(8,128)} %bitcast.60), calls=%async_computation.3 | async-start | bytes 4194304 | tf_op jit(solution)/shard_map/all_to_all | solution.py:445
  141.7 1.3 collective-permute-start.16
  143.0 2.2 collective-permute-start.17
  146.0 7.9 %shard_map.85 = (f32[8,64,256]{2,1,0:T(8,128)}, f32[4,64,256]{2,1,0:T(8,128)}, f32[4,64,256]{2,1,0:T(8,128)}, f32[8,64,256]{2,1,0:T(8,128)}, f32[8,64,256]{2,1,0...) custom-call(s32[56]{0:T(128)} %fusion.3.place_ref, ...), custom_call_target="tpu_custom_call" | custom-call | flops 1073741824 | bytes 13631488 | tf_op jit(solution)/shard_map/pallas_call | solution.py:295
  154.2 1.4 collective-permute-done.17.c_ref
  155.6 2.5 %collective-permute-start.18 = (f32[8,64,256]{2,1,0:T(8,128)}, f32[8,64,256]{2,1,0:T(8,128)S(1)}, u32[]{:S(2)}, u32[]{:S(2)}) collective-permute-start(f32[8,64,256]{2,1,0:T(8,128)} %get-tuple-element.105), channel_id=1, source_target_pairs={{0,192},{64,0},{128,64},{192,128},{1,193},{65,1},{129,65},{193,129... | collective-permute-start | bytes 1572872 | tf_op jit(solution)/shard_map/ppermute | solution.py:356
  158.5 1.7 collective-permute-start.20
  162.1 1.5 shard_map.86
  163.6 1.6 collective-permute-start.21
  165.2 2.5 %collective-permute-start.22 = (f32[4,64,256]{2,1,0:T(8,128)}, f32[4,64,256]{2,1,0:T(8,128)}, u32[]{:S(2)}, u32[]{:S(2)}) collective-permute-start(f32[4,64,256]{2,1,0:T(8,128)} %get-tuple-element.114), channel_id=1, source_target_pairs={{0,48},{16,0},{32,16},{48,32},{1,49},{17,1},{33,17},{49,33},{2,50}... | collective-permute-start | bytes 786440 | tf_op jit(solution)/shard_map/ppermute | solution.py:356
  167.7 2.4 %reduce_sum.57 = f32[64,1024]{1,0:T(8,128)} reduce(f32[8,64,1024]{2,1,0:T(8,128)} %all-to-all-done.3, f32[]{:T(128)} %constant.33.clone.1), dimensions={0}, to_apply=%region_3.4 | reduce | flops 458752 | bytes 2359300 | tf_op jit(solution)/shard_map/reduce_sum | solution.py:453
  170.2 1.8 reshape.185
  173.1 5.8 %collective-permute-done.22.above_ref = f32[4,64,256]{2,1,0:T(8,128)} collective-permute-done((f32[4,64,256]{2,1,0:T(8,128)}, f32[4,64,256]{2,1,0:T(8,128)}, u32[]{:S(2)}, u32[]{:S(2)}) %collective-permute-start.22) | collective-permute-done | bytes 262176 | tf_op jit(solution)/shard_map/ppermute | solution.py:356
  178.9 2.9 %collective-permute-done.19.b_ref = f32[8,64,256]{2,1,0:T(8,128)S(1)} collective-permute-done((f32[8,64,256]{2,1,0:T(8,128)}, f32[8,64,256]{2,1,0:T(8,128)S(1)}, u32[]{:S(2)}, u32[]{:S(2)}) %collective-permute-start.19) | collective-permute-done | bytes 524320 | tf_op jit(solution)/shard_map/ppermute | solution.py:356
  184.3 2.3 %shard_map.87 = (f32[8,64,256]{2,1,0:T(8,128)}, f32[8,64,256]{2,1,0:T(8,128)}) custom-call(s32[24]{0:T(128)S(1)} %reshape.178.index_ref, f32[8,64,256]{2,1,0:T(8,128)S(1)} %collective-permute-done.18.a_ref, f32[8,64,256]{2,1,0:T(8,128)S(1)} %collective-permute-done.19.b_ref, f32[8,64,256]{2,1,0:T(8,128)S(1)} %copy-done.13, f32[8,64,256]{2,1,0:T(8,128)S(1)} %copy-done.10, ...), custom_call_target="tpu_custom_call" | custom-call | flops 196608 | bytes 3145728 | tf_op jit(solution)/shard_map/pallas_call | solution.py:344
  186.7 1.5 collective-permute-start.26
  188.2 2.6 %collective-permute-start.27 = (f32[8,64,256]{2,1,0:T(8,128)}, f32[8,64,256]{2,1,0:T(8,128)S(1)}, u32[]{:S(2)}, u32[]{:S(2)}) collective-permute-start(f32[8,64,256]{2,1,0:T(8,128)} %get-tuple-element.137), channel_id=1, source_target_pairs={{0,48},{16,0},{32,16},{48,32},{1,49},{17,1},{33,17},{49,33},{2,50}... | collective-permute-start | bytes 1572872 | tf_op jit(solution)/shard_map/ppermute | solution.py:356
  191.5 5.8 %all-to-all-start.4 = ((f32[4,64,256]{2,1,0:T(8,128)}), f32[4,64,256]{2,1,0:T(8,128)S(1)}, u32[]{:S(2)}, u32[]{:S(2)}) async-start(f32[4,64,256]{2,1,0:T(8,128)} %copy.46), calls=%async_computation.4 | async-start | bytes 524288 | tf_op jit(solution)/shard_map/all_to_all | solution.py:460
  197.4 2.8 %collective-permute-start.24 = (f32[4,64,256]{2,1,0:T(8,128)}, f32[4,64,256]{2,1,0:T(8,128)S(1)}, u32[]{:S(2)}, u32[]{:S(2)}) collective-permute-start(f32[4,64,256]{2,1,0:T(8,128)} %get-tuple-element.133), channel_id=1, source_target_pairs={{0,128},{64,192},{128,0},{192,64},{1,129},{65,193},{129,1},{193,65... | collective-permute-start | bytes 786440 | tf_op jit(solution)/shard_map/ppermute | solution.py:356
  200.3 1.8 collective-permute-start.25
  202.0 2.0 all-to-all-done.4
  205.0 4.8 %all-to-all-start.5 = ((f32[4,32,128]{2,1,0:T(8,128)}), f32[4,32,128]{2,1,0:T(8,128)S(1)}, u32[]{:S(2)}, u32[]{:S(2)}) async-start(f32[4,32,128]{2,1,0:T(8,128)} %reshape.188), calls=%async_computation.5 | async-start | bytes 131072 | tf_op jit(solution)/shard_map/all_to_all | solution.py:462
  209.8 3.9 %collective-permute-done.24.b_ref = f32[4,64,256]{2,1,0:T(8,128)S(1)} collective-permute-done((f32[4,64,256]{2,1,0:T(8,128)}, f32[4,64,256]{2,1,0:T(8,128)S(1)}, u32[]{:S(2)}, u32[]{:S(2)}) %collective-permute-start.24) | collective-permute-done | bytes 262176 | tf_op jit(solution)/shard_map/ppermute | solution.py:356
  214.4 3.8 %all-to-all-done.5 = f32[4,32,128]{2,1,0:T(8,128)S(1)} async-done(((f32[4,32,128]{2,1,0:T(8,128)}), f32[4,32,128]{2,1,0:T(8,128)S(1)}, u32[]{:S(2)}, u32[]{:S(2)}) %all-to-all-start.5) | async-done | bytes 65568 | tf_op jit(solution)/shard_map/all_to_all | solution.py:462
  (122 shorter events, 28.8 us)
Async XLA Ops:
  7.2 14.7 %copy-start = (f32[2048,64]{0,1:T(8,128)S(1)}, f32[2048,64]{0,1:T(8,128)}, u32[]{:S(2)}) copy-start(f32[2048,64]{0,1:T(8,128)} %param.9) | copy-start | bytes 1572868
  8.3 24.1 %copy-start.3 = (f32[8,8,8,256]{3,2,0,1:T(8,128)}, f32[8,8,8,256]{3,2,0,1:T(8,128)S(1)}, u32[]{:S(2)}) copy-start(f32[8,8,8,256]{3,2,0,1:T(8,128)S(1)} %copy.57) | copy-start | bytes 1572868
  8.3 28.8 %collective-permute-start = (f32[8,64,256]{2,1,0:T(8,128)S(1)}, f32[8,64,256]{2,1,0:T(8,128)S(1)}, u32[]{:S(2)}, u32[]{:S(2)}) collective-permute-start(f32[8,64,256]{2,1,0:T(8,128)S(1)} %bitcast.56), channel_id=1, source_target_pairs={{0,48},{16,0},{32,16},{48,32},{1,49},{17,1},{33,17},{49,33},{2,50}... | collective-permute-start | bytes 1572872 | tf_op jit(solution)/shard_map/ppermute | solution.py:356
  14.7 26.3 %collective-permute-start.1 = (f32[8,64,256]{2,1,0:T(8,128)S(1)}, f32[8,64,256]{2,1,0:T(8,128)S(1)}, u32[]{:S(2)}, u32[]{:S(2)}) collective-permute-start(f32[8,64,256]{2,1,0:T(8,128)S(1)} %bitcast.57), channel_id=1, source_target_pairs={{0,16},{16,32},{32,48},{48,0},{1,17},{17,33},{33,49},{49,1},{2,18}... | collective-permute-start | bytes 1572872 | tf_op jit(solution)/shard_map/ppermute | solution.py:356
  17.0 15.4 %collective-permute-start.2 = (f32[4,64,256]{2,1,0:T(8,128)S(1)}, f32[4,64,256]{2,1,0:T(8,128)}, u32[]{:S(2)}, u32[]{:S(2)}) collective-permute-start(f32[4,64,256]{2,1,0:T(8,128)S(1)} %get-tuple-element.71), channel_id=1, source_target_pairs={{0,64},{64,128},{128,192},{192,0},{1,65},{65,129},{129,193},{193,1... | collective-permute-start | bytes 786440 | tf_op jit(solution)/shard_map/ppermute | solution.py:356
  18.6 13.9 %collective-permute-start.3 = (f32[4,64,256]{2,1,0:T(8,128)S(1)}, f32[4,64,256]{2,1,0:T(8,128)}, u32[]{:S(2)}, u32[]{:S(2)}) collective-permute-start(f32[4,64,256]{2,1,0:T(8,128)S(1)} %get-tuple-element.72), channel_id=1, source_target_pairs={{0,128},{64,192},{128,0},{192,64},{1,129},{65,193},{129,1},{193,65... | collective-permute-start | bytes 786440 | tf_op jit(solution)/shard_map/ppermute | solution.py:356
  19.7 12.9 %collective-permute-start.4 = (f32[4,64,256]{2,1,0:T(8,128)S(1)}, f32[4,64,256]{2,1,0:T(8,128)}, u32[]{:S(2)}, u32[]{:S(2)}) collective-permute-start(f32[4,64,256]{2,1,0:T(8,128)S(1)} %get-tuple-element.73), channel_id=1, source_target_pairs={{0,192},{64,0},{128,64},{192,128},{1,193},{65,1},{129,65},{193,129... | collective-permute-start | bytes 786440 | tf_op jit(solution)/shard_map/ppermute | solution.py:356
  22.7 20.2 %all-to-all-start = ((f32[16,64,128]{2,1,0:T(8,128)}), f32[16,64,128]{2,1,0:T(8,128)S(1)}, u32[]{:S(2)}, u32[]{:S(2)}) async-start(f32[16,64,128]{2,1,0:T(8,128)} %bitcast_bitcast_fusion.1), calls=%async_computation | async-start | bytes 1048576 | tf_op jit(solution)/shard_map/all_to_all | solution.py:364
  28.1 78.0 %all-gather.2.cloned.1.call-start = ((), (), s32[]{:S(2)}) async-start(), calls=%async_computation.6 | async-start | bytes 4456448 | tf_op jit(solution)/shard_map/all_gather | solution.py:422
  37.2 41.1 %copy-start.4 = (f32[8,64,256]{2,1,0:T(8,128)}, f32[8,64,256]{2,1,0:T(8,128)S(1)}, u32[]{:S(2)}) copy-start(f32[8,64,256]{2,1,0:T(8,128)S(1)} %collective-permute-done.up_ref.refs_2_) | copy-start | bytes 1572868
  41.0 36.8 %copy-start.5 = (f32[8,64,256]{2,1,0:T(8,128)}, f32[8,64,256]{2,1,0:T(8,128)S(1)}, u32[]{:S(2)}) copy-start(f32[8,64,256]{2,1,0:T(8,128)S(1)} %collective-permute-done.1.down_ref.refs_3_) | copy-start | bytes 1572868
  45.4 23.2 %collective-permute-start.7 = (f32[8,64,256]{2,1,0:T(8,128)}, f32[8,64,256]{2,1,0:T(8,128)}, u32[]{:S(2)}, u32[]{:S(2)}) collective-permute-start(f32[8,64,256]{2,1,0:T(8,128)} %get-tuple-element.79), channel_id=1, source_target_pairs={{0,64},{64,128},{128,192},{192,0},{1,65},{65,129},{129,193},{193,1... | collective-permute-start | bytes 1572872 | tf_op jit(solution)/shard_map/ppermute | solution.py:356
  46.8 21.8 %collective-permute-start.8 = (f32[8,64,256]{2,1,0:T(8,128)S(1)}, f32[8,64,256]{2,1,0:T(8,128)}, u32[]{:S(2)}, u32[]{:S(2)}) collective-permute-start(f32[8,64,256]{2,1,0:T(8,128)S(1)} %get-tuple-element.80), channel_id=1, source_target_pairs={{0,128},{64,192},{128,0},{192,64},{1,129},{65,193},{129,1},{193,65... | collective-permute-start | bytes 1572872 | tf_op jit(solution)/shard_map/ppermute | solution.py:356
  48.4 24.2 %collective-permute-start.9 = (f32[8,64,256]{2,1,0:T(8,128)S(1)}, f32[8,64,256]{2,1,0:T(8,128)}, u32[]{:S(2)}, u32[]{:S(2)}) collective-permute-start(f32[8,64,256]{2,1,0:T(8,128)S(1)} %get-tuple-element.81), channel_id=1, source_target_pairs={{0,192},{64,0},{128,64},{192,128},{1,193},{65,1},{129,65},{193,129... | collective-permute-start | bytes 1572872 | tf_op jit(solution)/shard_map/ppermute | solution.py:356
  50.1 14.3 %collective-permute-start.5 = (f32[4,64,256]{2,1,0:T(8,128)}, f32[4,64,256]{2,1,0:T(8,128)S(1)}, u32[]{:S(2)}, u32[]{:S(2)}) collective-permute-start(f32[4,64,256]{2,1,0:T(8,128)} %get-tuple-element.77), channel_id=1, source_target_pairs={{0,48},{16,0},{32,16},{48,32},{1,49},{17,1},{33,17},{49,33},{2,50}... | collective-permute-start | bytes 786440 | tf_op jit(solution)/shard_map/ppermute | solution.py:356
  53.4 15.2 %collective-permute-start.6 = (f32[4,64,256]{2,1,0:T(8,128)}, f32[4,64,256]{2,1,0:T(8,128)S(1)}, u32[]{:S(2)}, u32[]{:S(2)}) collective-permute-start(f32[4,64,256]{2,1,0:T(8,128)} %get-tuple-element.78), channel_id=1, source_target_pairs={{0,16},{16,32},{32,48},{48,0},{1,17},{17,33},{33,49},{49,1},{2,18}... | collective-permute-start | bytes 786440 | tf_op jit(solution)/shard_map/ppermute | solution.py:356
  64.4 13.9 %copy-start.7 = (f32[4,64,256]{2,1,0:T(8,128)}, f32[4,64,256]{2,1,0:T(8,128)S(1)}, u32[]{:S(2)}) copy-start(f32[4,64,256]{2,1,0:T(8,128)S(1)} %collective-permute-done.5.refs_0_.lo_ref) | copy-start | bytes 786436
  68.6 9.7 %copy-start.8 = (f32[4,64,256]{2,1,0:T(8,128)}, f32[4,64,256]{2,1,0:T(8,128)S(1)}, u32[]{:S(2)}) copy-start(f32[4,64,256]{2,1,0:T(8,128)S(1)} %collective-permute-done.6.refs_1_.hi_ref) | copy-start | bytes 786436
  73.3 15.0 %collective-permute-start.10 = (f32[4,64,256]{2,1,0:T(8,128)S(1)}, f32[4,64,256]{2,1,0:T(8,128)S(1)}, u32[]{:S(2)}, u32[]{:S(2)}) collective-permute-start(f32[4,64,256]{2,1,0:T(8,128)S(1)} %get-tuple-element.90), channel_id=1, source_target_pairs={{0,64},{64,128},{128,192},{192,0},{1,65},{65,129},{129,193},{193,1... | collective-permute-start | bytes 786440 | tf_op jit(solution)/shard_map/ppermute | solution.py:356
  74.5 13.8 %collective-permute-start.11 = (f32[4,64,256]{2,1,0:T(8,128)S(1)}, f32[4,64,256]{2,1,0:T(8,128)S(1)}, u32[]{:S(2)}, u32[]{:S(2)}) collective-permute-start(f32[4,64,256]{2,1,0:T(8,128)S(1)} %get-tuple-element.91), channel_id=1, source_target_pairs={{0,128},{64,192},{128,0},{192,64},{1,129},{65,193},{129,1},{193,65... | collective-permute-start | bytes 786440 | tf_op jit(solution)/shard_map/ppermute | solution.py:356
  76.2 12.1 %collective-permute-start.12 = (f32[4,64,256]{2,1,0:T(8,128)S(1)}, f32[4,64,256]{2,1,0:T(8,128)S(1)}, u32[]{:S(2)}, u32[]{:S(2)}) collective-permute-start(f32[4,64,256]{2,1,0:T(8,128)S(1)} %get-tuple-element.92), channel_id=1, source_target_pairs={{0,192},{64,0},{128,64},{192,128},{1,193},{65,1},{129,65},{193,129... | collective-permute-start | bytes 786440 | tf_op jit(solution)/shard_map/ppermute | solution.py:356
  78.3 10.0 %copy-start.1 = (bf16[12,256,256]{2,1,0:T(8,128)(2,1)S(1)}, bf16[12,256,256]{2,1,0:T(8,128)(2,1)}, u32[]{:S(2)}) copy-start(bf16[12,256,256]{2,1,0:T(8,128)(2,1)} %shard_map.77.tiles_ref) | copy-start | bytes 4718596
  78.3 10.0 %copy-start.16 = (s32[12]{0:T(128)S(1)}, s32[12]{0:T(128)}, u32[]{:S(2)}) copy-start(s32[12]{0:T(128)} %reshape.174.refs_ref) | copy-start | bytes 148
  88.3 1.0 copy-start.6
  112.4 20.1 %all-to-all-start.2 = ((f32[16,128,128]{2,1,0:T(8,128)}), f32[16,128,128]{2,1,0:T(8,128)S(1)}, u32[]{:S(2)}, u32[]{:S(2)}) async-start(f32[16,128,128]{2,1,0:T(8,128)} %get-tuple-element.95), calls=%async_computation.2 | async-start | bytes 2097152 | tf_op jit(solution)/shard_map/all_to_all | solution.py:364
  118.6 2.3 collective-permute-start.14
  119.7 1.6 collective-permute-start.13
  132.5 12.7 %copy-start.2 = (f32[16,128,128]{2,1,0:T(8,128)}, f32[16,128,128]{2,1,0:T(8,128)S(1)}, u32[]{:S(2)}) copy-start(f32[16,128,128]{2,1,0:T(8,128)S(1)} %all-to-all-done.2.back_ref) | copy-start | bytes 3145732
  132.5 35.2 %all-to-all-start.3 = ((f32[8,64,1024]{2,1,0:T(8,128)}), f32[8,64,1024]{2,1,0:T(8,128)}, u32[]{:S(2)}, u32[]{:S(2)}) async-start(f32[8,64,1024]{2,1,0:T(8,128)} %bitcast.60), calls=%async_computation.3 | async-start | bytes 4194304 | tf_op jit(solution)/shard_map/all_to_all | solution.py:445
  140.5 13.4 %collective-permute-start.15 = (f32[4,64,256]{2,1,0:T(8,128)S(1)}, f32[4,64,256]{2,1,0:T(8,128)S(1)}, u32[]{:S(2)}, u32[]{:S(2)}) collective-permute-start(f32[4,64,256]{2,1,0:T(8,128)S(1)} %get-tuple-element.98), channel_id=1, source_target_pairs={{0,192},{64,0},{128,64},{192,128},{1,193},{65,1},{129,65},{193,129... | collective-permute-start | bytes 786440 | tf_op jit(solution)/shard_map/ppermute | solution.py:356
  141.7 12.5 %collective-permute-start.16 = (f32[4,64,256]{2,1,0:T(8,128)S(1)}, f32[4,64,256]{2,1,0:T(8,128)S(1)}, u32[]{:S(2)}, u32[]{:S(2)}) collective-permute-start(f32[4,64,256]{2,1,0:T(8,128)S(1)} %get-tuple-element.99), channel_id=1, source_target_pairs={{0,128},{64,192},{128,0},{192,64},{1,129},{65,193},{129,1},{193,65... | collective-permute-start | bytes 786440 | tf_op jit(solution)/shard_map/ppermute | solution.py:356
  143.0 12.6 %collective-permute-start.17 = (f32[4,64,256]{2,1,0:T(8,128)S(1)}, f32[4,64,256]{2,1,0:T(8,128)S(1)}, u32[]{:S(2)}, u32[]{:S(2)}) collective-permute-start(f32[4,64,256]{2,1,0:T(8,128)S(1)} %get-tuple-element.100), channel_id=1, source_target_pairs={{0,64},{64,128},{128,192},{192,0},{1,65},{65,129},{129,193},{193,1... | collective-permute-start | bytes 786440 | tf_op jit(solution)/shard_map/ppermute | solution.py:356
  155.6 23.4 %collective-permute-start.18 = (f32[8,64,256]{2,1,0:T(8,128)}, f32[8,64,256]{2,1,0:T(8,128)S(1)}, u32[]{:S(2)}, u32[]{:S(2)}) collective-permute-start(f32[8,64,256]{2,1,0:T(8,128)} %get-tuple-element.105), channel_id=1, source_target_pairs={{0,192},{64,0},{128,64},{192,128},{1,193},{65,1},{129,65},{193,129... | collective-permute-start | bytes 1572872 | tf_op jit(solution)/shard_map/ppermute | solution.py:356
  158.1 23.7 %collective-permute-start.19 = (f32[8,64,256]{2,1,0:T(8,128)}, f32[8,64,256]{2,1,0:T(8,128)S(1)}, u32[]{:S(2)}, u32[]{:S(2)}) collective-permute-start(f32[8,64,256]{2,1,0:T(8,128)} %get-tuple-element.106), channel_id=1, source_target_pairs={{0,128},{64,192},{128,0},{192,64},{1,129},{65,193},{129,1},{193,65... | collective-permute-start | bytes 1572872 | tf_op jit(solution)/shard_map/ppermute | solution.py:356
  158.5 24.0 %collective-permute-start.20 = (f32[8,64,256]{2,1,0:T(8,128)}, f32[8,64,256]{2,1,0:T(8,128)S(1)}, u32[]{:S(2)}, u32[]{:S(2)}) collective-permute-start(f32[8,64,256]{2,1,0:T(8,128)} %get-tuple-element.107), channel_id=1, source_target_pairs={{0,64},{64,128},{128,192},{192,0},{1,65},{65,129},{129,193},{193,1... | collective-permute-start | bytes 1572872 | tf_op jit(solution)/shard_map/ppermute | solution.py:356
  162.1 21.2 %copy-start.10 = (f32[8,64,256]{2,1,0:T(8,128)S(1)}, f32[8,64,256]{2,1,0:T(8,128)}, u32[]{:S(2)}) copy-start(f32[8,64,256]{2,1,0:T(8,128)} %get-tuple-element.122.up_ref) | copy-start | bytes 1572868
  162.1 21.2 %copy-start.11 = (f32[8,64,256]{2,1,0:T(8,128)S(1)}, f32[8,64,256]{2,1,0:T(8,128)}, u32[]{:S(2)}) copy-start(f32[8,64,256]{2,1,0:T(8,128)} %get-tuple-element.123.down_ref) | copy-start | bytes 1572868
  163.6 9.5 %collective-permute-start.21 = (f32[4,64,256]{2,1,0:T(8,128)}, f32[4,64,256]{2,1,0:T(8,128)S(1)}, u32[]{:S(2)}, u32[]{:S(2)}) collective-permute-start(f32[4,64,256]{2,1,0:T(8,128)} %get-tuple-element.113), channel_id=1, source_target_pairs={{0,16},{16,32},{32,48},{48,0},{1,17},{17,33},{33,49},{49,1},{2,18}... | collective-permute-start | bytes 786440 | tf_op jit(solution)/shard_map/ppermute | solution.py:356
  165.2 13.7 %collective-permute-start.22 = (f32[4,64,256]{2,1,0:T(8,128)}, f32[4,64,256]{2,1,0:T(8,128)}, u32[]{:S(2)}, u32[]{:S(2)}) collective-permute-start(f32[4,64,256]{2,1,0:T(8,128)} %get-tuple-element.114), channel_id=1, source_target_pairs={{0,48},{16,0},{32,16},{48,32},{1,49},{17,1},{33,17},{49,33},{2,50}... | collective-permute-start | bytes 786440 | tf_op jit(solution)/shard_map/ppermute | solution.py:356
  184.3 6.5 %copy-start.17 = (f32[64,4,256]{2,1,0:T(4,128)S(1)}, f32[64,4,256]{2,1,0:T(4,128)}, u32[]{:S(2)}) copy-start(f32[64,4,256]{2,1,0:T(4,128)} %reshape.185) | copy-start | bytes 786436
  184.3 29.4 %copy-start.9 = (f32[8,64,256]{2,1,0:T(8,128)S(1)}, f32[8,64,256]{2,1,0:T(8,128)}, u32[]{:S(2)}) copy-start(f32[8,64,256]{2,1,0:T(8,128)} %get-tuple-element.135.diag_ref) | copy-start | bytes 1572868
  186.7 32.4 %collective-permute-start.26 = (f32[8,64,256]{2,1,0:T(8,128)}, f32[8,64,256]{2,1,0:T(8,128)S(1)}, u32[]{:S(2)}, u32[]{:S(2)}) collective-permute-start(f32[8,64,256]{2,1,0:T(8,128)} %get-tuple-element.136), channel_id=1, source_target_pairs={{0,16},{16,32},{32,48},{48,0},{1,17},{17,33},{33,49},{49,1},{2,18}... | collective-permute-start | bytes 1572872 | tf_op jit(solution)/shard_map/ppermute | solution.py:356
  188.2 30.8 %collective-permute-start.27 = (f32[8,64,256]{2,1,0:T(8,128)}, f32[8,64,256]{2,1,0:T(8,128)S(1)}, u32[]{:S(2)}, u32[]{:S(2)}) collective-permute-start(f32[8,64,256]{2,1,0:T(8,128)} %get-tuple-element.137), channel_id=1, source_target_pairs={{0,48},{16,0},{32,16},{48,32},{1,49},{17,1},{33,17},{49,33},{2,50}... | collective-permute-start | bytes 1572872 | tf_op jit(solution)/shard_map/ppermute | solution.py:356
  191.5 12.5 %all-to-all-start.4 = ((f32[4,64,256]{2,1,0:T(8,128)}), f32[4,64,256]{2,1,0:T(8,128)S(1)}, u32[]{:S(2)}, u32[]{:S(2)}) async-start(f32[4,64,256]{2,1,0:T(8,128)} %copy.46), calls=%async_computation.4 | async-start | bytes 524288 | tf_op jit(solution)/shard_map/all_to_all | solution.py:460
  197.3 12.5 %collective-permute-start.23 = (f32[4,64,256]{2,1,0:T(8,128)}, f32[4,64,256]{2,1,0:T(8,128)S(1)}, u32[]{:S(2)}, u32[]{:S(2)}) collective-permute-start(f32[4,64,256]{2,1,0:T(8,128)} %get-tuple-element.132), channel_id=1, source_target_pairs={{0,192},{64,0},{128,64},{192,128},{1,193},{65,1},{129,65},{193,129... | collective-permute-start | bytes 786440 | tf_op jit(solution)/shard_map/ppermute | solution.py:356
  197.4 16.2 %collective-permute-start.24 = (f32[4,64,256]{2,1,0:T(8,128)}, f32[4,64,256]{2,1,0:T(8,128)S(1)}, u32[]{:S(2)}, u32[]{:S(2)}) collective-permute-start(f32[4,64,256]{2,1,0:T(8,128)} %get-tuple-element.133), channel_id=1, source_target_pairs={{0,128},{64,192},{128,0},{192,64},{1,129},{65,193},{129,1},{193,65... | collective-permute-start | bytes 786440 | tf_op jit(solution)/shard_map/ppermute | solution.py:356
  200.3 13.4 %collective-permute-start.25 = (f32[4,64,256]{2,1,0:T(8,128)}, f32[4,64,256]{2,1,0:T(8,128)S(1)}, u32[]{:S(2)}, u32[]{:S(2)}) collective-permute-start(f32[4,64,256]{2,1,0:T(8,128)} %get-tuple-element.134), channel_id=1, source_target_pairs={{0,64},{64,128},{128,192},{192,0},{1,65},{65,129},{129,193},{193,1... | collective-permute-start | bytes 786440 | tf_op jit(solution)/shard_map/ppermute | solution.py:356
  205.0 13.2 %all-to-all-start.5 = ((f32[4,32,128]{2,1,0:T(8,128)}), f32[4,32,128]{2,1,0:T(8,128)S(1)}, u32[]{:S(2)}, u32[]{:S(2)}) async-start(f32[4,32,128]{2,1,0:T(8,128)} %reshape.188), calls=%async_computation.5 | async-start | bytes 131072 | tf_op jit(solution)/shard_map/all_to_all | solution.py:462
  (6 other events, 5.2 us)
Sparse Core Ops, SparseCore 0:
  43.1 47.2 all-gather.1

commit v6 on v5

--- a/solution.py
+++ b/solution.py
@@ -12,10 +12,12 @@
 COL = ("y", "zl", "c")
 NX, NZ, NY = 4, 4, 4
 BLK, FAN, W, C = 8, 8, 256, 64
+HALF = BLK // 2
 REFS = BLK * (FAN - 1)
 SLOTS = 4
 FAR = 60
 HELD = FAR + 1
+DISTANCES = (2, 1, 3)
 F = 1024
 CHUNK = 128
 f32, bf16 = jnp.float32, jnp.bfloat16
@@ -37,6 +39,7 @@
     rows = neighbours.reshape(NX, NZ, REFS)
     rows = lax.dynamic_index_in_dim(rows, me_z, 1, keepdims=False)
     rows = lax.dynamic_slice_in_dim(jnp.concatenate([rows, rows], axis=0), me_x, NX, 0)
+    rows = jnp.stack([rows[s] for s in (0,) + DISTANCES])
     owner, block = rows >> 3, rows & 7
     ref = jnp.arange(REFS)
     same = (owner[:, :, None] == owner[:, None, :]) & (ref[None, :, None] > ref[None, None, :])
@@ -50,11 +53,12 @@
     local = jnp.where(e == 2, 0, jnp.where(e == 1, 8, 16)) + block[0]
     start = jnp.where(e == 0, 24, jnp.where(e == 2, 60, 36 + (e >> 1) * 4))
     stride = jnp.where((e & 1) == 1, 8, 4)
-    place = jnp.where(s == 0, local, start + (s - 1) * stride + rank[0])
+    turn = jnp.where(s == 3, 2, jnp.where(s == 1, 1, 0))
+    place = jnp.where(s == 0, local, start + turn * stride + rank[0])
     near = table[0].reshape(12)
     mid = jnp.stack([table[1], table[3]], axis=1).reshape(24)
     far = table[2].reshape(12)
-    source = ((me_x - jnp.arange(1, NX)) & 3) * NZ + ((me_z + 2) & 3)
+    source = ((me_x - jnp.array(DISTANCES)) & 3) * NZ + ((me_z + 2) & 3)
     match = (owner[0][None, None, :] == source[:, None, None]) & (
         rank[0][None, None, :] == jnp.arange(SLOTS)[None, :, None]
     )
@@ -67,7 +71,7 @@
     for s in range(3):
         for slot in range(per):
             index = jnp.maximum(index_ref[s * per + slot] - 1, 0)
-            outs[s][slot] = sources[slot // SLOTS][index]
+            outs[s][slot] = sources[slot // SLOTS][:, pl.ds(pl.multiple_of(index * W, W), W)]
 
 
 def pick_near_kernel(index_ref, own_ref, *outs):
@@ -75,22 +79,22 @@
 
 
 def pick_mid_kernel(index_ref, up_ref, down_ref, lo_ref, hi_ref, *outs):
-    lo_ref[...] = up_ref[: BLK // 2]
-    hi_ref[...] = down_ref[BLK // 2 :]
+    lo_ref[...] = up_ref[:, : HALF * W]
+    hi_ref[...] = down_ref[:, HALF * W :]
     pick_slots(index_ref, (up_ref, down_ref), outs)
 
 
 def pick_far_kernel(index_ref, lo_ref, hi_ref, *refs):
     outs, held = refs[:3], refs[3]
-    held[: BLK // 2] = lo_ref[...]
-    held[BLK // 2 :] = hi_ref[...]
+    held[:, : HALF * W] = lo_ref[...]
+    held[:, HALF * W :] = hi_ref[...]
     pick_slots(index_ref, (held,), outs)
 
 
 def pick(kernel, shapes, scratch, index, *sources):
     return pl.pallas_call(
         kernel,
-        out_shape=[jax.ShapeDtypeStruct((n, C, W), f32) for n in shapes],
+        out_shape=[jax.ShapeDtypeStruct(shape, f32) for shape in shapes],
         in_specs=[SMEM] + [VMEM] * len(sources),
         out_specs=[VMEM] * len(shapes),
         scratch_shapes=scratch,
@@ -113,9 +117,15 @@
 
     @pl.when(i == 0)
     def _():
-        copies = [
-            pltpu.make_async_copy(ref, held.at[rows], sems.at[n]) for n, (rows, ref) in enumerate(places(sources))
-        ]
+        copies, block = [], 0
+        for ref in sources:
+            if len(ref.shape) == 3:
+                copies.append(pltpu.make_async_copy(ref, held.at[pl.ds(block, ref.shape[0])], sems.at[len(copies)]))
+                block += ref.shape[0]
+                continue
+            for start in range(0, ref.shape[1], W):
+                copies.append(pltpu.make_async_copy(ref.at[:, pl.ds(start, W)], held.at[block], sems.at[len(copies)]))
+                block += 1
         for copy in copies:
             copy.start()
         held[FAR] = jnp.zeros((C, W), f32)
@@ -125,7 +135,7 @@
     for j in range(2):
         acc = None
         for k in range(FAN):
-            block = own_ref[j] if k == 0 else held[place_ref[(2 * i + j) * (FAN - 1) + k - 1]]
+            block = own_ref[:, j * W : (j + 1) * W] if k == 0 else held[place_ref[(2 * i + j) * (FAN - 1) + k - 1]]
             part = lax.dot_general(
                 jnp.concatenate(split(block), axis=0),
                 tiles_ref[j, k],
@@ -142,11 +152,11 @@
         grid_spec=pltpu.PrefetchScalarGridSpec(
             num_scalar_prefetch=1,
             grid=(BLK // 2,),
-            in_specs=[pl.BlockSpec((2, C, W), lambda i, s: (i, 0, 0))]
+            in_specs=[pl.BlockSpec((C, 2 * W), lambda i, s: (0, i))]
             + [ANY] * len(sources)
             + [pl.BlockSpec((2, FAN, W, W), lambda i, s: (i, 0, 0, 0))],
             out_specs=pl.BlockSpec((2, C, W), lambda i, s: (i, 0, 0)),
-            scratch_shapes=[pltpu.VMEM((HELD, C, W), f32), pltpu.SemaphoreType.DMA((len(sources),))],
+            scratch_shapes=[pltpu.VMEM((HELD, C, W), f32), pltpu.SemaphoreType.DMA((30,))],
         ),
         out_shape=jax.ShapeDtypeStruct((BLK, C, W), f32),
         compiler_params=PARAMS,
@@ -204,7 +214,7 @@
     )(far_refs, part, *far, tiles)
 
 
-def dense_kernel(weight_ref, mixed_ref, cot_ref, slope_ref, out_ref, held, sems):
+def dense_kernel(weight_ref, mixed_ref, cot_ref, rows_ref, back_ref, held, sems):
     step = F // 2
     copies = []
     for j in range(F // step):
@@ -223,15 +233,15 @@
         low = jnp.dot(wlo, mhi, preferred_element_type=f32)
         pre = both[:, :CHUNK] + (both[:, CHUNK:] + low)
         sig = jax.nn.sigmoid(pre)
-        out_ref[pl.ds(j * step // C, step // C), C:] = (pre * sig).reshape(step // C, C, CHUNK)
+        rows_ref[rows, CHUNK:] = pre * sig
         slope = cot_ref[rows] * sig * (1.0 + pre * (1.0 - sig))
-        slope_ref[rows] = slope
+        rows_ref[rows, :CHUNK] = slope
         shi, slo = split(slope.T)
         both = jnp.dot(jnp.concatenate([shi, slo], axis=0), whi, preferred_element_type=f32)
         low = jnp.dot(shi, wlo, preferred_element_type=f32)
         part = both[:CHUNK] + (both[CHUNK:] + low)
         back = part if back is None else back + part
-    out_ref[:, :C] = back.T.reshape(16, C, CHUNK)
+    back_ref[...] = back.T.reshape(16, C, CHUNK)
 
 
 def dense(weight_t, mixed, cot):
@@ -239,7 +249,7 @@
         dense_kernel,
         in_specs=[ANY, VMEM, VMEM],
         out_specs=[VMEM, VMEM],
-        out_shape=[jax.ShapeDtypeStruct((F, CHUNK), f32), jax.ShapeDtypeStruct((16, 2 * C, CHUNK), f32)],
+        out_shape=[jax.ShapeDtypeStruct((F, 2 * CHUNK), f32), jax.ShapeDtypeStruct((16, C, CHUNK), f32)],
         scratch_shapes=[pltpu.VMEM((F, F), f32), pltpu.SemaphoreType.DMA((2,))],
         compiler_params=PARAMS,
         cost_estimate=pl.CostEstimate(flops=12 * F * F * CHUNK, bytes_accessed=8 << 20, transcendentals=F * CHUNK),
@@ -249,7 +259,7 @@
 def push_far_kernel(refs_ref, back_ref, tiles_ref, a_ref, b_ref, c_ref):
     for slot in range(12):
         i = jnp.maximum(refs_ref[slot] - 1, 0) // (FAN - 1)
-        block = jnp.concatenate([back_ref[2 * i, :C], back_ref[2 * i + 1, :C]], axis=1)
+        block = jnp.concatenate([back_ref[2 * i], back_ref[2 * i + 1]], axis=1)
         both = jnp.concatenate(split(block), axis=0)
         part = jnp.dot(both, tiles_ref[slot], preferred_element_type=f32)
         (a_ref, b_ref, c_ref)[slot // SLOTS][slot % SLOTS] = part[:C] + part[C:]
@@ -273,7 +283,7 @@
         copy.start()
     held[...] = jnp.zeros_like(held)
     for i in range(BLK):
-        block = jnp.concatenate([back_ref[2 * i, :C], back_ref[2 * i + 1, :C]], axis=1)
+        block = jnp.concatenate([back_ref[2 * i], back_ref[2 * i + 1]], axis=1)
         both = jnp.concatenate(split(block), axis=0)
         tile_copies[i].wait()
         for k in range(FAN):
@@ -357,14 +367,14 @@
 
 
 def over_x(pieces, sign):
-    return [shift(piece, "x", NX, sign * (s + 1)) for s, piece in enumerate(pieces)]
+    return [shift(piece, "x", NX, sign * s) for s, piece in zip(DISTANCES, pieces)]
 
 
 def over_col(value):
     return lax.all_to_all(value, COL, 0, 0, tiled=True)
 
 
-def grad_kernel(core_ref, slope_ref, other_ref, mixed_ref, far_ref, out_ref, wide):
+def grad_kernel(core_ref, mine_ref, other_ref, mixed_ref, far_ref, out_ref, wide):
     @pl.when(pl.program_id(0) == 0)
     def _():
         for n, ref in enumerate((mixed_ref, far_ref)):
@@ -373,15 +383,21 @@
                 start = (2 * m + n) * CHUNK
                 wide[:, start : start + CHUNK] = value
 
-    rows = out_ref.shape[0]
-    mine, other = split(slope_ref[...].reshape(rows, CHUNK)), split(other_ref[...])
-    left = jnp.concatenate([mine[0], other[0], mine[0], other[0], mine[1], other[1]], axis=1)
-    out_ref[...] = lax.dot_general(left, wide[...], (((1,), (1,)), ((), ())), preferred_element_type=f32)
-
-
-def grad_part(core, slope, other, mixed, mixed_other):
+    parts = out_ref.shape[0]
+    mine = mine_ref[...].reshape(parts * C, 2 * CHUNK)
+    other = other_ref[...]
+    (ahi, alo), (bhi, blo) = split(mine[:, :CHUNK]), split(other[:, :CHUNK])
+    left = jnp.concatenate([ahi, bhi, ahi, bhi, alo, blo], axis=1)
+    value = lax.dot_general(left, wide[...], (((1,), (1,)), ((), ())), preferred_element_type=f32)
+    out_ref[:, :, :F] = value.reshape(parts, C, F)
+    low = core_ref[0] == 0
+    mine, other = mine[:, CHUNK:], other[:, CHUNK:]
+    out_ref[:, :, F : F + CHUNK] = jnp.where(low, mine, other).reshape(parts, C, CHUNK)
+    out_ref[:, :, F + CHUNK :] = jnp.where(low, other, mine).reshape(parts, C, CHUNK)
+
+
+def grad_part(core, mine, other, mixed, mixed_other):
     steps = 4
-    rows = 8 * C // steps
     whole = pl.BlockSpec((F, CHUNK), lambda i, s: (0, 0))
     return pl.pallas_call(
         grad_kernel,
@@ -389,18 +405,18 @@
             num_scalar_prefetch=1,
             grid=(steps,),
             in_specs=[
-                pl.BlockSpec((8 // steps, 1, C, CHUNK), lambda i, s: (i, s[0], 0, 0)),
-                pl.BlockSpec((rows, CHUNK), lambda i, s: (i, 0)),
+                pl.BlockSpec((8 // steps, 1, C, 2 * CHUNK), lambda i, s: (i, s[0], 0, 0)),
+                pl.BlockSpec((8 * C // steps, 2 * CHUNK), lambda i, s: (i, 0)),
                 whole,
                 whole,
             ],
-            out_specs=pl.BlockSpec((rows, F), lambda i, s: (i, 0)),
+            out_specs=pl.BlockSpec((8 // steps, C, F + 2 * CHUNK), lambda i, s: (i, 0, 0)),
             scratch_shapes=[pltpu.VMEM((F, 6 * CHUNK), bf16)],
         ),
-        out_shape=jax.ShapeDtypeStruct((8 * C, F), f32),
+        out_shape=jax.ShapeDtypeStruct((8, C, F + 2 * CHUNK), f32),
         compiler_params=PARAMS,
         cost_estimate=pl.CostEstimate(flops=6 * F * F * CHUNK, bytes_accessed=4 << 20, transcendentals=0),
-    )(core.reshape(1).astype(jnp.int32), slope.reshape(8, 2, C, CHUNK), other, mixed, mixed_other)
+    )(core.reshape(1).astype(jnp.int32), mine, other, mixed, mixed_other)
 
 
 def after(values, others):
@@ -410,47 +426,48 @@
 
 def on_device(features, neighbours, tiles, weight, cotangent):
     near_at, mid_at, far_at, far_refs, place = tables(neighbours)
-    own = features.T.reshape(C, BLK, W).transpose(1, 0, 2)
+    own = features.T
     me_c = lax.axis_index("c")
 
     up = shift(own, "zh", NZ, -1)
     down = shift(own, "zh", NZ, 1)
-    near = over_x(pick(pick_near_kernel, (4,) * 3, [], near_at, own), 1)
+    near = over_x(pick(pick_near_kernel, ((4, C, W),) * 3, [], near_at, own), 1)
     cot = over_col(cotangent.T.reshape(C, 16, CHUNK).transpose(1, 0, 2)).reshape(F, CHUNK)
     some = far_tiles(far_refs, tiles)
     (up, down), (near, cot, weight_t, some) = after((up, down), (near, cot, weight.T, some))
     weight_t = lax.all_gather(weight_t, COL, axis=0, tiled=True)
-    lo, hi, *mid = pick(pick_mid_kernel, (4, 4) + (8,) * 3, [], mid_at, up, down)
+    lo, hi, *mid = pick(pick_mid_kernel, ((C, HALF * W),) * 2 + ((8, C, W),) * 3, [], mid_at, up, down)
     lo = shift(lo, "zh", NZ, -1)
     hi = shift(hi, "zh", NZ, 1)
     mid = over_x(mid, 1)
     lo, hi, mid = lax.optimization_barrier((lo, hi, mid))
-    far = pick(pick_far_kernel, (4,) * 3, [pltpu.VMEM((BLK, C, W), f32)], far_at, lo, hi)
+    far = pick(pick_far_kernel, ((4, C, W),) * 3, [pltpu.VMEM((C, BLK * W), f32)], far_at, lo, hi)
     far = over_x(far, 1)
     part = mix(place, own, [lo, hi, up, down, *near, *mid], tiles)
     mixed = mix_far(far_refs, part, far, some)
 
     mixed = over_col(mixed).reshape(F, CHUNK)
-    slope, back = dense(weight_t, mixed, cot)
+    rows, back = dense(weight_t, mixed, cot)
     back = over_col(back)
-    hidden = back[:, C:].transpose(1, 0, 2).reshape(C, 16 * CHUNK).T
-
-    other = lax.dynamic_index_in_dim(slope.reshape(8, 2, C, CHUNK), 1 - me_c, 1, keepdims=False)
-    other = shift(other.reshape(8 * C, CHUNK), "c", 2, 1)
-    grad = grad_part(me_c, slope, other, mixed, shift(mixed, "c", 2, 1))
+
+    rows = rows.reshape(8, 2, C, 2 * CHUNK)
+    other = lax.dynamic_index_in_dim(rows, 1 - me_c, 1, keepdims=False)
+    other = shift(other.reshape(8 * C, 2 * CHUNK), "c", 2, 1)
+    grad = grad_part(me_c, rows, other, mixed, shift(mixed, "c", 2, 1))
     back, grad = after(back, grad)
 
     far = push_far(far_refs, back, some)
     far = over_x(far, -1)
-    grad = lax.all_to_all(grad.reshape(8, C, F), ("y", "zl"), 0, 0, tiled=True)
+    grad = lax.all_to_all(grad, ("y", "zl"), 0, 0, tiled=True)
     diag, lo, hi, up, down, *pieces = push(place, back, tiles)
     near, mid = pieces[:3], pieces[3:]
-    far, (mid, hidden) = after(far, (mid, hidden))
+    far, mid = after(far, mid)
     mid = over_x(mid, -1)
     lo, hi = gather_sum(far_kernel, (4, 4), [pltpu.VMEM((BLK, C, W), f32)], far_at, *far, lo, hi)
     lo = shift(lo, "zh", NZ, 1)
     hi = shift(hi, "zh", NZ, -1)
-    grad = grad.sum(axis=0).reshape(C, NX, W).transpose(1, 0, 2)
+    hidden = grad[:, :, F:].transpose(1, 0, 2).reshape(C, 16 * CHUNK).T
+    grad = grad[:, :, :F].sum(axis=0).reshape(C, NX, W).transpose(1, 0, 2)
     (mid, lo, hi), (near, grad) = after((mid, lo, hi), (near, grad))
     up, down = gather_sum(mid_kernel, (8, 8), [], mid_at, *mid, up, down, lo, hi)
     (up, down), (near, grad) = after((up, down), (near, grad))

time: 231 us -> 222 us (0.961); the launches traced: 227 us -> 221 us
  starting transfers between devices: 75.8 us -> 69.5 us
    ppermute x28, waiting for transfers between devices: 45 us -> 34.6 us  [shift(): lax.ppermute(value, axis, [(i, (i + by) % size) for i in range(size)])]
    all_to_all x1, waiting for transfers between devices: 0.01 us -> 10.1 us  [on_device(): grad = lax.all_to_all(grad, ('y', 'zl'), 0, 0, tiled=True)]
    all_to_all x2, waiting for transfers between devices: 7.06 us -> 2.12 us  [over_col(): return lax.all_to_all(value, COL, 0, 0, tiled=True)]
    all_to_all x1, waiting for transfers between devices: 1.99 us -> 6.35 us  [on_device(): grad = lax.all_to_all(grad, 'x', 0, 0, tiled=True).sum(axis=0)]
    ppermute x28, starting transfers between devices: 46.5 us -> 43.1 us  [shift(): lax.ppermute(value, axis, [(i, (i + by) % size) for i in range(size)])]
    unnamed x42 -> x49, local copies, waits for them, and re-layouts: 7.75 us -> 8.14 us
  transfers between devices with their start and end apart: 34 -> 34, of which waited for: 19 -> 18; matrix products, arithmetic and copies ran while one was open for 6% -> 6% of each run, Pallas kernels for 15% -> 15%
where the time goes in v6:
time: 222 us; the launch traced here: 221 us
  starting transfers between devices  69.5 us (31%)
  waiting for transfers between devices  58.9 us (27%)
  Pallas kernels  42.5 us (19%)
  local copies, waits for them, and re-layouts  16.3 us (7%)
  blocking collectives  15.2 us (7%)
  between operations  14.5 us (7%)
  other arithmetic  3.97 us (2%)
    ppermute x28, starting transfers between devices, shift(): lax.ppermute(value, axis, [(i, (i + by) % size) for i in range(size)])  43.1 us
    ppermute x28, waiting for transfers between devices, shift(): lax.ppermute(value, axis, [(i, (i + by) % size) for i in range(size)])  34.6 us
    all_to_all x1, blocking collectives, over_col(): return lax.all_to_all(value, COL, 0, 0, tiled=True)  15.2 us
    all_to_all x2, starting transfers between devices, over_col(): return lax.all_to_all(value, COL, 0, 0, tiled=True)  11.5 us
    all_to_all x1, waiting for transfers between devices, on_device(): grad = lax.all_to_all(grad, ('y', 'zl'), 0, 0, tiled=True)  10.1 us
    pallas_call x1, Pallas kernels, mix(): pl.pallas_call(mixed_kernel, grid_spec=pltpu.PrefetchScalarGridSpec(num_s...  10.1 us
    unnamed x49, local copies, waits for them, and re-layouts  8.14 us
    pallas_call x1, Pallas kernels, push(): pl.pallas_call(push_kernel, in_specs=[SMEM, VMEM, ANY], out_specs=[VMEM]...  7.77 us
  transfers between devices with their start and end apart: 34, of which 18 were waited for; matrix products, arithmetic and copies ran while one was open for 6% of the time, Pallas kernels for 15%

profile of v6, /device:TPU:10, one launch (start us, length us, event | category | flops | bytes accessed | tf_op | source)
XLA Modules:
  0.0 220.8 jit_solution(14802372059969874045)
XLA Ops:
  7.2 6.4 %collective-permute-start = (f32[64,2048]{1,0:T(8,128)}, f32[64,2048]{1,0:T(8,128)S(1)}, u32[]{:S(2)}, u32[]{:S(2)}) collective-permute-start(f32[64,2048]{1,0:T(8,128)} %bitcast.46), channel_id=1, source_target_pairs={{0,48},{16,0},{32,16},{48,32},{1,49},{17,1},{33,17},{49,33},{2,50}... | collective-permute-start | bytes 1572872 | tf_op jit(solution)/shard_map/ppermute | solution.py:366
  17.0 2.2 %collective-permute-start.2 = (f32[4,64,256]{2,1,0:T(8,128)S(1)}, f32[4,64,256]{2,1,0:T(8,128)S(1)}, u32[]{:S(2)}, u32[]{:S(2)}) collective-permute-start(f32[4,64,256]{2,1,0:T(8,128)S(1)} %get-tuple-element.70), channel_id=1, source_target_pairs={{0,128},{64,192},{128,0},{192,64},{1,129},{65,193},{129,1},{193,65... | collective-permute-start | bytes 786440 | tf_op jit(solution)/shard_map/ppermute | solution.py:366
  19.2 2.0 collective-permute-start.4
  22.0 5.4 %all-to-all-start = ((f32[16,64,128]{2,1,0:T(8,128)}), f32[16,64,128]{2,1,0:T(8,128)S(1)}, u32[]{:S(2)}, u32[]{:S(2)}) async-start(f32[16,64,128]{2,1,0:T(8,128)} %bitcast_bitcast_fusion), calls=%async_computation | async-start | bytes 1048576 | tf_op jit(solution)/shard_map/all_to_all | solution.py:374
  28.4 3.4 %shard_map.86.tiles_ref = bf16[12,256,256]{2,1,0:T(8,128)(2,1)} custom-call(s32[12]{0:T(128)} %reshape.216.refs_ref, bf16[8,8,256,256]{3,2,1,0:T(8,128)(2,1)} %tiles_ref.3), custom_call_target="tpu_custom_call" | custom-call | bytes 3145728 | tf_op jit(solution)/shard_map/pallas_call | solution.py:182
  32.0 4.3 %collective-permute-done.up_ref.refs_2_ = f32[64,2048]{1,0:T(8,128)S(1)} collective-permute-done((f32[64,2048]{1,0:T(8,128)}, f32[64,2048]{1,0:T(8,128)S(1)}, u32[]{:S(2)}, u32[]{:S(2)}) %collective-permute-start) | collective-permute-done | bytes 524320 | tf_op jit(solution)/shard_map/ppermute | solution.py:366
  36.3 3.7 %collective-permute-done.1.down_ref.refs_3_ = f32[64,2048]{1,0:T(8,128)S(1)} collective-permute-done((f32[64,2048]{1,0:T(8,128)}, f32[64,2048]{1,0:T(8,128)S(1)}, u32[]{:S(2)}, u32[]{:S(2)}) %collective-permute-start.1) | collective-permute-done | bytes 524320 | tf_op jit(solution)/shard_map/ppermute | solution.py:366
  40.1 2.1 all-to-all-done
  43.1 1.6 shard_map.87
  44.6 1.9 collective-permute-start.7
  46.6 1.8 collective-permute-start.8
  48.6 3.2 %collective-permute-start.5 = (f32[64,1024]{1,0:T(8,128)}, f32[64,1024]{1,0:T(8,128)S(1)}, u32[]{:S(2)}, u32[]{:S(2)}) collective-permute-start(f32[64,1024]{1,0:T(8,128)} %get-tuple-element.76), channel_id=1, source_target_pairs={{0,48},{16,0},{32,16},{48,32},{1,49},{17,1},{33,17},{49,33},{2,50}... | collective-permute-start | bytes 786440 | tf_op jit(solution)/shard_map/ppermute | solution.py:366
  51.9 10.8 %collective-permute-done.5.refs_0_.lo_ref = f32[64,1024]{1,0:T(8,128)S(1)} collective-permute-done((f32[64,1024]{1,0:T(8,128)}, f32[64,1024]{1,0:T(8,128)S(1)}, u32[]{:S(2)}, u32[]{:S(2)}) %collective-permute-start.5) | collective-permute-done | bytes 262176 | tf_op jit(solution)/shard_map/ppermute | solution.py:366
  62.7 4.0 %collective-permute-done.6.refs_1_.hi_ref = f32[64,1024]{1,0:T(8,128)S(1)} collective-permute-done((f32[64,1024]{1,0:T(8,128)S(1)}, f32[64,1024]{1,0:T(8,128)S(1)}, u32[]{:S(2)}, u32[]{:S(2)}) %collective-permute-start.6) | collective-permute-done | bytes 262176 | tf_op jit(solution)/shard_map/ppermute | solution.py:366
  66.7 4.5 %collective-permute-done.8.refs_8_ = f32[8,64,256]{2,1,0:T(8,128)} collective-permute-done((f32[8,64,256]{2,1,0:T(8,128)S(1)}, f32[8,64,256]{2,1,0:T(8,128)}, u32[]{:S(2)}, u32[]{:S(2)}) %collective-permute-start.8) | collective-permute-done | bytes 524320 | tf_op jit(solution)/shard_map/ppermute | solution.py:366
  72.1 2.0 collective-permute-start.10
  74.1 1.5 collective-permute-start.11
  76.6 10.1 %shard_map.88.part_ref = f32[8,64,256]{2,1,0:T(8,128)} custom-call(s32[56]{0:T(128)} %fusion.5.place_ref, f32[64,2048]{1,0:T(8,128)} %bitcast.48, f32[64,1024]{1,0:T(8,128)} %copy-done.7, f32[64,1024]{1,0:T(8,128)} %copy-done.8, f32[64,2048]{1,0:T(8,128)} %copy-done.4, f32[64,2048]{1,0:T(8,128)} %copy-done.5, f32[4,64,256]{2,1,0:T(8,128)} %copy-done.20, ...), custom_call_target="tpu_custom_call" | custom-call | flops 1073741824 | bytes 13631488 | tf_op jit(solution)/shard_map/pallas_call | solution.py:150
  88.6 1.2 shard_map.90
  89.8 15.2 %all_to_all.30 = f32[16,64,128]{2,1,0:T(8,128)} all-to-all(f32[16,64,128]{2,1,0:T(8,128)S(1)} %shard_map.90), channel_id=1, replica_groups=mesh['x'=4,'zh'=4,'y'=4,'zl'=2,'c'=2] {'y','zl','c'}, dimensions={0} | all-to-all | bytes 1048576 | tf_op jit(solution)/shard_map/all_to_all | solution.py:374
  105.0 6.1 %shard_map.91 = (f32[1024,256]{1,0:T(8,128)}, f32[16,64,128]{2,1,0:T(8,128)}) custom-call(f32[1024,1024]{1,0:T(8,128)} %all-gather.2.cloned.1.call-done.weight_ref, f32[1024,128]{1,0:T(8,128)} %bitcast.52, f32[1024,128]{1,0:T(8,128)} %bitcast.56), custom_call_target="tpu_custom_call" | custom-call | flops 1610612736 | bytes 8388608 | tf_op jit(solution)/shard_map/pallas_call | solution.py:248
  111.1 6.1 %all-to-all-start.2 = ((f32[16,64,128]{2,1,0:T(8,128)}), f32[16,64,128]{2,1,0:T(8,128)S(1)}, u32[]{:S(2)}, u32[]{:S(2)}) async-start(f32[16,64,128]{2,1,0:T(8,128)} %get-tuple-element.94), calls=%async_computation.2 | async-start | bytes 1048576 | tf_op jit(solution)/shard_map/all_to_all | solution.py:374
  117.5 1.1 constant_dynamic-slice_fusion
  119.2 1.3 collective-permute-done.13.other_ref
  121.3 5.7 %shard_map.92 = f32[8,64,1280]{2,1,0:T(8,128)} custom-call(s32[1]{0:T(128)} %bitcast.10.core_ref, f32[8,2,64,256]{3,2,1,0:T(8,128)} %bitcast.51, f32[512,256]{1,0:T(8,128)} %copy-done.19, f32[1024,128]{1,0:T(8,128)} %bitcast.53, f32[1024,128]{1,0:T(8,128)} %copy-done.18), custom_call_target="tpu_custom_call" | custom-call | flops 805306368 | bytes 4194304 | tf_op jit(solution)/shard_map/pallas_call | solution.py:402
  127.0 5.8 %all-to-all-start.3 = ((f32[8,64,1280]{2,1,0:T(8,128)}), f32[8,64,1280]{2,1,0:T(8,128)}, u32[]{:S(2)}, u32[]{:S(2)}) async-start(f32[8,64,1280]{2,1,0:T(8,128)} %shard_map.92), calls=%async_computation.3 | async-start | bytes 5242880 | tf_op jit(solution)/shard_map/all_to_all | solution.py:461
  133.7 2.2 %collective-permute-start.15 = (f32[4,64,256]{2,1,0:T(8,128)S(1)}, f32[4,64,256]{2,1,0:T(8,128)S(1)}, u32[]{:S(2)}, u32[]{:S(2)}) collective-permute-start(f32[4,64,256]{2,1,0:T(8,128)S(1)} %get-tuple-element.98), channel_id=1, source_target_pairs={{0,128},{64,192},{128,0},{192,64},{1,129},{65,193},{129,1},{193,65... | collective-permute-start | bytes 786440 | tf_op jit(solution)/shard_map/ppermute | solution.py:366
  136.0 1.5 collective-permute-start.16
  138.0 7.8 %shard_map.94 = (f32[8,64,256]{2,1,0:T(8,128)}, f32[4,64,256]{2,1,0:T(8,128)}, f32[4,64,256]{2,1,0:T(8,128)}, f32[8,64,256]{2,1,0:T(8,128)}, f32[8,64,256]{2,1,0...) custom-call(s32[56]{0:T(128)} %fusion.5.place_ref, ...), custom_call_target="tpu_custom_call" | custom-call | flops 1073741824 | bytes 13631488 | tf_op jit(solution)/shard_map/pallas_call | solution.py:305
  145.8 3.1 %collective-permute-done.16.b_ref = f32[4,64,256]{2,1,0:T(8,128)S(1)} collective-permute-done((f32[4,64,256]{2,1,0:T(8,128)S(1)}, f32[4,64,256]{2,1,0:T(8,128)S(1)}, u32[]{:S(2)}, u32[]{:S(2)}) %collective-permute-start.16) | collective-permute-done | bytes 262176 | tf_op jit(solution)/shard_map/ppermute | solution.py:366
  149.1 2.0 collective-permute-start.18
  151.1 1.5 collective-permute-start.19
  155.0 1.5 shard_map.95
  156.5 1.5 collective-permute-start.21
  158.0 2.7 %collective-permute-start.22 = (f32[4,64,256]{2,1,0:T(8,128)}, f32[4,64,256]{2,1,0:T(8,128)}, u32[]{:S(2)}, u32[]{:S(2)}) collective-permute-start(f32[4,64,256]{2,1,0:T(8,128)} %get-tuple-element.113), channel_id=1, source_target_pairs={{0,48},{16,0},{32,16},{48,32},{1,49},{17,1},{33,17},{49,33},{2,50}... | collective-permute-start | bytes 786440 | tf_op jit(solution)/shard_map/ppermute | solution.py:366
  160.6 10.1 %all-to-all-done.3 = f32[8,64,1280]{2,1,0:T(8,128)} async-done(((f32[8,64,1280]{2,1,0:T(8,128)}), f32[8,64,1280]{2,1,0:T(8,128)}, u32[]{:S(2)}, u32[]{:S(2)}) %all-to-all-start.3) | async-done | bytes 2621472 | tf_op jit(solution)/shard_map/all_to_all | solution.py:461
  170.7 2.4 %slice_reduce_fusion = f32[64,1024]{1,0:T(8,128)} fusion(f32[8,64,1280]{2,1,0:T(8,128)} %all-to-all-done.3), kind=kLoop, calls=%fused_computation | loop fusion | flops 458752 | bytes 2359296 | tf_op jit(solution)/shard_map/reduce_sum | solution.py:470
  173.2 1.8 reshape.223
  174.9 1.2 collective-permute-done.21.below_ref
  176.2 2.2 %shard_map.96 = (f32[8,64,256]{2,1,0:T(8,128)}, f32[8,64,256]{2,1,0:T(8,128)}) custom-call(s32[24]{0:T(128)S(1)} %reshape.217.index_ref, f32[8,64,256]{2,1,0:T(8,128)S(1)} %collective-permute-done.18.a_ref, f32[8,64,256]{2,1,0:T(8,128)S(1)} %collective-permute-done.19.b_ref, f32[8,64,256]{2,1,0:T(8,128)S(1)} %collective-permute-done.20.c_ref, ...), custom_call_target="tpu_custom_call" | custom-call | flops 196608 | bytes 3145728 | tf_op jit(solution)/shard_map/pallas_call | solution.py:354
  179.5 3.1 %collective-permute-start.27 = (f32[8,64,256]{2,1,0:T(8,128)}, f32[8,64,256]{2,1,0:T(8,128)S(1)}, u32[]{:S(2)}, u32[]{:S(2)}) collective-permute-start(f32[8,64,256]{2,1,0:T(8,128)} %get-tuple-element.135), channel_id=1, source_target_pairs={{0,48},{16,0},{32,16},{48,32},{1,49},{17,1},{33,17},{49,33},{2,50}... | collective-permute-start | bytes 1572872 | tf_op jit(solution)/shard_map/ppermute | solution.py:366
  183.3 5.2 %all-to-all-start.4 = ((f32[4,64,256]{2,1,0:T(8,128)}), f32[4,64,256]{2,1,0:T(8,128)S(1)}, u32[]{:S(2)}, u32[]{:S(2)}) async-start(f32[4,64,256]{2,1,0:T(8,128)} %copy.42), calls=%async_computation.4 | async-start | bytes 524288 | tf_op jit(solution)/shard_map/all_to_all | solution.py:477
  188.5 2.1 collective-permute-start.23
  190.6 1.5 collective-permute-start.24
  192.6 6.3 %all-to-all-done.4 = f32[4,64,256]{2,1,0:T(8,128)S(1)} async-done(((f32[4,64,256]{2,1,0:T(8,128)}), f32[4,64,256]{2,1,0:T(8,128)S(1)}, u32[]{:S(2)}, u32[]{:S(2)}) %all-to-all-start.4) | async-done | bytes 262176 | tf_op jit(solution)/shard_map/all_to_all | solution.py:477
  199.9 3.9 %all-to-all-start.5 = ((f32[4,32,128]{2,1,0:T(8,128)}), f32[4,32,128]{2,1,0:T(8,128)S(1)}, u32[]{:S(2)}, u32[]{:S(2)}) async-start(f32[4,32,128]{2,1,0:T(8,128)} %reshape.226), calls=%async_computation.5 | async-start | bytes 131072 | tf_op jit(solution)/shard_map/all_to_all | solution.py:479
  203.9 1.1 slice_bitcast_fusion
  206.5 5.6 %all-to-all-done.5 = f32[4,32,128]{2,1,0:T(8,128)S(1)} async-done(((f32[4,32,128]{2,1,0:T(8,128)}), f32[4,32,128]{2,1,0:T(8,128)S(1)}, u32[]{:S(2)}, u32[]{:S(2)}) %all-to-all-start.5) | async-done | bytes 65568 | tf_op jit(solution)/shard_map/all_to_all | solution.py:479
  (130 shorter events, 22.5 us)
Async XLA Ops:
  7.2 14.0 %copy-start = (f32[2048,64]{0,1:T(8,128)S(1)}, f32[2048,64]{0,1:T(8,128)}, u32[]{:S(2)}) copy-start(f32[2048,64]{0,1:T(8,128)} %param.10) | copy-start | bytes 1572868
  7.2 20.3 %copy-start.22 = (s32[3]{0:T(128)S(1)}, s32[3]{0:T(128)}, u32[]{:S(2)}) copy-start(s32[3]{0:T(128)} %constant.14) | copy-start | bytes 40
  7.2 29.1 %collective-permute-start = (f32[64,2048]{1,0:T(8,128)}, f32[64,2048]{1,0:T(8,128)S(1)}, u32[]{:S(2)}, u32[]{:S(2)}) collective-permute-start(f32[64,2048]{1,0:T(8,128)} %bitcast.46), channel_id=1, source_target_pairs={{0,48},{16,0},{32,16},{48,32},{1,49},{17,1},{33,17},{49,33},{2,50}... | collective-permute-start | bytes 1572872 | tf_op jit(solution)/shard_map/ppermute | solution.py:366
  13.6 26.5 %collective-permute-start.1 = (f32[64,2048]{1,0:T(8,128)}, f32[64,2048]{1,0:T(8,128)S(1)}, u32[]{:S(2)}, u32[]{:S(2)}) collective-permute-start(f32[64,2048]{1,0:T(8,128)} %bitcast.47), channel_id=1, source_target_pairs={{0,16},{16,32},{32,48},{48,0},{1,17},{17,33},{33,49},{49,1},{2,18}... | collective-permute-start | bytes 1572872 | tf_op jit(solution)/shard_map/ppermute | solution.py:366
  17.0 14.8 %collective-permute-start.2 = (f32[4,64,256]{2,1,0:T(8,128)S(1)}, f32[4,64,256]{2,1,0:T(8,128)S(1)}, u32[]{:S(2)}, u32[]{:S(2)}) collective-permute-start(f32[4,64,256]{2,1,0:T(8,128)S(1)} %get-tuple-element.70), channel_id=1, source_target_pairs={{0,128},{64,192},{128,0},{192,64},{1,129},{65,193},{129,1},{193,65... | collective-permute-start | bytes 786440 | tf_op jit(solution)/shard_map/ppermute | solution.py:366
  19.2 12.8 %collective-permute-start.3 = (f32[4,64,256]{2,1,0:T(8,128)S(1)}, f32[4,64,256]{2,1,0:T(8,128)S(1)}, u32[]{:S(2)}, u32[]{:S(2)}) collective-permute-start(f32[4,64,256]{2,1,0:T(8,128)S(1)} %get-tuple-element.71), channel_id=1, source_target_pairs={{0,64},{64,128},{128,192},{192,0},{1,65},{65,129},{129,193},{193,1... | collective-permute-start | bytes 786440 | tf_op jit(solution)/shard_map/ppermute | solution.py:366
  19.2 12.9 %collective-permute-start.4 = (f32[4,64,256]{2,1,0:T(8,128)S(1)}, f32[4,64,256]{2,1,0:T(8,128)}, u32[]{:S(2)}, u32[]{:S(2)}) collective-permute-start(f32[4,64,256]{2,1,0:T(8,128)S(1)} %get-tuple-element.72), channel_id=1, source_target_pairs={{0,192},{64,0},{128,64},{192,128},{1,193},{65,1},{129,65},{193,129... | collective-permute-start | bytes 786440 | tf_op jit(solution)/shard_map/ppermute | solution.py:366
  22.0 20.1 %all-to-all-start = ((f32[16,64,128]{2,1,0:T(8,128)}), f32[16,64,128]{2,1,0:T(8,128)S(1)}, u32[]{:S(2)}, u32[]{:S(2)}) async-start(f32[16,64,128]{2,1,0:T(8,128)} %bitcast_bitcast_fusion), calls=%async_computation | async-start | bytes 1048576 | tf_op jit(solution)/shard_map/all_to_all | solution.py:374
  27.4 77.6 %all-gather.2.cloned.1.call-start = ((), (), s32[]{:S(2)}) async-start(), calls=%async_computation.6 | async-start | bytes 4456448 | tf_op jit(solution)/shard_map/all_gather | solution.py:438
  31.8 10.4 %copy-start.20 = (f32[4,64,256]{2,1,0:T(8,128)}, f32[4,64,256]{2,1,0:T(8,128)S(1)}, u32[]{:S(2)}) copy-start(f32[4,64,256]{2,1,0:T(8,128)S(1)} %collective-permute-done.2.refs_4_) | copy-start | bytes 786436
  32.0 10.2 %copy-start.21 = (f32[4,64,256]{2,1,0:T(8,128)}, f32[4,64,256]{2,1,0:T(8,128)S(1)}, u32[]{:S(2)}) copy-start(f32[4,64,256]{2,1,0:T(8,128)S(1)} %collective-permute-done.3.refs_5_) | copy-start | bytes 786436
  36.3 40.3 %copy-start.4 = (f32[64,2048]{1,0:T(8,128)}, f32[64,2048]{1,0:T(8,128)S(1)}, u32[]{:S(2)}) copy-start(f32[64,2048]{1,0:T(8,128)S(1)} %collective-permute-done.up_ref.refs_2_) | copy-start | bytes 1572868
  40.1 36.5 %copy-start.5 = (f32[64,2048]{1,0:T(8,128)}, f32[64,2048]{1,0:T(8,128)S(1)}, u32[]{:S(2)}) copy-start(f32[64,2048]{1,0:T(8,128)S(1)} %collective-permute-done.1.down_ref.refs_3_) | copy-start | bytes 1572868
  44.6 22.1 %collective-permute-start.7 = (f32[8,64,256]{2,1,0:T(8,128)}, f32[8,64,256]{2,1,0:T(8,128)}, u32[]{:S(2)}, u32[]{:S(2)}) collective-permute-start(f32[8,64,256]{2,1,0:T(8,128)} %get-tuple-element.78), channel_id=1, source_target_pairs={{0,128},{64,192},{128,0},{192,64},{1,129},{65,193},{129,1},{193,65... | collective-permute-start | bytes 1572872 | tf_op jit(solution)/shard_map/ppermute | solution.py:366
  46.6 24.7 %collective-permute-start.8 = (f32[8,64,256]{2,1,0:T(8,128)S(1)}, f32[8,64,256]{2,1,0:T(8,128)}, u32[]{:S(2)}, u32[]{:S(2)}) collective-permute-start(f32[8,64,256]{2,1,0:T(8,128)S(1)} %get-tuple-element.79), channel_id=1, source_target_pairs={{0,64},{64,128},{128,192},{192,0},{1,65},{65,129},{129,193},{193,1... | collective-permute-start | bytes 1572872 | tf_op jit(solution)/shard_map/ppermute | solution.py:366
  48.3 23.1 %collective-permute-start.9 = (f32[8,64,256]{2,1,0:T(8,128)S(1)}, f32[8,64,256]{2,1,0:T(8,128)}, u32[]{:S(2)}, u32[]{:S(2)}) collective-permute-start(f32[8,64,256]{2,1,0:T(8,128)S(1)} %get-tuple-element.80), channel_id=1, source_target_pairs={{0,192},{64,0},{128,64},{192,128},{1,193},{65,1},{129,65},{193,129... | collective-permute-start | bytes 1572872 | tf_op jit(solution)/shard_map/ppermute | solution.py:366
  48.6 14.1 %collective-permute-start.5 = (f32[64,1024]{1,0:T(8,128)}, f32[64,1024]{1,0:T(8,128)S(1)}, u32[]{:S(2)}, u32[]{:S(2)}) collective-permute-start(f32[64,1024]{1,0:T(8,128)} %get-tuple-element.76), channel_id=1, source_target_pairs={{0,48},{16,0},{32,16},{48,32},{1,49},{17,1},{33,17},{49,33},{2,50}... | collective-permute-start | bytes 786440 | tf_op jit(solution)/shard_map/ppermute | solution.py:366
  51.8 14.9 %collective-permute-start.6 = (f32[64,1024]{1,0:T(8,128)S(1)}, f32[64,1024]{1,0:T(8,128)S(1)}, u32[]{:S(2)}, u32[]{:S(2)}) collective-permute-start(f32[64,1024]{1,0:T(8,128)S(1)} %get-tuple-element.77), channel_id=1, source_target_pairs={{0,16},{16,32},{32,48},{48,0},{1,17},{17,33},{33,49},{49,1},{2,18}... | collective-permute-start | bytes 786440 | tf_op jit(solution)/shard_map/ppermute | solution.py:366
  62.7 13.9 %copy-start.7 = (f32[64,1024]{1,0:T(8,128)}, f32[64,1024]{1,0:T(8,128)S(1)}, u32[]{:S(2)}) copy-start(f32[64,1024]{1,0:T(8,128)S(1)} %collective-permute-done.5.refs_0_.lo_ref) | copy-start | bytes 786436
  66.7 9.3 %copy-start.8 = (f32[64,1024]{1,0:T(8,128)}, f32[64,1024]{1,0:T(8,128)S(1)}, u32[]{:S(2)}) copy-start(f32[64,1024]{1,0:T(8,128)S(1)} %collective-permute-done.6.refs_1_.hi_ref) | copy-start | bytes 786436
  72.1 14.6 %collective-permute-start.10 = (f32[4,64,256]{2,1,0:T(8,128)S(1)}, f32[4,64,256]{2,1,0:T(8,128)S(1)}, u32[]{:S(2)}, u32[]{:S(2)}) collective-permute-start(f32[4,64,256]{2,1,0:T(8,128)S(1)} %get-tuple-element.89), channel_id=1, source_target_pairs={{0,128},{64,192},{128,0},{192,64},{1,129},{65,193},{129,1},{193,65... | collective-permute-start | bytes 786440 | tf_op jit(solution)/shard_map/ppermute | solution.py:366
  74.1 13.3 %collective-permute-start.11 = (f32[4,64,256]{2,1,0:T(8,128)S(1)}, f32[4,64,256]{2,1,0:T(8,128)S(1)}, u32[]{:S(2)}, u32[]{:S(2)}) collective-permute-start(f32[4,64,256]{2,1,0:T(8,128)S(1)} %get-tuple-element.90), channel_id=1, source_target_pairs={{0,64},{64,128},{128,192},{192,0},{1,65},{65,129},{129,193},{193,1... | collective-permute-start | bytes 786440 | tf_op jit(solution)/shard_map/ppermute | solution.py:366
  75.6 11.9 %collective-permute-start.12 = (f32[4,64,256]{2,1,0:T(8,128)S(1)}, f32[4,64,256]{2,1,0:T(8,128)S(1)}, u32[]{:S(2)}, u32[]{:S(2)}) collective-permute-start(f32[4,64,256]{2,1,0:T(8,128)S(1)} %get-tuple-element.91), channel_id=1, source_target_pairs={{0,192},{64,0},{128,64},{192,128},{1,193},{65,1},{129,65},{193,129... | collective-permute-start | bytes 786440 | tf_op jit(solution)/shard_map/ppermute | solution.py:366
  76.6 10.9 %copy-start.1 = (bf16[12,256,256]{2,1,0:T(8,128)(2,1)S(1)}, bf16[12,256,256]{2,1,0:T(8,128)(2,1)}, u32[]{:S(2)}) copy-start(bf16[12,256,256]{2,1,0:T(8,128)(2,1)} %shard_map.86.tiles_ref) | copy-start | bytes 4718596
  76.6 10.9 %copy-start.14 = (s32[12]{0:T(128)S(1)}, s32[12]{0:T(128)}, u32[]{:S(2)}) copy-start(s32[12]{0:T(128)} %reshape.216.refs_ref) | copy-start | bytes 148
  105.0 12.2 %copy-start.15 = (f32[16,64,128]{2,1,0:T(8,128)S(1)}, f32[16,64,128]{2,1,0:T(8,128)}, u32[]{:S(2)}) copy-start(f32[16,64,128]{2,1,0:T(8,128)} %all_to_all.30) | copy-start | bytes 1572868
  111.1 15.9 %all-to-all-start.2 = ((f32[16,64,128]{2,1,0:T(8,128)}), f32[16,64,128]{2,1,0:T(8,128)S(1)}, u32[]{:S(2)}, u32[]{:S(2)}) async-start(f32[16,64,128]{2,1,0:T(8,128)} %get-tuple-element.94), calls=%async_computation.2 | async-start | bytes 1048576 | tf_op jit(solution)/shard_map/all_to_all | solution.py:374
  117.2 2.0 collective-permute-start.14
  118.6 2.0 collective-permute-start.13
  127.0 43.7 %all-to-all-start.3 = ((f32[8,64,1280]{2,1,0:T(8,128)}), f32[8,64,1280]{2,1,0:T(8,128)}, u32[]{:S(2)}, u32[]{:S(2)}) async-start(f32[8,64,1280]{2,1,0:T(8,128)} %shard_map.92), calls=%async_computation.3 | async-start | bytes 5242880 | tf_op jit(solution)/shard_map/all_to_all | solution.py:461
  133.7 12.0 %collective-permute-start.15 = (f32[4,64,256]{2,1,0:T(8,128)S(1)}, f32[4,64,256]{2,1,0:T(8,128)S(1)}, u32[]{:S(2)}, u32[]{:S(2)}) collective-permute-start(f32[4,64,256]{2,1,0:T(8,128)S(1)} %get-tuple-element.98), channel_id=1, source_target_pairs={{0,128},{64,192},{128,0},{192,64},{1,129},{65,193},{129,1},{193,65... | collective-permute-start | bytes 786440 | tf_op jit(solution)/shard_map/ppermute | solution.py:366
  136.0 13.0 %collective-permute-start.16 = (f32[4,64,256]{2,1,0:T(8,128)S(1)}, f32[4,64,256]{2,1,0:T(8,128)S(1)}, u32[]{:S(2)}, u32[]{:S(2)}) collective-permute-start(f32[4,64,256]{2,1,0:T(8,128)S(1)} %get-tuple-element.99), channel_id=1, source_target_pairs={{0,192},{64,0},{128,64},{192,128},{1,193},{65,1},{129,65},{193,129... | collective-permute-start | bytes 786440 | tf_op jit(solution)/shard_map/ppermute | solution.py:366
  137.5 11.6 %collective-permute-start.17 = (f32[4,64,256]{2,1,0:T(8,128)S(1)}, f32[4,64,256]{2,1,0:T(8,128)S(1)}, u32[]{:S(2)}, u32[]{:S(2)}) collective-permute-start(f32[4,64,256]{2,1,0:T(8,128)S(1)} %get-tuple-element.100), channel_id=1, source_target_pairs={{0,64},{64,128},{128,192},{192,0},{1,65},{65,129},{129,193},{193,1... | collective-permute-start | bytes 786440 | tf_op jit(solution)/shard_map/ppermute | solution.py:366
  145.8 30.4 %copy-start.10 = (f32[8,64,256]{2,1,0:T(8,128)S(1)}, f32[8,64,256]{2,1,0:T(8,128)}, u32[]{:S(2)}) copy-start(f32[8,64,256]{2,1,0:T(8,128)} %get-tuple-element.120.up_ref) | copy-start | bytes 1572868
  145.8 30.4 %copy-start.11 = (f32[8,64,256]{2,1,0:T(8,128)S(1)}, f32[8,64,256]{2,1,0:T(8,128)}, u32[]{:S(2)}) copy-start(f32[8,64,256]{2,1,0:T(8,128)} %get-tuple-element.121.down_ref) | copy-start | bytes 1572868
  149.1 27.1 %collective-permute-start.18 = (f32[8,64,256]{2,1,0:T(8,128)}, f32[8,64,256]{2,1,0:T(8,128)S(1)}, u32[]{:S(2)}, u32[]{:S(2)}) collective-permute-start(f32[8,64,256]{2,1,0:T(8,128)} %get-tuple-element.104), channel_id=1, source_target_pairs={{0,128},{64,192},{128,0},{192,64},{1,129},{65,193},{129,1},{193,65... | collective-permute-start | bytes 1572872 | tf_op jit(solution)/shard_map/ppermute | solution.py:366
  151.1 25.1 %collective-permute-start.19 = (f32[8,64,256]{2,1,0:T(8,128)}, f32[8,64,256]{2,1,0:T(8,128)S(1)}, u32[]{:S(2)}, u32[]{:S(2)}) collective-permute-start(f32[8,64,256]{2,1,0:T(8,128)} %get-tuple-element.105), channel_id=1, source_target_pairs={{0,192},{64,0},{128,64},{192,128},{1,193},{65,1},{129,65},{193,129... | collective-permute-start | bytes 1572872 | tf_op jit(solution)/shard_map/ppermute | solution.py:366
  152.6 23.6 %collective-permute-start.20 = (f32[8,64,256]{2,1,0:T(8,128)}, f32[8,64,256]{2,1,0:T(8,128)S(1)}, u32[]{:S(2)}, u32[]{:S(2)}) collective-permute-start(f32[8,64,256]{2,1,0:T(8,128)} %get-tuple-element.106), channel_id=1, source_target_pairs={{0,64},{64,128},{128,192},{192,0},{1,65},{65,129},{129,193},{193,1... | collective-permute-start | bytes 1572872 | tf_op jit(solution)/shard_map/ppermute | solution.py:366
  156.5 19.7 %collective-permute-start.21 = (f32[4,64,256]{2,1,0:T(8,128)}, f32[4,64,256]{2,1,0:T(8,128)S(1)}, u32[]{:S(2)}, u32[]{:S(2)}) collective-permute-start(f32[4,64,256]{2,1,0:T(8,128)} %get-tuple-element.112), channel_id=1, source_target_pairs={{0,16},{16,32},{32,48},{48,0},{1,17},{17,33},{33,49},{49,1},{2,18}... | collective-permute-start | bytes 786440 | tf_op jit(solution)/shard_map/ppermute | solution.py:366
  158.0 18.2 %collective-permute-start.22 = (f32[4,64,256]{2,1,0:T(8,128)}, f32[4,64,256]{2,1,0:T(8,128)}, u32[]{:S(2)}, u32[]{:S(2)}) collective-permute-start(f32[4,64,256]{2,1,0:T(8,128)} %get-tuple-element.113), channel_id=1, source_target_pairs={{0,48},{16,0},{32,16},{48,32},{1,49},{17,1},{33,17},{49,33},{2,50}... | collective-permute-start | bytes 786440 | tf_op jit(solution)/shard_map/ppermute | solution.py:366
  178.5 27.4 %copy-start.9 = (f32[8,64,256]{2,1,0:T(8,128)S(1)}, f32[8,64,256]{2,1,0:T(8,128)}, u32[]{:S(2)}) copy-start(f32[8,64,256]{2,1,0:T(8,128)} %get-tuple-element.133.diag_ref) | copy-start | bytes 1572868
  178.5 34.5 %collective-permute-start.26 = (f32[8,64,256]{2,1,0:T(8,128)}, f32[8,64,256]{2,1,0:T(8,128)S(1)}, u32[]{:S(2)}, u32[]{:S(2)}) collective-permute-start(f32[8,64,256]{2,1,0:T(8,128)} %get-tuple-element.134), channel_id=1, source_target_pairs={{0,16},{16,32},{32,48},{48,0},{1,17},{17,33},{33,49},{49,1},{2,18}... | collective-permute-start | bytes 1572872 | tf_op jit(solution)/shard_map/ppermute | solution.py:366
  179.5 33.5 %collective-permute-start.27 = (f32[8,64,256]{2,1,0:T(8,128)}, f32[8,64,256]{2,1,0:T(8,128)S(1)}, u32[]{:S(2)}, u32[]{:S(2)}) collective-permute-start(f32[8,64,256]{2,1,0:T(8,128)} %get-tuple-element.135), channel_id=1, source_target_pairs={{0,48},{16,0},{32,16},{48,32},{1,49},{17,1},{33,17},{49,33},{2,50}... | collective-permute-start | bytes 1572872 | tf_op jit(solution)/shard_map/ppermute | solution.py:366
  183.3 15.6 %all-to-all-start.4 = ((f32[4,64,256]{2,1,0:T(8,128)}), f32[4,64,256]{2,1,0:T(8,128)S(1)}, u32[]{:S(2)}, u32[]{:S(2)}) async-start(f32[4,64,256]{2,1,0:T(8,128)} %copy.42), calls=%async_computation.4 | async-start | bytes 524288 | tf_op jit(solution)/shard_map/all_to_all | solution.py:477
  188.5 17.3 %collective-permute-start.23 = (f32[4,64,256]{2,1,0:T(8,128)}, f32[4,64,256]{2,1,0:T(8,128)S(1)}, u32[]{:S(2)}, u32[]{:S(2)}) collective-permute-start(f32[4,64,256]{2,1,0:T(8,128)} %get-tuple-element.130), channel_id=1, source_target_pairs={{0,128},{64,192},{128,0},{192,64},{1,129},{65,193},{129,1},{193,65... | collective-permute-start | bytes 786440 | tf_op jit(solution)/shard_map/ppermute | solution.py:366
  190.6 15.2 %collective-permute-start.24 = (f32[4,64,256]{2,1,0:T(8,128)}, f32[4,64,256]{2,1,0:T(8,128)S(1)}, u32[]{:S(2)}, u32[]{:S(2)}) collective-permute-start(f32[4,64,256]{2,1,0:T(8,128)} %get-tuple-element.131), channel_id=1, source_target_pairs={{0,192},{64,0},{128,64},{192,128},{1,193},{65,1},{129,65},{193,129... | collective-permute-start | bytes 786440 | tf_op jit(solution)/shard_map/ppermute | solution.py:366
  192.0 13.8 %collective-permute-start.25 = (f32[4,64,256]{2,1,0:T(8,128)}, f32[4,64,256]{2,1,0:T(8,128)S(1)}, u32[]{:S(2)}, u32[]{:S(2)}) collective-permute-start(f32[4,64,256]{2,1,0:T(8,128)} %get-tuple-element.132), channel_id=1, source_target_pairs={{0,64},{64,128},{128,192},{192,0},{1,65},{65,129},{129,193},{193,1... | collective-permute-start | bytes 786440 | tf_op jit(solution)/shard_map/ppermute | solution.py:366
  199.9 12.2 %all-to-all-start.5 = ((f32[4,32,128]{2,1,0:T(8,128)}), f32[4,32,128]{2,1,0:T(8,128)S(1)}, u32[]{:S(2)}, u32[]{:S(2)}) async-start(f32[4,32,128]{2,1,0:T(8,128)} %reshape.226), calls=%async_computation.5 | async-start | bytes 131072 | tf_op jit(solution)/shard_map/all_to_all | solution.py:479
  (9 other events, 20.3 us)
Sparse Core Ops, SparseCore 0:
  42.3 46.7 all-gather.1

commit v7 on v6

--- a/solution.py
+++ b/solution.py
@@ -214,7 +214,7 @@
     )(far_refs, part, *far, tiles)
 
 
-def dense_kernel(weight_ref, mixed_ref, cot_ref, rows_ref, back_ref, held, sems):
+def dense_kernel(weight_ref, mixed_ref, zl_ref, mine_ref, other_ref, rows_ref, back_ref, held, sems):
     step = F // 2
     copies = []
     for j in range(F // step):
@@ -234,7 +234,12 @@
         pre = both[:, :CHUNK] + (both[:, CHUNK:] + low)
         sig = jax.nn.sigmoid(pre)
         rows_ref[rows, CHUNK:] = pre * sig
-        slope = cot_ref[rows] * sig * (1.0 + pre * (1.0 - sig))
+        pairs = []
+        for part in range(j * step // (2 * C), (j + 1) * step // (2 * C)):
+            y, zl = part // 2, part % 2
+            own = zl_ref[0] == zl
+            pairs += [jnp.where(own, mine_ref[2 * y + c], other_ref[2 * y + c]) for c in range(2)]
+        slope = jnp.concatenate(pairs, axis=0) * sig * (1.0 + pre * (1.0 - sig))
         rows_ref[rows, :CHUNK] = slope
         shi, slo = split(slope.T)
         both = jnp.dot(jnp.concatenate([shi, slo], axis=0), whi, preferred_element_type=f32)
@@ -244,16 +249,16 @@
     back_ref[...] = back.T.reshape(16, C, CHUNK)
 
 
-def dense(weight_t, mixed, cot):
+def dense(weight_t, mixed, me_l, cot_mine, cot_other):
     return pl.pallas_call(
         dense_kernel,
-        in_specs=[ANY, VMEM, VMEM],
+        in_specs=[ANY, VMEM, SMEM, VMEM, VMEM],
         out_specs=[VMEM, VMEM],
         out_shape=[jax.ShapeDtypeStruct((F, 2 * CHUNK), f32), jax.ShapeDtypeStruct((16, C, CHUNK), f32)],
         scratch_shapes=[pltpu.VMEM((F, F), f32), pltpu.SemaphoreType.DMA((2,))],
         compiler_params=PARAMS,
         cost_estimate=pl.CostEstimate(flops=12 * F * F * CHUNK, bytes_accessed=8 << 20, transcendentals=F * CHUNK),
-    )(weight_t, mixed, cot)
+    )(weight_t, mixed, me_l.reshape(1).astype(jnp.int32), cot_mine, cot_other)
 
 
 def push_far_kernel(refs_ref, back_ref, tiles_ref, a_ref, b_ref, c_ref):
@@ -432,7 +437,9 @@
     up = shift(own, "zh", NZ, -1)
     down = shift(own, "zh", NZ, 1)
     near = over_x(pick(pick_near_kernel, ((4, C, W),) * 3, [], near_at, own), 1)
-    cot = over_col(cotangent.T.reshape(C, 16, CHUNK).transpose(1, 0, 2)).reshape(F, CHUNK)
+    me_l = lax.axis_index("zl")
+    cot = cotangent.T.reshape(C, NY, 2, 2, CHUNK).transpose(1, 3, 2, 0, 4).reshape(8, 2, C, CHUNK)
+    cot = lax.all_to_all(cot, ("y", "c"), 0, 0, tiled=True)
     some = far_tiles(far_refs, tiles)
     (up, down), (near, cot, weight_t, some) = after((up, down), (near, cot, weight.T, some))
     weight_t = lax.all_gather(weight_t, COL, axis=0, tiled=True)
@@ -440,14 +447,18 @@
     lo = shift(lo, "zh", NZ, -1)
     hi = shift(hi, "zh", NZ, 1)
     mid = over_x(mid, 1)
-    lo, hi, mid = lax.optimization_barrier((lo, hi, mid))
+    cot_mine = lax.dynamic_index_in_dim(cot, me_l, 1, keepdims=False)
+    cot_other = lax.dynamic_index_in_dim(cot, 1 - me_l, 1, keepdims=False)
+    (lo, hi, mid), (cot_mine, cot_other) = after((lo, hi, mid), (cot_mine, cot_other))
+    cot_other = shift(cot_other, "zl", 2, 1)
     far = pick(pick_far_kernel, ((4, C, W),) * 3, [pltpu.VMEM((C, BLK * W), f32)], far_at, lo, hi)
     far = over_x(far, 1)
     part = mix(place, own, [lo, hi, up, down, *near, *mid], tiles)
+    part, cot_other = after(part, cot_other)
     mixed = mix_far(far_refs, part, far, some)
 
     mixed = over_col(mixed).reshape(F, CHUNK)
-    rows, back = dense(weight_t, mixed, cot)
+    rows, back = dense(weight_t, mixed, me_l, cot_mine, cot_other)
     back = over_col(back)
 
     rows = rows.reshape(8, 2, C, 2 * CHUNK)

time: 222 us -> 217 us (0.977)
  waiting for transfers between devices: 58.9 us -> 50.8 us
  starting transfers between devices: 69.5 us -> 72.3 us
  local copies, waits for them, and re-layouts: 16.3 us -> 19 us
    ppermute x28 -> x29, waiting for transfers between devices: 34.6 us -> 24.8 us  [shift(): lax.ppermute(value, axis, [(i, (i + by) % size) for i in range(size)])]
    all_to_all x2 -> x1, starting transfers between devices: 11.5 us -> 6.08 us  [over_col(): return lax.all_to_all(value, COL, 0, 0, tiled=True)]
    all_to_all x0 -> x1, starting transfers between devices: none -> 4.92 us  [on_device(): cot = lax.all_to_all(cot, ('y', 'c'), 0, 0, tiled=True)]
    all_to_all x0 -> x1, waiting for transfers between devices: none -> 4.51 us  [on_device(): cot = lax.all_to_all(cot, ('y', 'c'), 0, 0, tiled=True)]
    reshape x0 -> x2, local copies, waits for them, and re-layouts: none -> 2.44 us  [on_device(): cotangent.T.reshape(C, NY, 2, 2, CHUNK).transpose(1, 3, 2, 0, 4)]
    ppermute x28 -> x29, starting transfers between devices: 43.1 us -> 45.3 us  [shift(): lax.ppermute(value, axis, [(i, (i + by) % size) for i in range(size)])]
    unnamed x49 -> x53, local copies, waits for them, and re-layouts: 8.14 us -> 7.48 us
  transfers between devices with their start and end apart: 34 -> 35, of which waited for: 18 -> 14; matrix products, arithmetic and copies ran while one was open for 6% -> 8% of each run, Pallas kernels for 15% -> 16%
where the time goes in v7:
time: 217 us; the launch traced here: 216 us
  starting transfers between devices  72.3 us (33%)
  waiting for transfers between devices  50.8 us (23%)
  Pallas kernels  41.9 us (19%)
  local copies, waits for them, and re-layouts  19 us (9%)
  between operations  14.6 us (7%)
  blocking collectives  13.3 us (6%)
  other arithmetic  4.05 us (2%)
    ppermute x29, starting transfers between devices, shift(): lax.ppermute(value, axis, [(i, (i + by) % size) for i in range(size)])  45.3 us
    ppermute x29, waiting for transfers between devices, shift(): lax.ppermute(value, axis, [(i, (i + by) % size) for i in range(size)])  24.8 us
    all_to_all x1, blocking collectives, over_col(): return lax.all_to_all(value, COL, 0, 0, tiled=True)  13.3 us
    all_to_all x1, waiting for transfers between devices, on_device(): grad = lax.all_to_all(grad, ('y', 'zl'), 0, 0, tiled=True)  10.5 us
    pallas_call x1, Pallas kernels, mix(): pl.pallas_call(mixed_kernel, grid_spec=pltpu.PrefetchScalarGridSpec(num_s...  10.1 us
    pallas_call x1, Pallas kernels, push(): pl.pallas_call(push_kernel, in_specs=[SMEM, VMEM, ANY], out_specs=[VMEM]...  7.77 us
    unnamed x53, local copies, waits for them, and re-layouts  7.48 us
    pallas_call x1, Pallas kernels, dense(): pl.pallas_call(dense_kernel, in_specs=[ANY, VMEM, SMEM, VMEM, VMEM], out_...  6.12 us
  transfers between devices with their start and end apart: 35, of which 14 were waited for; matrix products, arithmetic and copies ran while one was open for 8% of the time, Pallas kernels for 16%

profile of v7, /device:TPU:10, one launch (start us, length us, event | category | flops | bytes accessed | tf_op | source)
XLA Modules:
  0.0 215.9 jit_solution(513561807739209663)
XLA Ops:
  7.2 6.4 %collective-permute-start = (f32[64,2048]{1,0:T(8,128)}, f32[64,2048]{1,0:T(8,128)S(1)}, u32[]{:S(2)}, u32[]{:S(2)}) collective-permute-start(f32[64,2048]{1,0:T(8,128)} %bitcast.46), channel_id=1, source_target_pairs={{0,48},{16,0},{32,16},{48,32},{1,49},{17,1},{33,17},{49,33},{2,50}... | collective-permute-start | bytes 1572872 | tf_op jit(solution)/shard_map/ppermute | solution.py:371
  16.9 2.2 %collective-permute-start.2 = (f32[4,64,256]{2,1,0:T(8,128)S(1)}, f32[4,64,256]{2,1,0:T(8,128)S(1)}, u32[]{:S(2)}, u32[]{:S(2)}) collective-permute-start(f32[4,64,256]{2,1,0:T(8,128)S(1)} %get-tuple-element.74), channel_id=1, source_target_pairs={{0,128},{64,192},{128,0},{192,64},{1,129},{65,193},{129,1},{193,65... | collective-permute-start | bytes 786440 | tf_op jit(solution)/shard_map/ppermute | solution.py:371
  19.2 2.0 collective-permute-start.4
  21.2 1.5 reshape.217
  23.6 4.9 %all-to-all-start = ((f32[8,2,64,128]{3,2,1,0:T(8,128)}), f32[8,2,64,128]{3,2,1,0:T(8,128)S(1)}, u32[]{:S(2)}, u32[]{:S(2)}) async-start(f32[8,2,64,128]{3,2,1,0:T(8,128)} %bitcast.4), calls=%async_computation | async-start | bytes 1048576 | tf_op jit(solution)/shard_map/all_to_all | solution.py:442
  29.4 3.4 %shard_map.86.tiles_ref = bf16[12,256,256]{2,1,0:T(8,128)(2,1)} custom-call(s32[12]{0:T(128)} %reshape.219.refs_ref, bf16[8,8,256,256]{3,2,1,0:T(8,128)(2,1)} %tiles_ref.3), custom_call_target="tpu_custom_call" | custom-call | bytes 3145728 | tf_op jit(solution)/shard_map/pallas_call | solution.py:182
  32.9 4.5 %all-to-all-done = f32[8,2,64,128]{3,2,1,0:T(8,128)S(1)} async-done(((f32[8,2,64,128]{3,2,1,0:T(8,128)}), f32[8,2,64,128]{3,2,1,0:T(8,128)S(1)}, u32[]{:S(2)}, u32[]{:S(2)}) %all-to-all-start) | async-done | bytes 524320 | tf_op jit(solution)/shard_map/all_to_all | solution.py:442
  37.4 2.6 %collective-permute-done.1.down_ref.refs_3_ = f32[64,2048]{1,0:T(8,128)S(1)} collective-permute-done((f32[64,2048]{1,0:T(8,128)}, f32[64,2048]{1,0:T(8,128)S(1)}, u32[]{:S(2)}, u32[]{:S(2)}) %collective-permute-start.1) | collective-permute-done | bytes 524320 | tf_op jit(solution)/shard_map/ppermute | solution.py:371
  40.2 1.4 shard_map.87
  41.6 2.1 collective-permute-start.7
  43.9 1.9 collective-permute-start.9
  45.8 2.2 %collective-permute-start.5 = (f32[64,1024]{1,0:T(8,128)}, f32[64,1024]{1,0:T(8,128)S(1)}, u32[]{:S(2)}, u32[]{:S(2)}) collective-permute-start(f32[64,1024]{1,0:T(8,128)} %get-tuple-element.80), channel_id=1, source_target_pairs={{0,48},{16,0},{32,16},{48,32},{1,49},{17,1},{33,17},{49,33},{2,50}... | collective-permute-start | bytes 786440 | tf_op jit(solution)/shard_map/ppermute | solution.py:371
  48.8 1.8 dynamic-slice_bitcast_fusion
  50.6 8.1 %collective-permute-done.5.refs_0_.lo_ref = f32[64,1024]{1,0:T(8,128)S(1)} collective-permute-done((f32[64,1024]{1,0:T(8,128)}, f32[64,1024]{1,0:T(8,128)S(1)}, u32[]{:S(2)}, u32[]{:S(2)}) %collective-permute-start.5) | collective-permute-done | bytes 262176 | tf_op jit(solution)/shard_map/ppermute | solution.py:371
  58.7 3.5 %collective-permute-done.6.refs_1_.hi_ref = f32[64,1024]{1,0:T(8,128)S(1)} collective-permute-done((f32[64,1024]{1,0:T(8,128)S(1)}, f32[64,1024]{1,0:T(8,128)S(1)}, u32[]{:S(2)}, u32[]{:S(2)}) %collective-permute-start.6) | collective-permute-done | bytes 262176 | tf_op jit(solution)/shard_map/ppermute | solution.py:371
  62.3 3.2 %collective-permute-done.8.refs_8_ = f32[8,64,256]{2,1,0:T(8,128)} collective-permute-done((f32[8,64,256]{2,1,0:T(8,128)S(1)}, f32[8,64,256]{2,1,0:T(8,128)}, u32[]{:S(2)}, u32[]{:S(2)}) %collective-permute-start.8) | collective-permute-done | bytes 524320 | tf_op jit(solution)/shard_map/ppermute | solution.py:371
  66.7 2.2 %collective-permute-start.11 = (f32[4,64,256]{2,1,0:T(8,128)S(1)}, f32[4,64,256]{2,1,0:T(8,128)S(1)}, u32[]{:S(2)}, u32[]{:S(2)}) collective-permute-start(f32[4,64,256]{2,1,0:T(8,128)S(1)} %get-tuple-element.96), channel_id=1, source_target_pairs={{0,128},{64,192},{128,0},{192,64},{1,129},{65,193},{129,1},{193,65... | collective-permute-start | bytes 786440 | tf_op jit(solution)/shard_map/ppermute | solution.py:371
  68.9 1.7 collective-permute-start.12
  70.9 3.0 %collective-permute-start.10 = (f32[8,64,128]{2,1,0:T(8,128)S(1)}, f32[8,64,128]{2,1,0:T(8,128)S(1)}, u32[]{:S(2)}, u32[]{:S(2)}) collective-permute-start(f32[8,64,128]{2,1,0:T(8,128)S(1)} %get-tuple-element.94), channel_id=1, source_target_pairs={{0,2},{2,0},{1,3},{3,1},{4,6},{6,4},{5,7},{7,5},{8,10},{10,8},{9,1... | collective-permute-start | bytes 786440 | tf_op jit(solution)/shard_map/ppermute | solution.py:371
  74.5 10.1 %shard_map.88.part_ref = f32[8,64,256]{2,1,0:T(8,128)} custom-call(s32[56]{0:T(128)} %fusion.5.place_ref, f32[64,2048]{1,0:T(8,128)} %bitcast.48, f32[64,1024]{1,0:T(8,128)} %copy-done.6, f32[64,1024]{1,0:T(8,128)} %copy-done.7, f32[64,2048]{1,0:T(8,128)} %copy-done.3, f32[64,2048]{1,0:T(8,128)} %copy-done.4, f32[4,64,256]{2,1,0:T(8,128)} %copy-done.19, ...), custom_call_target="tpu_custom_call" | custom-call | flops 1073741824 | bytes 13631488 | tf_op jit(solution)/shard_map/pallas_call | solution.py:150
  85.8 1.2 shard_map.90
  87.1 13.3 %all_to_all.30 = f32[16,64,128]{2,1,0:T(8,128)} all-to-all(f32[16,64,128]{2,1,0:T(8,128)S(1)} %shard_map.90), channel_id=1, replica_groups=mesh['x'=4,'zh'=4,'y'=4,'zl'=2,'c'=2] {'y','zl','c'}, dimensions={0} | all-to-all | bytes 1048576 | tf_op jit(solution)/shard_map/all_to_all | solution.py:379
  100.4 6.1 %shard_map.91 = (f32[1024,256]{1,0:T(8,128)}, f32[16,64,128]{2,1,0:T(8,128)}) custom-call(f32[1024,1024]{1,0:T(8,128)} %all-gather.2.cloned.1.call-done.weight_ref, f32[1024,128]{1,0:T(8,128)} %bitcast.52, s32[1]{0:T(128)} %bitcast.12.zl_ref, f32[8,64,128]{2,1,0:T(8,128)} %get-tuple-element.100.mine_ref, f32[8,64,128]{2,1,0:T(8,128)} %copy-done.24), custom_call_target="tpu_custom_call" | custom-call | flops 1610612736 | bytes 8388608 | tf_op jit(solution)/shard_map/pallas_call | solution.py:253
  106.6 6.1 %all-to-all-start.2 = ((f32[16,64,128]{2,1,0:T(8,128)}), f32[16,64,128]{2,1,0:T(8,128)S(1)}, u32[]{:S(2)}, u32[]{:S(2)}) async-start(f32[16,64,128]{2,1,0:T(8,128)} %get-tuple-element.102), calls=%async_computation.2 | async-start | bytes 1048576 | tf_op jit(solution)/shard_map/all_to_all | solution.py:379
  114.7 1.3 collective-permute-done.14.other_ref
  116.8 5.7 %shard_map.92 = f32[8,64,1280]{2,1,0:T(8,128)} custom-call(s32[1]{0:T(128)} %bitcast.13.core_ref, f32[8,2,64,256]{3,2,1,0:T(8,128)} %bitcast.51, f32[512,256]{1,0:T(8,128)} %copy-done.18, f32[1024,128]{1,0:T(8,128)} %bitcast.53, f32[1024,128]{1,0:T(8,128)} %copy-done.17), custom_call_target="tpu_custom_call" | custom-call | flops 805306368 | bytes 4194304 | tf_op jit(solution)/shard_map/pallas_call | solution.py:407
  122.4 5.8 %all-to-all-start.3 = ((f32[8,64,1280]{2,1,0:T(8,128)}), f32[8,64,1280]{2,1,0:T(8,128)}, u32[]{:S(2)}, u32[]{:S(2)}) async-start(f32[8,64,1280]{2,1,0:T(8,128)} %shard_map.92), calls=%async_computation.3 | async-start | bytes 5242880 | tf_op jit(solution)/shard_map/all_to_all | solution.py:472
  129.2 1.7 collective-permute-start.16
  130.9 2.2 %collective-permute-start.17 = (f32[4,64,256]{2,1,0:T(8,128)S(1)}, f32[4,64,256]{2,1,0:T(8,128)S(1)}, u32[]{:S(2)}, u32[]{:S(2)}) collective-permute-start(f32[4,64,256]{2,1,0:T(8,128)S(1)} %get-tuple-element.107), channel_id=1, source_target_pairs={{0,192},{64,0},{128,64},{192,128},{1,193},{65,1},{129,65},{193,129... | collective-permute-start | bytes 786440 | tf_op jit(solution)/shard_map/ppermute | solution.py:371
  133.0 7.8 %shard_map.94 = (f32[8,64,256]{2,1,0:T(8,128)}, f32[4,64,256]{2,1,0:T(8,128)}, f32[4,64,256]{2,1,0:T(8,128)}, f32[8,64,256]{2,1,0:T(8,128)}, f32[8,64,256]{2,1,0...) custom-call(s32[56]{0:T(128)} %fusion.5.place_ref, ...), custom_call_target="tpu_custom_call" | custom-call | flops 1073741824 | bytes 13631488 | tf_op jit(solution)/shard_map/pallas_call | solution.py:310
  140.9 3.4 %collective-permute-done.17.b_ref = f32[4,64,256]{2,1,0:T(8,128)S(1)} collective-permute-done((f32[4,64,256]{2,1,0:T(8,128)S(1)}, f32[4,64,256]{2,1,0:T(8,128)S(1)}, u32[]{:S(2)}, u32[]{:S(2)}) %collective-permute-start.17) | collective-permute-done | bytes 262176 | tf_op jit(solution)/shard_map/ppermute | solution.py:371
  144.7 1.3 collective-permute-start.19
  146.0 2.1 collective-permute-start.20
  150.1 1.4 shard_map.95
  151.5 1.2 collective-permute-start.22
  152.7 2.9 %collective-permute-start.23 = (f32[4,64,256]{2,1,0:T(8,128)S(1)}, f32[4,64,256]{2,1,0:T(8,128)S(1)}, u32[]{:S(2)}, u32[]{:S(2)}) collective-permute-start(f32[4,64,256]{2,1,0:T(8,128)S(1)} %get-tuple-element.121), channel_id=1, source_target_pairs={{0,48},{16,0},{32,16},{48,32},{1,49},{17,1},{33,17},{49,33},{2,50}... | collective-permute-start | bytes 786440 | tf_op jit(solution)/shard_map/ppermute | solution.py:371
  155.6 10.5 %all-to-all-done.3 = f32[8,64,1280]{2,1,0:T(8,128)} async-done(((f32[8,64,1280]{2,1,0:T(8,128)}), f32[8,64,1280]{2,1,0:T(8,128)}, u32[]{:S(2)}, u32[]{:S(2)}) %all-to-all-start.3) | async-done | bytes 2621472 | tf_op jit(solution)/shard_map/all_to_all | solution.py:472
  166.1 2.4 %slice_reduce_fusion = f32[64,1024]{1,0:T(8,128)} fusion(f32[8,64,1280]{2,1,0:T(8,128)} %all-to-all-done.3), kind=kLoop, calls=%fused_computation | loop fusion | flops 458752 | bytes 2359296 | tf_op jit(solution)/shard_map/reduce_sum | solution.py:481
  168.6 1.8 reshape.227
  170.3 1.4 collective-permute-done.22.below_ref
  171.8 1.8 shard_map.96
  174.6 3.1 %collective-permute-start.28 = (f32[8,64,256]{2,1,0:T(8,128)}, f32[8,64,256]{2,1,0:T(8,128)S(1)}, u32[]{:S(2)}, u32[]{:S(2)}) collective-permute-start(f32[8,64,256]{2,1,0:T(8,128)} %get-tuple-element.143), channel_id=1, source_target_pairs={{0,48},{16,0},{32,16},{48,32},{1,49},{17,1},{33,17},{49,33},{2,50}... | collective-permute-start | bytes 1572872 | tf_op jit(solution)/shard_map/ppermute | solution.py:371
  178.5 5.4 %all-to-all-start.4 = ((f32[4,64,256]{2,1,0:T(8,128)}), f32[4,64,256]{2,1,0:T(8,128)S(1)}, u32[]{:S(2)}, u32[]{:S(2)}) async-start(f32[4,64,256]{2,1,0:T(8,128)} %copy.42), calls=%async_computation.4 | async-start | bytes 524288 | tf_op jit(solution)/shard_map/all_to_all | solution.py:488
  183.9 2.1 collective-permute-start.24
  185.9 1.5 collective-permute-start.25
  188.0 5.3 %all-to-all-done.4 = f32[4,64,256]{2,1,0:T(8,128)S(1)} async-done(((f32[4,64,256]{2,1,0:T(8,128)}), f32[4,64,256]{2,1,0:T(8,128)S(1)}, u32[]{:S(2)}, u32[]{:S(2)}) %all-to-all-start.4) | async-done | bytes 262176 | tf_op jit(solution)/shard_map/all_to_all | solution.py:488
  194.2 4.8 %all-to-all-start.5 = ((f32[4,32,128]{2,1,0:T(8,128)}), f32[4,32,128]{2,1,0:T(8,128)S(1)}, u32[]{:S(2)}, u32[]{:S(2)}) async-start(f32[4,32,128]{2,1,0:T(8,128)} %reshape.230), calls=%async_computation.5 | async-start | bytes 131072 | tf_op jit(solution)/shard_map/all_to_all | solution.py:490
  201.7 5.6 %all-to-all-done.5 = f32[4,32,128]{2,1,0:T(8,128)S(1)} async-done(((f32[4,32,128]{2,1,0:T(8,128)}), f32[4,32,128]{2,1,0:T(8,128)S(1)}, u32[]{:S(2)}, u32[]{:S(2)}) %all-to-all-start.5) | async-done | bytes 65568 | tf_op jit(solution)/shard_map/all_to_all | solution.py:490
  (138 shorter events, 23.1 us)
Async XLA Ops:
  7.2 21.4 %copy-start.22 = (s32[3]{0:T(128)S(1)}, s32[3]{0:T(128)}, u32[]{:S(2)}) copy-start(s32[3]{0:T(128)} %constant.71) | copy-start | bytes 40
  7.2 30.3 %collective-permute-start = (f32[64,2048]{1,0:T(8,128)}, f32[64,2048]{1,0:T(8,128)S(1)}, u32[]{:S(2)}, u32[]{:S(2)}) collective-permute-start(f32[64,2048]{1,0:T(8,128)} %bitcast.46), channel_id=1, source_target_pairs={{0,48},{16,0},{32,16},{48,32},{1,49},{17,1},{33,17},{49,33},{2,50}... | collective-permute-start | bytes 1572872 | tf_op jit(solution)/shard_map/ppermute | solution.py:371
  13.6 26.5 %collective-permute-start.1 = (f32[64,2048]{1,0:T(8,128)}, f32[64,2048]{1,0:T(8,128)S(1)}, u32[]{:S(2)}, u32[]{:S(2)}) collective-permute-start(f32[64,2048]{1,0:T(8,128)} %bitcast.47), channel_id=1, source_target_pairs={{0,16},{16,32},{32,48},{48,0},{1,17},{17,33},{33,49},{49,1},{2,18}... | collective-permute-start | bytes 1572872 | tf_op jit(solution)/shard_map/ppermute | solution.py:371
  16.9 15.9 %collective-permute-start.2 = (f32[4,64,256]{2,1,0:T(8,128)S(1)}, f32[4,64,256]{2,1,0:T(8,128)S(1)}, u32[]{:S(2)}, u32[]{:S(2)}) collective-permute-start(f32[4,64,256]{2,1,0:T(8,128)S(1)} %get-tuple-element.74), channel_id=1, source_target_pairs={{0,128},{64,192},{128,0},{192,64},{1,129},{65,193},{129,1},{193,65... | collective-permute-start | bytes 786440 | tf_op jit(solution)/shard_map/ppermute | solution.py:371
  19.2 13.7 %collective-permute-start.3 = (f32[4,64,256]{2,1,0:T(8,128)S(1)}, f32[4,64,256]{2,1,0:T(8,128)S(1)}, u32[]{:S(2)}, u32[]{:S(2)}) collective-permute-start(f32[4,64,256]{2,1,0:T(8,128)S(1)} %get-tuple-element.75), channel_id=1, source_target_pairs={{0,64},{64,128},{128,192},{192,0},{1,65},{65,129},{129,193},{193,1... | collective-permute-start | bytes 786440 | tf_op jit(solution)/shard_map/ppermute | solution.py:371
  19.2 13.7 %collective-permute-start.4 = (f32[4,64,256]{2,1,0:T(8,128)S(1)}, f32[4,64,256]{2,1,0:T(8,128)S(1)}, u32[]{:S(2)}, u32[]{:S(2)}) collective-permute-start(f32[4,64,256]{2,1,0:T(8,128)S(1)} %get-tuple-element.76), channel_id=1, source_target_pairs={{0,192},{64,0},{128,64},{192,128},{1,193},{65,1},{129,65},{193,129... | collective-permute-start | bytes 786440 | tf_op jit(solution)/shard_map/ppermute | solution.py:371
  23.6 13.8 %all-to-all-start = ((f32[8,2,64,128]{3,2,1,0:T(8,128)}), f32[8,2,64,128]{3,2,1,0:T(8,128)S(1)}, u32[]{:S(2)}, u32[]{:S(2)}) async-start(f32[8,2,64,128]{3,2,1,0:T(8,128)} %bitcast.4), calls=%async_computation | async-start | bytes 1048576 | tf_op jit(solution)/shard_map/all_to_all | solution.py:442
  28.5 71.9 %all-gather.2.cloned.1.call-start = ((), (), s32[]{:S(2)}) async-start(), calls=%async_computation.6 | async-start | bytes 4456448 | tf_op jit(solution)/shard_map/all_gather | solution.py:445
  37.4 37.1 %copy-start.3 = (f32[64,2048]{1,0:T(8,128)}, f32[64,2048]{1,0:T(8,128)S(1)}, u32[]{:S(2)}) copy-start(f32[64,2048]{1,0:T(8,128)S(1)} %collective-permute-done.up_ref.refs_2_) | copy-start | bytes 1572868
  40.0 34.5 %copy-start.4 = (f32[64,2048]{1,0:T(8,128)}, f32[64,2048]{1,0:T(8,128)S(1)}, u32[]{:S(2)}) copy-start(f32[64,2048]{1,0:T(8,128)S(1)} %collective-permute-done.1.down_ref.refs_3_) | copy-start | bytes 1572868
  41.6 20.7 %collective-permute-start.7 = (f32[8,64,256]{2,1,0:T(8,128)S(1)}, f32[8,64,256]{2,1,0:T(8,128)}, u32[]{:S(2)}, u32[]{:S(2)}) collective-permute-start(f32[8,64,256]{2,1,0:T(8,128)S(1)} %get-tuple-element.82), channel_id=1, source_target_pairs={{0,128},{64,192},{128,0},{192,64},{1,129},{65,193},{129,1},{193,65... | collective-permute-start | bytes 1572872 | tf_op jit(solution)/shard_map/ppermute | solution.py:371
  43.8 21.8 %collective-permute-start.8 = (f32[8,64,256]{2,1,0:T(8,128)S(1)}, f32[8,64,256]{2,1,0:T(8,128)}, u32[]{:S(2)}, u32[]{:S(2)}) collective-permute-start(f32[8,64,256]{2,1,0:T(8,128)S(1)} %get-tuple-element.83), channel_id=1, source_target_pairs={{0,64},{64,128},{128,192},{192,0},{1,65},{65,129},{129,193},{193,1... | collective-permute-start | bytes 1572872 | tf_op jit(solution)/shard_map/ppermute | solution.py:371
  43.9 22.2 %collective-permute-start.9 = (f32[8,64,256]{2,1,0:T(8,128)S(1)}, f32[8,64,256]{2,1,0:T(8,128)}, u32[]{:S(2)}, u32[]{:S(2)}) collective-permute-start(f32[8,64,256]{2,1,0:T(8,128)S(1)} %get-tuple-element.84), channel_id=1, source_target_pairs={{0,192},{64,0},{128,64},{192,128},{1,193},{65,1},{129,65},{193,129... | collective-permute-start | bytes 1572872 | tf_op jit(solution)/shard_map/ppermute | solution.py:371
  45.8 13.0 %collective-permute-start.5 = (f32[64,1024]{1,0:T(8,128)}, f32[64,1024]{1,0:T(8,128)S(1)}, u32[]{:S(2)}, u32[]{:S(2)}) collective-permute-start(f32[64,1024]{1,0:T(8,128)} %get-tuple-element.80), channel_id=1, source_target_pairs={{0,48},{16,0},{32,16},{48,32},{1,49},{17,1},{33,17},{49,33},{2,50}... | collective-permute-start | bytes 786440 | tf_op jit(solution)/shard_map/ppermute | solution.py:371
  48.0 14.3 %collective-permute-start.6 = (f32[64,1024]{1,0:T(8,128)S(1)}, f32[64,1024]{1,0:T(8,128)S(1)}, u32[]{:S(2)}, u32[]{:S(2)}) collective-permute-start(f32[64,1024]{1,0:T(8,128)S(1)} %get-tuple-element.81), channel_id=1, source_target_pairs={{0,16},{16,32},{32,48},{48,0},{1,17},{17,33},{33,49},{49,1},{2,18}... | collective-permute-start | bytes 786440 | tf_op jit(solution)/shard_map/ppermute | solution.py:371
  58.7 15.8 %copy-start.6 = (f32[64,1024]{1,0:T(8,128)}, f32[64,1024]{1,0:T(8,128)S(1)}, u32[]{:S(2)}) copy-start(f32[64,1024]{1,0:T(8,128)S(1)} %collective-permute-done.5.refs_0_.lo_ref) | copy-start | bytes 786436
  62.3 12.2 %copy-start.7 = (f32[64,1024]{1,0:T(8,128)}, f32[64,1024]{1,0:T(8,128)S(1)}, u32[]{:S(2)}) copy-start(f32[64,1024]{1,0:T(8,128)S(1)} %collective-permute-done.6.refs_1_.hi_ref) | copy-start | bytes 786436
  66.7 18.0 %collective-permute-start.11 = (f32[4,64,256]{2,1,0:T(8,128)S(1)}, f32[4,64,256]{2,1,0:T(8,128)S(1)}, u32[]{:S(2)}, u32[]{:S(2)}) collective-permute-start(f32[4,64,256]{2,1,0:T(8,128)S(1)} %get-tuple-element.96), channel_id=1, source_target_pairs={{0,128},{64,192},{128,0},{192,64},{1,129},{65,193},{129,1},{193,65... | collective-permute-start | bytes 786440 | tf_op jit(solution)/shard_map/ppermute | solution.py:371
  68.9 15.8 %collective-permute-start.12 = (f32[4,64,256]{2,1,0:T(8,128)S(1)}, f32[4,64,256]{2,1,0:T(8,128)S(1)}, u32[]{:S(2)}, u32[]{:S(2)}) collective-permute-start(f32[4,64,256]{2,1,0:T(8,128)S(1)} %get-tuple-element.97), channel_id=1, source_target_pairs={{0,64},{64,128},{128,192},{192,0},{1,65},{65,129},{129,193},{193,1... | collective-permute-start | bytes 786440 | tf_op jit(solution)/shard_map/ppermute | solution.py:371
  70.6 14.1 %collective-permute-start.13 = (f32[4,64,256]{2,1,0:T(8,128)S(1)}, f32[4,64,256]{2,1,0:T(8,128)S(1)}, u32[]{:S(2)}, u32[]{:S(2)}) collective-permute-start(f32[4,64,256]{2,1,0:T(8,128)S(1)} %get-tuple-element.98), channel_id=1, source_target_pairs={{0,192},{64,0},{128,64},{192,128},{1,193},{65,1},{129,65},{193,129... | collective-permute-start | bytes 786440 | tf_op jit(solution)/shard_map/ppermute | solution.py:371
  70.9 13.8 %collective-permute-start.10 = (f32[8,64,128]{2,1,0:T(8,128)S(1)}, f32[8,64,128]{2,1,0:T(8,128)S(1)}, u32[]{:S(2)}, u32[]{:S(2)}) collective-permute-start(f32[8,64,128]{2,1,0:T(8,128)S(1)} %get-tuple-element.94), channel_id=1, source_target_pairs={{0,2},{2,0},{1,3},{3,1},{4,6},{6,4},{5,7},{7,5},{8,10},{10,8},{9,1... | collective-permute-start | bytes 786440 | tf_op jit(solution)/shard_map/ppermute | solution.py:371
  74.5 10.2 %copy-start = (bf16[12,256,256]{2,1,0:T(8,128)(2,1)S(1)}, bf16[12,256,256]{2,1,0:T(8,128)(2,1)}, u32[]{:S(2)}) copy-start(bf16[12,256,256]{2,1,0:T(8,128)(2,1)} %shard_map.86.tiles_ref) | copy-start | bytes 4718596
  74.5 10.2 %copy-start.13 = (s32[12]{0:T(128)S(1)}, s32[12]{0:T(128)}, u32[]{:S(2)}) copy-start(s32[12]{0:T(128)} %reshape.219.refs_ref) | copy-start | bytes 148
  84.7 15.7 %copy-start.24 = (f32[8,64,128]{2,1,0:T(8,128)}, f32[8,64,128]{2,1,0:T(8,128)S(1)}, u32[]{:S(2)}) copy-start(f32[8,64,128]{2,1,0:T(8,128)S(1)} %collective-permute-done.10.other_ref) | copy-start | bytes 786436
  100.4 12.2 %copy-start.15 = (f32[16,64,128]{2,1,0:T(8,128)S(1)}, f32[16,64,128]{2,1,0:T(8,128)}, u32[]{:S(2)}) copy-start(f32[16,64,128]{2,1,0:T(8,128)} %all_to_all.30) | copy-start | bytes 1572868
  106.6 15.9 %all-to-all-start.2 = ((f32[16,64,128]{2,1,0:T(8,128)}), f32[16,64,128]{2,1,0:T(8,128)S(1)}, u32[]{:S(2)}, u32[]{:S(2)}) async-start(f32[16,64,128]{2,1,0:T(8,128)} %get-tuple-element.102), calls=%async_computation.2 | async-start | bytes 1048576 | tf_op jit(solution)/shard_map/all_to_all | solution.py:379
  112.7 2.0 collective-permute-start.15
  114.0 2.0 collective-permute-start.14
  122.4 43.7 %all-to-all-start.3 = ((f32[8,64,1280]{2,1,0:T(8,128)}), f32[8,64,1280]{2,1,0:T(8,128)}, u32[]{:S(2)}, u32[]{:S(2)}) async-start(f32[8,64,1280]{2,1,0:T(8,128)} %shard_map.92), calls=%async_computation.3 | async-start | bytes 5242880 | tf_op jit(solution)/shard_map/all_to_all | solution.py:472
  129.2 11.7 %collective-permute-start.16 = (f32[4,64,256]{2,1,0:T(8,128)S(1)}, f32[4,64,256]{2,1,0:T(8,128)S(1)}, u32[]{:S(2)}, u32[]{:S(2)}) collective-permute-start(f32[4,64,256]{2,1,0:T(8,128)S(1)} %get-tuple-element.106), channel_id=1, source_target_pairs={{0,128},{64,192},{128,0},{192,64},{1,129},{65,193},{129,1},{193,65... | collective-permute-start | bytes 786440 | tf_op jit(solution)/shard_map/ppermute | solution.py:371
  130.9 13.3 %collective-permute-start.17 = (f32[4,64,256]{2,1,0:T(8,128)S(1)}, f32[4,64,256]{2,1,0:T(8,128)S(1)}, u32[]{:S(2)}, u32[]{:S(2)}) collective-permute-start(f32[4,64,256]{2,1,0:T(8,128)S(1)} %get-tuple-element.107), channel_id=1, source_target_pairs={{0,192},{64,0},{128,64},{192,128},{1,193},{65,1},{129,65},{193,129... | collective-permute-start | bytes 786440 | tf_op jit(solution)/shard_map/ppermute | solution.py:371
  133.0 11.6 %collective-permute-start.18 = (f32[4,64,256]{2,1,0:T(8,128)S(1)}, f32[4,64,256]{2,1,0:T(8,128)S(1)}, u32[]{:S(2)}, u32[]{:S(2)}) collective-permute-start(f32[4,64,256]{2,1,0:T(8,128)S(1)} %get-tuple-element.108), channel_id=1, source_target_pairs={{0,64},{64,128},{128,192},{192,0},{1,65},{65,129},{129,193},{193,1... | collective-permute-start | bytes 786440 | tf_op jit(solution)/shard_map/ppermute | solution.py:371
  140.8 30.9 %copy-start.9 = (f32[8,64,256]{2,1,0:T(8,128)S(1)}, f32[8,64,256]{2,1,0:T(8,128)}, u32[]{:S(2)}) copy-start(f32[8,64,256]{2,1,0:T(8,128)} %get-tuple-element.128.up_ref) | copy-start | bytes 1572868
  140.8 30.9 %copy-start.10 = (f32[8,64,256]{2,1,0:T(8,128)S(1)}, f32[8,64,256]{2,1,0:T(8,128)}, u32[]{:S(2)}) copy-start(f32[8,64,256]{2,1,0:T(8,128)} %get-tuple-element.129.down_ref) | copy-start | bytes 1572868
  144.7 27.0 %collective-permute-start.19 = (f32[8,64,256]{2,1,0:T(8,128)}, f32[8,64,256]{2,1,0:T(8,128)S(1)}, u32[]{:S(2)}, u32[]{:S(2)}) collective-permute-start(f32[8,64,256]{2,1,0:T(8,128)} %get-tuple-element.112), channel_id=1, source_target_pairs={{0,128},{64,192},{128,0},{192,64},{1,129},{65,193},{129,1},{193,65... | collective-permute-start | bytes 1572872 | tf_op jit(solution)/shard_map/ppermute | solution.py:371
  146.0 25.7 %collective-permute-start.20 = (f32[8,64,256]{2,1,0:T(8,128)}, f32[8,64,256]{2,1,0:T(8,128)S(1)}, u32[]{:S(2)}, u32[]{:S(2)}) collective-permute-start(f32[8,64,256]{2,1,0:T(8,128)} %get-tuple-element.113), channel_id=1, source_target_pairs={{0,192},{64,0},{128,64},{192,128},{1,193},{65,1},{129,65},{193,129... | collective-permute-start | bytes 1572872 | tf_op jit(solution)/shard_map/ppermute | solution.py:371
  148.2 23.6 %collective-permute-start.21 = (f32[8,64,256]{2,1,0:T(8,128)}, f32[8,64,256]{2,1,0:T(8,128)S(1)}, u32[]{:S(2)}, u32[]{:S(2)}) collective-permute-start(f32[8,64,256]{2,1,0:T(8,128)} %get-tuple-element.114), channel_id=1, source_target_pairs={{0,64},{64,128},{128,192},{192,0},{1,65},{65,129},{129,193},{193,1... | collective-permute-start | bytes 1572872 | tf_op jit(solution)/shard_map/ppermute | solution.py:371
  151.5 20.2 %collective-permute-start.22 = (f32[4,64,256]{2,1,0:T(8,128)}, f32[4,64,256]{2,1,0:T(8,128)S(1)}, u32[]{:S(2)}, u32[]{:S(2)}) collective-permute-start(f32[4,64,256]{2,1,0:T(8,128)} %get-tuple-element.120), channel_id=1, source_target_pairs={{0,16},{16,32},{32,48},{48,0},{1,17},{17,33},{33,49},{49,1},{2,18}... | collective-permute-start | bytes 786440 | tf_op jit(solution)/shard_map/ppermute | solution.py:371
  152.7 19.1 %collective-permute-start.23 = (f32[4,64,256]{2,1,0:T(8,128)S(1)}, f32[4,64,256]{2,1,0:T(8,128)S(1)}, u32[]{:S(2)}, u32[]{:S(2)}) collective-permute-start(f32[4,64,256]{2,1,0:T(8,128)S(1)} %get-tuple-element.121), channel_id=1, source_target_pairs={{0,48},{16,0},{32,16},{48,32},{1,49},{17,1},{33,17},{49,33},{2,50}... | collective-permute-start | bytes 786440 | tf_op jit(solution)/shard_map/ppermute | solution.py:371
  171.7 15.7 %copy-start.23 = (f32[4,64,256]{2,1,0:T(8,128)S(1)}, f32[4,64,256]{2,1,0:T(8,128)}, u32[]{:S(2)}) copy-start(f32[4,64,256]{2,1,0:T(8,128)} %get-tuple-element.140) | copy-start | bytes 786436
  173.6 27.4 %copy-start.8 = (f32[8,64,256]{2,1,0:T(8,128)S(1)}, f32[8,64,256]{2,1,0:T(8,128)}, u32[]{:S(2)}) copy-start(f32[8,64,256]{2,1,0:T(8,128)} %get-tuple-element.141.diag_ref) | copy-start | bytes 1572868
  173.6 34.5 %collective-permute-start.27 = (f32[8,64,256]{2,1,0:T(8,128)}, f32[8,64,256]{2,1,0:T(8,128)S(1)}, u32[]{:S(2)}, u32[]{:S(2)}) collective-permute-start(f32[8,64,256]{2,1,0:T(8,128)} %get-tuple-element.142), channel_id=1, source_target_pairs={{0,16},{16,32},{32,48},{48,0},{1,17},{17,33},{33,49},{49,1},{2,18}... | collective-permute-start | bytes 1572872 | tf_op jit(solution)/shard_map/ppermute | solution.py:371
  174.6 33.5 %collective-permute-start.28 = (f32[8,64,256]{2,1,0:T(8,128)}, f32[8,64,256]{2,1,0:T(8,128)S(1)}, u32[]{:S(2)}, u32[]{:S(2)}) collective-permute-start(f32[8,64,256]{2,1,0:T(8,128)} %get-tuple-element.143), channel_id=1, source_target_pairs={{0,48},{16,0},{32,16},{48,32},{1,49},{17,1},{33,17},{49,33},{2,50}... | collective-permute-start | bytes 1572872 | tf_op jit(solution)/shard_map/ppermute | solution.py:371
  178.5 14.8 %all-to-all-start.4 = ((f32[4,64,256]{2,1,0:T(8,128)}), f32[4,64,256]{2,1,0:T(8,128)S(1)}, u32[]{:S(2)}, u32[]{:S(2)}) async-start(f32[4,64,256]{2,1,0:T(8,128)} %copy.42), calls=%async_computation.4 | async-start | bytes 524288 | tf_op jit(solution)/shard_map/all_to_all | solution.py:488
  183.9 17.1 %collective-permute-start.24 = (f32[4,64,256]{2,1,0:T(8,128)}, f32[4,64,256]{2,1,0:T(8,128)S(1)}, u32[]{:S(2)}, u32[]{:S(2)}) collective-permute-start(f32[4,64,256]{2,1,0:T(8,128)} %get-tuple-element.138), channel_id=1, source_target_pairs={{0,128},{64,192},{128,0},{192,64},{1,129},{65,193},{129,1},{193,65... | collective-permute-start | bytes 786440 | tf_op jit(solution)/shard_map/ppermute | solution.py:371
  185.9 15.0 %collective-permute-start.25 = (f32[4,64,256]{2,1,0:T(8,128)}, f32[4,64,256]{2,1,0:T(8,128)S(1)}, u32[]{:S(2)}, u32[]{:S(2)}) collective-permute-start(f32[4,64,256]{2,1,0:T(8,128)} %get-tuple-element.139), channel_id=1, source_target_pairs={{0,192},{64,0},{128,64},{192,128},{1,193},{65,1},{129,65},{193,129... | collective-permute-start | bytes 786440 | tf_op jit(solution)/shard_map/ppermute | solution.py:371
  187.4 13.6 %collective-permute-start.26 = (f32[4,64,256]{2,1,0:T(8,128)S(1)}, f32[4,64,256]{2,1,0:T(8,128)S(1)}, u32[]{:S(2)}, u32[]{:S(2)}) collective-permute-start(f32[4,64,256]{2,1,0:T(8,128)S(1)} %copy-done.23), channel_id=1, source_target_pairs={{0,64},{64,128},{128,192},{192,0},{1,65},{65,129},{129,193},{193,1... | collective-permute-start | bytes 786440 | tf_op jit(solution)/shard_map/ppermute | solution.py:371
  194.2 13.1 %all-to-all-start.5 = ((f32[4,32,128]{2,1,0:T(8,128)}), f32[4,32,128]{2,1,0:T(8,128)S(1)}, u32[]{:S(2)}, u32[]{:S(2)}) async-start(f32[4,32,128]{2,1,0:T(8,128)} %reshape.230), calls=%async_computation.5 | async-start | bytes 131072 | tf_op jit(solution)/shard_map/all_to_all | solution.py:490
  (12 other events, 43.7 us)
Sparse Core Ops, SparseCore 0:
  40.2 45.3 all-gather.1

commit v8 on v7

--- a/solution.py
+++ b/solution.py
@@ -112,53 +112,49 @@
 
 
 def mixed_kernel(place_ref, own_ref, *refs):
-    sources, tiles_ref, out_ref, held, sems = refs[:10], *refs[10:]
-    i = pl.program_id(0)
-
-    @pl.when(i == 0)
-    def _():
-        copies, block = [], 0
-        for ref in sources:
-            if len(ref.shape) == 3:
-                copies.append(pltpu.make_async_copy(ref, held.at[pl.ds(block, ref.shape[0])], sems.at[len(copies)]))
-                block += ref.shape[0]
-                continue
-            for start in range(0, ref.shape[1], W):
-                copies.append(pltpu.make_async_copy(ref.at[:, pl.ds(start, W)], held.at[block], sems.at[len(copies)]))
-                block += 1
-        for copy in copies:
-            copy.start()
-        held[FAR] = jnp.zeros((C, W), f32)
-        for copy in copies:
-            copy.wait()
-
-    for j in range(2):
+    sources, tiles_ref, out_ref, held, tiles, sems, tile_sems = refs[:10], *refs[10:]
+    tile_copies = [pltpu.make_async_copy(tiles_ref.at[i], tiles.at[i], tile_sems.at[i]) for i in range(BLK)]
+    copies, block = [], 0
+    for ref in sources:
+        if len(ref.shape) == 3:
+            copies.append(pltpu.make_async_copy(ref, held.at[pl.ds(block, ref.shape[0])], sems.at[len(copies)]))
+            block += ref.shape[0]
+            continue
+        for start in range(0, ref.shape[1], W):
+            copies.append(pltpu.make_async_copy(ref.at[:, pl.ds(start, W)], held.at[block], sems.at[len(copies)]))
+            block += 1
+    for copy in copies + tile_copies:
+        copy.start()
+    held[FAR] = jnp.zeros((C, W), f32)
+    for copy in copies:
+        copy.wait()
+    for i in range(BLK):
+        tile_copies[i].wait()
         acc = None
         for k in range(FAN):
-            block = own_ref[:, j * W : (j + 1) * W] if k == 0 else held[place_ref[(2 * i + j) * (FAN - 1) + k - 1]]
+            block = own_ref[:, i * W : (i + 1) * W] if k == 0 else held[place_ref[i * (FAN - 1) + k - 1]]
             part = lax.dot_general(
+                tiles[i, k],
                 jnp.concatenate(split(block), axis=0),
-                tiles_ref[j, k],
                 (((1,), (1,)), ((), ())),
                 preferred_element_type=f32,
             )
             acc = part if acc is None else acc + part
-        out_ref[j] = acc[:C] + acc[C:]
+        out_ref[i] = (acc[:, :C] + acc[:, C:]).T
 
 
 def mix(place, own, sources, tiles):
     return pl.pallas_call(
         mixed_kernel,
-        grid_spec=pltpu.PrefetchScalarGridSpec(
-            num_scalar_prefetch=1,
-            grid=(BLK // 2,),
-            in_specs=[pl.BlockSpec((C, 2 * W), lambda i, s: (0, i))]
-            + [ANY] * len(sources)
-            + [pl.BlockSpec((2, FAN, W, W), lambda i, s: (i, 0, 0, 0))],
-            out_specs=pl.BlockSpec((2, C, W), lambda i, s: (i, 0, 0)),
-            scratch_shapes=[pltpu.VMEM((HELD, C, W), f32), pltpu.SemaphoreType.DMA((30,))],
-        ),
+        in_specs=[SMEM, VMEM] + [ANY] * (len(sources) + 1),
+        out_specs=VMEM,
         out_shape=jax.ShapeDtypeStruct((BLK, C, W), f32),
+        scratch_shapes=[
+            pltpu.VMEM((HELD, C, W), f32),
+            pltpu.VMEM((BLK, FAN, W, W), bf16),
+            pltpu.SemaphoreType.DMA((30,)),
+            pltpu.SemaphoreType.DMA((BLK,)),
+        ],
         compiler_params=PARAMS,
         cost_estimate=pl.CostEstimate(flops=2 * 64 * W * W * 2 * C, bytes_accessed=13 << 20, transcendentals=0),
     )(place, own, *sources, tiles)

time: 217 us -> 219 us (level)
  Pallas kernels: 41.9 us -> 44.8 us
    pallas_call x1, Pallas kernels: 10.1 us -> 13 us  [mix(): pl.pallas_call(mixed_kernel, in_specs=[SMEM, VMEM] + [ANY] * (len(sources...]
  transfers between devices with their start and end apart: 35 -> 35, of which waited for: 14 -> 13; matrix products, arithmetic and copies ran while one was open for 8% -> 8% of each run, Pallas kernels for 16% -> 17%
where the time goes in v8:
time: 219 us; the launch traced here: 218 us
  starting transfers between devices  70.9 us (32%)
  waiting for transfers between devices  51.3 us (23%)
  Pallas kernels  44.8 us (20%)
  local copies, waits for them, and re-layouts  19 us (9%)
  between operations  14.5 us (7%)
  blocking collectives  13.1 us (6%)
  other arithmetic  4.05 us (2%)
    ppermute x29, starting transfers between devices, shift(): lax.ppermute(value, axis, [(i, (i + by) % size) for i in range(size)])  45.3 us
    ppermute x29, waiting for transfers between devices, shift(): lax.ppermute(value, axis, [(i, (i + by) % size) for i in range(size)])  24.3 us
    all_to_all x1, blocking collectives, over_col(): return lax.all_to_all(value, COL, 0, 0, tiled=True)  13.1 us
    pallas_call x1, Pallas kernels, mix(): pl.pallas_call(mixed_kernel, in_specs=[SMEM, VMEM] + [ANY] * (len(sources...  13 us
    all_to_all x1, waiting for transfers between devices, on_device(): grad = lax.all_to_all(grad, ('y', 'zl'), 0, 0, tiled=True)  10.7 us
    pallas_call x1, Pallas kernels, push(): pl.pallas_call(push_kernel, in_specs=[SMEM, VMEM, ANY], out_specs=[VMEM]...  7.77 us
    unnamed x53, local copies, waits for them, and re-layouts  7.48 us
    all_to_all x1, waiting for transfers between devices, on_device(): grad = lax.all_to_all(grad, 'x', 0, 0, tiled=True).sum(axis=0)  6.34 us
  transfers between devices with their start and end apart: 35, of which 13 were waited for; matrix products, arithmetic and copies ran while one was open for 8% of the time, Pallas kernels for 17%

profile of v8, /device:TPU:10, one launch (start us, length us, event | category | flops | bytes accessed | tf_op | source)
XLA Modules:
  0.0 217.7 jit_solution(1035803289473448754)
XLA Ops:
  7.2 6.4 %collective-permute-start = (f32[64,2048]{1,0:T(8,128)}, f32[64,2048]{1,0:T(8,128)S(1)}, u32[]{:S(2)}, u32[]{:S(2)}) collective-permute-start(f32[64,2048]{1,0:T(8,128)} %bitcast.46), channel_id=1, source_target_pairs={{0,48},{16,0},{32,16},{48,32},{1,49},{17,1},{33,17},{49,33},{2,50}... | collective-permute-start | bytes 1572872 | tf_op jit(solution)/shard_map/ppermute | solution.py:367
  16.9 2.2 %collective-permute-start.2 = (f32[4,64,256]{2,1,0:T(8,128)S(1)}, f32[4,64,256]{2,1,0:T(8,128)S(1)}, u32[]{:S(2)}, u32[]{:S(2)}) collective-permute-start(f32[4,64,256]{2,1,0:T(8,128)S(1)} %get-tuple-element.74), channel_id=1, source_target_pairs={{0,128},{64,192},{128,0},{192,64},{1,129},{65,193},{129,1},{193,65... | collective-permute-start | bytes 786440 | tf_op jit(solution)/shard_map/ppermute | solution.py:367
  19.2 2.0 collective-permute-start.4
  21.2 1.5 reshape.217
  23.6 4.9 %all-to-all-start = ((f32[8,2,64,128]{3,2,1,0:T(8,128)}), f32[8,2,64,128]{3,2,1,0:T(8,128)S(1)}, u32[]{:S(2)}, u32[]{:S(2)}) async-start(f32[8,2,64,128]{3,2,1,0:T(8,128)} %bitcast.4), calls=%async_computation | async-start | bytes 1048576 | tf_op jit(solution)/shard_map/all_to_all | solution.py:438
  29.4 3.4 %shard_map.86.tiles_ref = bf16[12,256,256]{2,1,0:T(8,128)(2,1)} custom-call(s32[12]{0:T(128)} %reshape.219.refs_ref, bf16[8,8,256,256]{3,2,1,0:T(8,128)(2,1)} %tiles_ref.3), custom_call_target="tpu_custom_call" | custom-call | bytes 3145728 | tf_op jit(solution)/shard_map/pallas_call | solution.py:178
  32.9 4.5 %all-to-all-done = f32[8,2,64,128]{3,2,1,0:T(8,128)S(1)} async-done(((f32[8,2,64,128]{3,2,1,0:T(8,128)}), f32[8,2,64,128]{3,2,1,0:T(8,128)S(1)}, u32[]{:S(2)}, u32[]{:S(2)}) %all-to-all-start) | async-done | bytes 524320 | tf_op jit(solution)/shard_map/all_to_all | solution.py:438
  37.4 2.6 %collective-permute-done.1.down_ref.refs_3_ = f32[64,2048]{1,0:T(8,128)S(1)} collective-permute-done((f32[64,2048]{1,0:T(8,128)}, f32[64,2048]{1,0:T(8,128)S(1)}, u32[]{:S(2)}, u32[]{:S(2)}) %collective-permute-start.1) | collective-permute-done | bytes 524320 | tf_op jit(solution)/shard_map/ppermute | solution.py:367
  40.2 1.4 shard_map.87
  41.6 2.1 collective-permute-start.7
  43.9 1.9 collective-permute-start.9
  45.8 2.2 %collective-permute-start.5 = (f32[64,1024]{1,0:T(8,128)}, f32[64,1024]{1,0:T(8,128)S(1)}, u32[]{:S(2)}, u32[]{:S(2)}) collective-permute-start(f32[64,1024]{1,0:T(8,128)} %get-tuple-element.80), channel_id=1, source_target_pairs={{0,48},{16,0},{32,16},{48,32},{1,49},{17,1},{33,17},{49,33},{2,50}... | collective-permute-start | bytes 786440 | tf_op jit(solution)/shard_map/ppermute | solution.py:367
  48.8 1.8 dynamic-slice_bitcast_fusion
  50.6 8.1 %collective-permute-done.5.refs_0_.lo_ref = f32[64,1024]{1,0:T(8,128)S(1)} collective-permute-done((f32[64,1024]{1,0:T(8,128)}, f32[64,1024]{1,0:T(8,128)S(1)}, u32[]{:S(2)}, u32[]{:S(2)}) %collective-permute-start.5) | collective-permute-done | bytes 262176 | tf_op jit(solution)/shard_map/ppermute | solution.py:367
  58.7 3.5 %collective-permute-done.6.refs_1_.hi_ref = f32[64,1024]{1,0:T(8,128)S(1)} collective-permute-done((f32[64,1024]{1,0:T(8,128)S(1)}, f32[64,1024]{1,0:T(8,128)S(1)}, u32[]{:S(2)}, u32[]{:S(2)}) %collective-permute-start.6) | collective-permute-done | bytes 262176 | tf_op jit(solution)/shard_map/ppermute | solution.py:367
  62.3 3.2 %collective-permute-done.8.refs_8_ = f32[8,64,256]{2,1,0:T(8,128)} collective-permute-done((f32[8,64,256]{2,1,0:T(8,128)S(1)}, f32[8,64,256]{2,1,0:T(8,128)}, u32[]{:S(2)}, u32[]{:S(2)}) %collective-permute-start.8) | collective-permute-done | bytes 524320 | tf_op jit(solution)/shard_map/ppermute | solution.py:367
  66.7 2.2 collective-permute-start.11
  68.9 1.7 collective-permute-start.12
  70.9 3.0 %collective-permute-start.10 = (f32[8,64,128]{2,1,0:T(8,128)S(1)}, f32[8,64,128]{2,1,0:T(8,128)S(1)}, u32[]{:S(2)}, u32[]{:S(2)}) collective-permute-start(f32[8,64,128]{2,1,0:T(8,128)S(1)} %get-tuple-element.94), channel_id=1, source_target_pairs={{0,2},{2,0},{1,3},{3,1},{4,6},{6,4},{5,7},{7,5},{8,10},{10,8},{9,1... | collective-permute-start | bytes 786440 | tf_op jit(solution)/shard_map/ppermute | solution.py:367
  74.5 13.0 %shard_map.88.part_ref = f32[8,64,256]{2,1,0:T(8,128)} custom-call(s32[56]{0:T(128)} %fusion.5.place_ref, f32[64,2048]{1,0:T(8,128)} %bitcast.48, f32[64,1024]{1,0:T(8,128)} %copy-done.6, f32[64,1024]{1,0:T(8,128)} %copy-done.7, f32[64,2048]{1,0:T(8,128)} %copy-done.3, f32[64,2048]{1,0:T(8,128)} %copy-done.4, f32[4,64,256]{2,1,0:T(8,128)} %copy-done.19, ...), custom_call_target="tpu_custom_call" | custom-call | flops 1073741824 | bytes 13631488 | tf_op jit(solution)/shard_map/pallas_call | solution.py:147
  87.7 1.1 copy-done.5
  88.7 1.2 shard_map.90
  90.0 13.1 %all_to_all.30 = f32[16,64,128]{2,1,0:T(8,128)} all-to-all(f32[16,64,128]{2,1,0:T(8,128)S(1)} %shard_map.90), channel_id=1, replica_groups=mesh['x'=4,'zh'=4,'y'=4,'zl'=2,'c'=2] {'y','zl','c'}, dimensions={0} | all-to-all | bytes 1048576 | tf_op jit(solution)/shard_map/all_to_all | solution.py:375
  103.1 6.1 %shard_map.91 = (f32[1024,256]{1,0:T(8,128)}, f32[16,64,128]{2,1,0:T(8,128)}) custom-call(f32[1024,1024]{1,0:T(8,128)} %all-gather.2.cloned.1.call-done.weight_ref, f32[1024,128]{1,0:T(8,128)} %bitcast.52, s32[1]{0:T(128)} %bitcast.12.zl_ref, f32[8,64,128]{2,1,0:T(8,128)} %get-tuple-element.100.mine_ref, f32[8,64,128]{2,1,0:T(8,128)} %copy-done.24), custom_call_target="tpu_custom_call" | custom-call | flops 1610612736 | bytes 8388608 | tf_op jit(solution)/shard_map/pallas_call | solution.py:249
  109.2 6.1 %all-to-all-start.2 = ((f32[16,64,128]{2,1,0:T(8,128)}), f32[16,64,128]{2,1,0:T(8,128)S(1)}, u32[]{:S(2)}, u32[]{:S(2)}) async-start(f32[16,64,128]{2,1,0:T(8,128)} %get-tuple-element.102), calls=%async_computation.2 | async-start | bytes 1048576 | tf_op jit(solution)/shard_map/all_to_all | solution.py:375
  117.3 1.3 collective-permute-done.14.other_ref
  119.4 5.7 %shard_map.92 = f32[8,64,1280]{2,1,0:T(8,128)} custom-call(s32[1]{0:T(128)} %bitcast.13.core_ref, f32[8,2,64,256]{3,2,1,0:T(8,128)} %bitcast.51, f32[512,256]{1,0:T(8,128)} %copy-done.18, f32[1024,128]{1,0:T(8,128)} %bitcast.53, f32[1024,128]{1,0:T(8,128)} %copy-done.17), custom_call_target="tpu_custom_call" | custom-call | flops 805306368 | bytes 4194304 | tf_op jit(solution)/shard_map/pallas_call | solution.py:403
  125.1 5.8 %all-to-all-start.3 = ((f32[8,64,1280]{2,1,0:T(8,128)}), f32[8,64,1280]{2,1,0:T(8,128)}, u32[]{:S(2)}, u32[]{:S(2)}) async-start(f32[8,64,1280]{2,1,0:T(8,128)} %shard_map.92), calls=%async_computation.3 | async-start | bytes 5242880 | tf_op jit(solution)/shard_map/all_to_all | solution.py:468
  131.8 1.6 collective-permute-start.16
  133.4 1.5 collective-permute-start.17
  135.5 7.8 %shard_map.94 = (f32[8,64,256]{2,1,0:T(8,128)}, f32[4,64,256]{2,1,0:T(8,128)}, f32[4,64,256]{2,1,0:T(8,128)}, f32[8,64,256]{2,1,0:T(8,128)}, f32[8,64,256]{2,1,0...) custom-call(s32[56]{0:T(128)} %fusion.5.place_ref, ...), custom_call_target="tpu_custom_call" | custom-call | flops 1073741824 | bytes 13631488 | tf_op jit(solution)/shard_map/pallas_call | solution.py:306
  143.3 3.7 %collective-permute-done.17.b_ref = f32[4,64,256]{2,1,0:T(8,128)S(1)} collective-permute-done((f32[4,64,256]{2,1,0:T(8,128)S(1)}, f32[4,64,256]{2,1,0:T(8,128)S(1)}, u32[]{:S(2)}, u32[]{:S(2)}) %collective-permute-start.17) | collective-permute-done | bytes 262176 | tf_op jit(solution)/shard_map/ppermute | solution.py:367
  147.0 1.6 collective-permute-start.19
  148.6 1.4 collective-permute-start.20
  152.6 1.4 shard_map.95
  154.0 4.1 %collective-permute-start.23 = (f32[4,64,256]{2,1,0:T(8,128)S(1)}, f32[4,64,256]{2,1,0:T(8,128)S(1)}, u32[]{:S(2)}, u32[]{:S(2)}) collective-permute-start(f32[4,64,256]{2,1,0:T(8,128)S(1)} %get-tuple-element.121), channel_id=1, source_target_pairs={{0,48},{16,0},{32,16},{48,32},{1,49},{17,1},{33,17},{49,33},{2,50}... | collective-permute-start | bytes 786440 | tf_op jit(solution)/shard_map/ppermute | solution.py:367
  158.1 10.7 %all-to-all-done.3 = f32[8,64,1280]{2,1,0:T(8,128)} async-done(((f32[8,64,1280]{2,1,0:T(8,128)}), f32[8,64,1280]{2,1,0:T(8,128)}, u32[]{:S(2)}, u32[]{:S(2)}) %all-to-all-start.3) | async-done | bytes 2621472 | tf_op jit(solution)/shard_map/all_to_all | solution.py:468
  168.8 2.4 %slice_reduce_fusion = f32[64,1024]{1,0:T(8,128)} fusion(f32[8,64,1280]{2,1,0:T(8,128)} %all-to-all-done.3), kind=kLoop, calls=%fused_computation | loop fusion | flops 458752 | bytes 2359296 | tf_op jit(solution)/shard_map/reduce_sum | solution.py:477
  171.3 1.8 reshape.227
  173.9 1.8 shard_map.96
  176.0 4.0 %collective-permute-start.28 = (f32[8,64,256]{2,1,0:T(8,128)}, f32[8,64,256]{2,1,0:T(8,128)S(1)}, u32[]{:S(2)}, u32[]{:S(2)}) collective-permute-start(f32[8,64,256]{2,1,0:T(8,128)} %get-tuple-element.143), channel_id=1, source_target_pairs={{0,48},{16,0},{32,16},{48,32},{1,49},{17,1},{33,17},{49,33},{2,50}... | collective-permute-start | bytes 1572872 | tf_op jit(solution)/shard_map/ppermute | solution.py:367
  180.7 5.5 %all-to-all-start.4 = ((f32[4,64,256]{2,1,0:T(8,128)}), f32[4,64,256]{2,1,0:T(8,128)S(1)}, u32[]{:S(2)}, u32[]{:S(2)}) async-start(f32[4,64,256]{2,1,0:T(8,128)} %copy.42), calls=%async_computation.4 | async-start | bytes 524288 | tf_op jit(solution)/shard_map/all_to_all | solution.py:484
  186.2 2.1 collective-permute-start.24
  188.3 1.5 collective-permute-start.25
  190.3 6.3 %all-to-all-done.4 = f32[4,64,256]{2,1,0:T(8,128)S(1)} async-done(((f32[4,64,256]{2,1,0:T(8,128)}), f32[4,64,256]{2,1,0:T(8,128)S(1)}, u32[]{:S(2)}, u32[]{:S(2)}) %all-to-all-start.4) | async-done | bytes 262176 | tf_op jit(solution)/shard_map/all_to_all | solution.py:484
  197.7 3.3 %all-to-all-start.5 = ((f32[4,32,128]{2,1,0:T(8,128)}), f32[4,32,128]{2,1,0:T(8,128)S(1)}, u32[]{:S(2)}, u32[]{:S(2)}) async-start(f32[4,32,128]{2,1,0:T(8,128)} %reshape.230), calls=%async_computation.5 | async-start | bytes 131072 | tf_op jit(solution)/shard_map/all_to_all | solution.py:486
  200.9 1.1 slice_bitcast_fusion
  203.6 5.5 %all-to-all-done.5 = f32[4,32,128]{2,1,0:T(8,128)S(1)} async-done(((f32[4,32,128]{2,1,0:T(8,128)}), f32[4,32,128]{2,1,0:T(8,128)S(1)}, u32[]{:S(2)}, u32[]{:S(2)}) %all-to-all-start.5) | async-done | bytes 65568 | tf_op jit(solution)/shard_map/all_to_all | solution.py:486
  (138 shorter events, 21.9 us)
Async XLA Ops:
  7.2 21.4 %copy-start.22 = (s32[3]{0:T(128)S(1)}, s32[3]{0:T(128)}, u32[]{:S(2)}) copy-start(s32[3]{0:T(128)} %constant.71) | copy-start | bytes 40
  7.2 30.3 %collective-permute-start = (f32[64,2048]{1,0:T(8,128)}, f32[64,2048]{1,0:T(8,128)S(1)}, u32[]{:S(2)}, u32[]{:S(2)}) collective-permute-start(f32[64,2048]{1,0:T(8,128)} %bitcast.46), channel_id=1, source_target_pairs={{0,48},{16,0},{32,16},{48,32},{1,49},{17,1},{33,17},{49,33},{2,50}... | collective-permute-start | bytes 1572872 | tf_op jit(solution)/shard_map/ppermute | solution.py:367
  13.6 26.5 %collective-permute-start.1 = (f32[64,2048]{1,0:T(8,128)}, f32[64,2048]{1,0:T(8,128)S(1)}, u32[]{:S(2)}, u32[]{:S(2)}) collective-permute-start(f32[64,2048]{1,0:T(8,128)} %bitcast.47), channel_id=1, source_target_pairs={{0,16},{16,32},{32,48},{48,0},{1,17},{17,33},{33,49},{49,1},{2,18}... | collective-permute-start | bytes 1572872 | tf_op jit(solution)/shard_map/ppermute | solution.py:367
  16.9 15.9 %collective-permute-start.2 = (f32[4,64,256]{2,1,0:T(8,128)S(1)}, f32[4,64,256]{2,1,0:T(8,128)S(1)}, u32[]{:S(2)}, u32[]{:S(2)}) collective-permute-start(f32[4,64,256]{2,1,0:T(8,128)S(1)} %get-tuple-element.74), channel_id=1, source_target_pairs={{0,128},{64,192},{128,0},{192,64},{1,129},{65,193},{129,1},{193,65... | collective-permute-start | bytes 786440 | tf_op jit(solution)/shard_map/ppermute | solution.py:367
  19.2 13.7 %collective-permute-start.3 = (f32[4,64,256]{2,1,0:T(8,128)S(1)}, f32[4,64,256]{2,1,0:T(8,128)S(1)}, u32[]{:S(2)}, u32[]{:S(2)}) collective-permute-start(f32[4,64,256]{2,1,0:T(8,128)S(1)} %get-tuple-element.75), channel_id=1, source_target_pairs={{0,64},{64,128},{128,192},{192,0},{1,65},{65,129},{129,193},{193,1... | collective-permute-start | bytes 786440 | tf_op jit(solution)/shard_map/ppermute | solution.py:367
  19.2 13.7 %collective-permute-start.4 = (f32[4,64,256]{2,1,0:T(8,128)S(1)}, f32[4,64,256]{2,1,0:T(8,128)S(1)}, u32[]{:S(2)}, u32[]{:S(2)}) collective-permute-start(f32[4,64,256]{2,1,0:T(8,128)S(1)} %get-tuple-element.76), channel_id=1, source_target_pairs={{0,192},{64,0},{128,64},{192,128},{1,193},{65,1},{129,65},{193,129... | collective-permute-start | bytes 786440 | tf_op jit(solution)/shard_map/ppermute | solution.py:367
  23.6 13.8 %all-to-all-start = ((f32[8,2,64,128]{3,2,1,0:T(8,128)}), f32[8,2,64,128]{3,2,1,0:T(8,128)S(1)}, u32[]{:S(2)}, u32[]{:S(2)}) async-start(f32[8,2,64,128]{3,2,1,0:T(8,128)} %bitcast.4), calls=%async_computation | async-start | bytes 1048576 | tf_op jit(solution)/shard_map/all_to_all | solution.py:438
  28.5 74.6 %all-gather.2.cloned.1.call-start = ((), (), s32[]{:S(2)}) async-start(), calls=%async_computation.6 | async-start | bytes 4456448 | tf_op jit(solution)/shard_map/all_gather | solution.py:441
  37.4 37.1 %copy-start.3 = (f32[64,2048]{1,0:T(8,128)}, f32[64,2048]{1,0:T(8,128)S(1)}, u32[]{:S(2)}) copy-start(f32[64,2048]{1,0:T(8,128)S(1)} %collective-permute-done.up_ref.refs_2_) | copy-start | bytes 1572868
  40.0 34.4 %copy-start.4 = (f32[64,2048]{1,0:T(8,128)}, f32[64,2048]{1,0:T(8,128)S(1)}, u32[]{:S(2)}) copy-start(f32[64,2048]{1,0:T(8,128)S(1)} %collective-permute-done.1.down_ref.refs_3_) | copy-start | bytes 1572868
  41.6 20.7 %collective-permute-start.7 = (f32[8,64,256]{2,1,0:T(8,128)S(1)}, f32[8,64,256]{2,1,0:T(8,128)}, u32[]{:S(2)}, u32[]{:S(2)}) collective-permute-start(f32[8,64,256]{2,1,0:T(8,128)S(1)} %get-tuple-element.82), channel_id=1, source_target_pairs={{0,128},{64,192},{128,0},{192,64},{1,129},{65,193},{129,1},{193,65... | collective-permute-start | bytes 1572872 | tf_op jit(solution)/shard_map/ppermute | solution.py:367
  43.7 21.8 %collective-permute-start.8 = (f32[8,64,256]{2,1,0:T(8,128)S(1)}, f32[8,64,256]{2,1,0:T(8,128)}, u32[]{:S(2)}, u32[]{:S(2)}) collective-permute-start(f32[8,64,256]{2,1,0:T(8,128)S(1)} %get-tuple-element.83), channel_id=1, source_target_pairs={{0,64},{64,128},{128,192},{192,0},{1,65},{65,129},{129,193},{193,1... | collective-permute-start | bytes 1572872 | tf_op jit(solution)/shard_map/ppermute | solution.py:367
  43.9 22.2 %collective-permute-start.9 = (f32[8,64,256]{2,1,0:T(8,128)S(1)}, f32[8,64,256]{2,1,0:T(8,128)}, u32[]{:S(2)}, u32[]{:S(2)}) collective-permute-start(f32[8,64,256]{2,1,0:T(8,128)S(1)} %get-tuple-element.84), channel_id=1, source_target_pairs={{0,192},{64,0},{128,64},{192,128},{1,193},{65,1},{129,65},{193,129... | collective-permute-start | bytes 1572872 | tf_op jit(solution)/shard_map/ppermute | solution.py:367
  45.8 13.0 %collective-permute-start.5 = (f32[64,1024]{1,0:T(8,128)}, f32[64,1024]{1,0:T(8,128)S(1)}, u32[]{:S(2)}, u32[]{:S(2)}) collective-permute-start(f32[64,1024]{1,0:T(8,128)} %get-tuple-element.80), channel_id=1, source_target_pairs={{0,48},{16,0},{32,16},{48,32},{1,49},{17,1},{33,17},{49,33},{2,50}... | collective-permute-start | bytes 786440 | tf_op jit(solution)/shard_map/ppermute | solution.py:367
  48.0 14.3 %collective-permute-start.6 = (f32[64,1024]{1,0:T(8,128)S(1)}, f32[64,1024]{1,0:T(8,128)S(1)}, u32[]{:S(2)}, u32[]{:S(2)}) collective-permute-start(f32[64,1024]{1,0:T(8,128)S(1)} %get-tuple-element.81), channel_id=1, source_target_pairs={{0,16},{16,32},{32,48},{48,0},{1,17},{17,33},{33,49},{49,1},{2,18}... | collective-permute-start | bytes 786440 | tf_op jit(solution)/shard_map/ppermute | solution.py:367
  58.7 15.7 %copy-start.6 = (f32[64,1024]{1,0:T(8,128)}, f32[64,1024]{1,0:T(8,128)S(1)}, u32[]{:S(2)}) copy-start(f32[64,1024]{1,0:T(8,128)S(1)} %collective-permute-done.5.refs_0_.lo_ref) | copy-start | bytes 786436
  62.3 12.2 %copy-start.7 = (f32[64,1024]{1,0:T(8,128)}, f32[64,1024]{1,0:T(8,128)S(1)}, u32[]{:S(2)}) copy-start(f32[64,1024]{1,0:T(8,128)S(1)} %collective-permute-done.6.refs_1_.hi_ref) | copy-start | bytes 786436
  66.7 20.9 %collective-permute-start.11 = (f32[4,64,256]{2,1,0:T(8,128)S(1)}, f32[4,64,256]{2,1,0:T(8,128)S(1)}, u32[]{:S(2)}, u32[]{:S(2)}) collective-permute-start(f32[4,64,256]{2,1,0:T(8,128)S(1)} %get-tuple-element.96), channel_id=1, source_target_pairs={{0,128},{64,192},{128,0},{192,64},{1,129},{65,193},{129,1},{193,65... | collective-permute-start | bytes 786440 | tf_op jit(solution)/shard_map/ppermute | solution.py:367
  68.9 18.7 %collective-permute-start.12 = (f32[4,64,256]{2,1,0:T(8,128)S(1)}, f32[4,64,256]{2,1,0:T(8,128)S(1)}, u32[]{:S(2)}, u32[]{:S(2)}) collective-permute-start(f32[4,64,256]{2,1,0:T(8,128)S(1)} %get-tuple-element.97), channel_id=1, source_target_pairs={{0,64},{64,128},{128,192},{192,0},{1,65},{65,129},{129,193},{193,1... | collective-permute-start | bytes 786440 | tf_op jit(solution)/shard_map/ppermute | solution.py:367
  70.6 17.0 %collective-permute-start.13 = (f32[4,64,256]{2,1,0:T(8,128)S(1)}, f32[4,64,256]{2,1,0:T(8,128)S(1)}, u32[]{:S(2)}, u32[]{:S(2)}) collective-permute-start(f32[4,64,256]{2,1,0:T(8,128)S(1)} %get-tuple-element.98), channel_id=1, source_target_pairs={{0,192},{64,0},{128,64},{192,128},{1,193},{65,1},{129,65},{193,129... | collective-permute-start | bytes 786440 | tf_op jit(solution)/shard_map/ppermute | solution.py:367
  70.9 16.7 %collective-permute-start.10 = (f32[8,64,128]{2,1,0:T(8,128)S(1)}, f32[8,64,128]{2,1,0:T(8,128)S(1)}, u32[]{:S(2)}, u32[]{:S(2)}) collective-permute-start(f32[8,64,128]{2,1,0:T(8,128)S(1)} %get-tuple-element.94), channel_id=1, source_target_pairs={{0,2},{2,0},{1,3},{3,1},{4,6},{6,4},{5,7},{7,5},{8,10},{10,8},{9,1... | collective-permute-start | bytes 786440 | tf_op jit(solution)/shard_map/ppermute | solution.py:367
  74.5 13.1 %copy-start = (bf16[12,256,256]{2,1,0:T(8,128)(2,1)S(1)}, bf16[12,256,256]{2,1,0:T(8,128)(2,1)}, u32[]{:S(2)}) copy-start(bf16[12,256,256]{2,1,0:T(8,128)(2,1)} %shard_map.86.tiles_ref) | copy-start | bytes 4718596
  74.5 13.1 %copy-start.13 = (s32[12]{0:T(128)S(1)}, s32[12]{0:T(128)}, u32[]{:S(2)}) copy-start(s32[12]{0:T(128)} %reshape.219.refs_ref) | copy-start | bytes 148
  87.6 15.5 %copy-start.24 = (f32[8,64,128]{2,1,0:T(8,128)}, f32[8,64,128]{2,1,0:T(8,128)S(1)}, u32[]{:S(2)}) copy-start(f32[8,64,128]{2,1,0:T(8,128)S(1)} %collective-permute-done.10.other_ref) | copy-start | bytes 786436
  103.1 12.2 %copy-start.15 = (f32[16,64,128]{2,1,0:T(8,128)S(1)}, f32[16,64,128]{2,1,0:T(8,128)}, u32[]{:S(2)}) copy-start(f32[16,64,128]{2,1,0:T(8,128)} %all_to_all.30) | copy-start | bytes 1572868
  109.2 15.9 %all-to-all-start.2 = ((f32[16,64,128]{2,1,0:T(8,128)}), f32[16,64,128]{2,1,0:T(8,128)S(1)}, u32[]{:S(2)}, u32[]{:S(2)}) async-start(f32[16,64,128]{2,1,0:T(8,128)} %get-tuple-element.102), calls=%async_computation.2 | async-start | bytes 1048576 | tf_op jit(solution)/shard_map/all_to_all | solution.py:375
  115.3 2.0 collective-permute-start.15
  116.6 2.0 collective-permute-start.14
  125.1 43.7 %all-to-all-start.3 = ((f32[8,64,1280]{2,1,0:T(8,128)}), f32[8,64,1280]{2,1,0:T(8,128)}, u32[]{:S(2)}, u32[]{:S(2)}) async-start(f32[8,64,1280]{2,1,0:T(8,128)} %shard_map.92), calls=%async_computation.3 | async-start | bytes 5242880 | tf_op jit(solution)/shard_map/all_to_all | solution.py:468
  131.8 11.5 %collective-permute-start.16 = (f32[4,64,256]{2,1,0:T(8,128)S(1)}, f32[4,64,256]{2,1,0:T(8,128)S(1)}, u32[]{:S(2)}, u32[]{:S(2)}) collective-permute-start(f32[4,64,256]{2,1,0:T(8,128)S(1)} %get-tuple-element.106), channel_id=1, source_target_pairs={{0,128},{64,192},{128,0},{192,64},{1,129},{65,193},{129,1},{193,65... | collective-permute-start | bytes 786440 | tf_op jit(solution)/shard_map/ppermute | solution.py:367
  133.4 13.6 %collective-permute-start.17 = (f32[4,64,256]{2,1,0:T(8,128)S(1)}, f32[4,64,256]{2,1,0:T(8,128)S(1)}, u32[]{:S(2)}, u32[]{:S(2)}) collective-permute-start(f32[4,64,256]{2,1,0:T(8,128)S(1)} %get-tuple-element.107), channel_id=1, source_target_pairs={{0,192},{64,0},{128,64},{192,128},{1,193},{65,1},{129,65},{193,129... | collective-permute-start | bytes 786440 | tf_op jit(solution)/shard_map/ppermute | solution.py:367
  134.9 12.1 %collective-permute-start.18 = (f32[4,64,256]{2,1,0:T(8,128)S(1)}, f32[4,64,256]{2,1,0:T(8,128)S(1)}, u32[]{:S(2)}, u32[]{:S(2)}) collective-permute-start(f32[4,64,256]{2,1,0:T(8,128)S(1)} %get-tuple-element.108), channel_id=1, source_target_pairs={{0,64},{64,128},{128,192},{192,0},{1,65},{65,129},{129,193},{193,1... | collective-permute-start | bytes 786440 | tf_op jit(solution)/shard_map/ppermute | solution.py:367
  143.3 30.6 %copy-start.9 = (f32[8,64,256]{2,1,0:T(8,128)S(1)}, f32[8,64,256]{2,1,0:T(8,128)}, u32[]{:S(2)}) copy-start(f32[8,64,256]{2,1,0:T(8,128)} %get-tuple-element.128.up_ref) | copy-start | bytes 1572868
  143.3 30.6 %copy-start.10 = (f32[8,64,256]{2,1,0:T(8,128)S(1)}, f32[8,64,256]{2,1,0:T(8,128)}, u32[]{:S(2)}) copy-start(f32[8,64,256]{2,1,0:T(8,128)} %get-tuple-element.129.down_ref) | copy-start | bytes 1572868
  147.0 26.0 %collective-permute-start.19 = (f32[8,64,256]{2,1,0:T(8,128)}, f32[8,64,256]{2,1,0:T(8,128)S(1)}, u32[]{:S(2)}, u32[]{:S(2)}) collective-permute-start(f32[8,64,256]{2,1,0:T(8,128)} %get-tuple-element.112), channel_id=1, source_target_pairs={{0,128},{64,192},{128,0},{192,64},{1,129},{65,193},{129,1},{193,65... | collective-permute-start | bytes 1572872 | tf_op jit(solution)/shard_map/ppermute | solution.py:367
  148.6 25.3 %collective-permute-start.20 = (f32[8,64,256]{2,1,0:T(8,128)}, f32[8,64,256]{2,1,0:T(8,128)S(1)}, u32[]{:S(2)}, u32[]{:S(2)}) collective-permute-start(f32[8,64,256]{2,1,0:T(8,128)} %get-tuple-element.113), channel_id=1, source_target_pairs={{0,192},{64,0},{128,64},{192,128},{1,193},{65,1},{129,65},{193,129... | collective-permute-start | bytes 1572872 | tf_op jit(solution)/shard_map/ppermute | solution.py:367
  150.0 23.9 %collective-permute-start.21 = (f32[8,64,256]{2,1,0:T(8,128)}, f32[8,64,256]{2,1,0:T(8,128)S(1)}, u32[]{:S(2)}, u32[]{:S(2)}) collective-permute-start(f32[8,64,256]{2,1,0:T(8,128)} %get-tuple-element.114), channel_id=1, source_target_pairs={{0,64},{64,128},{128,192},{192,0},{1,65},{65,129},{129,193},{193,1... | collective-permute-start | bytes 1572872 | tf_op jit(solution)/shard_map/ppermute | solution.py:367
  154.0 19.1 %collective-permute-start.22 = (f32[4,64,256]{2,1,0:T(8,128)}, f32[4,64,256]{2,1,0:T(8,128)S(1)}, u32[]{:S(2)}, u32[]{:S(2)}) collective-permute-start(f32[4,64,256]{2,1,0:T(8,128)} %get-tuple-element.120), channel_id=1, source_target_pairs={{0,16},{16,32},{32,48},{48,0},{1,17},{17,33},{33,49},{49,1},{2,18}... | collective-permute-start | bytes 786440 | tf_op jit(solution)/shard_map/ppermute | solution.py:367
  154.0 19.0 %collective-permute-start.23 = (f32[4,64,256]{2,1,0:T(8,128)S(1)}, f32[4,64,256]{2,1,0:T(8,128)S(1)}, u32[]{:S(2)}, u32[]{:S(2)}) collective-permute-start(f32[4,64,256]{2,1,0:T(8,128)S(1)} %get-tuple-element.121), channel_id=1, source_target_pairs={{0,48},{16,0},{32,16},{48,32},{1,49},{17,1},{33,17},{49,33},{2,50}... | collective-permute-start | bytes 786440 | tf_op jit(solution)/shard_map/ppermute | solution.py:367
  173.0 16.7 %copy-start.23 = (f32[4,64,256]{2,1,0:T(8,128)S(1)}, f32[4,64,256]{2,1,0:T(8,128)}, u32[]{:S(2)}) copy-start(f32[4,64,256]{2,1,0:T(8,128)} %get-tuple-element.140) | copy-start | bytes 786436
  175.8 27.1 %copy-start.8 = (f32[8,64,256]{2,1,0:T(8,128)S(1)}, f32[8,64,256]{2,1,0:T(8,128)}, u32[]{:S(2)}) copy-start(f32[8,64,256]{2,1,0:T(8,128)} %get-tuple-element.141.diag_ref) | copy-start | bytes 1572868
  175.8 34.1 %collective-permute-start.27 = (f32[8,64,256]{2,1,0:T(8,128)}, f32[8,64,256]{2,1,0:T(8,128)S(1)}, u32[]{:S(2)}, u32[]{:S(2)}) collective-permute-start(f32[8,64,256]{2,1,0:T(8,128)} %get-tuple-element.142), channel_id=1, source_target_pairs={{0,16},{16,32},{32,48},{48,0},{1,17},{17,33},{33,49},{49,1},{2,18}... | collective-permute-start | bytes 1572872 | tf_op jit(solution)/shard_map/ppermute | solution.py:367
  176.0 33.9 %collective-permute-start.28 = (f32[8,64,256]{2,1,0:T(8,128)}, f32[8,64,256]{2,1,0:T(8,128)S(1)}, u32[]{:S(2)}, u32[]{:S(2)}) collective-permute-start(f32[8,64,256]{2,1,0:T(8,128)} %get-tuple-element.143), channel_id=1, source_target_pairs={{0,48},{16,0},{32,16},{48,32},{1,49},{17,1},{33,17},{49,33},{2,50}... | collective-permute-start | bytes 1572872 | tf_op jit(solution)/shard_map/ppermute | solution.py:367
  180.7 16.0 %all-to-all-start.4 = ((f32[4,64,256]{2,1,0:T(8,128)}), f32[4,64,256]{2,1,0:T(8,128)S(1)}, u32[]{:S(2)}, u32[]{:S(2)}) async-start(f32[4,64,256]{2,1,0:T(8,128)} %copy.42), calls=%async_computation.4 | async-start | bytes 524288 | tf_op jit(solution)/shard_map/all_to_all | solution.py:484
  186.2 16.7 %collective-permute-start.24 = (f32[4,64,256]{2,1,0:T(8,128)}, f32[4,64,256]{2,1,0:T(8,128)S(1)}, u32[]{:S(2)}, u32[]{:S(2)}) collective-permute-start(f32[4,64,256]{2,1,0:T(8,128)} %get-tuple-element.138), channel_id=1, source_target_pairs={{0,128},{64,192},{128,0},{192,64},{1,129},{65,193},{129,1},{193,65... | collective-permute-start | bytes 786440 | tf_op jit(solution)/shard_map/ppermute | solution.py:367
  188.3 14.6 %collective-permute-start.25 = (f32[4,64,256]{2,1,0:T(8,128)}, f32[4,64,256]{2,1,0:T(8,128)S(1)}, u32[]{:S(2)}, u32[]{:S(2)}) collective-permute-start(f32[4,64,256]{2,1,0:T(8,128)} %get-tuple-element.139), channel_id=1, source_target_pairs={{0,192},{64,0},{128,64},{192,128},{1,193},{65,1},{129,65},{193,129... | collective-permute-start | bytes 786440 | tf_op jit(solution)/shard_map/ppermute | solution.py:367
  189.7 13.1 %collective-permute-start.26 = (f32[4,64,256]{2,1,0:T(8,128)S(1)}, f32[4,64,256]{2,1,0:T(8,128)S(1)}, u32[]{:S(2)}, u32[]{:S(2)}) collective-permute-start(f32[4,64,256]{2,1,0:T(8,128)S(1)} %copy-done.23), channel_id=1, source_target_pairs={{0,64},{64,128},{128,192},{192,0},{1,65},{65,129},{129,193},{193,1... | collective-permute-start | bytes 786440 | tf_op jit(solution)/shard_map/ppermute | solution.py:367
  197.7 11.4 %all-to-all-start.5 = ((f32[4,32,128]{2,1,0:T(8,128)}), f32[4,32,128]{2,1,0:T(8,128)S(1)}, u32[]{:S(2)}, u32[]{:S(2)}) async-start(f32[4,32,128]{2,1,0:T(8,128)} %reshape.230), calls=%async_computation.5 | async-start | bytes 131072 | tf_op jit(solution)/shard_map/all_to_all | solution.py:486
  (12 other events, 43.2 us)
Sparse Core Ops, SparseCore 0:
  40.2 45.3 all-gather.1
